TPU v7x, 32 devices: a whole 2x2x4 slice. The times are simulated.
32 devices in a mesh: dp: 4 (over y, core), space: 8 (over z, x).
Axes of the slice: x: 2, y: 2, z: 4, core: 2. Of those that a mesh axis runs over, the one named last changes fastest.
Arguments:
- snapshot: bfloat16 [4, 32, 64, 1024], P('dp', 'space'), may hold values from -6 to 6
- conv_one: bfloat16 [864, 128], replicated, may hold values from -0.21875 to 0.21875
- conv_two: bfloat16 [3456, 256], replicated, may hold values from -0.0546875 to 0.0546875
- cotangent: bfloat16 [4, 256, 8, 128], P('dp', 'space'), may hold values from -0.046875 to 0.046875
Outputs:
- latent: bfloat16 [4, 256, 8, 128], P('dp', 'space')
- grad_one: float32 [128, 864], P('space')
- grad_two: float32 [256, 3456], P('space')
All inputs are finite; a program needn't handle non-finite values.
Results may differ from a plain program's by a relative error of at most 0.0049.
Values may be sent and summed in bfloat16 or wider, within the bound.
No kernel may reach another device: no remote copies, remote signals or barrier semaphores. Data moves between devices by JAX's collectives and lax.ppermute only.
A program may use at most 64 MiB of HBM per device.

v0:
```python
import jax
import jax.numpy as jnp
from jax import lax
from jax.sharding import PartitionSpec as P


def from_behind(block, axis, distance):
    devices = range(lax.axis_size(axis))
    route = [(i - distance, i) for i in devices if i - distance in devices]
    return lax.ppermute(block, axis, route)


def patches(padded, out_x, out_y, out_z):
    channels = padded.shape[3]
    grown = jnp.pad(padded, ((0, 1), (0, 1), (0, 1), (0, 0)))
    phased = grown.reshape(out_x + 1, 2, out_y + 1, 2, out_z + 1, 2, channels)
    pieces = []
    for tap_x in range(3):
        for tap_y in range(3):
            for tap_z in range(3):
                start = (tap_x // 2, tap_x % 2, tap_y // 2, tap_y % 2, tap_z // 2, tap_z % 2, 0)
                limit = (
                    tap_x // 2 + out_x,
                    tap_x % 2 + 1,
                    tap_y // 2 + out_y,
                    tap_y % 2 + 1,
                    tap_z // 2 + out_z,
                    tap_z % 2 + 1,
                    channels,
                )
                pieces.append(
                    lax.slice(phased, start, limit).reshape(out_x, out_y, out_z, channels)
                )
    stacked = jnp.concatenate(pieces, axis=3)
    return stacked.reshape(out_x * out_y * out_z, 27 * channels)


def fold_axis(blocks, space, tap):
    first_tap = lax.index_in_dim(blocks, 0, tap, keepdims=False)
    middle_tap = lax.index_in_dim(blocks, 1, tap, keepdims=False)
    last_tap = lax.index_in_dim(blocks, 2, tap, keepdims=False)
    after = [(0, 0)] * first_tap.ndim
    before = [(0, 0)] * first_tap.ndim
    after[space] = (0, 1)
    before[space] = (1, 0)
    even_cells = jnp.pad(first_tap, after) + jnp.pad(last_tap, before)
    odd_cells = jnp.pad(middle_tap, after)
    joined = jnp.stack([even_cells, odd_cells], axis=space + 1)
    shape = list(even_cells.shape)
    shape[space] = 2 * shape[space]
    return joined.reshape(shape)


def spread_taps(back_rows, out_x, out_y, out_z):
    channels = back_rows.shape[1] // 27
    blocks = back_rows.reshape(out_x, out_y, out_z, 3, 3, 3, channels)
    blocks = fold_axis(blocks, 2, 5)
    blocks = fold_axis(blocks, 1, 4)
    blocks = fold_axis(blocks, 0, 3)
    return blocks[: 2 * out_x + 1, : 2 * out_y + 1, : 2 * out_z + 1]


def silu_slope(values):
    logistic = jax.nn.sigmoid(values)
    return logistic * (1.0 + values * (1.0 - logistic))


def on_device(snapshot, conv_one, conv_two, cotangent):
    in_width = conv_one.shape[0] // 27
    mid_width = conv_one.shape[1]
    out_width = conv_two.shape[1]
    slab_cells = snapshot[0]
    extent_x, extent_y = (slab_cells.shape[0], slab_cells.shape[1])
    fine_grid = slab_cells.reshape(extent_x, extent_y, -1, in_width)
    extent_z = fine_grid.shape[2]
    half_x, half_y, half_z = (extent_x // 2, extent_y // 2, extent_z // 2)
    quarter_x, quarter_y, quarter_z = (extent_x // 4, extent_y // 4, extent_z // 4)
    lower_plane = from_behind(slab_cells[extent_x - 1 :], "space", 1)
    joined = jnp.concatenate(
        [lower_plane.reshape(1, extent_y, extent_z, in_width), fine_grid], axis=0
    )
    padded = jnp.pad(joined, ((0, 0), (1, 0), (1, 0), (0, 0)))
    patch_one = patches(padded, half_x, half_y, half_z)
    hidden_pre = jnp.dot(patch_one, conv_one, preferred_element_type=jnp.float32)
    hidden = jax.nn.silu(hidden_pre).astype(jnp.bfloat16)
    act_grid = hidden.reshape(half_x, half_y, half_z, mid_width)
    act_lower = from_behind(act_grid[half_x - 1 :], "space", 1)
    act_pad = jnp.pad(
        jnp.concatenate([act_lower, act_grid], axis=0), ((0, 0), (1, 0), (1, 0), (0, 0))
    )
    patch_two = patches(act_pad, quarter_x, quarter_y, quarter_z)
    latent_rows = jnp.dot(patch_two, conv_two, preferred_element_type=jnp.float32).astype(
        jnp.bfloat16
    )
    latent_slab = latent_rows.reshape(quarter_x, -1, out_width).transpose(2, 0, 1)
    latent = lax.all_to_all(latent_slab, "space", split_axis=0, concat_axis=1, tiled=True)[None]
    upstream = lax.all_to_all(cotangent[0], "space", split_axis=1, concat_axis=0, tiled=True)
    grad_grid = upstream.transpose(1, 2, 0)
    grad_rows = grad_grid.reshape(-1, out_width)
    term_two = lax.dot_general(
        patch_two, grad_rows, (((0,), (0,)), ((), ())), preferred_element_type=jnp.float32
    ).T
    back_rows = lax.dot_general(
        grad_rows, conv_two, (((1,), (1,)), ((), ())), preferred_element_type=jnp.float32
    )
    grad_pad = spread_taps(back_rows, quarter_x, quarter_y, quarter_z)
    upper_plane = from_behind(grad_pad[0:1, 1:, 1:], "space", -1)
    grad_act = jnp.concatenate(
        [grad_pad[1:half_x, 1:, 1:], grad_pad[half_x:, 1:, 1:] + upper_plane], axis=0
    )
    grad_pre = (grad_act.reshape(-1, mid_width) * silu_slope(hidden_pre)).astype(jnp.bfloat16)
    term_one = lax.dot_general(
        patch_one, grad_pre, (((0,), (0,)), ((), ())), preferred_element_type=jnp.float32
    ).T
    summed = lax.psum((term_one, term_two), "dp")
    shares = (
        lax.psum_scatter(summed[0], "space", scatter_dimension=0, tiled=True),
        lax.psum_scatter(summed[1], "space", scatter_dimension=0, tiled=True),
    )
    return (latent, shares[0], shares[1])


def solution(mesh):
    placed = (P("dp", "space", None, None), P(), P(), P("dp", "space", None, None))
    return jax.shard_map(
        on_device,
        mesh=mesh,
        in_specs=placed,
        out_specs=(P("dp", "space", None, None), P("space", None), P("space", None)),
        check_vma=False,
    )
```

profile of v0, /device:TPU:0, one launch (start us, length us, event | category | flops | bytes accessed | tf_op | source)
XLA Modules:
  0.0 328.7 jit_solution(645473647259848543)
XLA Ops:
  7.2 1.6 copy.254
  8.8 7.3 %all-to-all-start.1 = ((bf16[32,8,128]{2,0,1:T(8,128)(2,1)}), bf16[32,8,128]{2,0,1:T(8,128)(2,1)S(1)}, u32[]{:S(2)}, u32[]{:S(2)}) async-start(bf16[32,8,128]{2,0,1:T(8,128)(2,1)} %bitcast.179), calls=%async_computation.1 | async-start | bytes 131072 | tf_op jit(solution)/shard_map/all_to_all | solution.py:97
  16.1 1.5 copy.144
  17.6 0.7 slice_bitcast_fusion.9
  18.3 3.9 %collective-permute-start = (bf16[1,64,1024]{1,2,0:T(8,128)(2,1)}, bf16[1,64,1024]{1,2,0:T(8,128)(2,1)S(1)}, u32[]{:S(2)}, u32[]{:S(2)}) collective-permute-start(bf16[1,64,1024]{1,2,0:T(8,128)(2,1)} %slice_bitcast_fusion.9), channel_id=1, source_target_pairs={{0,1},{1,2},{2,3},{3,4},{4,5},{5,6},{6,7},{8,9},{9,10},{10,11},{11... | collective-permute-start | bytes 393224 | tf_op jit(solution)/shard_map/ppermute | solution.py:10
  22.2 0.7 all-to-all-done.1
  23.1 0.7 convolution_bitcast_fusion.1
  24.3 0.4 copy.181
  25.1 1.0 copy.184
  26.0 0.6 slice_bitcast_fusion.8
  26.9 0.5 add_bitcast_fusion.2
  27.4 0.5 pad_maximum_fusion.3
  27.9 0.6 copy.185
  28.6 1.0 copy-done.3
  29.6 1.2 fusion.11
  30.8 1.5 collective-permute-start.2
  32.3 1.3 pad_maximum_fusion.2
  33.6 3.9 %copy.225 = bf16[5,64,32,32]{3,1,2,0:T(8,128)(2,1)} copy(bf16[5,64,32,32]{1,3,2,0:T(8,128)(2,1)} %pad_maximum_fusion.2) | data formatting | bytes 1310720
  37.6 4.9 %pad.74 = bf16[6,66,34,32]{3,1,2,0:T(8,128)(2,1)} pad(bf16[5,64,32,32]{3,1,2,0:T(8,128)(2,1)} %copy.225, bf16[]{:T(256)} %constant.6.clone.1), padding=0_1x1_1x1_1x0_0 | pad | bytes 1517058 | tf_op jit(solution)/shard_map/jit(_pad)/pad | solution.py:15
  42.4 8.2 %reshape.213 = bf16[3,2,33,2,17,2,32]{6,3,2,5,4,1,0:T(2,128)(2,1)} reshape(bf16[6,66,34,32]{3,1,2,0:T(8,128)(2,1)} %pad.74) | data formatting | bytes 1723392 | tf_op jit(solution)/shard_map/reshape | solution.py:16
  50.6 15.0 %fusion.9 = (bf16[2,1,32,1,16,1,32]{6,3,2,5,4,1,0:T(2,128)(2,1)S(1)}, bf16[2,1,32,1,16,1,32]{6,3,2,5,4,1,0:T(2,128)(2,1)S(1)}, bf16[2,1,32,1,16,1,32]{6,3,2,5,4,...) fusion(bf16[3,2,33,2,17,2,32]{6,3,2,5,4,1,0:T(2,128)(2,1)} %res, ...), kind=kLoop, calls=%fused_computation.67 | loop fusion | bytes 2490368 | tf_op jit(solution)/shard_map/slice | solution.py:32
  65.6 5.1 %fusion.10 = (bf16[2,1,32,1,16,1,32]{6,3,2,5,4,1,0:T(2,128)(2,1)S(1)}, bf16[2,1,32,1,16,1,32]{6,3,2,5,4,1,0:T(2,128)(2,1)S(1)}, bf16[2,1,32,1,16,1,32]{6,3,2,5,4...) fusion(bf16[3,2,33,2,17,2,32]{6,3,2,5,4,1,0:T(2,128)(2,1)S(1)} , ...), kind=kLoop, calls=%fused_computation.68 | loop fusion | bytes 1048576 | tf_op jit(solution)/shard_map/slice | solution.py:32
  72.7 1.0 copy.161
  73.7 1.0 copy.162
  74.7 1.0 copy.163
  75.7 1.0 copy.164
  76.7 1.0 copy.165
  77.7 1.0 copy.166
  78.8 1.0 copy.167
  79.8 1.0 copy.168
  80.8 1.0 copy.169
  81.8 1.0 copy.170
  82.8 1.0 copy.171
  83.9 1.0 copy.172
  84.9 1.0 copy.173
  85.9 1.0 copy.154
  87.0 1.0 copy.147
  88.0 1.0 copy.148
  89.0 1.0 copy.149
  90.0 1.0 copy.150
  91.0 1.0 copy.151
  92.1 1.0 copy.152
  93.1 1.0 copy.153
  94.1 7.9 %concatenate.153 = bf16[1024,864]{1,0:T(8,128)(2,1)} concatenate(bf16[1024,32]{1,0:T(8,128)(2,1)} %bitcast.208, bf16[1024,32]{1,0:T(8,128)(2,1)} %bitcast.209, bf16[1024,32]{1,0:T(8,128)(2,1)} %bitcast.210, bf16[1024,32]{1,0:T(8,128)(2,1)} %bitcast.211, bf16[1024,32]{1,0:T(8,128)(2,1)} %bitcast.212, bf16[1024,32]{1,0:T(8,128)(2,1)} %bitcast.213, bf16[1024,32]{1,0:T(8,128)(2,1)} %bitcast.214, ...), dimensions={1} | concatenate | bytes 3538944 | tf_op jit(solution)/shard_map/concatenate | solution.py:34
  102.1 1.9 slice_add_fusion
  103.9 1.4 pad_maximum_fusion.4
  105.4 0.8 fusion.7
  106.4 4.8 %collective-permute-start.1 = (bf16[1,32,16,128]{3,0,2,1:T(2,128)(2,1)S(1)}, bf16[1,32,16,128]{3,0,2,1:T(2,128)(2,1)S(1)}, u32[]{:S(2)}, u32[]{:S(2)}) collective-permute-start(bf16[1,32,16,128]{3,0,2,1:T(2,128)(2,1)S(1)} %copy.174), channel_id=1, source_target_pairs={{0,1},{1,2},{2,3},{3,4},{4,5},{5,6},{6,7},{8,9},{9,10},{10,11},{11... | collective-permute-start | bytes 393224 | tf_op jit(solution)/shard_map/ppermute | solution.py:10
  111.5 3.3 %collective-permute-done.1 = bf16[1,32,16,128]{3,0,2,1:T(2,128)(2,1)S(1)} collective-permute-done((bf16[1,32,16,128]{3,0,2,1:T(2,128)(2,1)S(1)}, bf16[1,32,16,128]{3,0,2,1:T(2,128)(2,1)S(1)}, u32[]{:S(2)}, u32[]{:S(2)}) %collective-permute-start.1) | collective-permute-done | bytes 131104 | tf_op jit(solution)/shard_map/ppermute | solution.py:10
  114.9 0.6 fusion.5
  116.0 0.9 fusion.12
  117.5 2.5 convolution_bitcast_fusion
  119.9 5.2 %copy.190 = f32[256,3456]{1,0:T(8,128)} copy(f32[256,3456]{0,1:T(8,128)} %convolution_bitcast_fusion) | data formatting | bytes 7077888
  125.2 2.7 fusion.14
  128.0 78.8 %reduce-scatter.7.cloned.1.call-done = f32[32,3456]{1,0:T(8,128)} async-done(((f32[256,3456]{1,0:T(8,128)}), f32[32,3456]{1,0:T(8,128)}) %reduce-scatter.7.cloned.1.call-update) | async-done | bytes 442384
  206.8 2.8 copy.191
  210.1 0.5 broadcast.39
  210.6 0.7 reduce
  211.4 11.2 %all_to_all.33 = bf16[8,2,2048]{2,1,0:T(2,128)(2,1)S(1)} all-to-all(bf16[8,2,2048]{2,1,0:T(2,128)(2,1)S(1)} %reshape.227), channel_id=1, replica_groups=mesh['dp'=4,'space'=8] {'space'}, dimensions={0} | all-to-all | bytes 131072 | tf_op jit(solution)/shard_map/all_to_all | solution.py:96
  222.7 0.7 copy.187
  223.4 48.2 %reduce-scatter.5.cloned.1.call-done = f32[16,864]{1,0:T(8,128)} async-done(((f32[128,864]{1,0:T(8,128)}), f32[16,864]{1,0:T(8,128)}) %reduce-scatter.5.cloned.1.call-update) | async-done | bytes 55312 | tf_op jit(solution)/shard_map/reduce_scatter | solution.py:117
  271.6 12.4 %psum.16 = f32[16,864]{1,0:T(8,128)} all-reduce(f32[16,864]{1,0:T(8,128)} %reduce-scatter.5.cloned.1.call-done), channel_id=1, replica_groups=mesh['dp'=4,'space'=8] {'dp'}, use_global_device_ids=true, to_apply=%region_0.1 | all-reduce | flops 13824 | bytes 110592 | tf_op jit(solution)/shard_map/psum | solution.py:115
  284.0 35.4 %all-reduce.15.cloned.1.call-done = f32[32,3456]{0,1:T(8,128)} async-done(((f32[32,3456]{0,1:T(8,128)}), f32[32,3456]{0,1:T(8,128)}) %all-reduce.15.cloned.1.call-update) | async-done | bytes 442384 | tf_op jit(solution)/shard_map/psum | solution.py:115
  319.4 2.7 copy.188
  (70 shorter events, 5.3 us)
Async XLA Ops:
  7.2 15.9 %copy-start = (bf16[3456,256]{1,0:T(8,128)(2,1)S(1)}, bf16[3456,256]{1,0:T(8,128)(2,1)}, u32[]{:S(2)}) copy-start(bf16[3456,256]{1,0:T(8,128)(2,1)} %param.6) | copy-start | bytes 5308420
  8.8 14.2 %all-to-all-start.1 = ((bf16[32,8,128]{2,0,1:T(8,128)(2,1)}), bf16[32,8,128]{2,0,1:T(8,128)(2,1)S(1)}, u32[]{:S(2)}, u32[]{:S(2)}) async-start(bf16[32,8,128]{2,0,1:T(8,128)(2,1)} %bitcast.179), calls=%async_computation.1 | async-start | bytes 131072 | tf_op jit(solution)/shard_map/all_to_all | solution.py:97
  16.0 190.8 %reduce-scatter.7.cloned.1.call-start = ((), (), s32[]{:S(2)}) async-start(), calls=%async_computation.6 | async-start | bytes 3981312
  18.3 14.0 %collective-permute-start = (bf16[1,64,1024]{1,2,0:T(8,128)(2,1)}, bf16[1,64,1024]{1,2,0:T(8,128)(2,1)S(1)}, u32[]{:S(2)}, u32[]{:S(2)}) collective-permute-start(bf16[1,64,1024]{1,2,0:T(8,128)(2,1)} %slice_bitcast_fusion.9), channel_id=1, source_target_pairs={{0,1},{1,2},{2,3},{3,4},{4,5},{5,6},{6,7},{8,9},{9,10},{10,11},{11... | collective-permute-start | bytes 393224 | tf_op jit(solution)/shard_map/ppermute | solution.py:10
  28.6 1.0 copy-start.3
  30.8 71.2 %collective-permute-start.2 = (f32[1,32,16,128]{3,0,2,1:T(1,128)}, f32[1,32,16,128]{3,0,2,1:T(1,128)}, u32[]{:S(2)}, u32[]{:S(2)}) collective-permute-start(f32[1,32,16,128]{3,0,2,1:T(1,128)} %get-tuple-element.52), channel_id=1, source_target_pairs={{1,0},{2,1},{3,2},{4,3},{5,4},{6,5},{7,6},{9,8},{10,9},{11,10},{12... | collective-permute-start | bytes 786440 | tf_op jit(solution)/shard_map/ppermute | solution.py:10
  50.6 15.0 %copy-start.1 = (bf16[3,2,33,2,17,2,32]{6,3,2,5,4,1,0:T(2,128)(2,1)S(1)}, bf16[3,2,33,2,17,2,32]{6,3,2,5,4,1,0:T(2,128)(2,1)}, u32[]{:S(2)}) copy-start(bf16[3,2,33,2,17,2,32]{6,3,2,5,4,1,0:T(2,128)(2,1)} %reshape.213) | copy-start | bytes 2585092
  102.0 3.4 %copy-start.2 = (bf16[1024,864]{1,0:T(8,128)(2,1)S(1)}, bf16[1024,864]{1,0:T(8,128)(2,1)}, u32[]{:S(2)}) copy-start(bf16[1024,864]{1,0:T(8,128)(2,1)} %concatenate.153) | copy-start | bytes 5308420
  102.0 3.4 %copy-start.4 = (bf16[864,128]{1,0:T(8,128)(2,1)S(1)}, bf16[864,128]{1,0:T(8,128)(2,1)}, u32[]{:S(2)}) copy-start(bf16[864,128]{1,0:T(8,128)(2,1)} %param.5) | copy-start | bytes 663556
  106.4 8.4 %collective-permute-start.1 = (bf16[1,32,16,128]{3,0,2,1:T(2,128)(2,1)S(1)}, bf16[1,32,16,128]{3,0,2,1:T(2,128)(2,1)S(1)}, u32[]{:S(2)}, u32[]{:S(2)}) collective-permute-start(bf16[1,32,16,128]{3,0,2,1:T(2,128)(2,1)S(1)} %copy.174), channel_id=1, source_target_pairs={{0,1},{1,2},{2,3},{3,4},{4,5},{5,6},{6,7},{8,9},{9,10},{10,11},{11... | collective-permute-start | bytes 393224 | tf_op jit(solution)/shard_map/ppermute | solution.py:10
  125.1 146.5 %reduce-scatter.5.cloned.1.call-start = ((), (), s32[]{:S(2)}) async-start(), calls=%async_computation.4 | async-start | bytes 516096 | tf_op jit(solution)/shard_map/reduce_scatter | solution.py:117
  127.9 191.4 %all-reduce.15.cloned.1.call-start = ((), (), s32[]{:S(2)}) async-start(), calls=%async_computation.5 | async-start | bytes 3538944 | tf_op jit(solution)/shard_map/psum | solution.py:115
Sparse Core Ops, SparseCore 0:
  125.2 81.5 reduce-scatter.6
  210.1 61.4 reduce-scatter.4
  274.1 45.1 all-reduce.14
where the time goes:
time: 330 us; the launch traced here: 329 us
  waiting for transfers between devices  167 us (51%)
  local copies, waits for them, and re-layouts  92.2 us (28%)
  blocking collectives  23.6 us (7%)
  starting transfers between devices  17.5 us (5%)
  between operations  14.3 us (4%)
  other arithmetic  7.38 us (2%)
  matrix products  7.11 us (2%)
    unnamed x4, waiting for transfers between devices  78.9 us
    reduce_scatter x1, waiting for transfers between devices, on_device(): lax.psum_scatter(summed[0], 'space', scatter_dimension=0, tiled=True)  48.2 us
    slice x31, local copies, waits for them, and re-layouts, patches(): lax.slice(phased, start, limit).reshape(out_x, out_y, out_z, channels)  44.7 us
    psum x1, waiting for transfers between devices, on_device(): summed = lax.psum((term_one, term_two), 'dp')  35.4 us
    unnamed x47, local copies, waits for them, and re-layouts  20.1 us
    psum x1, blocking collectives, on_device(): summed = lax.psum((term_one, term_two), 'dp')  12.4 us
    all_to_all x1, blocking collectives, on_device(): lax.all_to_all(latent_slab, 'space', split_axis=0, concat_axis=1, tiled=T...  11.2 us
    ppermute x3, starting transfers between devices, from_behind(): return lax.ppermute(block, axis, route)  10.2 us
  transfers between devices with their start and end apart: 7, of which 5 were waited for; matrix products, arithmetic and copies ran while one was open for 26% of the time, Pallas kernels for 0%

commit v1 on v0

v1 whole, which is shorter than its diff:
```python
import functools

import jax
import jax.numpy as jnp
from jax import lax
from jax.experimental import pallas as pl
from jax.experimental.pallas import tpu as pltpu
from jax.sharding import PartitionSpec as P

F32 = jnp.float32
BF16 = jnp.bfloat16
VMEM_LIMIT = 40 * 1024 * 1024

NJ, NK, CELLS = 16, 8, 128
TAP_PHASE = {0: (1, 1), 1: (0, 0), 2: (1, 0)}


def dot(a, b):
    return jnp.dot(a, b, preferred_element_type=F32)


def iota(shape, axis):
    return lax.broadcasted_iota(jnp.int32, shape, axis)


def one_hot(mask):
    return jnp.where(mask, 1.0, 0.0).astype(BF16)


def cell_order(shifted):
    width = CELLS * (4 if shifted else 1)
    row, col = iota((CELLS, width), 0), iota((CELLS, width), 1)
    v, cell = col // CELLS, col % CELLS
    to_j, to_k = cell % NJ + v // 2, cell // NJ + v % 2
    return one_hot((to_k < NK) & (row == to_j * NK + to_k))


def kernel_a(snap, halo, w1, h0, h1, slope_t, p1, w_ext):
    row, col = iota((80, 64), 0), iota((80, 64), 1)
    pick = one_hot(col == 4 * (row % NJ) + row // NJ - 1)
    for plane in range(5):
        rows = halo[0] if plane == 0 else snap[plane - 1]
        picked = dot(pick, rows).astype(BF16)
        for i in range(2):
            a = plane - 2 * i
            if not 0 <= a <= 2:
                continue
            for p in range(2):
                for b in range(3):
                    rho = 2 * p + b
                    for k in range(NK):
                        at = (2 * i + p) * CELLS + k * NJ
                        p1[at : at + NJ, (3 * a + b) * 128 : (3 * a + b + 1) * 128] = picked[
                            rho * NJ : (rho + 1) * NJ, k * 128 : (k + 1) * 128
                        ]
    for t in range(9):
        base, src = t * 128, t * 96
        zeros = jnp.zeros((128, 128), BF16)
        w_ext[base : base + 64, 0:128] = w1[src + 32 : src + 96, :]
        w_ext[base + 64 : base + 128, 0:128] = zeros[:64]
        w_ext[base : base + 32, 128:256] = zeros[:32]
        w_ext[base + 32 : base + 128, 128:256] = w1[src : src + 96, :]
        w_ext[base : base + 96, 256:384] = zeros[:96]
        w_ext[base + 96 : base + 128, 256:384] = w1[src : src + 32, :]
    for i in range(2):
        hidden = h0 if i == 0 else h1
        for p in range(2):
            at = (2 * i + p) * CELLS
            full = dot(p1[at : at + CELLS, :], w_ext[...])
            before = jnp.concatenate(
                [jnp.zeros((NJ, 128), F32), full[: CELLS - NJ, 256:384]], axis=0
            )
            for q, pre in enumerate((full[:, 0:128] + before, full[:, 128:256])):
                logistic = 1.0 / (1.0 + jnp.exp(-pre))
                hidden[2 * p + q] = (pre * logistic).astype(BF16)
                slope = logistic * (1.0 + pre * (1.0 - logistic))
                slope_t[4 * i + 2 * p + q] = slope.T


def kernel_b(pieces, rows_per, place, cot, w2, slope_t, p1, *rest):
    outs, (grad_t,) = rest[:-1], rest[-1:]
    sources = cot.shape[0]
    moved = dot(cot[...].reshape(-1, CELLS), cell_order(True))
    moved = moved.reshape(sources * pieces, 2, rows_per, 4 * CELLS)
    planes = [moved[:, s].reshape(-1, 4 * CELLS).astype(BF16) for s in range(2)]
    for i in range(2):
        for p in range(2):
            for q in range(2):
                total = None
                for a in (1,) if i == 0 else (2, 0):
                    source = planes[1 if a == 0 else 0]
                    for b in (1,) if p == 0 else (2, 0):
                        for c in (1,) if q == 0 else (2, 0):
                            v = 2 * (b == 0) + (c == 0)
                            tap = 9 * a + 3 * b + c
                            term = dot(
                                w2[tap * 128 : (tap + 1) * 128, :],
                                source[:, v * CELLS : (v + 1) * CELLS],
                            )
                            total = term if total is None else total + term
                pre_t = total * slope_t[4 * i + 2 * p + q]
                at = (2 * i + p) * CELLS
                grad_t[q * 128 : (q + 1) * 128, at : at + CELLS] = pre_t.astype(BF16)
                if q == 0:
                    ahead = pltpu.roll(pre_t, CELLS - NJ, axis=1)
                    ahead = jnp.where(iota((128, CELLS), 1) < CELLS - NJ, ahead, 0.0)
                    grad_t[256:384, at : at + CELLS] = ahead.astype(BF16)
    lane = iota((128, 128), 1)
    frames = []
    for t in range(9):
        full = dot(grad_t[...], p1[:, t * 128 : (t + 1) * 128])
        side = jnp.where(lane < 64, full[0:128], full[256:384])
        side = jnp.where((lane < 64) | (lane >= 96), side, 0.0)
        own = jnp.where(lane < 32, 0.0, full[128:256])
        frames.append(own + pltpu.roll(side, 64, axis=1))
    if pieces == 1:
        for t in range(9):
            outs[0][:, t * 128 : (t + 1) * 128] = frames[t]
        return
    owned = 128 // sources
    share = owned // pieces
    frames = [frame.astype(BF16) for frame in frames]
    for k in range(pieces):
        q = place[0] ^ k
        height = sources * 2 * share
        row, col = iota((height, 128), 0), iota((height, 128), 1)
        chosen = one_hot(col == row // (2 * share) * owned + q * share + row % share)
        for t in range(5):
            low = dot(chosen, frames[t])
            high = dot(chosen, frames[t + 5]) if t < 4 else jnp.zeros_like(low)
            half = iota(low.shape, 0) % (2 * share) // share
            outs[k][:, t * 128 : (t + 1) * 128] = jnp.where(half == 0, low, high).astype(BF16)


def kernel_latent(h0, h1, below, w2, out):
    totals = {}
    for b in range(3):
        p, sj = TAP_PHASE[b]
        for c in range(3):
            q, sk = TAP_PHASE[c]
            for a, plane in enumerate((below, h0, h1)):
                tap = 9 * a + 3 * b + c
                term = dot(plane[2 * p + q], w2[tap * 128 : (tap + 1) * 128, :])
                v = 2 * sj + sk
                totals[v] = totals[v] + term if v in totals else term
    width = totals[0].shape[1]
    zero = jnp.zeros((NJ, width), F32)

    def later(value):
        return jnp.concatenate([zero, value[: CELLS - NJ]], axis=0)

    inner = totals[2] + later(totals[3])
    inner = jnp.where(iota(inner.shape, 0) % NJ == 0, 0.0, pltpu.roll(inner, 1, axis=0))
    rows = totals[0] + later(totals[1]) + inner
    row, col = iota((CELLS, CELLS), 0), iota((CELLS, CELLS), 1)
    back = one_hot((row // NJ == col % NK) & (row % NJ == col // NK))
    out[...] = dot(rows.T.astype(BF16), back).astype(BF16)


def kernel_two(samples, rows_per, *refs):
    cots, refs = refs[:samples], refs[samples:]
    hidden_0, refs = refs[:samples], refs[samples:]
    hidden_1, refs = refs[:samples], refs[samples:]
    packed = len(refs) > 1
    out = refs[-1]
    order = cell_order(True)
    moved = []
    for cot in cots:
        value = dot(cot[...].reshape(-1, CELLS), order)
        value = value.reshape(-1, 2, rows_per, 4 * CELLS)
        moved.append([value[:, s].reshape(-1, 4 * CELLS).astype(BF16) for s in range(2)])
    left = {}
    for s in range(2):
        for v in range(4):
            left[s, v] = jnp.concatenate(
                [m[s][:, v * CELLS : (v + 1) * CELLS] for m in moved], axis=1
            )
    height = left[0, 0].shape[0]
    for p in range(2):
        for q in range(2):
            phase = 2 * p + q
            right_0 = jnp.concatenate([h[phase] for h in hidden_0], axis=0)
            right_1 = jnp.concatenate([h[phase] for h in hidden_1], axis=0)
            both = jnp.concatenate([right_0, right_1], axis=1)
            taps = [
                (b, c)
                for b in range(3)
                for c in range(3)
                if TAP_PHASE[b][0] == p and TAP_PHASE[c][0] == q
            ]
            shifts = [2 * TAP_PHASE[b][1] + TAP_PHASE[c][1] for b, c in taps]
            same = dot(jnp.concatenate([left[0, v] for v in shifts], axis=0), both)
            above = dot(jnp.concatenate([left[1, v] for v in shifts], axis=0), right_1)
            for n, (b, c) in enumerate(taps):
                rows = slice(n * height, (n + 1) * height)
                for a, value in (
                    (0, above[rows]),
                    (1, same[rows, 0:128]),
                    (2, same[rows, 128:256]),
                ):
                    at = (9 * a + 3 * b + c) * 128
                    if packed:
                        value = value.reshape(-1, rows_per, 128)
                        out[:, :, at : at + 128] = value.astype(out.dtype)
                    else:
                        out[:, at : at + 128] = value
    if packed:
        *parts, latent, _ = refs
        total = parts[0][...].astype(F32)
        for part in parts[1:]:
            total = total + part[...].astype(F32)
        wide = 27 * 128
        out[:, :, wide : wide + 640] = total.reshape(-1, rows_per, 640).astype(BF16)
        cells = latent[...].astype(F32).reshape(out.shape[0], -1, rows_per, CELLS)
        for w in range(cells.shape[1]):
            at = wide + 640 + w * 128
            out[:, :, at : at + 128] = cells[:, w].astype(BF16)


def kernel_sum(got, total_out, latent):
    sources, rows_per, _ = got.shape
    wide = 27 * 128 + 640
    for at in range(0, wide, 512):
        total = got[0, :, at : at + 512].astype(F32)
        for src in range(1, sources):
            total = total + got[src, :, at : at + 512].astype(F32)
        total_out[:, at : at + 512] = total.astype(BF16)
    height = sources * rows_per
    row, col = iota((height, height), 0), iota((height, height), 1)
    swap = one_hot((row // sources == col % rows_per) & (row % sources == col // rows_per))
    for w in range(latent.shape[0] // rows_per):
        at = wide + w * 128
        cells = got[:, :, at : at + 128].astype(F32).reshape(height, 128).astype(BF16)
        moved = dot(swap, cells).reshape(rows_per, sources, 128).astype(BF16)
        latent[w * rows_per : (w + 1) * rows_per] = moved


def kernel_final(pieces, place, *refs):
    parts, (one, two, joined) = refs[:pieces], refs[pieces:]
    rows_per = parts[0].shape[0]
    wide = 27 * 128
    share = rows_per // 2
    for k in range(pieces):
        q = place[0] ^ k
        at = pl.multiple_of(q * rows_per, rows_per)
        two[pl.ds(at, rows_per), :] = parts[k][:, :wide].astype(F32)
        joined[pl.ds(at, rows_per), :] = parts[k][:, wide : wide + 640].astype(F32)
    owned = pieces * share
    row, col = iota((owned, 2 * owned), 0), iota((owned, 2 * owned), 1)
    for half in range(2):
        chosen = one_hot(col == row // share * rows_per + half * share + row % share)
        value = dot(chosen, joined[...].astype(BF16))
        for t in range(5 - half):
            at = (5 * half + t) * 96
            one[:, at : at + 96] = value[:, t * 128 + 32 : (t + 1) * 128]


def call(kernel, out_shape, *args, scalars=0, scratch=(), flops=0):
    vmem = pl.BlockSpec(memory_space=pltpu.VMEM)
    smem = pl.BlockSpec(memory_space=pltpu.SMEM)
    single = isinstance(out_shape, jax.ShapeDtypeStruct)
    moved = sum(x.size * x.dtype.itemsize for x in args)
    return pl.pallas_call(
        kernel,
        out_shape=out_shape,
        in_specs=[smem] * scalars + [vmem] * (len(args) - scalars),
        out_specs=vmem if single else [vmem] * len(out_shape),
        scratch_shapes=list(scratch),
        cost_estimate=pl.CostEstimate(flops=flops, bytes_accessed=moved, transcendentals=0),
        compiler_params=pltpu.CompilerParams(vmem_limit_bytes=VMEM_LIMIT),
    )(*args)


def shape(dims, dtype):
    return jax.ShapeDtypeStruct(dims, dtype)


def swap_ranks(block, axis, k):
    return lax.ppermute(block, axis, [(i, i ^ k) for i in range(lax.axis_size(axis))])


def from_below(block, axis):
    return lax.ppermute(block, axis, [(i - 1, i) for i in range(1, lax.axis_size(axis))])


def on_device(snapshot, conv_one, conv_two, cotangent):
    slabs, samples = lax.axis_size("space"), lax.axis_size("dp")
    group = cotangent.shape[1]
    shared = samples == 4 and slabs == 8
    pieces = samples if shared else 1
    rows_per = group // pieces
    place = lax.axis_index("dp").astype(jnp.int32).reshape(1)

    slab = snapshot[0]
    halo = from_below(slab[3:], "space")
    by_plane = cotangent[0].transpose(1, 0, 2).reshape(slabs, pieces, 1, rows_per, CELLS)
    next_plane = jnp.pad(by_plane[1:], ((0, 1), (0, 0), (0, 0), (0, 0), (0, 0)))
    parcels = jnp.concatenate([by_plane, next_plane], axis=2).reshape(slabs, 2 * group, CELLS)
    cot = lax.all_to_all(parcels, "space", split_axis=0, concat_axis=0, tiled=True)

    h0, h1, slope_t, p1 = call(
        kernel_a,
        (
            shape((4, CELLS, 128), BF16),
            shape((4, CELLS, 128), BF16),
            shape((8, 128, CELLS), F32),
            shape((4 * CELLS, 9 * 128), BF16),
        ),
        slab,
        halo,
        conv_one,
        scratch=[pltpu.VMEM((9 * 128, 384), BF16)],
        flops=10**9,
    )
    below = from_below(h1, "space")

    if shared:
        one_shape = [shape((slabs * rows_per, 640), BF16)] * pieces
    else:
        one_shape = [shape((128, 9 * 128), F32)]
    ones = call(
        functools.partial(kernel_b, pieces, rows_per),
        one_shape,
        place,
        cot,
        conv_two,
        slope_t,
        p1,
        scalars=1,
        scratch=[pltpu.VMEM((384, 4 * CELLS), BF16)],
        flops=10**9,
    )
    latent_t = call(
        kernel_latent, shape((256, CELLS), BF16), h0, h1, below, conv_two, flops=10**9
    )

    if not shared:
        spread = latent_t.reshape(slabs, group, CELLS)
        latent = lax.all_to_all(spread, "space", split_axis=0, concat_axis=0, tiled=True)
        two = call(
            functools.partial(kernel_two, 1, rows_per),
            shape((256, 27 * 128), F32),
            cot,
            h0,
            h1,
            flops=10**9,
        )
        one = ones[0].reshape(128, 9, 128)[:, :, 32:].reshape(128, 864)
        one, two = lax.psum((one, two), "dp")
        one = lax.psum_scatter(one, "space", scatter_dimension=0, tiled=True)
        two = lax.psum_scatter(two, "space", scatter_dimension=0, tiled=True)
        return latent.transpose(1, 0, 2)[None], one, two

    def exchange(block):
        across = swap_ranks(block, "dp", 2)
        beside = swap_ranks(block, "dp", 1)
        return [block, beside, across, swap_ranks(across, "dp", 1)]

    all_h1 = exchange(h1)
    all_h0 = exchange(h0)
    cots, part_ones = [], []
    for k in range(pieces):
        piece = lax.dynamic_slice_in_dim(cot, (place[0] ^ k) * 2 * rows_per, 2 * rows_per, 1)
        cots.append(swap_ranks(piece, "dp", k) if k else piece)
        part_ones.append(swap_ranks(ones[k], "dp", k) if k else ones[k])
    width = 27 * 128 + 640 + group // rows_per * CELLS
    parcel = call(
        functools.partial(kernel_two, samples, rows_per),
        shape((slabs, rows_per, width), BF16),
        *cots,
        *all_h0,
        *all_h1,
        *part_ones,
        latent_t,
        flops=10**9,
    )
    got = lax.all_to_all(parcel, "space", split_axis=0, concat_axis=0, tiled=True)
    total, latent = call(
        kernel_sum,
        (shape((rows_per, 27 * 128 + 640), BF16), shape((group, slabs, CELLS), BF16)),
        got,
        flops=10**6,
    )
    totals = [swap_ranks(total, "dp", k) if k else total for k in range(pieces)]
    one, two = call(
        functools.partial(kernel_final, pieces),
        (shape((16, 864), F32), shape((32, 27 * 128), F32)),
        place,
        *totals,
        scalars=1,
        scratch=[pltpu.VMEM((4 * rows_per, 640), F32)],
        flops=10**6,
    )
    return latent[None], one, two


def solution(mesh):
    placed = (P("dp", "space", None, None), P(), P(), P("dp", "space", None, None))
    return jax.shard_map(
        on_device,
        mesh=mesh,
        in_specs=placed,
        out_specs=(P("dp", "space", None, None), P("space", None), P("space", None)),
        check_vma=False,
    )
```

time: 330 us -> 75.3 us (0.23)
  waiting for transfers between devices: 167 us -> 13.4 us
  local copies, waits for them, and re-layouts: 92.2 us -> 6.95 us
  between operations: 14.3 us -> 0.79 us
  matrix products: 7.11 us -> 0 us
  starting transfers between devices: 17.5 us -> 24.5 us
  Pallas kernels: 0 us -> 6.8 us
  other arithmetic: 7.38 us -> 0.68 us
    unnamed x4 -> x0, waiting for transfers between devices: 78.9 us -> none
    reduce_scatter x1 -> x0, waiting for transfers between devices: 48.2 us -> none  [on_device(): lax.psum_scatter(summed[0], 'space', scatter_dimension=0, tiled=True)]
    slice x35 -> x3, local copies, waits for them, and re-layouts: 46.8 us -> 1.78 us  [the longest x1 0.91 us: on_device(): halo = from_below(slab[3:], 'space')]
    psum x1 -> x0, waiting for transfers between devices: 35.4 us -> none  [on_device(): summed = lax.psum((term_one, term_two), 'dp')]
    unnamed x47 -> x10, local copies, waits for them, and re-layouts: 20.1 us -> 4.29 us
    psum x1 -> x0, blocking collectives: 12.4 us -> none  [on_device(): summed = lax.psum((term_one, term_two), 'dp')]
    all_to_all x1, blocking collectives: 11.2 us -> 21.7 us  [on_device(): lax.all_to_all(parcel, 'space', split_axis=0, concat_axis=0, tiled=True)]
    ppermute x3 -> x17, waiting for transfers between devices: 3.32 us -> 13.4 us  [the longest x15 10.9 us: swap_ranks(): lax.ppermute(block, axis, [(i, i ^ k) for i in range(lax.axis_size(axis))])]
  transfers between devices with their start and end apart: 7 -> 18, of which waited for: 5 -> 7; matrix products, arithmetic and copies ran while one was open for 26% -> 1% of each run, Pallas kernels for 0% -> 6%
where the time goes in v1:
time: 75.3 us; the launch traced here: 74.8 us
  starting transfers between devices  24.5 us (33%)
  blocking collectives  21.7 us (29%)
  waiting for transfers between devices  13.4 us (18%)
  local copies, waits for them, and re-layouts  6.95 us (9%)
  Pallas kernels  6.8 us (9%)
  between operations  0.79 us (1%)
    all_to_all x1, blocking collectives, on_device(): lax.all_to_all(parcel, 'space', split_axis=0, concat_axis=0, tiled=True)  21.7 us
    ppermute x15, waiting for transfers between devices, swap_ranks(): lax.ppermute(block, axis, [(i, i ^ k) for i in range(lax.axis_size(axis))])  10.9 us
    ppermute x15, starting transfers between devices, swap_ranks(): lax.ppermute(block, axis, [(i, i ^ k) for i in range(lax.axis_size(axis))])  9.24 us
    ppermute x2, starting transfers between devices, from_below(): lax.ppermute(block, axis, [(i - 1, i) for i in range(1, lax.axis_size(axi...  8.02 us
    all_to_all x1, starting transfers between devices, on_device(): lax.all_to_all(parcels, 'space', split_axis=0, concat_axis=0, tiled=True)  7.25 us
    pallas_call x6, Pallas kernels, call(): pl.pallas_call(kernel, out_shape=out_shape, in_specs=[smem] * scalars + [...  6.8 us
    unnamed x10, local copies, waits for them, and re-layouts  4.29 us
    ppermute x2, waiting for transfers between devices, from_below(): lax.ppermute(block, axis, [(i - 1, i) for i in range(1, lax.axis_size(axi...  2.5 us
  transfers between devices with their start and end apart: 18, of which 7 were waited for; matrix products, arithmetic and copies ran while one was open for 1% of the time, Pallas kernels for 6%

profile of v1, /device:TPU:0, one launch (start us, length us, event | category | flops | bytes accessed | tf_op | source)
XLA Modules:
  0.0 74.8 jit_solution(17937435624213205587)
XLA Ops:
  0.6 0.9 %slice.16 = bf16[7,32,128]{2,0,1:T(8,128)(2,1)S(1)} slice(bf16[8,32,128]{2,0,1:T(8,128)(2,1)} %bitcast.13), slice={[1:8], [0:32], [0:128]} | slice | bytes 114688 | tf_op jit(solution)/shard_map/slice | solution.py:297
  1.5 0.9 %copy.8 = bf16[8,4,1,8,128]{4,3,2,1,0:T(8,128)(2,1)S(1)} copy(bf16[8,4,1,8,128]{4,0,3,1,2:T(8,128)(2,1)} %bitcast.14) | data formatting | bytes 131072 | tf_op jit(solution)/shard_map/reshape | solution.py:296
  2.4 0.7 fusion.1
  3.0 7.3 %all-to-all-start = ((bf16[8,64,128]{2,1,0:T(8,128)(2,1)}), bf16[8,64,128]{2,1,0:T(8,128)(2,1)S(1)}, u32[]{:S(2)}, u32[]{:S(2)}) async-start(bf16[8,64,128]{2,1,0:T(8,128)(2,1)} %bitcast.5), calls=%async_computation | async-start | bytes 262144 | tf_op jit(solution)/shard_map/all_to_all | solution.py:299
  10.3 0.9 %slice_bitcast_fusion = bf16[1,64,1024]{2,1,0:T(8,128)(2,1)S(1)} fusion(bf16[1,4,64,1024]{3,2,1,0:T(8,128)(2,1)} %param.4), kind=kLoop, calls=%fused_computation.3 | loop fusion | bytes 262144 | tf_op jit(solution)/shard_map/slice | solution.py:295
  11.2 3.9 %collective-permute-start.3 = (bf16[1,64,1024]{2,1,0:T(8,128)(2,1)S(1)}, bf16[1,64,1024]{2,1,0:T(8,128)(2,1)S(1)}, u32[]{:S(2)}, u32[]{:S(2)}) collective-permute-start(bf16[1,64,1024]{2,1,0:T(8,128)(2,1)S(1)} %slice_bitcast_fusion), channel_id=1, source_target_pairs={{0,1},{1,2},{2,3},{3,4},{4,5},{5,6},{6,7},{8,9},{9,10},{10,11},{11... | collective-permute-start | bytes 393224 | tf_op jit(solution)/shard_map/ppermute | solution.py:283
  15.2 2.5 %collective-permute-done.3.halo = bf16[1,64,1024]{2,1,0:T(8,128)(2,1)S(1)} collective-permute-done((bf16[1,64,1024]{2,1,0:T(8,128)(2,1)S(1)}, bf16[1,64,1024]{2,1,0:T(8,128)(2,1)S(1)}, u32[]{:S(2)}, u32[]{:S(2)}) %collective-permute-start.3) | collective-permute-done | bytes 131104 | tf_op jit(solution)/shard_map/ppermute | solution.py:283
  17.7 0.0 copy-start
  17.7 1.0 %copy-done = bf16[1,4,64,1024]{3,2,1,0:T(8,128)(2,1)S(1)} copy-done((bf16[1,4,64,1024]{3,2,1,0:T(8,128)(2,1)S(1)}, bf16[1,4,64,1024]{3,2,1,0:T(8,128)(2,1)}, u32[]{:S(2)}) %copy-start) | copy-done | bytes 524312
  18.7 0.0 copy-start.2
  18.7 0.9 %copy-done.2 = bf16[864,128]{1,0:T(8,128)(2,1)S(1)} copy-done((bf16[864,128]{1,0:T(8,128)(2,1)S(1)}, bf16[864,128]{1,0:T(8,128)(2,1)}, u32[]{:S(2)}) %copy-start.2) | copy-done | bytes 221208
  19.7 0.0 copy-start.1
  19.7 1.2 %shard_map.67 = (bf16[4,128,128]{2,1,0:T(8,128)(2,1)S(1)}, bf16[4,128,128]{2,1,0:T(8,128)(2,1)S(1)}, f32[8,128,128]{2,1,0:T(8,128)S(1)}, bf16[512,1152]{1,0:T(8,128)(2,1)S(1)}) custom-call(bf16[4,64,1024]{2,1,0:T(8,128)(2,1)S(1)} %bitcast.12, bf16[1,64,1024]{2,1,0:T(8,128)(2,1)S(1)} %collective-permute-done.3.halo, bf16[864,128]{1,0:T(8,128)(2,1)S(1)} %copy-done.2), custom_call_target="tpu_custom_call" | custom-call | flops 1000000000 | bytes 876544 | tf_op jit(solution)/shard_map/pallas_call | solution.py:263
  20.9 0.0 copy-start.3
  20.9 1.0 %copy-done.3 = bf16[512,1152]{1,0:T(8,128)(2,1)} copy-done((bf16[512,1152]{1,0:T(8,128)(2,1)}, bf16[512,1152]{1,0:T(8,128)(2,1)S(1)}, u32[]{:S(2)}) %copy-start.3) | copy-done | bytes 1179672
  21.9 1.5 %collective-permute-start.5 = (bf16[4,128,128]{2,1,0:T(8,128)(2,1)S(1)}, bf16[4,128,128]{2,1,0:T(8,128)(2,1)S(1)}, u32[]{:S(2)}, u32[]{:S(2)}) collective-permute-start(bf16[4,128,128]{2,1,0:T(8,128)(2,1)S(1)} %get-tuple-element.15.h0.refs_4_), channel_id=1, source_target_pairs={{0,16},{8,24},{16,0},{24,8},{1,17},{9,25},{17,1},{25,9},{2,18},{10... | collective-permute-start | bytes 393224 | tf_op jit(solution)/shard_map/ppermute | solution.py:279
  23.5 0.5 collective-permute-start.8
  24.0 0.0 all-to-all-done.cot
  24.0 0.1 collective-permute-start.2
  24.1 1.6 %collective-permute-start.1 = (bf16[8,16,128]{2,1,0:T(8,128)(2,1)S(1)}, bf16[8,16,128]{2,1,0:T(8,128)(2,1)S(1)}, u32[]{:S(2)}, u32[]{:S(2)}) collective-permute-start(bf16[8,16,128]{2,1,0:T(8,128)(2,1)S(1)} %get-tuple-element.28), channel_id=1, source_target_pairs={{0,16},{8,24},{16,0},{24,8},{1,17},{9,25},{17,1},{25,9},{2,18},{10... | collective-permute-start | bytes 98312 | tf_op jit(solution)/shard_map/ppermute | solution.py:279
  25.7 0.3 collective-permute-start
  25.9 3.0 %collective-permute-done.2.refs_3_ = bf16[8,16,128]{2,1,0:T(8,128)(2,1)S(1)} collective-permute-done((bf16[8,16,128]{2,1,0:T(8,128)(2,1)S(1)}, bf16[8,16,128]{2,1,0:T(8,128)(2,1)S(1)}, u32[]{:S(2)}, u32[]{:S(2)}) %collective-permute-start.2) | collective-permute-done | bytes 32800 | tf_op jit(solution)/shard_map/ppermute | solution.py:279
  29.0 0.8 %collective-permute-start.4 = (bf16[4,128,128]{2,1,0:T(8,128)(2,1)S(1)}, bf16[4,128,128]{2,1,0:T(8,128)(2,1)S(1)}, u32[]{:S(2)}, u32[]{:S(2)}) collective-permute-start(bf16[4,128,128]{2,1,0:T(8,128)(2,1)S(1)} %get-tuple-element.15.h0.refs_4_), channel_id=1, source_target_pairs={{0,8},{8,0},{16,24},{24,16},{1,9},{9,1},{17,25},{25,17},{2,10},{10... | collective-permute-start | bytes 393224 | tf_op jit(solution)/shard_map/ppermute | solution.py:279
  29.7 0.5 collective-permute-done.1.refs_2_
  30.3 4.1 %collective-permute-start.13 = (bf16[4,128,128]{2,1,0:T(8,128)(2,1)S(1)}, bf16[4,128,128]{2,1,0:T(8,128)(2,1)S(1)}, u32[]{:S(2)}, u32[]{:S(2)}) collective-permute-start(bf16[4,128,128]{2,1,0:T(8,128)(2,1)S(1)} %get-tuple-element.16.h1.refs_8_), channel_id=1, source_target_pairs={{0,1},{1,2},{2,3},{3,4},{4,5},{5,6},{6,7},{8,9},{9,10},{10,11},{11... | collective-permute-start | bytes 393224 | tf_op jit(solution)/shard_map/ppermute | solution.py:283
  34.4 0.0 collective-permute-done.refs_1_
  34.4 0.1 collective-permute-start.7
  34.5 0.0 collective-permute-done.5.refs_6_
  34.5 0.5 collective-permute-start.6
  35.0 0.0 collective-permute-done.8.refs_10_
  35.0 0.1 collective-permute-start.9
  35.0 0.0 copy-done.1
  35.0 0.0 copy-start.4
  35.1 1.3 %copy-done.4 = bf16[512,1152]{1,0:T(8,128)(2,1)S(1)} copy-done((bf16[512,1152]{1,0:T(8,128)(2,1)S(1)}, bf16[512,1152]{1,0:T(8,128)(2,1)}, u32[]{:S(2)}) %copy-start.4) | copy-done | bytes 1179672
  36.3 2.3 %shard_map.68 = (bf16[64,640]{1,0:T(8,128)(2,1)S(1)}, bf16[64,640]{1,0:T(8,128)(2,1)S(1)}, bf16[64,640]{1,0:T(8,128)(2,1)S(1)}, bf16[64,640]{1,0:T(8,128)(2,1)S(1)}) custom-call(s32[1]{0:T(128)} %bitcast.8.place, bf16[8,64,128]{2,1,0:T(8,128)(2,1)S(1)} %all-to-all-done.cot, bf16[3456,256]{1,0:T(8,128)(2,1)S(1)} %copy-done.1, ...), custom_call_target="tpu_custom_call" | custom-call | flops 1000000000 | bytes 3604484 | tf_op jit(solution)/shard_map/pallas_call | solution.py:263
  38.7 0.0 collective-permute-done.4.refs_5_
  38.7 0.5 collective-permute-start.10
  39.2 0.0 collective-permute-done.13.below
  39.2 1.5 %collective-permute-start.11 = (bf16[64,640]{1,0:T(8,128)(2,1)S(1)}, bf16[64,640]{1,0:T(8,128)(2,1)S(1)}, u32[]{:S(2)}, u32[]{:S(2)}) collective-permute-start(bf16[64,640]{1,0:T(8,128)(2,1)S(1)} %get-tuple-element.21), channel_id=1, source_target_pairs={{0,16},{8,24},{16,0},{24,8},{1,17},{9,25},{17,1},{25,9},{2,18},{10... | collective-permute-start | bytes 245768 | tf_op jit(solution)/shard_map/ppermute | solution.py:279
  40.7 0.0 collective-permute-done.7.refs_9_
  40.7 0.0 collective-permute-start.12
  40.7 0.8 %shard_map.69.refs_16_ = bf16[256,128]{1,0:T(8,128)(2,1)S(1)} custom-call(bf16[4,128,128]{2,1,0:T(8,128)(2,1)S(1)} %get-tuple-element.15.h0.refs_4_, bf16[4,128,128]{2,1,0:T(8,128)(2,1)S(1)} %get-tuple-element.16.h1.refs_8_, bf16[4,128,128]{2,1,0:T(8,128)(2,1)S(1)} %collective-permute-done.13.below, bf16[3456,256]{1,0:T(8,128)(2,1)S(1)} %copy-done.1), custom_call_target="tpu_custom_call" | custom-call | flops 1000000000 | bytes 2162688 | tf_op jit(solution)/shard_map/pallas_call | solution.py:263
  41.5 0.0 collective-permute-done.10.refs_13_
  41.5 2.1 %collective-permute-done.11.refs_14_ = bf16[64,640]{1,0:T(8,128)(2,1)S(1)} collective-permute-done((bf16[64,640]{1,0:T(8,128)(2,1)S(1)}, bf16[64,640]{1,0:T(8,128)(2,1)S(1)}, u32[]{:S(2)}, u32[]{:S(2)}) %collective-permute-start.11) | collective-permute-done | bytes 81952 | tf_op jit(solution)/shard_map/ppermute | solution.py:279
  43.6 1.8 %collective-permute-done.12.refs_15_ = bf16[64,640]{1,0:T(8,128)(2,1)S(1)} collective-permute-done((bf16[64,640]{1,0:T(8,128)(2,1)S(1)}, bf16[64,640]{1,0:T(8,128)(2,1)S(1)}, u32[]{:S(2)}, u32[]{:S(2)}) %collective-permute-start.12) | collective-permute-done | bytes 81952 | tf_op jit(solution)/shard_map/ppermute | solution.py:279
  45.4 0.0 collective-permute-done.6.refs_7_
  45.4 0.0 collective-permute-done.9.refs_11_
  45.4 0.7 shard_map.70
  46.1 21.7 %all_to_all.10.got = bf16[8,8,4608]{2,1,0:T(8,128)(2,1)S(1)} all-to-all(bf16[8,8,4608]{2,1,0:T(8,128)(2,1)S(1)} %shard_map.70), channel_id=1, replica_groups=mesh['dp'=4,'space'=8] {'space'}, dimensions={0} | all-to-all | bytes 1179648 | tf_op jit(solution)/shard_map/all_to_all | solution.py:377
  67.8 0.8 %shard_map.71 = (bf16[8,4096]{1,0:T(8,128)(2,1)S(1)}, bf16[32,8,128]{2,1,0:T(8,128)(2,1)}) custom-call(bf16[8,8,4608]{2,1,0:T(8,128)(2,1)S(1)} %all_to_all.10.got), custom_call_target="tpu_custom_call" | custom-call | flops 1000000 | bytes 589824 | tf_op jit(solution)/shard_map/pallas_call | solution.py:263
  68.7 0.0 collective-permute-start.16
  68.7 1.2 %collective-permute-start.15 = (bf16[8,4096]{1,0:T(8,128)(2,1)S(1)}, bf16[8,4096]{1,0:T(8,128)(2,1)S(1)}, u32[]{:S(2)}, u32[]{:S(2)}) collective-permute-start(bf16[8,4096]{1,0:T(8,128)(2,1)S(1)} %get-tuple-element.24.refs_0_), channel_id=1, source_target_pairs={{0,16},{8,24},{16,0},{24,8},{1,17},{9,25},{17,1},{25,9},{2,18},{10... | collective-permute-start | bytes 196616 | tf_op jit(solution)/shard_map/ppermute | solution.py:279
  69.9 0.6 collective-permute-start.14
  70.5 2.5 %collective-permute-done.16.refs_3_ = bf16[8,4096]{1,0:T(8,128)(2,1)S(1)} collective-permute-done((bf16[8,4096]{1,0:T(8,128)(2,1)S(1)}, bf16[8,4096]{1,0:T(8,128)(2,1)S(1)}, u32[]{:S(2)}, u32[]{:S(2)}) %collective-permute-start.16) | collective-permute-done | bytes 65568 | tf_op jit(solution)/shard_map/ppermute | solution.py:279
  73.1 0.9 %collective-permute-done.15.refs_2_ = bf16[8,4096]{1,0:T(8,128)(2,1)S(1)} collective-permute-done((bf16[8,4096]{1,0:T(8,128)(2,1)S(1)}, bf16[8,4096]{1,0:T(8,128)(2,1)S(1)}, u32[]{:S(2)}, u32[]{:S(2)}) %collective-permute-start.15) | collective-permute-done | bytes 65568 | tf_op jit(solution)/shard_map/ppermute | solution.py:279
  74.0 0.0 collective-permute-done.14.refs_1_
  74.0 0.9 %shard_map.72 = (f32[16,864]{1,0:T(8,128)}, f32[32,3456]{1,0:T(8,128)}) custom-call(s32[1]{0:T(128)} %bitcast.8.place, bf16[8,4096]{1,0:T(8,128)(2,1)S(1)} %get-tuple-element.24.refs_0_, bf16[8,4096]{1,0:T(8,128)(2,1)S(1)} %collective-permute-done.14.refs_1_, bf16[8,4096]{1,0:T(8,128)(2,1)S(1)} %collective-permute-done.15.refs_2_, ...), custom_call_target="tpu_custom_call" | custom-call | flops 1000000 | bytes 262148 | tf_op jit(solution)/shard_map/pallas_call | solution.py:263
  (2 shorter events, 0.0 us)
Async XLA Ops:
  3.0 20.9 %all-to-all-start = ((bf16[8,64,128]{2,1,0:T(8,128)(2,1)}), bf16[8,64,128]{2,1,0:T(8,128)(2,1)S(1)}, u32[]{:S(2)}, u32[]{:S(2)}) async-start(bf16[8,64,128]{2,1,0:T(8,128)(2,1)} %bitcast.5), calls=%async_computation | async-start | bytes 262144 | tf_op jit(solution)/shard_map/all_to_all | solution.py:299
  11.2 6.5 %collective-permute-start.3 = (bf16[1,64,1024]{2,1,0:T(8,128)(2,1)S(1)}, bf16[1,64,1024]{2,1,0:T(8,128)(2,1)S(1)}, u32[]{:S(2)}, u32[]{:S(2)}) collective-permute-start(bf16[1,64,1024]{2,1,0:T(8,128)(2,1)S(1)} %slice_bitcast_fusion), channel_id=1, source_target_pairs={{0,1},{1,2},{2,3},{3,4},{4,5},{5,6},{6,7},{8,9},{9,10},{10,11},{11... | collective-permute-start | bytes 393224 | tf_op jit(solution)/shard_map/ppermute | solution.py:283
  17.7 1.0 %copy-start = (bf16[1,4,64,1024]{3,2,1,0:T(8,128)(2,1)S(1)}, bf16[1,4,64,1024]{3,2,1,0:T(8,128)(2,1)}, u32[]{:S(2)}) copy-start(bf16[1,4,64,1024]{3,2,1,0:T(8,128)(2,1)} %param.4) | copy-start | bytes 1572868
  18.7 0.9 %copy-start.2 = (bf16[864,128]{1,0:T(8,128)(2,1)S(1)}, bf16[864,128]{1,0:T(8,128)(2,1)}, u32[]{:S(2)}) copy-start(bf16[864,128]{1,0:T(8,128)(2,1)} %w1.1) | copy-start | bytes 663556
  19.7 15.4 %copy-start.1 = (bf16[3456,256]{1,0:T(8,128)(2,1)S(1)}, bf16[3456,256]{1,0:T(8,128)(2,1)}, u32[]{:S(2)}) copy-start(bf16[3456,256]{1,0:T(8,128)(2,1)} %w2.3) | copy-start | bytes 5308420
  20.9 1.0 %copy-start.3 = (bf16[512,1152]{1,0:T(8,128)(2,1)}, bf16[512,1152]{1,0:T(8,128)(2,1)S(1)}, u32[]{:S(2)}) copy-start(bf16[512,1152]{1,0:T(8,128)(2,1)S(1)} %get-tuple-element.18.p1) | copy-start | bytes 3538948
  21.9 12.5 %collective-permute-start.5 = (bf16[4,128,128]{2,1,0:T(8,128)(2,1)S(1)}, bf16[4,128,128]{2,1,0:T(8,128)(2,1)S(1)}, u32[]{:S(2)}, u32[]{:S(2)}) collective-permute-start(bf16[4,128,128]{2,1,0:T(8,128)(2,1)S(1)} %get-tuple-element.15.h0.refs_4_), channel_id=1, source_target_pairs={{0,16},{8,24},{16,0},{24,8},{1,17},{9,25},{17,1},{25,9},{2,18},{10... | collective-permute-start | bytes 393224 | tf_op jit(solution)/shard_map/ppermute | solution.py:279
  23.5 11.5 %collective-permute-start.8 = (bf16[4,128,128]{2,1,0:T(8,128)(2,1)S(1)}, bf16[4,128,128]{2,1,0:T(8,128)(2,1)S(1)}, u32[]{:S(2)}, u32[]{:S(2)}) collective-permute-start(bf16[4,128,128]{2,1,0:T(8,128)(2,1)S(1)} %get-tuple-element.16.h1.refs_8_), channel_id=1, source_target_pairs={{0,16},{8,24},{16,0},{24,8},{1,17},{9,25},{17,1},{25,9},{2,18},{10... | collective-permute-start | bytes 393224 | tf_op jit(solution)/shard_map/ppermute | solution.py:279
  24.0 5.0 %collective-permute-start.2 = (bf16[8,16,128]{2,1,0:T(8,128)(2,1)S(1)}, bf16[8,16,128]{2,1,0:T(8,128)(2,1)S(1)}, u32[]{:S(2)}, u32[]{:S(2)}) collective-permute-start(bf16[8,16,128]{2,1,0:T(8,128)(2,1)S(1)} %get-tuple-element.27), channel_id=1, source_target_pairs={{0,24},{8,16},{16,8},{24,0},{1,25},{9,17},{17,9},{25,1},{2,26},{10... | collective-permute-start | bytes 98312 | tf_op jit(solution)/shard_map/ppermute | solution.py:279
  24.1 6.2 %collective-permute-start.1 = (bf16[8,16,128]{2,1,0:T(8,128)(2,1)S(1)}, bf16[8,16,128]{2,1,0:T(8,128)(2,1)S(1)}, u32[]{:S(2)}, u32[]{:S(2)}) collective-permute-start(bf16[8,16,128]{2,1,0:T(8,128)(2,1)S(1)} %get-tuple-element.28), channel_id=1, source_target_pairs={{0,16},{8,24},{16,0},{24,8},{1,17},{9,25},{17,1},{25,9},{2,18},{10... | collective-permute-start | bytes 98312 | tf_op jit(solution)/shard_map/ppermute | solution.py:279
  25.7 8.7 %collective-permute-start = (bf16[8,16,128]{2,1,0:T(8,128)(2,1)S(1)}, bf16[8,16,128]{2,1,0:T(8,128)(2,1)S(1)}, u32[]{:S(2)}, u32[]{:S(2)}) collective-permute-start(bf16[8,16,128]{2,1,0:T(8,128)(2,1)S(1)} %get-tuple-element.29), channel_id=1, source_target_pairs={{0,8},{8,0},{16,24},{24,16},{1,9},{9,1},{17,25},{25,17},{2,10},{10... | collective-permute-start | bytes 98312 | tf_op jit(solution)/shard_map/ppermute | solution.py:279
  29.0 9.7 %collective-permute-start.4 = (bf16[4,128,128]{2,1,0:T(8,128)(2,1)S(1)}, bf16[4,128,128]{2,1,0:T(8,128)(2,1)S(1)}, u32[]{:S(2)}, u32[]{:S(2)}) collective-permute-start(bf16[4,128,128]{2,1,0:T(8,128)(2,1)S(1)} %get-tuple-element.15.h0.refs_4_), channel_id=1, source_target_pairs={{0,8},{8,0},{16,24},{24,16},{1,9},{9,1},{17,25},{25,17},{2,10},{10... | collective-permute-start | bytes 393224 | tf_op jit(solution)/shard_map/ppermute | solution.py:279
  30.3 8.9 %collective-permute-start.13 = (bf16[4,128,128]{2,1,0:T(8,128)(2,1)S(1)}, bf16[4,128,128]{2,1,0:T(8,128)(2,1)S(1)}, u32[]{:S(2)}, u32[]{:S(2)}) collective-permute-start(bf16[4,128,128]{2,1,0:T(8,128)(2,1)S(1)} %get-tuple-element.16.h1.refs_8_), channel_id=1, source_target_pairs={{0,1},{1,2},{2,3},{3,4},{4,5},{5,6},{6,7},{8,9},{9,10},{10,11},{11... | collective-permute-start | bytes 393224 | tf_op jit(solution)/shard_map/ppermute | solution.py:283
  34.4 6.3 %collective-permute-start.7 = (bf16[4,128,128]{2,1,0:T(8,128)(2,1)S(1)}, bf16[4,128,128]{2,1,0:T(8,128)(2,1)S(1)}, u32[]{:S(2)}, u32[]{:S(2)}) collective-permute-start(bf16[4,128,128]{2,1,0:T(8,128)(2,1)S(1)} %get-tuple-element.16.h1.refs_8_), channel_id=1, source_target_pairs={{0,8},{8,0},{16,24},{24,16},{1,9},{9,1},{17,25},{25,17},{2,10},{10... | collective-permute-start | bytes 393224 | tf_op jit(solution)/shard_map/ppermute | solution.py:279
  34.5 10.9 %collective-permute-start.6 = (bf16[4,128,128]{2,1,0:T(8,128)(2,1)S(1)}, bf16[4,128,128]{2,1,0:T(8,128)(2,1)S(1)}, u32[]{:S(2)}, u32[]{:S(2)}) collective-permute-start(bf16[4,128,128]{2,1,0:T(8,128)(2,1)S(1)} %collective-permute-done.5.refs_6_), channel_id=1, source_target_pairs={{0,8},{8,0},{16,24},{24,16},{1,9},{9,1},{17,25},{25,17},{2,10},{10... | collective-permute-start | bytes 393224 | tf_op jit(solution)/shard_map/ppermute | solution.py:279
  35.0 10.5 %collective-permute-start.9 = (bf16[4,128,128]{2,1,0:T(8,128)(2,1)S(1)}, bf16[4,128,128]{2,1,0:T(8,128)(2,1)S(1)}, u32[]{:S(2)}, u32[]{:S(2)}) collective-permute-start(bf16[4,128,128]{2,1,0:T(8,128)(2,1)S(1)} %collective-permute-done.8.refs_10_), channel_id=1, source_target_pairs={{0,8},{8,0},{16,24},{24,16},{1,9},{9,1},{17,25},{25,17},{2,10},{10... | collective-permute-start | bytes 393224 | tf_op jit(solution)/shard_map/ppermute | solution.py:279
  35.0 1.3 %copy-start.4 = (bf16[512,1152]{1,0:T(8,128)(2,1)S(1)}, bf16[512,1152]{1,0:T(8,128)(2,1)}, u32[]{:S(2)}) copy-start(bf16[512,1152]{1,0:T(8,128)(2,1)} %copy-done.3) | copy-start | bytes 3538948
  38.7 2.9 %collective-permute-start.10 = (bf16[64,640]{1,0:T(8,128)(2,1)S(1)}, bf16[64,640]{1,0:T(8,128)(2,1)S(1)}, u32[]{:S(2)}, u32[]{:S(2)}) collective-permute-start(bf16[64,640]{1,0:T(8,128)(2,1)S(1)} %get-tuple-element.20), channel_id=1, source_target_pairs={{0,8},{8,0},{16,24},{24,16},{1,9},{9,1},{17,25},{25,17},{2,10},{10... | collective-permute-start | bytes 245768 | tf_op jit(solution)/shard_map/ppermute | solution.py:279
  39.2 4.4 %collective-permute-start.11 = (bf16[64,640]{1,0:T(8,128)(2,1)S(1)}, bf16[64,640]{1,0:T(8,128)(2,1)S(1)}, u32[]{:S(2)}, u32[]{:S(2)}) collective-permute-start(bf16[64,640]{1,0:T(8,128)(2,1)S(1)} %get-tuple-element.21), channel_id=1, source_target_pairs={{0,16},{8,24},{16,0},{24,8},{1,17},{9,25},{17,1},{25,9},{2,18},{10... | collective-permute-start | bytes 245768 | tf_op jit(solution)/shard_map/ppermute | solution.py:279
  40.7 4.7 %collective-permute-start.12 = (bf16[64,640]{1,0:T(8,128)(2,1)S(1)}, bf16[64,640]{1,0:T(8,128)(2,1)S(1)}, u32[]{:S(2)}, u32[]{:S(2)}) collective-permute-start(bf16[64,640]{1,0:T(8,128)(2,1)S(1)} %get-tuple-element.22), channel_id=1, source_target_pairs={{0,24},{8,16},{16,8},{24,0},{1,25},{9,17},{17,9},{25,1},{2,26},{10... | collective-permute-start | bytes 245768 | tf_op jit(solution)/shard_map/ppermute | solution.py:279
  68.7 4.4 %collective-permute-start.16 = (bf16[8,4096]{1,0:T(8,128)(2,1)S(1)}, bf16[8,4096]{1,0:T(8,128)(2,1)S(1)}, u32[]{:S(2)}, u32[]{:S(2)}) collective-permute-start(bf16[8,4096]{1,0:T(8,128)(2,1)S(1)} %get-tuple-element.24.refs_0_), channel_id=1, source_target_pairs={{0,24},{8,16},{16,8},{24,0},{1,25},{9,17},{17,9},{25,1},{2,26},{10... | collective-permute-start | bytes 196616 | tf_op jit(solution)/shard_map/ppermute | solution.py:279
  68.7 5.3 %collective-permute-start.15 = (bf16[8,4096]{1,0:T(8,128)(2,1)S(1)}, bf16[8,4096]{1,0:T(8,128)(2,1)S(1)}, u32[]{:S(2)}, u32[]{:S(2)}) collective-permute-start(bf16[8,4096]{1,0:T(8,128)(2,1)S(1)} %get-tuple-element.24.refs_0_), channel_id=1, source_target_pairs={{0,16},{8,24},{16,0},{24,8},{1,17},{9,25},{17,1},{25,9},{2,18},{10... | collective-permute-start | bytes 196616 | tf_op jit(solution)/shard_map/ppermute | solution.py:279
  69.9 4.1 %collective-permute-start.14 = (bf16[8,4096]{1,0:T(8,128)(2,1)S(1)}, bf16[8,4096]{1,0:T(8,128)(2,1)S(1)}, u32[]{:S(2)}, u32[]{:S(2)}) collective-permute-start(bf16[8,4096]{1,0:T(8,128)(2,1)S(1)} %get-tuple-element.24.refs_0_), channel_id=1, source_target_pairs={{0,8},{8,0},{16,24},{24,16},{1,9},{9,1},{17,25},{25,17},{2,10},{10... | collective-permute-start | bytes 196616 | tf_op jit(solution)/shard_map/ppermute | solution.py:279

commit v2 on v1

--- a/solution.py
+++ b/solution.py
@@ -35,24 +35,22 @@
     return one_hot((to_k < NK) & (row == to_j * NK + to_k))
 
 
-def kernel_a(snap, halo, w1, h0, h1, slope_t, p1, w_ext):
+def fill_patches(planes, p1):
     row, col = iota((80, 64), 0), iota((80, 64), 1)
     pick = one_hot(col == 4 * (row % NJ) + row // NJ - 1)
-    for plane in range(5):
-        rows = halo[0] if plane == 0 else snap[plane - 1]
+    for a, rows in enumerate(planes):
         picked = dot(pick, rows).astype(BF16)
-        for i in range(2):
-            a = plane - 2 * i
-            if not 0 <= a <= 2:
-                continue
-            for p in range(2):
-                for b in range(3):
-                    rho = 2 * p + b
-                    for k in range(NK):
-                        at = (2 * i + p) * CELLS + k * NJ
-                        p1[at : at + NJ, (3 * a + b) * 128 : (3 * a + b + 1) * 128] = picked[
-                            rho * NJ : (rho + 1) * NJ, k * 128 : (k + 1) * 128
-                        ]
+        for p in range(2):
+            for b in range(3):
+                rho = 2 * p + b
+                for k in range(NK):
+                    at = p * CELLS + k * NJ
+                    p1[at : at + NJ, (3 * a + b) * 128 : (3 * a + b + 1) * 128] = picked[
+                        rho * NJ : (rho + 1) * NJ, k * 128 : (k + 1) * 128
+                    ]
+
+
+def widen(w1, w_ext):
     for t in range(9):
         base, src = t * 128, t * 96
         zeros = jnp.zeros((128, 128), BF16)
@@ -62,22 +60,43 @@
         w_ext[base + 32 : base + 128, 128:256] = w1[src : src + 96, :]
         w_ext[base : base + 96, 256:384] = zeros[:96]
         w_ext[base + 96 : base + 128, 256:384] = w1[src : src + 32, :]
-    for i in range(2):
-        hidden = h0 if i == 0 else h1
-        for p in range(2):
-            at = (2 * i + p) * CELLS
-            full = dot(p1[at : at + CELLS, :], w_ext[...])
-            before = jnp.concatenate(
-                [jnp.zeros((NJ, 128), F32), full[: CELLS - NJ, 256:384]], axis=0
-            )
-            for q, pre in enumerate((full[:, 0:128] + before, full[:, 128:256])):
-                logistic = 1.0 / (1.0 + jnp.exp(-pre))
-                hidden[2 * p + q] = (pre * logistic).astype(BF16)
-                slope = logistic * (1.0 + pre * (1.0 - logistic))
-                slope_t[4 * i + 2 * p + q] = slope.T
-
-
-def kernel_b(pieces, rows_per, place, cot, w2, slope_t, p1, *rest):
+
+
+def fill_hidden(p1, w_ext, hidden, slope_t):
+    for p in range(2):
+        full = dot(p1[p * CELLS : (p + 1) * CELLS, :], w_ext[...])
+        before = jnp.concatenate(
+            [jnp.zeros((NJ, 128), F32), full[: CELLS - NJ, 256:384]], axis=0
+        )
+        for q, pre in enumerate((full[:, 0:128] + before, full[:, 128:256])):
+            logistic = 1.0 / (1.0 + jnp.exp(-pre))
+            hidden[2 * p + q] = (pre * logistic).astype(BF16)
+            slope = logistic * (1.0 + pre * (1.0 - logistic))
+            slope_t[2 * p + q] = slope.T
+
+
+def kernel_upper(pieces, cot, snap, w1, parcels, halo, hidden, slope_t, p1, w_ext):
+    group, slabs = cot.shape[:2]
+    rows_per = group // pieces
+    halo[0] = snap[3]
+    flat = cot[...].astype(F32).reshape(-1, CELLS).astype(BF16)
+    row, col = iota((2 * group * slabs, group * slabs), 0), iota((2 * group * slabs, group * slabs), 1)
+    slab = row // (2 * group) + row // rows_per % 2
+    channel = row % (2 * group) // (2 * rows_per) * rows_per + row % rows_per
+    chosen = one_hot((slab < slabs) & (col == channel * slabs + slab))
+    parcels[...] = dot(chosen, flat).astype(BF16).reshape(slabs, 2 * group, CELLS)
+    fill_patches([snap[1], snap[2], snap[3]], p1)
+    widen(w1, w_ext)
+    fill_hidden(p1, w_ext, hidden, slope_t)
+
+
+def kernel_lower(snap, halo, w1, hidden, slope_t, p1, w_ext):
+    fill_patches([halo[0], snap[0], snap[1]], p1)
+    widen(w1, w_ext)
+    fill_hidden(p1, w_ext, hidden, slope_t)
+
+
+def kernel_b(pieces, rows_per, place, cot, w2, slope_0, slope_1, p1_0, p1_1, *rest):
     outs, (grad_t,) = rest[:-1], rest[-1:]
     sources = cot.shape[0]
     moved = dot(cot[...].reshape(-1, CELLS), cell_order(True))
@@ -98,7 +117,7 @@
                                 source[:, v * CELLS : (v + 1) * CELLS],
                             )
                             total = term if total is None else total + term
-                pre_t = total * slope_t[4 * i + 2 * p + q]
+                pre_t = total * (slope_0, slope_1)[i][2 * p + q]
                 at = (2 * i + p) * CELLS
                 grad_t[q * 128 : (q + 1) * 128, at : at + CELLS] = pre_t.astype(BF16)
                 if q == 0:
@@ -108,7 +127,9 @@
     lane = iota((128, 128), 1)
     frames = []
     for t in range(9):
-        full = dot(grad_t[...], p1[:, t * 128 : (t + 1) * 128])
+        cols = slice(t * 128, (t + 1) * 128)
+        full = dot(grad_t[:, : 2 * CELLS], p1_0[:, cols])
+        full = full + dot(grad_t[:, 2 * CELLS :], p1_1[:, cols])
         side = jnp.where(lane < 64, full[0:128], full[256:384])
         side = jnp.where((lane < 64) | (lane >= 96), side, 0.0)
         own = jnp.where(lane < 32, 0.0, full[128:256])
@@ -157,94 +178,97 @@
     out[...] = dot(rows.T.astype(BF16), back).astype(BF16)
 
 
-def kernel_two(samples, rows_per, *refs):
-    cots, refs = refs[:samples], refs[samples:]
-    hidden_0, refs = refs[:samples], refs[samples:]
-    hidden_1, refs = refs[:samples], refs[samples:]
-    packed = len(refs) > 1
-    out = refs[-1]
+def moved_rows(cots, rows_per, plane):
     order = cell_order(True)
     moved = []
     for cot in cots:
         value = dot(cot[...].reshape(-1, CELLS), order)
         value = value.reshape(-1, 2, rows_per, 4 * CELLS)
-        moved.append([value[:, s].reshape(-1, 4 * CELLS).astype(BF16) for s in range(2)])
-    left = {}
-    for s in range(2):
-        for v in range(4):
-            left[s, v] = jnp.concatenate(
-                [m[s][:, v * CELLS : (v + 1) * CELLS] for m in moved], axis=1
-            )
-    height = left[0, 0].shape[0]
+        moved.append(value[:, plane].reshape(-1, 4 * CELLS).astype(BF16))
+    return [
+        jnp.concatenate([m[:, v * CELLS : (v + 1) * CELLS] for m in moved], axis=1)
+        for v in range(4)
+    ]
+
+
+def kernel_two(samples, rows_per, upper, packed, *refs):
+    cots, hidden, refs = refs[:samples], refs[samples : 2 * samples], refs[2 * samples :]
+    out = refs[-1]
+    taps_x = (0, 2) if upper else (1,)
+    left = {a: moved_rows(cots, rows_per, 1 if a == 0 else 0) for a in taps_x}
+    height = left[taps_x[0]][0].shape[0]
     for p in range(2):
         for q in range(2):
-            phase = 2 * p + q
-            right_0 = jnp.concatenate([h[phase] for h in hidden_0], axis=0)
-            right_1 = jnp.concatenate([h[phase] for h in hidden_1], axis=0)
-            both = jnp.concatenate([right_0, right_1], axis=1)
+            right = jnp.concatenate([h[2 * p + q] for h in hidden], axis=0)
             taps = [
-                (b, c)
+                (n, b, c)
+                for n in range(len(taps_x))
                 for b in range(3)
                 for c in range(3)
                 if TAP_PHASE[b][0] == p and TAP_PHASE[c][0] == q
             ]
-            shifts = [2 * TAP_PHASE[b][1] + TAP_PHASE[c][1] for b, c in taps]
-            same = dot(jnp.concatenate([left[0, v] for v in shifts], axis=0), both)
-            above = dot(jnp.concatenate([left[1, v] for v in shifts], axis=0), right_1)
-            for n, (b, c) in enumerate(taps):
-                rows = slice(n * height, (n + 1) * height)
-                for a, value in (
-                    (0, above[rows]),
-                    (1, same[rows, 0:128]),
-                    (2, same[rows, 128:256]),
-                ):
-                    at = (9 * a + 3 * b + c) * 128
-                    if packed:
-                        value = value.reshape(-1, rows_per, 128)
-                        out[:, :, at : at + 128] = value.astype(out.dtype)
-                    else:
-                        out[:, at : at + 128] = value
-    if packed:
+            rows = [left[taps_x[n]][2 * TAP_PHASE[b][1] + TAP_PHASE[c][1]] for n, b, c in taps]
+            value = dot(jnp.concatenate(rows, axis=0), right)
+            for at, (n, b, c) in enumerate(taps):
+                part = value[at * height : (at + 1) * height]
+                to = (9 * n + 3 * b + c) * 128
+                if packed:
+                    out[:, :, to : to + 128] = part.reshape(-1, rows_per, 128).astype(BF16)
+                else:
+                    out[:, to : to + 128] = part
+    if packed and not upper:
         *parts, latent, _ = refs
         total = parts[0][...].astype(F32)
         for part in parts[1:]:
             total = total + part[...].astype(F32)
-        wide = 27 * 128
-        out[:, :, wide : wide + 640] = total.reshape(-1, rows_per, 640).astype(BF16)
+        out[:, :, 1152:1792] = total.reshape(-1, rows_per, 640).astype(BF16)
         cells = latent[...].astype(F32).reshape(out.shape[0], -1, rows_per, CELLS)
         for w in range(cells.shape[1]):
-            at = wide + 640 + w * 128
+            at = 1792 + w * 128
             out[:, :, at : at + 128] = cells[:, w].astype(BF16)
 
 
-def kernel_sum(got, total_out, latent):
+def add_sources(got, total_out):
+    sources, width = got.shape[0], total_out.shape[1]
+    for at in range(0, width, 256):
+        total = got[0, :, at : at + 256].astype(F32)
+        for src in range(1, sources):
+            total = total + got[src, :, at : at + 256].astype(F32)
+        total_out[:, at : at + 256] = total.astype(BF16)
+
+
+def kernel_sum_upper(got, total_out):
+    add_sources(got, total_out)
+
+
+def kernel_sum_lower(got, total_out, latent):
     sources, rows_per, _ = got.shape
-    wide = 27 * 128 + 640
-    for at in range(0, wide, 512):
-        total = got[0, :, at : at + 512].astype(F32)
-        for src in range(1, sources):
-            total = total + got[src, :, at : at + 512].astype(F32)
-        total_out[:, at : at + 512] = total.astype(BF16)
+    add_sources(got, total_out)
     height = sources * rows_per
     row, col = iota((height, height), 0), iota((height, height), 1)
     swap = one_hot((row // sources == col % rows_per) & (row % sources == col // rows_per))
     for w in range(latent.shape[0] // rows_per):
-        at = wide + w * 128
+        at = 1792 + w * 128
         cells = got[:, :, at : at + 128].astype(F32).reshape(height, 128).astype(BF16)
         moved = dot(swap, cells).reshape(rows_per, sources, 128).astype(BF16)
         latent[w * rows_per : (w + 1) * rows_per] = moved
 
 
 def kernel_final(pieces, place, *refs):
-    parts, (one, two, joined) = refs[:pieces], refs[pieces:]
-    rows_per = parts[0].shape[0]
-    wide = 27 * 128
+    uppers, lowers, (one, two, joined) = (
+        refs[:pieces],
+        refs[pieces : 2 * pieces],
+        refs[2 * pieces :],
+    )
+    rows_per = uppers[0].shape[0]
     share = rows_per // 2
     for k in range(pieces):
         q = place[0] ^ k
         at = pl.multiple_of(q * rows_per, rows_per)
-        two[pl.ds(at, rows_per), :] = parts[k][:, :wide].astype(F32)
-        joined[pl.ds(at, rows_per), :] = parts[k][:, wide : wide + 640].astype(F32)
+        two[pl.ds(at, rows_per), 0:1152] = uppers[k][:, 0:1152].astype(F32)
+        two[pl.ds(at, rows_per), 1152:2304] = lowers[k][:, 0:1152].astype(F32)
+        two[pl.ds(at, rows_per), 2304:3456] = uppers[k][:, 1152:2304].astype(F32)
+        joined[pl.ds(at, rows_per), :] = lowers[k][:, 1152:1792].astype(F32)
     owned = pieces * share
     row, col = iota((owned, 2 * owned), 0), iota((owned, 2 * owned), 1)
     for half in range(2):
@@ -292,27 +316,27 @@
     place = lax.axis_index("dp").astype(jnp.int32).reshape(1)
 
     slab = snapshot[0]
-    halo = from_below(slab[3:], "space")
-    by_plane = cotangent[0].transpose(1, 0, 2).reshape(slabs, pieces, 1, rows_per, CELLS)
-    next_plane = jnp.pad(by_plane[1:], ((0, 1), (0, 0), (0, 0), (0, 0), (0, 0)))
-    parcels = jnp.concatenate([by_plane, next_plane], axis=2).reshape(slabs, 2 * group, CELLS)
+    plane_shapes = (
+        shape((4, CELLS, 128), BF16),
+        shape((4, 128, CELLS), F32),
+        shape((2 * CELLS, 9 * 128), BF16),
+    )
+    wide = [pltpu.VMEM((9 * 128, 384), BF16)]
+    parcels, last, h1, slope_1, p1_1 = call(
+        functools.partial(kernel_upper, pieces),
+        (shape((slabs, 2 * group, CELLS), BF16), shape((1,) + slab.shape[1:], BF16)) + plane_shapes,
+        cotangent[0],
+        slab,
+        conv_one,
+        scratch=wide,
+        flops=10**9,
+    )
+    halo = from_below(last, "space")
     cot = lax.all_to_all(parcels, "space", split_axis=0, concat_axis=0, tiled=True)
-
-    h0, h1, slope_t, p1 = call(
-        kernel_a,
-        (
-            shape((4, CELLS, 128), BF16),
-            shape((4, CELLS, 128), BF16),
-            shape((8, 128, CELLS), F32),
-            shape((4 * CELLS, 9 * 128), BF16),
-        ),
-        slab,
-        halo,
-        conv_one,
-        scratch=[pltpu.VMEM((9 * 128, 384), BF16)],
-        flops=10**9,
-    )
     below = from_below(h1, "space")
+    h0, slope_0, p1_0 = call(
+        kernel_lower, plane_shapes, slab, halo, conv_one, scratch=wide, flops=10**9
+    )
 
     if shared:
         one_shape = [shape((slabs * rows_per, 640), BF16)] * pieces
@@ -324,8 +348,10 @@
         place,
         cot,
         conv_two,
-        slope_t,
-        p1,
+        slope_0,
+        slope_1,
+        p1_0,
+        p1_1,
         scalars=1,
         scratch=[pltpu.VMEM((384, 4 * CELLS), BF16)],
         flops=10**9,
@@ -337,14 +363,17 @@
     if not shared:
         spread = latent_t.reshape(slabs, group, CELLS)
         latent = lax.all_to_all(spread, "space", split_axis=0, concat_axis=0, tiled=True)
-        two = call(
-            functools.partial(kernel_two, 1, rows_per),
-            shape((256, 27 * 128), F32),
-            cot,
-            h0,
-            h1,
-            flops=10**9,
-        )
+        halves = [
+            call(
+                functools.partial(kernel_two, 1, rows_per, upper, False),
+                shape((256, (18 if upper else 9) * 128), F32),
+                cot,
+                hidden,
+                flops=10**9,
+            )
+            for upper, hidden in ((True, h1), (False, h0))
+        ]
+        two = jnp.concatenate([halves[0][:, :1152], halves[1], halves[0][:, 1152:]], axis=1)
         one = ones[0].reshape(128, 9, 128)[:, :, 32:].reshape(128, 864)
         one, two = lax.psum((one, two), "dp")
         one = lax.psum_scatter(one, "space", scatter_dimension=0, tiled=True)
@@ -363,25 +392,39 @@
         piece = lax.dynamic_slice_in_dim(cot, (place[0] ^ k) * 2 * rows_per, 2 * rows_per, 1)
         cots.append(swap_ranks(piece, "dp", k) if k else piece)
         part_ones.append(swap_ranks(ones[k], "dp", k) if k else ones[k])
-    width = 27 * 128 + 640 + group // rows_per * CELLS
-    parcel = call(
-        functools.partial(kernel_two, samples, rows_per),
-        shape((slabs, rows_per, width), BF16),
+    parcel_shape = shape((slabs, rows_per, 18 * 128), BF16)
+    upper = call(
+        functools.partial(kernel_two, samples, rows_per, True, True),
+        parcel_shape,
+        *cots,
+        *all_h1,
+        flops=10**9,
+    )
+    got_upper = lax.all_to_all(upper, "space", split_axis=0, concat_axis=0, tiled=True)
+    lower = call(
+        functools.partial(kernel_two, samples, rows_per, False, True),
+        parcel_shape,
         *cots,
         *all_h0,
-        *all_h1,
         *part_ones,
         latent_t,
         flops=10**9,
     )
-    got = lax.all_to_all(parcel, "space", split_axis=0, concat_axis=0, tiled=True)
-    total, latent = call(
-        kernel_sum,
-        (shape((rows_per, 27 * 128 + 640), BF16), shape((group, slabs, CELLS), BF16)),
-        got,
+    got_lower = lax.all_to_all(lower, "space", split_axis=0, concat_axis=0, tiled=True)
+    total_upper = call(
+        kernel_sum_upper, shape((rows_per, 18 * 128), BF16), got_upper, flops=10**6
+    )
+    total_lower, latent = call(
+        kernel_sum_lower,
+        (shape((rows_per, 14 * 128), BF16), shape((group, slabs, CELLS), BF16)),
+        got_lower,
         flops=10**6,
     )
-    totals = [swap_ranks(total, "dp", k) if k else total for k in range(pieces)]
+    totals = [
+        swap_ranks(total, "dp", k) if k else total
+        for total in (total_upper, total_lower)
+        for k in range(pieces)
+    ]
     one, two = call(
         functools.partial(kernel_final, pieces),
         (shape((16, 864), F32), shape((32, 27 * 128), F32)),

time: 75.3 us -> 68.1 us (0.904)
  blocking collectives: 21.7 us -> 0 us
  starting transfers between devices: 24.5 us -> 34.2 us
  waiting for transfers between devices: 13.4 us -> 20.2 us
  local copies, waits for them, and re-layouts: 6.95 us -> 2.84 us
  Pallas kernels: 6.8 us -> 9.51 us
    all_to_all x1 -> x0, blocking collectives: 21.7 us -> none  [on_device(): lax.all_to_all(parcel, 'space', split_axis=0, concat_axis=0, tiled=True)]
    all_to_all x0 -> x2, starting transfers between devices: none -> 10.8 us  [the longest x1 5.65 us: on_device(): lax.all_to_all(lower, 'space', split_axis=0, concat_axis=0, tiled=True)]
    all_to_all x0 -> x2, waiting for transfers between devices: none -> 8.28 us  [the longest x1 8.27 us: on_device(): lax.all_to_all(lower, 'space', split_axis=0, concat_axis=0, tiled=True)]
    pallas_call x6 -> x9, Pallas kernels: 6.8 us -> 9.51 us  [call(): pl.pallas_call(kernel, out_shape=out_shape, in_specs=[smem] * scalars + [...]
    ppermute x2, waiting for transfers between devices: 2.5 us -> 0.01 us  [from_below(): lax.ppermute(block, axis, [(i - 1, i) for i in range(1, lax.axis_size(axi...]
    all_to_all x1, waiting for transfers between devices: 0.01 us -> 2.37 us  [on_device(): lax.all_to_all(parcels, 'space', split_axis=0, concat_axis=0, tiled=True)]
    ppermute x2, starting transfers between devices: 8.02 us -> 6.03 us  [from_below(): lax.ppermute(block, axis, [(i - 1, i) for i in range(1, lax.axis_size(axi...]
    slice x3 -> x0, local copies, waits for them, and re-layouts: 1.78 us -> none  [the longest x1 0.91 us: on_device(): halo = from_below(slab[3:], 'space')]
  transfers between devices with their start and end apart: 18 -> 23, of which waited for: 7 -> 8; matrix products, arithmetic and copies ran while one was open for 1% -> 0% of each run, Pallas kernels for 6% -> 11%
where the time goes in v2:
time: 68.1 us; the launch traced here: 67.5 us
  starting transfers between devices  34.2 us (50%)
  waiting for transfers between devices  20.2 us (30%)
  Pallas kernels  9.51 us (14%)
  local copies, waits for them, and re-layouts  2.84 us (4%)
  between operations  0.77 us (1%)
    ppermute x18, starting transfers between devices, swap_ranks(): lax.ppermute(block, axis, [(i, i ^ k) for i in range(lax.axis_size(axis))])  10.1 us
    ppermute x18, waiting for transfers between devices, swap_ranks(): lax.ppermute(block, axis, [(i, i ^ k) for i in range(lax.axis_size(axis))])  9.57 us
    pallas_call x9, Pallas kernels, call(): pl.pallas_call(kernel, out_shape=out_shape, in_specs=[smem] * scalars + [...  9.51 us
    all_to_all x1, waiting for transfers between devices, on_device(): lax.all_to_all(lower, 'space', split_axis=0, concat_axis=0, tiled=True)  8.27 us
    all_to_all x1, starting transfers between devices, on_device(): lax.all_to_all(parcels, 'space', split_axis=0, concat_axis=0, tiled=True)  7.25 us
    ppermute x2, starting transfers between devices, from_below(): lax.ppermute(block, axis, [(i - 1, i) for i in range(1, lax.axis_size(axi...  6.03 us
    all_to_all x1, starting transfers between devices, on_device(): lax.all_to_all(lower, 'space', split_axis=0, concat_axis=0, tiled=True)  5.65 us
    all_to_all x1, starting transfers between devices, on_device(): lax.all_to_all(upper, 'space', split_axis=0, concat_axis=0, tiled=True)  5.13 us
  transfers between devices with their start and end apart: 23, of which 8 were waited for; matrix products, arithmetic and copies ran while one was open for 0% of the time, Pallas kernels for 11%

profile of v2, /device:TPU:0, one launch (start us, length us, event | category | flops | bytes accessed | tf_op | source)
XLA Modules:
  0.0 67.5 jit_solution(11263235925380788274)
XLA Ops:
  0.6 0.0 copy-start.1
  0.6 1.0 %copy-done.1 = bf16[1,4,64,1024]{3,2,1,0:T(8,128)(2,1)S(1)} copy-done((bf16[1,4,64,1024]{3,2,1,0:T(8,128)(2,1)S(1)}, bf16[1,4,64,1024]{3,2,1,0:T(8,128)(2,1)}, u32[]{:S(2)}) %copy-start.1) | copy-done | bytes 524312
  1.7 0.0 copy-start.3
  1.7 0.9 %copy-done.3 = bf16[864,128]{1,0:T(8,128)(2,1)S(1)} copy-done((bf16[864,128]{1,0:T(8,128)(2,1)S(1)}, bf16[864,128]{1,0:T(8,128)(2,1)}, u32[]{:S(2)}) %copy-start.3) | copy-done | bytes 221208
  2.6 0.0 copy-start.5
  2.6 0.8 %copy-done.5 = bf16[1,32,8,128]{3,2,1,0:T(8,128)(2,1)S(1)} copy-done((bf16[1,32,8,128]{3,2,1,0:T(8,128)(2,1)S(1)}, bf16[1,32,8,128]{3,2,1,0:T(8,128)(2,1)}, u32[]{:S(2)}) %copy-start.5) | copy-done | bytes 65560
  3.5 1.1 %shard_map.67 = (bf16[8,64,128]{2,1,0:T(8,128)(2,1)}, bf16[1,64,1024]{2,1,0:T(8,128)(2,1)S(1)}, bf16[4,128,128]{2,1,0:T(8,128)(2,1)S(1)}, f32[4,128,128]{2,1,0:T(8,128)S(1)}, bf16[256,1152]{1,0:T(8,128)(2,1)S(1)}) custom-call(bf16[32,8,128]{2,1,0:T(8,128)(2,1)S(1)} %bitcast.6, bf16[4,64,1024]{2,1,0:T(8,128)(2,1)S(1)} %bitcast.4, bf16[864,128]{1,0:T(8,128)(2,1)S(1)} %copy-done.3), custom_call_target="tpu_custom_call" | custom-call | flops 1000000000 | bytes 811008 | tf_op jit(solution)/shard_map/pallas_call | solution.py:287
  4.5 7.3 %all-to-all-start = ((bf16[8,64,128]{2,1,0:T(8,128)(2,1)}), bf16[8,64,128]{2,1,0:T(8,128)(2,1)S(1)}, u32[]{:S(2)}, u32[]{:S(2)}) async-start(bf16[8,64,128]{2,1,0:T(8,128)(2,1)} %get-tuple-element.19), calls=%async_computation | async-start | bytes 262144 | tf_op jit(solution)/shard_map/all_to_all | solution.py:335
  11.8 1.5 %collective-permute-start.12 = (bf16[4,128,128]{2,1,0:T(8,128)(2,1)S(1)}, bf16[4,128,128]{2,1,0:T(8,128)(2,1)S(1)}, u32[]{:S(2)}, u32[]{:S(2)}) collective-permute-start(bf16[4,128,128]{2,1,0:T(8,128)(2,1)S(1)} %get-tuple-element.30.h1.refs_4_), channel_id=1, source_target_pairs={{0,16},{8,24},{16,0},{24,8},{1,17},{9,25},{17,1},{25,9},{2,18},{10... | collective-permute-start | bytes 393224 | tf_op jit(solution)/shard_map/ppermute | solution.py:303
  13.3 0.0 collective-permute-start.11
  13.3 3.4 %collective-permute-done.12.refs_6_ = bf16[4,128,128]{2,1,0:T(8,128)(2,1)S(1)} collective-permute-done((bf16[4,128,128]{2,1,0:T(8,128)(2,1)S(1)}, bf16[4,128,128]{2,1,0:T(8,128)(2,1)S(1)}, u32[]{:S(2)}, u32[]{:S(2)}) %collective-permute-start.12) | collective-permute-done | bytes 131104 | tf_op jit(solution)/shard_map/ppermute | solution.py:303
  16.8 0.0 collective-permute-start.13
  16.8 2.4 %all-to-all-done.cot = bf16[8,64,128]{2,1,0:T(8,128)(2,1)S(1)} async-done(((bf16[8,64,128]{2,1,0:T(8,128)(2,1)}), bf16[8,64,128]{2,1,0:T(8,128)(2,1)S(1)}, u32[]{:S(2)}, u32[]{:S(2)}) %all-to-all-start) | async-done | bytes 131104 | tf_op jit(solution)/shard_map/all_to_all | solution.py:335
  19.2 0.1 collective-permute-start.2
  19.2 1.6 %collective-permute-start.1 = (bf16[8,16,128]{2,1,0:T(8,128)(2,1)S(1)}, bf16[8,16,128]{2,1,0:T(8,128)(2,1)S(1)}, u32[]{:S(2)}, u32[]{:S(2)}) collective-permute-start(bf16[8,16,128]{2,1,0:T(8,128)(2,1)S(1)} %get-tuple-element.36), channel_id=1, source_target_pairs={{0,16},{8,24},{16,0},{24,8},{1,17},{9,25},{17,1},{25,9},{2,18},{10... | collective-permute-start | bytes 98312 | tf_op jit(solution)/shard_map/ppermute | solution.py:303
  20.8 0.3 collective-permute-start
  21.1 0.0 collective-permute-done.11.refs_5_
  21.1 2.1 %collective-permute-start.3 = (bf16[1,64,1024]{2,1,0:T(8,128)(2,1)S(1)}, bf16[1,64,1024]{2,1,0:T(8,128)(2,1)S(1)}, u32[]{:S(2)}, u32[]{:S(2)}) collective-permute-start(bf16[1,64,1024]{2,1,0:T(8,128)(2,1)S(1)} %get-tuple-element.20), channel_id=1, source_target_pairs={{0,1},{1,2},{2,3},{3,4},{4,5},{5,6},{6,7},{8,9},{9,10},{10,11},{11... | collective-permute-start | bytes 393224 | tf_op jit(solution)/shard_map/ppermute | solution.py:307
  23.2 0.0 collective-permute-done.2.refs_3_
  23.2 0.0 collective-permute-done.1.refs_2_
  23.3 0.0 collective-permute-done.refs_1_
  23.3 0.0 collective-permute-done.13.refs_7_
  23.3 0.0 copy-start.4
  23.3 1.4 %shard_map.73 = bf16[8,8,2304]{2,1,0:T(8,128)(2,1)} custom-call(bf16[8,16,128]{2,1,0:T(8,128)(2,1)S(1)} %get-tuple-element.38.refs_0_, bf16[8,16,128]{2,1,0:T(8,128)(2,1)S(1)} %collective-permute-done.refs_1_, bf16[8,16,128]{2,1,0:T(8,128)(2,1)S(1)} %collective-permute-done.1.refs_2_, bf16[8,16,128]{2,1,0:T(8,128)(2,1)S(1)} %collective-permute-done.2.refs_3_, ...), custom_call_target="tpu_custom_call" | custom-call | flops 1000000000 | bytes 655360 | tf_op jit(solution)/shard_map/pallas_call | solution.py:287
  24.7 5.1 %all-to-all-start.2 = ((bf16[8,8,2304]{2,1,0:T(8,128)(2,1)}), bf16[8,8,2304]{2,1,0:T(8,128)(2,1)S(1)}, u32[]{:S(2)}, u32[]{:S(2)}) async-start(bf16[8,8,2304]{2,1,0:T(8,128)(2,1)} %shard_map.73), calls=%async_computation.2 | async-start | bytes 589824 | tf_op jit(solution)/shard_map/all_to_all | solution.py:403
  29.8 0.0 collective-permute-done.3.halo
  29.8 0.0 copy-done.2
  29.9 0.0 copy-done.4
  29.9 0.8 %shard_map.68 = (bf16[4,128,128]{2,1,0:T(8,128)(2,1)S(1)}, f32[4,128,128]{2,1,0:T(8,128)S(1)}, bf16[256,1152]{1,0:T(8,128)(2,1)S(1)}) custom-call(bf16[4,64,1024]{2,1,0:T(8,128)(2,1)S(1)} %bitcast.5, bf16[1,64,1024]{2,1,0:T(8,128)(2,1)S(1)} %collective-permute-done.3.halo, bf16[864,128]{1,0:T(8,128)(2,1)S(1)} %copy-done.4), custom_call_target="tpu_custom_call" | custom-call | flops 1000000000 | bytes 876544 | tf_op jit(solution)/shard_map/pallas_call | solution.py:287
  30.6 0.7 %collective-permute-start.5 = (bf16[4,128,128]{2,1,0:T(8,128)(2,1)S(1)}, bf16[4,128,128]{2,1,0:T(8,128)(2,1)S(1)}, u32[]{:S(2)}, u32[]{:S(2)}) collective-permute-start(bf16[4,128,128]{2,1,0:T(8,128)(2,1)S(1)} %get-tuple-element.21.h0.refs_4_), channel_id=1, source_target_pairs={{0,16},{8,24},{16,0},{24,8},{1,17},{9,25},{17,1},{25,9},{2,18},{10... | collective-permute-start | bytes 393224 | tf_op jit(solution)/shard_map/ppermute | solution.py:303
  31.3 3.9 %collective-permute-start.10 = (bf16[4,128,128]{2,1,0:T(8,128)(2,1)S(1)}, bf16[4,128,128]{2,1,0:T(8,128)(2,1)S(1)}, u32[]{:S(2)}, u32[]{:S(2)}) collective-permute-start(bf16[4,128,128]{2,1,0:T(8,128)(2,1)S(1)} %get-tuple-element.30.h1.refs_4_), channel_id=1, source_target_pairs={{0,1},{1,2},{2,3},{3,4},{4,5},{5,6},{6,7},{8,9},{9,10},{10,11},{11... | collective-permute-start | bytes 393224 | tf_op jit(solution)/shard_map/ppermute | solution.py:307
  35.2 0.1 collective-permute-start.4
  35.3 0.3 collective-permute-done.5.refs_6_
  35.7 0.2 collective-permute-start.6
  35.8 0.0 copy-done
  35.8 2.5 %shard_map.69 = (bf16[64,640]{1,0:T(8,128)(2,1)S(1)}, bf16[64,640]{1,0:T(8,128)(2,1)S(1)}, bf16[64,640]{1,0:T(8,128)(2,1)S(1)}, bf16[64,640]{1,0:T(8,128)(2,1)S(1)}) custom-call(s32[1]{0:T(128)} %bitcast.2.place, bf16[8,64,128]{2,1,0:T(8,128)(2,1)S(1)} %all-to-all-done.cot, bf16[3456,256]{1,0:T(8,128)(2,1)S(1)} %copy-done, ...), custom_call_target="tpu_custom_call" | custom-call | flops 1000000000 | bytes 3604484 | tf_op jit(solution)/shard_map/pallas_call | solution.py:287
  38.3 0.4 collective-permute-start.7
  38.7 1.1 %collective-permute-start.8 = (bf16[64,640]{1,0:T(8,128)(2,1)S(1)}, bf16[64,640]{1,0:T(8,128)(2,1)S(1)}, u32[]{:S(2)}, u32[]{:S(2)}) collective-permute-start(bf16[64,640]{1,0:T(8,128)(2,1)S(1)} %get-tuple-element.28), channel_id=1, source_target_pairs={{0,16},{8,24},{16,0},{24,8},{1,17},{9,25},{17,1},{25,9},{2,18},{10... | collective-permute-start | bytes 245768 | tf_op jit(solution)/shard_map/ppermute | solution.py:303
  39.8 0.0 collective-permute-done.10.below
  39.8 0.4 collective-permute-start.9
  40.2 0.8 %shard_map.70.refs_12_ = bf16[256,128]{1,0:T(8,128)(2,1)S(1)} custom-call(bf16[4,128,128]{2,1,0:T(8,128)(2,1)S(1)} %get-tuple-element.21.h0.refs_4_, bf16[4,128,128]{2,1,0:T(8,128)(2,1)S(1)} %get-tuple-element.30.h1.refs_4_, bf16[4,128,128]{2,1,0:T(8,128)(2,1)S(1)} %collective-permute-done.10.below, bf16[3456,256]{1,0:T(8,128)(2,1)S(1)} %copy-done), custom_call_target="tpu_custom_call" | custom-call | flops 1000000000 | bytes 2162688 | tf_op jit(solution)/shard_map/pallas_call | solution.py:287
  41.1 0.0 collective-permute-done.4.refs_5_
  41.1 0.0 collective-permute-done.7.refs_9_
  41.1 2.6 %collective-permute-done.8.refs_10_ = bf16[64,640]{1,0:T(8,128)(2,1)S(1)} collective-permute-done((bf16[64,640]{1,0:T(8,128)(2,1)S(1)}, bf16[64,640]{1,0:T(8,128)(2,1)S(1)}, u32[]{:S(2)}, u32[]{:S(2)}) %collective-permute-start.8) | collective-permute-done | bytes 81952 | tf_op jit(solution)/shard_map/ppermute | solution.py:303
  43.7 0.8 %collective-permute-done.9.refs_11_ = bf16[64,640]{1,0:T(8,128)(2,1)S(1)} collective-permute-done((bf16[64,640]{1,0:T(8,128)(2,1)S(1)}, bf16[64,640]{1,0:T(8,128)(2,1)S(1)}, u32[]{:S(2)}, u32[]{:S(2)}) %collective-permute-start.9) | collective-permute-done | bytes 81952 | tf_op jit(solution)/shard_map/ppermute | solution.py:303
  44.5 0.0 collective-permute-done.6.refs_7_
  44.5 1.3 %shard_map.71 = bf16[8,8,2304]{2,1,0:T(8,128)(2,1)} custom-call(bf16[8,16,128]{2,1,0:T(8,128)(2,1)S(1)} %get-tuple-element.38.refs_0_, bf16[8,16,128]{2,1,0:T(8,128)(2,1)S(1)} %collective-permute-done.refs_1_, bf16[8,16,128]{2,1,0:T(8,128)(2,1)S(1)} %collective-permute-done.1.refs_2_, bf16[8,16,128]{2,1,0:T(8,128)(2,1)S(1)} %collective-permute-done.2.refs_3_, ...), custom_call_target="tpu_custom_call" | custom-call | flops 1000000000 | bytes 1048576 | tf_op jit(solution)/shard_map/pallas_call | solution.py:287
  45.8 0.0 all-to-all-done.2.got
  45.8 5.7 %all-to-all-start.1 = ((bf16[8,8,2304]{2,1,0:T(8,128)(2,1)}), bf16[8,8,2304]{2,1,0:T(8,128)(2,1)S(1)}, u32[]{:S(2)}, u32[]{:S(2)}) async-start(bf16[8,8,2304]{2,1,0:T(8,128)(2,1)} %shard_map.71), calls=%async_computation.1 | async-start | bytes 589824 | tf_op jit(solution)/shard_map/all_to_all | solution.py:413
  51.5 0.8 %collective-permute-start.16 = (bf16[8,2304]{1,0:T(8,128)(2,1)S(1)}, bf16[8,2304]{1,0:T(8,128)(2,1)S(1)}, u32[]{:S(2)}, u32[]{:S(2)}) collective-permute-start(bf16[8,2304]{1,0:T(8,128)(2,1)S(1)} %shard_map.74.refs_0_), channel_id=1, source_target_pairs={{0,24},{8,16},{16,8},{24,0},{1,25},{9,17},{17,9},{25,1},{2,26},{10... | collective-permute-start | bytes 110600 | tf_op jit(solution)/shard_map/ppermute | solution.py:303
  52.2 1.2 %collective-permute-start.15 = (bf16[8,2304]{1,0:T(8,128)(2,1)S(1)}, bf16[8,2304]{1,0:T(8,128)(2,1)S(1)}, u32[]{:S(2)}, u32[]{:S(2)}) collective-permute-start(bf16[8,2304]{1,0:T(8,128)(2,1)S(1)} %shard_map.74.refs_0_), channel_id=1, source_target_pairs={{0,16},{8,24},{16,0},{24,8},{1,17},{9,25},{17,1},{25,9},{2,18},{10... | collective-permute-start | bytes 110600 | tf_op jit(solution)/shard_map/ppermute | solution.py:303
  53.4 0.0 collective-permute-start.14
  53.4 8.3 %all-to-all-done.1.got = bf16[8,8,2304]{2,1,0:T(8,128)(2,1)S(1)} async-done(((bf16[8,8,2304]{2,1,0:T(8,128)(2,1)}), bf16[8,8,2304]{2,1,0:T(8,128)(2,1)S(1)}, u32[]{:S(2)}, u32[]{:S(2)}) %all-to-all-start.1) | async-done | bytes 294944 | tf_op jit(solution)/shard_map/all_to_all | solution.py:413
  61.7 0.8 %shard_map.72 = (bf16[8,1792]{1,0:T(8,128)(2,1)S(1)}, bf16[32,8,128]{2,1,0:T(8,128)(2,1)}) custom-call(bf16[8,8,2304]{2,1,0:T(8,128)(2,1)S(1)} %all-to-all-done.1.got), custom_call_target="tpu_custom_call" | custom-call | flops 1000000 | bytes 294912 | tf_op jit(solution)/shard_map/pallas_call | solution.py:287
  62.5 0.0 collective-permute-start.19
  62.5 1.1 %collective-permute-start.18 = (bf16[8,1792]{1,0:T(8,128)(2,1)S(1)}, bf16[8,1792]{1,0:T(8,128)(2,1)S(1)}, u32[]{:S(2)}, u32[]{:S(2)}) collective-permute-start(bf16[8,1792]{1,0:T(8,128)(2,1)S(1)} %get-tuple-element.32.refs_4_), channel_id=1, source_target_pairs={{0,16},{8,24},{16,0},{24,8},{1,17},{9,25},{17,1},{25,9},{2,18},{10... | collective-permute-start | bytes 86024 | tf_op jit(solution)/shard_map/ppermute | solution.py:303
  63.6 0.0 collective-permute-done.16.refs_3_
  63.6 0.8 %collective-permute-start.17 = (bf16[8,1792]{1,0:T(8,128)(2,1)S(1)}, bf16[8,1792]{1,0:T(8,128)(2,1)S(1)}, u32[]{:S(2)}, u32[]{:S(2)}) collective-permute-start(bf16[8,1792]{1,0:T(8,128)(2,1)S(1)} %get-tuple-element.32.refs_4_), channel_id=1, source_target_pairs={{0,8},{8,0},{16,24},{24,16},{1,9},{9,1},{17,25},{25,17},{2,10},{10... | collective-permute-start | bytes 86024 | tf_op jit(solution)/shard_map/ppermute | solution.py:303
  64.4 0.0 collective-permute-done.15.refs_2_
  64.4 0.0 collective-permute-done.14.refs_1_
  64.4 1.4 %collective-permute-done.19.refs_7_ = bf16[8,1792]{1,0:T(8,128)(2,1)S(1)} collective-permute-done((bf16[8,1792]{1,0:T(8,128)(2,1)S(1)}, bf16[8,1792]{1,0:T(8,128)(2,1)S(1)}, u32[]{:S(2)}, u32[]{:S(2)}) %collective-permute-start.19) | collective-permute-done | bytes 28704 | tf_op jit(solution)/shard_map/ppermute | solution.py:303
  65.8 0.9 %collective-permute-done.18.refs_6_ = bf16[8,1792]{1,0:T(8,128)(2,1)S(1)} collective-permute-done((bf16[8,1792]{1,0:T(8,128)(2,1)S(1)}, bf16[8,1792]{1,0:T(8,128)(2,1)S(1)}, u32[]{:S(2)}, u32[]{:S(2)}) %collective-permute-start.18) | collective-permute-done | bytes 28704 | tf_op jit(solution)/shard_map/ppermute | solution.py:303
  66.7 0.0 collective-permute-done.17.refs_5_
  66.7 0.9 %shard_map.75 = (f32[16,864]{1,0:T(8,128)}, f32[32,3456]{1,0:T(8,128)}) custom-call(s32[1]{0:T(128)} %bitcast.2.place, bf16[8,2304]{1,0:T(8,128)(2,1)S(1)} %shard_map.74.refs_0_, bf16[8,2304]{1,0:T(8,128)(2,1)S(1)} %collective-permute-done.14.refs_1_, bf16[8,2304]{1,0:T(8,128)(2,1)S(1)} %collective-permute-done.15.refs_2_, ...), custom_call_target="tpu_custom_call" | custom-call | flops 1000000 | bytes 262148 | tf_op jit(solution)/shard_map/pallas_call | solution.py:287
  (4 shorter events, 0.1 us)
Async XLA Ops:
  0.6 1.0 %copy-start.1 = (bf16[1,4,64,1024]{3,2,1,0:T(8,128)(2,1)S(1)}, bf16[1,4,64,1024]{3,2,1,0:T(8,128)(2,1)}, u32[]{:S(2)}) copy-start(bf16[1,4,64,1024]{3,2,1,0:T(8,128)(2,1)} %param.4) | copy-start | bytes 1572868
  1.7 0.9 %copy-start.3 = (bf16[864,128]{1,0:T(8,128)(2,1)S(1)}, bf16[864,128]{1,0:T(8,128)(2,1)}, u32[]{:S(2)}) copy-start(bf16[864,128]{1,0:T(8,128)(2,1)} %w1.3) | copy-start | bytes 663556
  2.6 0.8 %copy-start.5 = (bf16[1,32,8,128]{3,2,1,0:T(8,128)(2,1)S(1)}, bf16[1,32,8,128]{3,2,1,0:T(8,128)(2,1)}, u32[]{:S(2)}) copy-start(bf16[1,32,8,128]{3,2,1,0:T(8,128)(2,1)} %param.7) | copy-start | bytes 196612
  4.5 14.6 %all-to-all-start = ((bf16[8,64,128]{2,1,0:T(8,128)(2,1)}), bf16[8,64,128]{2,1,0:T(8,128)(2,1)S(1)}, u32[]{:S(2)}, u32[]{:S(2)}) async-start(bf16[8,64,128]{2,1,0:T(8,128)(2,1)} %get-tuple-element.19), calls=%async_computation | async-start | bytes 262144 | tf_op jit(solution)/shard_map/all_to_all | solution.py:335
  11.8 5.0 %collective-permute-start.12 = (bf16[4,128,128]{2,1,0:T(8,128)(2,1)S(1)}, bf16[4,128,128]{2,1,0:T(8,128)(2,1)S(1)}, u32[]{:S(2)}, u32[]{:S(2)}) collective-permute-start(bf16[4,128,128]{2,1,0:T(8,128)(2,1)S(1)} %get-tuple-element.30.h1.refs_4_), channel_id=1, source_target_pairs={{0,16},{8,24},{16,0},{24,8},{1,17},{9,25},{17,1},{25,9},{2,18},{10... | collective-permute-start | bytes 393224 | tf_op jit(solution)/shard_map/ppermute | solution.py:303
  13.3 7.8 %collective-permute-start.11 = (bf16[4,128,128]{2,1,0:T(8,128)(2,1)S(1)}, bf16[4,128,128]{2,1,0:T(8,128)(2,1)S(1)}, u32[]{:S(2)}, u32[]{:S(2)}) collective-permute-start(bf16[4,128,128]{2,1,0:T(8,128)(2,1)S(1)} %get-tuple-element.30.h1.refs_4_), channel_id=1, source_target_pairs={{0,8},{8,0},{16,24},{24,16},{1,9},{9,1},{17,25},{25,17},{2,10},{10... | collective-permute-start | bytes 393224 | tf_op jit(solution)/shard_map/ppermute | solution.py:303
  16.8 6.5 %collective-permute-start.13 = (bf16[4,128,128]{2,1,0:T(8,128)(2,1)S(1)}, bf16[4,128,128]{2,1,0:T(8,128)(2,1)S(1)}, u32[]{:S(2)}, u32[]{:S(2)}) collective-permute-start(bf16[4,128,128]{2,1,0:T(8,128)(2,1)S(1)} %collective-permute-done.12.refs_6_), channel_id=1, source_target_pairs={{0,8},{8,0},{16,24},{24,16},{1,9},{9,1},{17,25},{25,17},{2,10},{10... | collective-permute-start | bytes 393224 | tf_op jit(solution)/shard_map/ppermute | solution.py:303
  19.2 4.1 %collective-permute-start.2 = (bf16[8,16,128]{2,1,0:T(8,128)(2,1)S(1)}, bf16[8,16,128]{2,1,0:T(8,128)(2,1)S(1)}, u32[]{:S(2)}, u32[]{:S(2)}) collective-permute-start(bf16[8,16,128]{2,1,0:T(8,128)(2,1)S(1)} %get-tuple-element.35), channel_id=1, source_target_pairs={{0,24},{8,16},{16,8},{24,0},{1,25},{9,17},{17,9},{25,1},{2,26},{10... | collective-permute-start | bytes 98312 | tf_op jit(solution)/shard_map/ppermute | solution.py:303
  19.2 4.0 %collective-permute-start.1 = (bf16[8,16,128]{2,1,0:T(8,128)(2,1)S(1)}, bf16[8,16,128]{2,1,0:T(8,128)(2,1)S(1)}, u32[]{:S(2)}, u32[]{:S(2)}) collective-permute-start(bf16[8,16,128]{2,1,0:T(8,128)(2,1)S(1)} %get-tuple-element.36), channel_id=1, source_target_pairs={{0,16},{8,24},{16,0},{24,8},{1,17},{9,25},{17,1},{25,9},{2,18},{10... | collective-permute-start | bytes 98312 | tf_op jit(solution)/shard_map/ppermute | solution.py:303
  20.8 2.4 %collective-permute-start = (bf16[8,16,128]{2,1,0:T(8,128)(2,1)S(1)}, bf16[8,16,128]{2,1,0:T(8,128)(2,1)S(1)}, u32[]{:S(2)}, u32[]{:S(2)}) collective-permute-start(bf16[8,16,128]{2,1,0:T(8,128)(2,1)S(1)} %get-tuple-element.37), channel_id=1, source_target_pairs={{0,8},{8,0},{16,24},{24,16},{1,9},{9,1},{17,25},{25,17},{2,10},{10... | collective-permute-start | bytes 98312 | tf_op jit(solution)/shard_map/ppermute | solution.py:303
  21.1 8.7 %collective-permute-start.3 = (bf16[1,64,1024]{2,1,0:T(8,128)(2,1)S(1)}, bf16[1,64,1024]{2,1,0:T(8,128)(2,1)S(1)}, u32[]{:S(2)}, u32[]{:S(2)}) collective-permute-start(bf16[1,64,1024]{2,1,0:T(8,128)(2,1)S(1)} %get-tuple-element.20), channel_id=1, source_target_pairs={{0,1},{1,2},{2,3},{3,4},{4,5},{5,6},{6,7},{8,9},{9,10},{10,11},{11... | collective-permute-start | bytes 393224 | tf_op jit(solution)/shard_map/ppermute | solution.py:307
  23.3 6.6 %copy-start.2 = (bf16[1,4,64,1024]{3,2,1,0:T(8,128)(2,1)S(1)}, bf16[1,4,64,1024]{3,2,1,0:T(8,128)(2,1)}, u32[]{:S(2)}) copy-start(bf16[1,4,64,1024]{3,2,1,0:T(8,128)(2,1)} %param.4) | copy-start | bytes 1572868
  23.3 6.6 %copy-start.4 = (bf16[864,128]{1,0:T(8,128)(2,1)S(1)}, bf16[864,128]{1,0:T(8,128)(2,1)}, u32[]{:S(2)}) copy-start(bf16[864,128]{1,0:T(8,128)(2,1)} %w1.3) | copy-start | bytes 663556
  24.7 21.1 %all-to-all-start.2 = ((bf16[8,8,2304]{2,1,0:T(8,128)(2,1)}), bf16[8,8,2304]{2,1,0:T(8,128)(2,1)S(1)}, u32[]{:S(2)}, u32[]{:S(2)}) async-start(bf16[8,8,2304]{2,1,0:T(8,128)(2,1)} %shard_map.73), calls=%async_computation.2 | async-start | bytes 589824 | tf_op jit(solution)/shard_map/all_to_all | solution.py:403
  29.8 6.0 %copy-start = (bf16[3456,256]{1,0:T(8,128)(2,1)S(1)}, bf16[3456,256]{1,0:T(8,128)(2,1)}, u32[]{:S(2)}) copy-start(bf16[3456,256]{1,0:T(8,128)(2,1)} %w2.3) | copy-start | bytes 5308420
  30.6 5.0 %collective-permute-start.5 = (bf16[4,128,128]{2,1,0:T(8,128)(2,1)S(1)}, bf16[4,128,128]{2,1,0:T(8,128)(2,1)S(1)}, u32[]{:S(2)}, u32[]{:S(2)}) collective-permute-start(bf16[4,128,128]{2,1,0:T(8,128)(2,1)S(1)} %get-tuple-element.21.h0.refs_4_), channel_id=1, source_target_pairs={{0,16},{8,24},{16,0},{24,8},{1,17},{9,25},{17,1},{25,9},{2,18},{10... | collective-permute-start | bytes 393224 | tf_op jit(solution)/shard_map/ppermute | solution.py:303
  31.3 8.5 %collective-permute-start.10 = (bf16[4,128,128]{2,1,0:T(8,128)(2,1)S(1)}, bf16[4,128,128]{2,1,0:T(8,128)(2,1)S(1)}, u32[]{:S(2)}, u32[]{:S(2)}) collective-permute-start(bf16[4,128,128]{2,1,0:T(8,128)(2,1)S(1)} %get-tuple-element.30.h1.refs_4_), channel_id=1, source_target_pairs={{0,1},{1,2},{2,3},{3,4},{4,5},{5,6},{6,7},{8,9},{9,10},{10,11},{11... | collective-permute-start | bytes 393224 | tf_op jit(solution)/shard_map/ppermute | solution.py:307
  35.2 5.8 %collective-permute-start.4 = (bf16[4,128,128]{2,1,0:T(8,128)(2,1)S(1)}, bf16[4,128,128]{2,1,0:T(8,128)(2,1)S(1)}, u32[]{:S(2)}, u32[]{:S(2)}) collective-permute-start(bf16[4,128,128]{2,1,0:T(8,128)(2,1)S(1)} %get-tuple-element.21.h0.refs_4_), channel_id=1, source_target_pairs={{0,8},{8,0},{16,24},{24,16},{1,9},{9,1},{17,25},{25,17},{2,10},{10... | collective-permute-start | bytes 393224 | tf_op jit(solution)/shard_map/ppermute | solution.py:303
  35.7 8.9 %collective-permute-start.6 = (bf16[4,128,128]{2,1,0:T(8,128)(2,1)S(1)}, bf16[4,128,128]{2,1,0:T(8,128)(2,1)S(1)}, u32[]{:S(2)}, u32[]{:S(2)}) collective-permute-start(bf16[4,128,128]{2,1,0:T(8,128)(2,1)S(1)} %collective-permute-done.5.refs_6_), channel_id=1, source_target_pairs={{0,8},{8,0},{16,24},{24,16},{1,9},{9,1},{17,25},{25,17},{2,10},{10... | collective-permute-start | bytes 393224 | tf_op jit(solution)/shard_map/ppermute | solution.py:303
  38.3 2.8 %collective-permute-start.7 = (bf16[64,640]{1,0:T(8,128)(2,1)S(1)}, bf16[64,640]{1,0:T(8,128)(2,1)S(1)}, u32[]{:S(2)}, u32[]{:S(2)}) collective-permute-start(bf16[64,640]{1,0:T(8,128)(2,1)S(1)} %get-tuple-element.27), channel_id=1, source_target_pairs={{0,8},{8,0},{16,24},{24,16},{1,9},{9,1},{17,25},{25,17},{2,10},{10... | collective-permute-start | bytes 245768 | tf_op jit(solution)/shard_map/ppermute | solution.py:303
  38.7 5.0 %collective-permute-start.8 = (bf16[64,640]{1,0:T(8,128)(2,1)S(1)}, bf16[64,640]{1,0:T(8,128)(2,1)S(1)}, u32[]{:S(2)}, u32[]{:S(2)}) collective-permute-start(bf16[64,640]{1,0:T(8,128)(2,1)S(1)} %get-tuple-element.28), channel_id=1, source_target_pairs={{0,16},{8,24},{16,0},{24,8},{1,17},{9,25},{17,1},{25,9},{2,18},{10... | collective-permute-start | bytes 245768 | tf_op jit(solution)/shard_map/ppermute | solution.py:303
  39.8 4.7 %collective-permute-start.9 = (bf16[64,640]{1,0:T(8,128)(2,1)S(1)}, bf16[64,640]{1,0:T(8,128)(2,1)S(1)}, u32[]{:S(2)}, u32[]{:S(2)}) collective-permute-start(bf16[64,640]{1,0:T(8,128)(2,1)S(1)} %get-tuple-element.29), channel_id=1, source_target_pairs={{0,24},{8,16},{16,8},{24,0},{1,25},{9,17},{17,9},{25,1},{2,26},{10... | collective-permute-start | bytes 245768 | tf_op jit(solution)/shard_map/ppermute | solution.py:303
  45.8 15.9 %all-to-all-start.1 = ((bf16[8,8,2304]{2,1,0:T(8,128)(2,1)}), bf16[8,8,2304]{2,1,0:T(8,128)(2,1)S(1)}, u32[]{:S(2)}, u32[]{:S(2)}) async-start(bf16[8,8,2304]{2,1,0:T(8,128)(2,1)} %shard_map.71), calls=%async_computation.1 | async-start | bytes 589824 | tf_op jit(solution)/shard_map/all_to_all | solution.py:413
  51.5 12.1 %collective-permute-start.16 = (bf16[8,2304]{1,0:T(8,128)(2,1)S(1)}, bf16[8,2304]{1,0:T(8,128)(2,1)S(1)}, u32[]{:S(2)}, u32[]{:S(2)}) collective-permute-start(bf16[8,2304]{1,0:T(8,128)(2,1)S(1)} %shard_map.74.refs_0_), channel_id=1, source_target_pairs={{0,24},{8,16},{16,8},{24,0},{1,25},{9,17},{17,9},{25,1},{2,26},{10... | collective-permute-start | bytes 110600 | tf_op jit(solution)/shard_map/ppermute | solution.py:303
  52.2 12.1 %collective-permute-start.15 = (bf16[8,2304]{1,0:T(8,128)(2,1)S(1)}, bf16[8,2304]{1,0:T(8,128)(2,1)S(1)}, u32[]{:S(2)}, u32[]{:S(2)}) collective-permute-start(bf16[8,2304]{1,0:T(8,128)(2,1)S(1)} %shard_map.74.refs_0_), channel_id=1, source_target_pairs={{0,16},{8,24},{16,0},{24,8},{1,17},{9,25},{17,1},{25,9},{2,18},{10... | collective-permute-start | bytes 110600 | tf_op jit(solution)/shard_map/ppermute | solution.py:303
  53.4 10.9 %collective-permute-start.14 = (bf16[8,2304]{1,0:T(8,128)(2,1)S(1)}, bf16[8,2304]{1,0:T(8,128)(2,1)S(1)}, u32[]{:S(2)}, u32[]{:S(2)}) collective-permute-start(bf16[8,2304]{1,0:T(8,128)(2,1)S(1)} %shard_map.74.refs_0_), channel_id=1, source_target_pairs={{0,8},{8,0},{16,24},{24,16},{1,9},{9,1},{17,25},{25,17},{2,10},{10... | collective-permute-start | bytes 110600 | tf_op jit(solution)/shard_map/ppermute | solution.py:303
  62.5 3.3 %collective-permute-start.19 = (bf16[8,1792]{1,0:T(8,128)(2,1)S(1)}, bf16[8,1792]{1,0:T(8,128)(2,1)S(1)}, u32[]{:S(2)}, u32[]{:S(2)}) collective-permute-start(bf16[8,1792]{1,0:T(8,128)(2,1)S(1)} %get-tuple-element.32.refs_4_), channel_id=1, source_target_pairs={{0,24},{8,16},{16,8},{24,0},{1,25},{9,17},{17,9},{25,1},{2,26},{10... | collective-permute-start | bytes 86024 | tf_op jit(solution)/shard_map/ppermute | solution.py:303
  62.5 4.2 %collective-permute-start.18 = (bf16[8,1792]{1,0:T(8,128)(2,1)S(1)}, bf16[8,1792]{1,0:T(8,128)(2,1)S(1)}, u32[]{:S(2)}, u32[]{:S(2)}) collective-permute-start(bf16[8,1792]{1,0:T(8,128)(2,1)S(1)} %get-tuple-element.32.refs_4_), channel_id=1, source_target_pairs={{0,16},{8,24},{16,0},{24,8},{1,17},{9,25},{17,1},{25,9},{2,18},{10... | collective-permute-start | bytes 86024 | tf_op jit(solution)/shard_map/ppermute | solution.py:303
  63.6 3.1 %collective-permute-start.17 = (bf16[8,1792]{1,0:T(8,128)(2,1)S(1)}, bf16[8,1792]{1,0:T(8,128)(2,1)S(1)}, u32[]{:S(2)}, u32[]{:S(2)}) collective-permute-start(bf16[8,1792]{1,0:T(8,128)(2,1)S(1)} %get-tuple-element.32.refs_4_), channel_id=1, source_target_pairs={{0,8},{8,0},{16,24},{24,16},{1,9},{9,1},{17,25},{25,17},{2,10},{10... | collective-permute-start | bytes 86024 | tf_op jit(solution)/shard_map/ppermute | solution.py:303

commit v3 on v1

v3 whole, which is shorter than its diff:
```python
import functools

import jax
import jax.numpy as jnp
from jax import lax
from jax.experimental import pallas as pl
from jax.experimental.pallas import tpu as pltpu
from jax.sharding import PartitionSpec as P

F32 = jnp.float32
BF16 = jnp.bfloat16
VMEM_LIMIT = 16 * 1024 * 1024

FLOPS_PACK, FLOPS_BACK = 10**9, 10**9

NJ, NK, CELLS = 16, 8, 128
ONE_AT, ONE_END, LATENT_AT, NEXT_AT, WIDTH = 3456, 4320, 4352, 4864, 5376
HIDDEN_AT, PACK = (0, 8), 16
TAP_PHASE = {0: (1, 1), 1: (0, 0), 2: (1, 0)}


def dot(a, b):
    return jnp.dot(a, b, preferred_element_type=F32)


def iota(shape, axis):
    return lax.broadcasted_iota(jnp.int32, shape, axis)


def one_hot(mask):
    return jnp.where(mask, 1.0, 0.0).astype(BF16)


def cell_order(shifted):
    width = CELLS * (4 if shifted else 1)
    row, col = iota((CELLS, width), 0), iota((CELLS, width), 1)
    v, cell = col // CELLS, col % CELLS
    to_j, to_k = cell % NJ + v // 2, cell // NJ + v % 2
    return one_hot((to_k < NK) & (row == to_j * NK + to_k))


def fill_patches(planes, p1):
    row, col = iota((80, 64), 0), iota((80, 64), 1)
    pick = one_hot(col == 4 * (row % NJ) + row // NJ - 1)
    for a, rows in enumerate(planes):
        picked = dot(pick, rows).astype(BF16)
        for p in range(2):
            for b in range(3):
                rho = 2 * p + b
                for k in range(NK):
                    at = p * CELLS + k * NJ
                    p1[at : at + NJ, (3 * a + b) * 128 : (3 * a + b + 1) * 128] = picked[
                        rho * NJ : (rho + 1) * NJ, k * 128 : (k + 1) * 128
                    ]


def widen(w1, w_ext):
    for t in range(9):
        base, src = t * 128, t * 96
        zeros = jnp.zeros((128, 128), BF16)
        w_ext[base : base + 64, 0:128] = w1[src + 32 : src + 96, :]
        w_ext[base + 64 : base + 128, 0:128] = zeros[:64]
        w_ext[base : base + 32, 128:256] = zeros[:32]
        w_ext[base + 32 : base + 128, 128:256] = w1[src : src + 96, :]
        w_ext[base : base + 96, 256:384] = zeros[:96]
        w_ext[base + 96 : base + 128, 256:384] = w1[src : src + 32, :]


def fill_hidden(p1, w_ext, hidden, slope_t):
    for p in range(2):
        full = dot(p1[p * CELLS : (p + 1) * CELLS, :], w_ext[...])
        before = jnp.concatenate(
            [jnp.zeros((NJ, 128), F32), full[: CELLS - NJ, 256:384]], axis=0
        )
        for q, pre in enumerate((full[:, 0:128] + before, full[:, 128:256])):
            logistic = 1.0 / (1.0 + jnp.exp(-pre))
            hidden[2 * p + q] = (pre * logistic).astype(BF16)
            if slope_t is not None:
                slope = logistic * (1.0 + pre * (1.0 - logistic))
                slope_t[2 * p + q] = slope.T


def kernel_parcels(pieces, cot_hbm, snap, parcels, halo, cot, sems):
    last = pltpu.make_async_copy(snap.at[pl.ds(3, 1)], halo, sems.at[0])
    whole = pltpu.make_async_copy(cot_hbm, cot, sems.at[1])
    whole.start()
    last.start()
    group, slabs = cot.shape[:2]
    rows_per = group // pieces
    row, col = iota((2 * group * slabs, group * slabs), 0), iota((2 * group * slabs, group * slabs), 1)
    slab = row // (2 * group) + row // rows_per % 2
    channel = row % (2 * group) // (2 * rows_per) * rows_per + row % rows_per
    chosen = one_hot((slab < slabs) & (col == channel * slabs + slab))
    whole.wait()
    flat = cot[...].astype(F32).reshape(-1, CELLS).astype(BF16)
    parcels[...] = dot(chosen, flat).astype(BF16).reshape(slabs, 2 * group, CELLS)
    last.wait()


class Phases:
    def __init__(self, pack, i):
        self.pack, self.at = pack, HIDDEN_AT[i]

    def __setitem__(self, phase, value):
        at = self.at + 2 * phase
        self.pack[at : at + 2] = value.reshape(2, 64, 128)

    def __getitem__(self, phase):
        at = self.at + 2 * phase
        return self.pack[at : at + 2].reshape(CELLS, 128)


def hidden_planes(snap, halo, w_ext, p1, hidden, slope_t):
    for i, planes in enumerate(([halo[0], snap[0], snap[1]], [snap[1], snap[2], snap[3]])):
        fill_patches(planes, p1.at[i])
        fill_hidden(p1.at[i], w_ext, hidden(i), None if slope_t is None else slope_t.at[i])


def kernel_pack(snap_hbm, halo, w1_hbm, pack, snap, w1, p1, w_ext, sems):
    copies = [
        pltpu.make_async_copy(w1_hbm, w1, sems.at[0]),
        pltpu.make_async_copy(snap_hbm, snap, sems.at[1]),
    ]
    for copy in copies:
        copy.start()
    copies[0].wait()
    widen(w1, w_ext)
    copies[1].wait()
    hidden_planes(snap, halo, w_ext, p1, lambda i: Phases(pack, i), None)


def kernel_back(pieces, rows_per, place, snap_hbm, halo, w1_hbm, w2_hbm, cot, *rest):
    *outs, parts, snap, w1, p1, w_ext, w2, hidden, slope_t, grad_t, sems = rest
    copies = [
        pltpu.make_async_copy(w1_hbm, w1, sems.at[0]),
        pltpu.make_async_copy(snap_hbm, snap, sems.at[1]),
        pltpu.make_async_copy(w2_hbm, w2, sems.at[2]),
    ]
    for copy in copies:
        copy.start()
    copies[0].wait()
    widen(w1, w_ext)
    copies[1].wait()
    hidden_planes(snap, halo, w_ext, p1, lambda i: hidden.at[i], slope_t)
    copies[2].wait()
    grad_one_share(pieces, rows_per, place, w2, cot, outs, p1, slope_t, grad_t)
    latent_parts(hidden, w2, parts)


def grad_one_share(pieces, rows_per, place, w2, cot, outs, p1, slope_t, grad_t):
    sources = cot.shape[0]
    moved = dot(cot[...].reshape(-1, CELLS), cell_order(True))
    moved = moved.reshape(sources * pieces, 2, rows_per, 4 * CELLS)
    planes = [moved[:, s].reshape(-1, 4 * CELLS).astype(BF16) for s in range(2)]
    for i in range(2):
        for p in range(2):
            for q in range(2):
                total = None
                for a in (1,) if i == 0 else (2, 0):
                    source = planes[1 if a == 0 else 0]
                    for b in (1,) if p == 0 else (2, 0):
                        for c in (1,) if q == 0 else (2, 0):
                            v = 2 * (b == 0) + (c == 0)
                            tap = 9 * a + 3 * b + c
                            term = dot(
                                w2[tap * 128 : (tap + 1) * 128, :],
                                source[:, v * CELLS : (v + 1) * CELLS],
                            )
                            total = term if total is None else total + term
                pre_t = total * slope_t[i, 2 * p + q]
                at = (2 * i + p) * CELLS
                grad_t[q * 128 : (q + 1) * 128, at : at + CELLS] = pre_t.astype(BF16)
                if q == 0:
                    ahead = pltpu.roll(pre_t, CELLS - NJ, axis=1)
                    ahead = jnp.where(iota((128, CELLS), 1) < CELLS - NJ, ahead, 0.0)
                    grad_t[256:384, at : at + CELLS] = ahead.astype(BF16)
    lane = iota((128, 128), 1)
    frames = []
    for t in range(9):
        cols = slice(t * 128, (t + 1) * 128)
        full = dot(grad_t[:, : 2 * CELLS], p1[0, :, cols])
        full = full + dot(grad_t[:, 2 * CELLS :], p1[1, :, cols])
        side = jnp.where(lane < 64, full[0:128], full[256:384])
        side = jnp.where((lane < 64) | (lane >= 96), side, 0.0)
        own = jnp.where(lane < 32, 0.0, full[128:256])
        frames.append(own + pltpu.roll(side, 64, axis=1))
    if pieces == 1:
        for t in range(9):
            outs[0][:, t * 96 : (t + 1) * 96] = frames[t][:, 32:]
        return
    owned = 128 // sources
    share = owned // 2
    row, col = iota((128 // 2, 128), 0), iota((128 // 2, 128), 1)
    frames = [frame.astype(BF16) for frame in frames]
    for k in range(2):
        half = (place[0] ^ k) & 1
        chosen = one_hot(col == row // share * owned + half * share + row % share)
        for t in range(9):
            value = dot(chosen, frames[t])
            outs[k][:, t * 96 : (t + 1) * 96] = value[:, 32:].astype(BF16)


def latent_parts(hidden, w2, parts):
    row, col = iota((CELLS, CELLS), 0), iota((CELLS, CELLS), 1)
    back = one_hot((row // NJ == col % NK) & (row % NJ == col // NK))
    for part, taps_x in enumerate(((1, 2), (0,))):
        totals = {}
        for b in range(3):
            p, sj = TAP_PHASE[b]
            for c in range(3):
                q, sk = TAP_PHASE[c]
                for a in taps_x:
                    tap = 9 * a + 3 * b + c
                    plane = 0 if a == 1 else 1
                    term = dot(hidden[plane, 2 * p + q], w2[tap * 128 : (tap + 1) * 128, :])
                    v = 2 * sj + sk
                    totals[v] = totals[v] + term if v in totals else term
        zero = jnp.zeros((NJ, totals[0].shape[1]), F32)

        def later(value):
            return jnp.concatenate([zero, value[: CELLS - NJ]], axis=0)

        inner = totals[2] + later(totals[3])
        inner = jnp.where(iota(inner.shape, 0) % NJ == 0, 0.0, pltpu.roll(inner, 1, axis=0))
        rows = totals[0] + later(totals[1]) + inner
        parts[part] = dot(rows.T.astype(BF16), back).astype(BF16)


def moved_rows(cots, rows_per, order):
    moved = []
    for cot in cots:
        value = dot(cot[...].reshape(-1, CELLS), order).reshape(-1, 2, rows_per, 4 * CELLS)
        moved.append([value[:, s].reshape(-1, 4 * CELLS).astype(BF16) for s in range(2)])
    return [
        [
            jnp.concatenate([m[s][:, v * CELLS : (v + 1) * CELLS] for m in moved], axis=1)
            for v in range(4)
        ]
        for s in range(2)
    ]


def kernel_two(samples, rows_per, *refs):
    packs, cots, refs = refs[:samples], refs[samples : 2 * samples], refs[2 * samples :]
    packed = samples > 1
    out = refs[-1]
    left = moved_rows(cots, rows_per, cell_order(True))
    height = left[0][0].shape[0]
    for p in range(2):
        for q in range(2):
            right_0, right_1 = [
                jnp.concatenate([Phases(pack, i)[2 * p + q] for pack in packs], axis=0)
                for i in range(2)
            ]
            both = jnp.concatenate([right_0, right_1], axis=1)
            taps = [
                (b, c)
                for b in range(3)
                for c in range(3)
                if TAP_PHASE[b][0] == p and TAP_PHASE[c][0] == q
            ]
            shifts = [2 * TAP_PHASE[b][1] + TAP_PHASE[c][1] for b, c in taps]
            same = dot(jnp.concatenate([left[0][v] for v in shifts], axis=0), both)
            above = dot(jnp.concatenate([left[1][v] for v in shifts], axis=0), right_1)
            for n, (b, c) in enumerate(taps):
                rows = slice(n * height, (n + 1) * height)
                parts = (above[rows], same[rows, 0:128], same[rows, 128:256])
                for a, value in enumerate(parts):
                    to = (9 * a + 3 * b + c) * 128
                    if packed:
                        out[:, :, to : to + 128] = value.reshape(-1, rows_per, 128).astype(BF16)
                    else:
                        out[:, to : to + 128] = value
    if packed:
        own, other, latent, _ = refs
        total = own[...].astype(F32) + other[...].astype(F32)
        out[:, :, ONE_AT:ONE_END] = total.reshape(-1, rows_per, 864).astype(BF16)
        out[:, :, ONE_END:LATENT_AT] = jnp.zeros(
            (out.shape[0], rows_per, LATENT_AT - ONE_END), BF16
        )
        for part, start in enumerate((LATENT_AT, NEXT_AT)):
            cells = latent[part].astype(F32).reshape(out.shape[0], -1, rows_per, CELLS)
            for w in range(cells.shape[1]):
                to = start + w * 128
                out[:, :, to : to + 128] = cells[:, w].astype(BF16)


def kernel_sum(got, total_out, latent):
    sources, rows_per, _ = got.shape
    for at in range(0, LATENT_AT, 256):
        total = got[0, :, at : at + 256].astype(F32)
        for src in range(1, sources):
            total = total + got[src, :, at : at + 256].astype(F32)
        total_out[:, at : at + 256] = total.astype(BF16)
    height = sources * rows_per
    row, col = iota((height, height), 0), iota((height, height), 1)
    swap = one_hot((row // sources == col % rows_per) & (row % sources == col // rows_per))
    for w in range(latent.shape[0] // rows_per):
        own, next_ = [
            got[:, :, at : at + 128].astype(F32)
            for at in (LATENT_AT + w * 128, NEXT_AT + w * 128)
        ]
        cells = own + jnp.concatenate([jnp.zeros_like(next_[:1]), next_[:-1]], axis=0)
        cells = cells.reshape(height, 128).astype(BF16)
        moved = dot(swap, cells).reshape(rows_per, sources, 128).astype(BF16)
        latent[w * rows_per : (w + 1) * rows_per] = moved


def kernel_final(pieces, place, *refs):
    parts, (one, two) = refs[:pieces], refs[pieces:]
    rows_per = parts[0].shape[0]
    for k in range(pieces):
        at = pl.multiple_of((place[0] ^ k) * rows_per, rows_per)
        two[pl.ds(at, rows_per), :] = parts[k][:, 0:ONE_AT].astype(F32)
    for k in range(2):
        at = pl.multiple_of(((place[0] ^ k) & 1) * rows_per, rows_per)
        shares = [parts[n][:, ONE_AT:ONE_END].astype(F32) for n in (k, k ^ 2)]
        one[pl.ds(at, rows_per), :] = shares[0] + shares[1]


def call(kernel, out_shape, *args, spaces=None, scratch=(), flops=10**9):
    spaces = spaces or {}
    single = isinstance(out_shape, jax.ShapeDtypeStruct)
    vmem = pl.BlockSpec(memory_space=pltpu.VMEM)
    moved = sum(x.size * x.dtype.itemsize for x in args)
    return pl.pallas_call(
        kernel,
        out_shape=out_shape,
        in_specs=[
            pl.BlockSpec(memory_space=spaces.get(n, pltpu.VMEM)) for n in range(len(args))
        ],
        out_specs=vmem if single else [vmem] * len(out_shape),
        scratch_shapes=list(scratch),
        cost_estimate=pl.CostEstimate(flops=flops, bytes_accessed=moved, transcendentals=0),
        compiler_params=pltpu.CompilerParams(vmem_limit_bytes=VMEM_LIMIT),
    )(*args)


def shape(dims, dtype):
    return jax.ShapeDtypeStruct(dims, dtype)


def swap_ranks(block, axis, k):
    return lax.ppermute(block, axis, [(i, i ^ k) for i in range(lax.axis_size(axis))])


def first_of(value, *others):
    return lax.optimization_barrier((value, *others))[0]


def from_below(block, axis):
    return lax.ppermute(block, axis, [(i - 1, i) for i in range(1, lax.axis_size(axis))])


def on_device(snapshot, conv_one, conv_two, cotangent):
    slabs, samples = lax.axis_size("space"), lax.axis_size("dp")
    group = cotangent.shape[1]
    shared = samples == 4 and slabs == 8
    pieces = samples if shared else 1
    rows_per = group // pieces
    place = lax.axis_index("dp").astype(jnp.int32).reshape(1)

    slab = snapshot[0]
    parcels, last = call(
        functools.partial(kernel_parcels, pieces),
        (shape((slabs, 2 * group, CELLS), BF16), shape((1,) + slab.shape[1:], BF16)),
        cotangent[0],
        slab,
        spaces={0: pltpu.HBM, 1: pltpu.HBM},
        scratch=[pltpu.VMEM((group, slabs, CELLS), BF16), pltpu.SemaphoreType.DMA((2,))],
    )
    halo = from_below(last, "space")
    cot = lax.all_to_all(parcels, "space", split_axis=0, concat_axis=0, tiled=True)
    forward = [
        pltpu.VMEM(slab.shape, BF16),
        pltpu.VMEM(conv_one.shape, BF16),
        pltpu.VMEM((2, 2 * CELLS, 9 * 128), BF16),
        pltpu.VMEM((9 * 128, 384), BF16),
    ]
    pack = call(
        kernel_pack,
        shape((PACK, 64, CELLS), BF16),
        slab,
        halo,
        conv_one,
        spaces={0: pltpu.HBM, 2: pltpu.HBM},
        scratch=forward + [pltpu.SemaphoreType.DMA((2,))],
        flops=FLOPS_PACK,
    )
    if shared:
        one_shape = (shape((64, 864), BF16),) * 2
    else:
        one_shape = (shape((128, 864), F32),)
    *ones, parts = call(
        functools.partial(kernel_back, pieces, rows_per),
        one_shape + (shape((2, 256, CELLS), BF16),),
        place,
        slab,
        halo,
        conv_one,
        conv_two,
        cot,
        spaces={0: pltpu.SMEM, 1: pltpu.HBM, 3: pltpu.HBM, 4: pltpu.HBM},
        scratch=forward
        + [
            pltpu.VMEM(conv_two.shape, BF16),
            pltpu.VMEM((2, 4, CELLS, 128), BF16),
            pltpu.VMEM((2, 4, 128, CELLS), F32),
            pltpu.VMEM((384, 4 * CELLS), BF16),
            pltpu.SemaphoreType.DMA((3,)),
        ],
        flops=FLOPS_BACK,
    )

    if not shared:
        spread = parts.reshape(2, slabs, group, CELLS).transpose(1, 0, 2, 3)
        spread = lax.all_to_all(spread, "space", split_axis=0, concat_axis=0, tiled=True)
        next_ = jnp.pad(spread[:-1, 1].astype(F32), ((1, 0), (0, 0), (0, 0)))
        latent = (spread[:, 0].astype(F32) + next_).astype(BF16)
        two = call(
            functools.partial(kernel_two, 1, rows_per),
            shape((256, 27 * 128), F32),
            pack,
            cot,
        )
        one, two = lax.psum((ones[0], two), "dp")
        one = lax.psum_scatter(one, "space", scatter_dimension=0, tiled=True)
        two = lax.psum_scatter(two, "space", scatter_dimension=0, tiled=True)
        return latent.transpose(1, 0, 2)[None], one, two

    across = swap_ranks(pack, "dp", 2)
    beside = swap_ranks(pack, "dp", 1)
    cots = []
    for k in range(pieces):
        piece = lax.dynamic_slice_in_dim(cot, (place[0] ^ k) * 2 * rows_per, 2 * rows_per, 1)
        cots.append(swap_ranks(piece, "dp", k) if k else piece)
    parcel = call(
        functools.partial(kernel_two, samples, rows_per),
        shape((slabs, rows_per, WIDTH), BF16),
        pack,
        beside,
        across,
        swap_ranks(first_of(across, *ones, *cots[1:]), "dp", 1),
        *cots,
        ones[0],
        swap_ranks(ones[1], "dp", 1),
        parts,
    )
    got = lax.all_to_all(parcel, "space", split_axis=0, concat_axis=0, tiled=True)
    total, latent = call(
        kernel_sum,
        (shape((rows_per, LATENT_AT), BF16), shape((group, slabs, CELLS), BF16)),
        got,
    )
    totals = [swap_ranks(total, "dp", k) if k else total for k in range(pieces)]
    one, two = call(
        functools.partial(kernel_final, pieces),
        (shape((16, 864), F32), shape((32, 27 * 128), F32)),
        place,
        *totals,
        spaces={0: pltpu.SMEM},
    )
    return latent[None], one, two


def solution(mesh):
    placed = (P("dp", "space", None, None), P(), P(), P("dp", "space", None, None))
    return jax.shard_map(
        on_device,
        mesh=mesh,
        in_specs=placed,
        out_specs=(P("dp", "space", None, None), P("space", None), P("space", None)),
        check_vma=False,
    )
```

time: 75.3 us -> 60.8 us (0.81)
  starting transfers between devices: 24.5 us -> 15.6 us
  waiting for transfers between devices: 13.4 us -> 8.69 us
  Pallas kernels: 6.8 us -> 10.6 us
  local copies, waits for them, and re-layouts: 6.95 us -> 3.44 us
    ppermute x15 -> x10, waiting for transfers between devices: 10.9 us -> 5.1 us  [swap_ranks(): lax.ppermute(block, axis, [(i, i ^ k) for i in range(lax.axis_size(axis))])]
    pallas_call x6, Pallas kernels: 6.8 us -> 10.6 us  [call(): pl.pallas_call(kernel, out_shape=out_shape, in_specs=[pl.BlockSpec(memory...]
    all_to_all x1, waiting for transfers between devices: 0.01 us -> 3.59 us  [on_device(): lax.all_to_all(parcels, 'space', split_axis=0, concat_axis=0, tiled=True)]
    ppermute x15 -> x10, starting transfers between devices: 9.24 us -> 5.88 us  [swap_ranks(): lax.ppermute(block, axis, [(i, i ^ k) for i in range(lax.axis_size(axis))])]
    ppermute x2 -> x1, starting transfers between devices: 8.02 us -> 4.85 us  [from_below(): lax.ppermute(block, axis, [(i - 1, i) for i in range(1, lax.axis_size(axi...]
    ppermute x2 -> x1, waiting for transfers between devices: 2.5 us -> 0.01 us  [from_below(): lax.ppermute(block, axis, [(i - 1, i) for i in range(1, lax.axis_size(axi...]
    all_to_all x1, starting transfers between devices: 7.25 us -> 4.89 us  [on_device(): lax.all_to_all(parcels, 'space', split_axis=0, concat_axis=0, tiled=True)]
    slice x3 -> x0, local copies, waits for them, and re-layouts: 1.78 us -> none  [the longest x1 0.91 us: on_device(): halo = from_below(slab[3:], 'space')]
  transfers between devices with their start and end apart: 18 -> 12, of which waited for: 7 -> 4; matrix products, arithmetic and copies ran while one was open for 1% -> 0% of each run, Pallas kernels for 6% -> 11%
where the time goes in v3:
time: 60.8 us; the launch traced here: 60.5 us
  blocking collectives  21.4 us (35%)
  starting transfers between devices  15.6 us (26%)
  Pallas kernels  10.6 us (17%)
  waiting for transfers between devices  8.69 us (14%)
  local copies, waits for them, and re-layouts  3.44 us (6%)
  between operations  0.77 us (1%)
    all_to_all x1, blocking collectives, on_device(): lax.all_to_all(parcel, 'space', split_axis=0, concat_axis=0, tiled=True)  21.4 us
    pallas_call x6, Pallas kernels, call(): pl.pallas_call(kernel, out_shape=out_shape, in_specs=[pl.BlockSpec(memory...  10.6 us
    ppermute x10, starting transfers between devices, swap_ranks(): lax.ppermute(block, axis, [(i, i ^ k) for i in range(lax.axis_size(axis))])  5.88 us
    ppermute x10, waiting for transfers between devices, swap_ranks(): lax.ppermute(block, axis, [(i, i ^ k) for i in range(lax.axis_size(axis))])  5.1 us
    all_to_all x1, starting transfers between devices, on_device(): lax.all_to_all(parcels, 'space', split_axis=0, concat_axis=0, tiled=True)  4.89 us
    ppermute x1, starting transfers between devices, from_below(): lax.ppermute(block, axis, [(i - 1, i) for i in range(1, lax.axis_size(axi...  4.85 us
    all_to_all x1, waiting for transfers between devices, on_device(): lax.all_to_all(parcels, 'space', split_axis=0, concat_axis=0, tiled=True)  3.59 us
    unnamed x14, local copies, waits for them, and re-layouts  3.42 us
  transfers between devices with their start and end apart: 12, of which 4 were waited for; matrix products, arithmetic and copies ran while one was open for 0% of the time, Pallas kernels for 11%

profile of v3, /device:TPU:0, one launch (start us, length us, event | category | flops | bytes accessed | tf_op | source)
XLA Modules:
  0.0 60.5 jit_solution(1783232529675851102)
XLA Ops:
  0.6 0.0 copy-start.1
  0.6 1.0 %copy-done.1 = bf16[1,4,64,1024]{3,2,1,0:T(8,128)(2,1)S(1)} copy-done((bf16[1,4,64,1024]{3,2,1,0:T(8,128)(2,1)S(1)}, bf16[1,4,64,1024]{3,2,1,0:T(8,128)(2,1)}, u32[]{:S(2)}) %copy-start.1) | copy-done | bytes 524312
  1.7 0.0 copy-start.6
  1.7 0.8 %copy-done.6 = bf16[1,32,8,128]{3,2,1,0:T(8,128)(2,1)S(1)} copy-done((bf16[1,32,8,128]{3,2,1,0:T(8,128)(2,1)S(1)}, bf16[1,32,8,128]{3,2,1,0:T(8,128)(2,1)}, u32[]{:S(2)}) %copy-start.6) | copy-done | bytes 65560
  2.5 0.0 copy-start.2
  2.5 0.0 copy-start.3
  2.5 1.4 %shard_map.67 = (bf16[8,64,128]{2,1,0:T(8,128)(2,1)}, bf16[1,64,1024]{2,1,0:T(8,128)(2,1)S(1)}) custom-call(bf16[32,8,128]{2,1,0:T(8,128)(2,1)S(1)} %bitcast.7, bf16[4,64,1024]{2,1,0:T(8,128)(2,1)S(1)} %bitcast.4), custom_call_target="tpu_custom_call" | custom-call | flops 1000000000 | bytes 589824 | tf_op jit(solution)/shard_map/pallas_call | solution.py:326
  3.9 4.9 %collective-permute-start = (bf16[1,64,1024]{2,1,0:T(8,128)(2,1)S(1)}, bf16[1,64,1024]{2,1,0:T(8,128)(2,1)S(1)}, u32[]{:S(2)}, u32[]{:S(2)}) collective-permute-start(bf16[1,64,1024]{2,1,0:T(8,128)(2,1)S(1)} %get-tuple-element.13), channel_id=1, source_target_pairs={{0,1},{1,2},{2,3},{3,4},{4,5},{5,6},{6,7},{8,9},{9,10},{10,11},{11... | collective-permute-start | bytes 393224 | tf_op jit(solution)/shard_map/ppermute | solution.py:352
  8.7 4.9 %all-to-all-start = ((bf16[8,64,128]{2,1,0:T(8,128)(2,1)}), bf16[8,64,128]{2,1,0:T(8,128)(2,1)S(1)}, u32[]{:S(2)}, u32[]{:S(2)}) async-start(bf16[8,64,128]{2,1,0:T(8,128)(2,1)} %get-tuple-element.14), calls=%async_computation | async-start | bytes 262144 | tf_op jit(solution)/shard_map/all_to_all | solution.py:373
  13.6 0.0 copy-start
  13.6 0.0 collective-permute-done.halo
  13.6 0.0 copy-done.2
  13.6 0.0 copy-done.3
  13.7 1.5 %shard_map.68.refs_0_ = bf16[16,64,128]{2,1,0:T(8,128)(2,1)S(1)} custom-call(bf16[4,64,1024]{2,1,0:T(8,128)(2,1)S(1)} %bitcast.5, bf16[1,64,1024]{2,1,0:T(8,128)(2,1)S(1)} %collective-permute-done.halo, bf16[864,128]{1,0:T(8,128)(2,1)S(1)} %copy-done.3), custom_call_target="tpu_custom_call" | custom-call | flops 1000000000 | bytes 876544 | tf_op jit(solution)/shard_map/pallas_call | solution.py:326
  15.2 0.0 copy-start.4
  15.2 0.6 %copy-done.4 = bf16[1,64,1024]{2,1,0:T(8,128)(2,1)} copy-done((bf16[1,64,1024]{2,1,0:T(8,128)(2,1)}, bf16[1,64,1024]{2,1,0:T(8,128)(2,1)S(1)}, u32[]{:S(2)}) %copy-start.4) | copy-done | bytes 131096
  15.9 1.5 %collective-permute-start.2 = (bf16[16,64,128]{2,1,0:T(8,128)(2,1)S(1)}, bf16[16,64,128]{2,1,0:T(8,128)(2,1)S(1)}, u32[]{:S(2)}, u32[]{:S(2)}) collective-permute-start(bf16[16,64,128]{2,1,0:T(8,128)(2,1)S(1)} %shard_map.68.refs_0_), channel_id=1, source_target_pairs={{0,16},{8,24},{16,0},{24,8},{1,17},{9,25},{17,1},{25,9},{2,18},{10... | collective-permute-start | bytes 786440 | tf_op jit(solution)/shard_map/ppermute | solution.py:344
  17.4 0.0 collective-permute-start.1
  17.4 3.6 %all-to-all-done.cot = bf16[8,64,128]{2,1,0:T(8,128)(2,1)S(1)} async-done(((bf16[8,64,128]{2,1,0:T(8,128)(2,1)}), bf16[8,64,128]{2,1,0:T(8,128)(2,1)S(1)}, u32[]{:S(2)}, u32[]{:S(2)}) %all-to-all-start) | async-done | bytes 131104 | tf_op jit(solution)/shard_map/all_to_all | solution.py:373
  21.0 0.1 collective-permute-start.5
  21.1 1.6 %collective-permute-start.4 = (bf16[8,16,128]{2,1,0:T(8,128)(2,1)S(1)}, bf16[8,16,128]{2,1,0:T(8,128)(2,1)S(1)}, u32[]{:S(2)}, u32[]{:S(2)}) collective-permute-start(bf16[8,16,128]{2,1,0:T(8,128)(2,1)S(1)} %get-tuple-element.25), channel_id=1, source_target_pairs={{0,16},{8,24},{16,0},{24,8},{1,17},{9,25},{17,1},{25,9},{2,18},{10... | collective-permute-start | bytes 98312 | tf_op jit(solution)/shard_map/ppermute | solution.py:344
  22.7 0.3 collective-permute-start.3
  22.9 0.0 copy-done
  22.9 0.0 copy-start.5
  22.9 0.9 %copy-done.5 = bf16[1,64,1024]{2,1,0:T(8,128)(2,1)S(1)} copy-done((bf16[1,64,1024]{2,1,0:T(8,128)(2,1)S(1)}, bf16[1,64,1024]{2,1,0:T(8,128)(2,1)}, u32[]{:S(2)}) %copy-start.5) | copy-done | bytes 131096
  23.8 5.3 %shard_map.69 = (bf16[64,864]{1,0:T(8,128)(2,1)S(1)}, bf16[64,864]{1,0:T(8,128)(2,1)S(1)}, bf16[2,256,128]{2,1,0:T(8,128)(2,1)S(1)}) custom-call(s32[1]{0:T(128)} %bitcast.2.place, bf16[4,64,1024]{2,1,0:T(8,128)(2,1)S(1)} %bitcast.6, bf16[1,64,1024]{2,1,0:T(8,128)(2,1)S(1)} %copy-done.5, bf16[864,128]{1,0:T(8,128)(2,1)S(1)} %copy-done.3, ...), custom_call_target="tpu_custom_call" | custom-call | flops 1000000000 | bytes 2777092 | tf_op jit(solution)/shard_map/pallas_call | solution.py:326
  29.1 0.0 collective-permute-done.5.refs_7_
  29.1 0.0 collective-permute-done.4.refs_6_
  29.1 0.0 collective-permute-done.3.refs_5_
  29.2 0.0 collective-permute-done.2.refs_2_
  29.2 0.3 collective-permute-start.6
  29.5 0.3 collective-permute-start.7
  29.7 1.2 %collective-permute-done.7.refs_9_ = bf16[64,864]{1,0:T(8,128)(2,1)S(1)} collective-permute-done((bf16[64,864]{1,0:T(8,128)(2,1)S(1)}, bf16[64,864]{1,0:T(8,128)(2,1)S(1)}, u32[]{:S(2)}, u32[]{:S(2)}) %collective-permute-start.7) | collective-permute-done | bytes 110624 | tf_op jit(solution)/shard_map/ppermute | solution.py:344
  30.9 0.0 collective-permute-done.1.refs_1_
  30.9 0.0 collective-permute-done.6.refs_3_
  30.9 0.7 %shard_map.70 = bf16[8,8,5376]{2,1,0:T(8,128)(2,1)S(1)} custom-call(bf16[16,64,128]{2,1,0:T(8,128)(2,1)S(1)} %shard_map.68.refs_0_, bf16[16,64,128]{2,1,0:T(8,128)(2,1)S(1)} %collective-permute-done.1.refs_1_, bf16[16,64,128]{2,1,0:T(8,128)(2,1)S(1)} %collective-permute-done.2.refs_2_, bf16[16,64,128]{2,1,0:T(8,128)(2,1)S(1)} %collective-permute-done.6.refs_3_, ...), custom_call_target="tpu_custom_call" | custom-call | flops 1000000000 | bytes 1531904 | tf_op jit(solution)/shard_map/pallas_call | solution.py:326
  31.6 21.4 %all_to_all.10.got = bf16[8,8,5376]{2,1,0:T(8,128)(2,1)S(1)} all-to-all(bf16[8,8,5376]{2,1,0:T(8,128)(2,1)S(1)} %shard_map.70), channel_id=1, replica_groups=mesh['dp'=4,'space'=8] {'space'}, dimensions={0} | all-to-all | bytes 1376256 | tf_op jit(solution)/shard_map/all_to_all | solution.py:449
  53.0 0.9 %shard_map.71 = (bf16[8,4352]{1,0:T(8,128)(2,1)S(1)}, bf16[32,8,128]{2,1,0:T(8,128)(2,1)}) custom-call(bf16[8,8,5376]{2,1,0:T(8,128)(2,1)S(1)} %all_to_all.10.got), custom_call_target="tpu_custom_call" | custom-call | flops 1000000000 | bytes 688128 | tf_op jit(solution)/shard_map/pallas_call | solution.py:326
  53.9 0.0 collective-permute-start.10
  53.9 1.4 %collective-permute-start.9 = (bf16[8,4352]{1,0:T(8,128)(2,1)S(1)}, bf16[8,4352]{1,0:T(8,128)(2,1)S(1)}, u32[]{:S(2)}, u32[]{:S(2)}) collective-permute-start(bf16[8,4352]{1,0:T(8,128)(2,1)S(1)} %get-tuple-element.20.refs_0_), channel_id=1, source_target_pairs={{0,16},{8,24},{16,0},{24,8},{1,17},{9,25},{17,1},{25,9},{2,18},{10... | collective-permute-start | bytes 208904 | tf_op jit(solution)/shard_map/ppermute | solution.py:344
  55.3 0.5 collective-permute-start.8
  55.8 2.6 %collective-permute-done.10.refs_3_ = bf16[8,4352]{1,0:T(8,128)(2,1)S(1)} collective-permute-done((bf16[8,4352]{1,0:T(8,128)(2,1)S(1)}, bf16[8,4352]{1,0:T(8,128)(2,1)S(1)}, u32[]{:S(2)}, u32[]{:S(2)}) %collective-permute-start.10) | collective-permute-done | bytes 69664 | tf_op jit(solution)/shard_map/ppermute | solution.py:344
  58.4 1.3 %collective-permute-done.9.refs_2_ = bf16[8,4352]{1,0:T(8,128)(2,1)S(1)} collective-permute-done((bf16[8,4352]{1,0:T(8,128)(2,1)S(1)}, bf16[8,4352]{1,0:T(8,128)(2,1)S(1)}, u32[]{:S(2)}, u32[]{:S(2)}) %collective-permute-start.9) | collective-permute-done | bytes 69664 | tf_op jit(solution)/shard_map/ppermute | solution.py:344
  59.7 0.0 collective-permute-done.8.refs_1_
  59.7 0.8 %shard_map.72 = (f32[16,864]{1,0:T(8,128)}, f32[32,3456]{1,0:T(8,128)}) custom-call(s32[1]{0:T(128)} %bitcast.2.place, bf16[8,4352]{1,0:T(8,128)(2,1)S(1)} %get-tuple-element.20.refs_0_, bf16[8,4352]{1,0:T(8,128)(2,1)S(1)} %collective-permute-done.8.refs_1_, bf16[8,4352]{1,0:T(8,128)(2,1)S(1)} %collective-permute-done.9.refs_2_, ...), custom_call_target="tpu_custom_call" | custom-call | flops 1000000000 | bytes 278532 | tf_op jit(solution)/shard_map/pallas_call | solution.py:326
  (1 shorter events, 0.0 us)
Async XLA Ops:
  0.6 1.0 %copy-start.1 = (bf16[1,4,64,1024]{3,2,1,0:T(8,128)(2,1)S(1)}, bf16[1,4,64,1024]{3,2,1,0:T(8,128)(2,1)}, u32[]{:S(2)}) copy-start(bf16[1,4,64,1024]{3,2,1,0:T(8,128)(2,1)} %param.4) | copy-start | bytes 1572868
  1.7 0.8 %copy-start.6 = (bf16[1,32,8,128]{3,2,1,0:T(8,128)(2,1)S(1)}, bf16[1,32,8,128]{3,2,1,0:T(8,128)(2,1)}, u32[]{:S(2)}) copy-start(bf16[1,32,8,128]{3,2,1,0:T(8,128)(2,1)} %param.7) | copy-start | bytes 196612
  2.5 11.1 %copy-start.2 = (bf16[1,4,64,1024]{3,2,1,0:T(8,128)(2,1)S(1)}, bf16[1,4,64,1024]{3,2,1,0:T(8,128)(2,1)}, u32[]{:S(2)}) copy-start(bf16[1,4,64,1024]{3,2,1,0:T(8,128)(2,1)} %param.4) | copy-start | bytes 1572868
  2.5 11.1 %copy-start.3 = (bf16[864,128]{1,0:T(8,128)(2,1)S(1)}, bf16[864,128]{1,0:T(8,128)(2,1)}, u32[]{:S(2)}) copy-start(bf16[864,128]{1,0:T(8,128)(2,1)} %w1_hbm.3) | copy-start | bytes 663556
  3.9 9.8 %collective-permute-start = (bf16[1,64,1024]{2,1,0:T(8,128)(2,1)S(1)}, bf16[1,64,1024]{2,1,0:T(8,128)(2,1)S(1)}, u32[]{:S(2)}, u32[]{:S(2)}) collective-permute-start(bf16[1,64,1024]{2,1,0:T(8,128)(2,1)S(1)} %get-tuple-element.13), channel_id=1, source_target_pairs={{0,1},{1,2},{2,3},{3,4},{4,5},{5,6},{6,7},{8,9},{9,10},{10,11},{11... | collective-permute-start | bytes 393224 | tf_op jit(solution)/shard_map/ppermute | solution.py:352
  8.7 12.2 %all-to-all-start = ((bf16[8,64,128]{2,1,0:T(8,128)(2,1)}), bf16[8,64,128]{2,1,0:T(8,128)(2,1)S(1)}, u32[]{:S(2)}, u32[]{:S(2)}) async-start(bf16[8,64,128]{2,1,0:T(8,128)(2,1)} %get-tuple-element.14), calls=%async_computation | async-start | bytes 262144 | tf_op jit(solution)/shard_map/all_to_all | solution.py:373
  13.6 9.3 %copy-start = (bf16[3456,256]{1,0:T(8,128)(2,1)S(1)}, bf16[3456,256]{1,0:T(8,128)(2,1)}, u32[]{:S(2)}) copy-start(bf16[3456,256]{1,0:T(8,128)(2,1)} %w2_hbm.1) | copy-start | bytes 5308420
  15.2 0.6 %copy-start.4 = (bf16[1,64,1024]{2,1,0:T(8,128)(2,1)}, bf16[1,64,1024]{2,1,0:T(8,128)(2,1)S(1)}, u32[]{:S(2)}) copy-start(bf16[1,64,1024]{2,1,0:T(8,128)(2,1)S(1)} %collective-permute-done.halo) | copy-start | bytes 393220
  15.9 13.3 %collective-permute-start.2 = (bf16[16,64,128]{2,1,0:T(8,128)(2,1)S(1)}, bf16[16,64,128]{2,1,0:T(8,128)(2,1)S(1)}, u32[]{:S(2)}, u32[]{:S(2)}) collective-permute-start(bf16[16,64,128]{2,1,0:T(8,128)(2,1)S(1)} %shard_map.68.refs_0_), channel_id=1, source_target_pairs={{0,16},{8,24},{16,0},{24,8},{1,17},{9,25},{17,1},{25,9},{2,18},{10... | collective-permute-start | bytes 786440 | tf_op jit(solution)/shard_map/ppermute | solution.py:344
  17.4 13.6 %collective-permute-start.1 = (bf16[16,64,128]{2,1,0:T(8,128)(2,1)S(1)}, bf16[16,64,128]{2,1,0:T(8,128)(2,1)S(1)}, u32[]{:S(2)}, u32[]{:S(2)}) collective-permute-start(bf16[16,64,128]{2,1,0:T(8,128)(2,1)S(1)} %shard_map.68.refs_0_), channel_id=1, source_target_pairs={{0,8},{8,0},{16,24},{24,16},{1,9},{9,1},{17,25},{25,17},{2,10},{10... | collective-permute-start | bytes 786440 | tf_op jit(solution)/shard_map/ppermute | solution.py:344
  21.0 8.1 %collective-permute-start.5 = (bf16[8,16,128]{2,1,0:T(8,128)(2,1)S(1)}, bf16[8,16,128]{2,1,0:T(8,128)(2,1)S(1)}, u32[]{:S(2)}, u32[]{:S(2)}) collective-permute-start(bf16[8,16,128]{2,1,0:T(8,128)(2,1)S(1)} %get-tuple-element.24), channel_id=1, source_target_pairs={{0,24},{8,16},{16,8},{24,0},{1,25},{9,17},{17,9},{25,1},{2,26},{10... | collective-permute-start | bytes 98312 | tf_op jit(solution)/shard_map/ppermute | solution.py:344
  21.1 8.1 %collective-permute-start.4 = (bf16[8,16,128]{2,1,0:T(8,128)(2,1)S(1)}, bf16[8,16,128]{2,1,0:T(8,128)(2,1)S(1)}, u32[]{:S(2)}, u32[]{:S(2)}) collective-permute-start(bf16[8,16,128]{2,1,0:T(8,128)(2,1)S(1)} %get-tuple-element.25), channel_id=1, source_target_pairs={{0,16},{8,24},{16,0},{24,8},{1,17},{9,25},{17,1},{25,9},{2,18},{10... | collective-permute-start | bytes 98312 | tf_op jit(solution)/shard_map/ppermute | solution.py:344
  22.7 6.5 %collective-permute-start.3 = (bf16[8,16,128]{2,1,0:T(8,128)(2,1)S(1)}, bf16[8,16,128]{2,1,0:T(8,128)(2,1)S(1)}, u32[]{:S(2)}, u32[]{:S(2)}) collective-permute-start(bf16[8,16,128]{2,1,0:T(8,128)(2,1)S(1)} %get-tuple-element.26), channel_id=1, source_target_pairs={{0,8},{8,0},{16,24},{24,16},{1,9},{9,1},{17,25},{25,17},{2,10},{10... | collective-permute-start | bytes 98312 | tf_op jit(solution)/shard_map/ppermute | solution.py:344
  22.9 0.9 %copy-start.5 = (bf16[1,64,1024]{2,1,0:T(8,128)(2,1)S(1)}, bf16[1,64,1024]{2,1,0:T(8,128)(2,1)}, u32[]{:S(2)}) copy-start(bf16[1,64,1024]{2,1,0:T(8,128)(2,1)} %copy-done.4) | copy-start | bytes 393220
  29.2 1.8 %collective-permute-start.6 = (bf16[16,64,128]{2,1,0:T(8,128)(2,1)S(1)}, bf16[16,64,128]{2,1,0:T(8,128)(2,1)S(1)}, u32[]{:S(2)}, u32[]{:S(2)}) collective-permute-start(bf16[16,64,128]{2,1,0:T(8,128)(2,1)S(1)} %collective-permute-done.2.refs_2_), channel_id=1, source_target_pairs={{0,8},{8,0},{16,24},{24,16},{1,9},{9,1},{17,25},{25,17},{2,10},{10... | collective-permute-start | bytes 786440 | tf_op jit(solution)/shard_map/ppermute | solution.py:344
  29.5 1.5 %collective-permute-start.7 = (bf16[64,864]{1,0:T(8,128)(2,1)S(1)}, bf16[64,864]{1,0:T(8,128)(2,1)S(1)}, u32[]{:S(2)}, u32[]{:S(2)}) collective-permute-start(bf16[64,864]{1,0:T(8,128)(2,1)S(1)} %get-tuple-element.16), channel_id=1, source_target_pairs={{0,8},{8,0},{16,24},{24,16},{1,9},{9,1},{17,25},{25,17},{2,10},{10... | collective-permute-start | bytes 331784 | tf_op jit(solution)/shard_map/ppermute | solution.py:344
  53.9 4.5 %collective-permute-start.10 = (bf16[8,4352]{1,0:T(8,128)(2,1)S(1)}, bf16[8,4352]{1,0:T(8,128)(2,1)S(1)}, u32[]{:S(2)}, u32[]{:S(2)}) collective-permute-start(bf16[8,4352]{1,0:T(8,128)(2,1)S(1)} %get-tuple-element.20.refs_0_), channel_id=1, source_target_pairs={{0,24},{8,16},{16,8},{24,0},{1,25},{9,17},{17,9},{25,1},{2,26},{10... | collective-permute-start | bytes 208904 | tf_op jit(solution)/shard_map/ppermute | solution.py:344
  53.9 5.8 %collective-permute-start.9 = (bf16[8,4352]{1,0:T(8,128)(2,1)S(1)}, bf16[8,4352]{1,0:T(8,128)(2,1)S(1)}, u32[]{:S(2)}, u32[]{:S(2)}) collective-permute-start(bf16[8,4352]{1,0:T(8,128)(2,1)S(1)} %get-tuple-element.20.refs_0_), channel_id=1, source_target_pairs={{0,16},{8,24},{16,0},{24,8},{1,17},{9,25},{17,1},{25,9},{2,18},{10... | collective-permute-start | bytes 208904 | tf_op jit(solution)/shard_map/ppermute | solution.py:344
  55.3 4.4 %collective-permute-start.8 = (bf16[8,4352]{1,0:T(8,128)(2,1)S(1)}, bf16[8,4352]{1,0:T(8,128)(2,1)S(1)}, u32[]{:S(2)}, u32[]{:S(2)}) collective-permute-start(bf16[8,4352]{1,0:T(8,128)(2,1)S(1)} %get-tuple-element.20.refs_0_), channel_id=1, source_target_pairs={{0,8},{8,0},{16,24},{24,16},{1,9},{9,1},{17,25},{25,17},{2,10},{10... | collective-permute-start | bytes 208904 | tf_op jit(solution)/shard_map/ppermute | solution.py:344

commit v4 on v3

--- a/solution.py
+++ b/solution.py
@@ -11,10 +11,8 @@
 BF16 = jnp.bfloat16
 VMEM_LIMIT = 16 * 1024 * 1024
 
-FLOPS_PACK, FLOPS_BACK = 10**9, 10**9
-
 NJ, NK, CELLS = 16, 8, 128
-ONE_AT, ONE_END, LATENT_AT, NEXT_AT, WIDTH = 3456, 4320, 4352, 4864, 5376
+ONE_AT, WIDTH = 3456, 4320
 HIDDEN_AT, PACK = (0, 8), 16
 TAP_PHASE = {0: (1, 1), 1: (0, 0), 2: (1, 0)}
 
@@ -75,12 +73,11 @@
         for q, pre in enumerate((full[:, 0:128] + before, full[:, 128:256])):
             logistic = 1.0 / (1.0 + jnp.exp(-pre))
             hidden[2 * p + q] = (pre * logistic).astype(BF16)
-            if slope_t is not None:
-                slope = logistic * (1.0 + pre * (1.0 - logistic))
-                slope_t[2 * p + q] = slope.T
-
-
-def kernel_parcels(pieces, cot_hbm, snap, parcels, halo, cot, sems):
+            slope = logistic * (1.0 + pre * (1.0 - logistic))
+            slope_t[2 * p + q] = slope.T
+
+
+def kernel_parcels(pieces, _, __, cot_hbm, snap, parcels, halo, cot, sems):
     last = pltpu.make_async_copy(snap.at[pl.ds(3, 1)], halo, sems.at[0])
     whole = pltpu.make_async_copy(cot_hbm, cot, sems.at[1])
     whole.start()
@@ -110,44 +107,27 @@
         return self.pack[at : at + 2].reshape(CELLS, 128)
 
 
-def hidden_planes(snap, halo, w_ext, p1, hidden, slope_t):
+def kernel_pack(snap, halo, w1, pack, slope_t, p1, w_ext):
+    widen(w1, w_ext)
     for i, planes in enumerate(([halo[0], snap[0], snap[1]], [snap[1], snap[2], snap[3]])):
         fill_patches(planes, p1.at[i])
-        fill_hidden(p1.at[i], w_ext, hidden(i), None if slope_t is None else slope_t.at[i])
-
-
-def kernel_pack(snap_hbm, halo, w1_hbm, pack, snap, w1, p1, w_ext, sems):
-    copies = [
-        pltpu.make_async_copy(w1_hbm, w1, sems.at[0]),
-        pltpu.make_async_copy(snap_hbm, snap, sems.at[1]),
-    ]
-    for copy in copies:
-        copy.start()
-    copies[0].wait()
-    widen(w1, w_ext)
-    copies[1].wait()
-    hidden_planes(snap, halo, w_ext, p1, lambda i: Phases(pack, i), None)
-
-
-def kernel_back(pieces, rows_per, place, snap_hbm, halo, w1_hbm, w2_hbm, cot, *rest):
-    *outs, parts, snap, w1, p1, w_ext, w2, hidden, slope_t, grad_t, sems = rest
-    copies = [
-        pltpu.make_async_copy(w1_hbm, w1, sems.at[0]),
-        pltpu.make_async_copy(snap_hbm, snap, sems.at[1]),
-        pltpu.make_async_copy(w2_hbm, w2, sems.at[2]),
-    ]
-    for copy in copies:
-        copy.start()
-    copies[0].wait()
-    widen(w1, w_ext)
-    copies[1].wait()
-    hidden_planes(snap, halo, w_ext, p1, lambda i: hidden.at[i], slope_t)
-    copies[2].wait()
-    grad_one_share(pieces, rows_per, place, w2, cot, outs, p1, slope_t, grad_t)
-    latent_parts(hidden, w2, parts)
-
-
-def grad_one_share(pieces, rows_per, place, w2, cot, outs, p1, slope_t, grad_t):
+        fill_hidden(p1.at[i], w_ext, Phases(pack, i), slope_t.at[i])
+
+
+def kernel_pieces(place, slot, cot, *outs):
+    height = outs[0].shape[1]
+    for k, out in enumerate(outs):
+        at = pl.multiple_of((place[0] ^ k) * height, height)
+        for n in range(out.shape[0]):
+            out[n] = cot[slot[0] ^ n, pl.ds(at, height), :]
+
+
+def kernel_back(pieces, rows_per, place, slot, slope_t, p1, w2, cot, *rest):
+    *outs, grad_t = rest
+    grad_one_share(pieces, rows_per, place, slot, w2, cot, outs, p1, slope_t, grad_t)
+
+
+def grad_one_share(pieces, rows_per, place, slot, w2, cot, outs, p1, slope_t, grad_t):
     sources = cot.shape[0]
     moved = dot(cot[...].reshape(-1, CELLS), cell_order(True))
     moved = moved.reshape(sources * pieces, 2, rows_per, 4 * CELLS)
@@ -194,13 +174,15 @@
     frames = [frame.astype(BF16) for frame in frames]
     for k in range(2):
         half = (place[0] ^ k) & 1
-        chosen = one_hot(col == row // share * owned + half * share + row % share)
+        chosen = one_hot(col == (row // share ^ slot[0]) * owned + half * share + row % share)
         for t in range(9):
             value = dot(chosen, frames[t])
             outs[k][:, t * 96 : (t + 1) * 96] = value[:, 32:].astype(BF16)
 
 
-def latent_parts(hidden, w2, parts):
+def kernel_latent(pack, w2, parts):
+    owners = parts.shape[0]
+    group = parts.shape[1] // 2
     row, col = iota((CELLS, CELLS), 0), iota((CELLS, CELLS), 1)
     back = one_hot((row // NJ == col % NK) & (row % NJ == col // NK))
     for part, taps_x in enumerate(((1, 2), (0,))):
@@ -211,8 +193,8 @@
                 q, sk = TAP_PHASE[c]
                 for a in taps_x:
                     tap = 9 * a + 3 * b + c
-                    plane = 0 if a == 1 else 1
-                    term = dot(hidden[plane, 2 * p + q], w2[tap * 128 : (tap + 1) * 128, :])
+                    hidden = Phases(pack, 0 if a == 1 else 1)[2 * p + q]
+                    term = dot(hidden, w2[tap * 128 : (tap + 1) * 128, :])
                     v = 2 * sj + sk
                     totals[v] = totals[v] + term if v in totals else term
         zero = jnp.zeros((NJ, totals[0].shape[1]), F32)
@@ -223,7 +205,8 @@
         inner = totals[2] + later(totals[3])
         inner = jnp.where(iota(inner.shape, 0) % NJ == 0, 0.0, pltpu.roll(inner, 1, axis=0))
         rows = totals[0] + later(totals[1]) + inner
-        parts[part] = dot(rows.T.astype(BF16), back).astype(BF16)
+        value = dot(rows.T.astype(BF16), back).reshape(owners, group, CELLS)
+        parts[:, part * group : (part + 1) * group] = value.astype(BF16)
 
 
 def moved_rows(cots, rows_per, order):
@@ -243,7 +226,8 @@
 def kernel_two(samples, rows_per, *refs):
     packs, cots, refs = refs[:samples], refs[samples : 2 * samples], refs[2 * samples :]
     packed = samples > 1
-    out = refs[-1]
+    if packed:
+        ones, outs = refs[:2], refs[2:]
     left = moved_rows(cots, rows_per, cell_order(True))
     height = left[0][0].shape[0]
     for p in range(2):
@@ -268,42 +252,47 @@
                 for a, value in enumerate(parts):
                     to = (9 * a + 3 * b + c) * 128
                     if packed:
-                        out[:, :, to : to + 128] = value.reshape(-1, rows_per, 128).astype(BF16)
+                        spread(value.reshape(-1, rows_per, 128), outs, to)
                     else:
-                        out[:, to : to + 128] = value
+                        refs[0][:, to : to + 128] = value
     if packed:
-        own, other, latent, _ = refs
-        total = own[...].astype(F32) + other[...].astype(F32)
-        out[:, :, ONE_AT:ONE_END] = total.reshape(-1, rows_per, 864).astype(BF16)
-        out[:, :, ONE_END:LATENT_AT] = jnp.zeros(
-            (out.shape[0], rows_per, LATENT_AT - ONE_END), BF16
-        )
-        for part, start in enumerate((LATENT_AT, NEXT_AT)):
-            cells = latent[part].astype(F32).reshape(out.shape[0], -1, rows_per, CELLS)
-            for w in range(cells.shape[1]):
-                to = start + w * 128
-                out[:, :, to : to + 128] = cells[:, w].astype(BF16)
-
-
-def kernel_sum(got, total_out, latent):
-    sources, rows_per, _ = got.shape
-    for at in range(0, LATENT_AT, 256):
-        total = got[0, :, at : at + 256].astype(F32)
-        for src in range(1, sources):
-            total = total + got[src, :, at : at + 256].astype(F32)
-        total_out[:, at : at + 256] = total.astype(BF16)
-    height = sources * rows_per
+        total = ones[0][...].astype(F32) + ones[1][...].astype(F32)
+        spread(total.reshape(-1, rows_per, WIDTH - ONE_AT), outs, ONE_AT)
+
+
+def spread(value, outs, at):
+    kept, near_1, near_2, near_3, lent, own_far = outs
+    lanes = slice(at, at + value.shape[2])
+    kept[:, lanes] = value[0]
+    for n, near in enumerate((near_1, near_2, near_3), 1):
+        near[:, lanes] = value[n].astype(BF16)
+    for n in range(2):
+        own_far[n, :, lanes] = value[4 + 2 * n]
+        lent[n, :, lanes] = value[5 + 2 * n].astype(BF16)
+
+
+def kernel_far(lent, own_far, *outs):
+    for n, out in enumerate(outs):
+        out[...] = (own_far[n] + lent[n].astype(F32)).astype(BF16)
+
+
+def kernel_sum(kept, *refs):
+    *others, total_out = refs
+    total = kept[...]
+    for other in others:
+        total = total + other[...].astype(F32)
+    total_out[...] = total.astype(BF16)
+
+
+def kernel_join(got, latent):
+    slabs, group = got.shape[0], got.shape[1] // 2
+    next_ = got[:, group:].astype(F32)
+    next_ = jnp.concatenate([jnp.zeros_like(next_[:1]), next_[:-1]], axis=0)
+    cells = (got[:, :group].astype(F32) + next_).reshape(-1, CELLS).astype(BF16)
+    height = slabs * group
     row, col = iota((height, height), 0), iota((height, height), 1)
-    swap = one_hot((row // sources == col % rows_per) & (row % sources == col // rows_per))
-    for w in range(latent.shape[0] // rows_per):
-        own, next_ = [
-            got[:, :, at : at + 128].astype(F32)
-            for at in (LATENT_AT + w * 128, NEXT_AT + w * 128)
-        ]
-        cells = own + jnp.concatenate([jnp.zeros_like(next_[:1]), next_[:-1]], axis=0)
-        cells = cells.reshape(height, 128).astype(BF16)
-        moved = dot(swap, cells).reshape(rows_per, sources, 128).astype(BF16)
-        latent[w * rows_per : (w + 1) * rows_per] = moved
+    swap = one_hot((row // slabs == col % group) & (row % slabs == col // group))
+    latent[...] = dot(swap, cells).reshape(group, slabs, CELLS).astype(BF16)
 
 
 def kernel_final(pieces, place, *refs):
@@ -314,25 +303,26 @@
         two[pl.ds(at, rows_per), :] = parts[k][:, 0:ONE_AT].astype(F32)
     for k in range(2):
         at = pl.multiple_of(((place[0] ^ k) & 1) * rows_per, rows_per)
-        shares = [parts[n][:, ONE_AT:ONE_END].astype(F32) for n in (k, k ^ 2)]
+        shares = [parts[n][:, ONE_AT:WIDTH].astype(F32) for n in (k, k ^ 2)]
         one[pl.ds(at, rows_per), :] = shares[0] + shares[1]
 
 
-def call(kernel, out_shape, *args, spaces=None, scratch=(), flops=10**9):
-    spaces = spaces or {}
+def call(kernel, out_shape, *args, spaces=None, out_spaces=None, scratch=(), vmem=VMEM_LIMIT):
+    spaces, out_spaces = spaces or {}, out_spaces or {}
     single = isinstance(out_shape, jax.ShapeDtypeStruct)
-    vmem = pl.BlockSpec(memory_space=pltpu.VMEM)
+
+    def spec(n, of):
+        return pl.BlockSpec(memory_space=of.get(n, pltpu.VMEM))
+
     moved = sum(x.size * x.dtype.itemsize for x in args)
     return pl.pallas_call(
         kernel,
         out_shape=out_shape,
-        in_specs=[
-            pl.BlockSpec(memory_space=spaces.get(n, pltpu.VMEM)) for n in range(len(args))
-        ],
-        out_specs=vmem if single else [vmem] * len(out_shape),
+        in_specs=[spec(n, spaces) for n in range(len(args))],
+        out_specs=spec(0, {}) if single else [spec(n, out_spaces) for n in range(len(out_shape))],
         scratch_shapes=list(scratch),
-        cost_estimate=pl.CostEstimate(flops=flops, bytes_accessed=moved, transcendentals=0),
-        compiler_params=pltpu.CompilerParams(vmem_limit_bytes=VMEM_LIMIT),
+        cost_estimate=pl.CostEstimate(flops=10**9, bytes_accessed=moved, transcendentals=0),
+        compiler_params=pltpu.CompilerParams(vmem_limit_bytes=vmem),
     )(*args)
 
 
@@ -358,85 +348,87 @@
     shared = samples == 4 and slabs == 8
     pieces = samples if shared else 1
     rows_per = group // pieces
-    place = lax.axis_index("dp").astype(jnp.int32).reshape(1)
 
     slab = snapshot[0]
+    place, slot = [
+        lax.axis_index(axis).astype(jnp.int32).reshape(1) for axis in ("dp", "space")
+    ]
     parcels, last = call(
         functools.partial(kernel_parcels, pieces),
         (shape((slabs, 2 * group, CELLS), BF16), shape((1,) + slab.shape[1:], BF16)),
+        place,
+        slot,
         cotangent[0],
         slab,
-        spaces={0: pltpu.HBM, 1: pltpu.HBM},
+        spaces={0: pltpu.SMEM, 1: pltpu.SMEM, 2: pltpu.HBM, 3: pltpu.HBM},
         scratch=[pltpu.VMEM((group, slabs, CELLS), BF16), pltpu.SemaphoreType.DMA((2,))],
+        vmem=60 * 1024 * 1024,
     )
     halo = from_below(last, "space")
     cot = lax.all_to_all(parcels, "space", split_axis=0, concat_axis=0, tiled=True)
-    forward = [
-        pltpu.VMEM(slab.shape, BF16),
-        pltpu.VMEM(conv_one.shape, BF16),
-        pltpu.VMEM((2, 2 * CELLS, 9 * 128), BF16),
-        pltpu.VMEM((9 * 128, 384), BF16),
-    ]
-    pack = call(
+    pack, slope_t, p1 = call(
         kernel_pack,
-        shape((PACK, 64, CELLS), BF16),
+        (
+            shape((PACK, 64, CELLS), BF16),
+            shape((2, 4, 128, CELLS), F32),
+            shape((2, 2 * CELLS, 9 * 128), BF16),
+        ),
         slab,
         halo,
         conv_one,
-        spaces={0: pltpu.HBM, 2: pltpu.HBM},
-        scratch=forward + [pltpu.SemaphoreType.DMA((2,))],
-        flops=FLOPS_PACK,
-    )
-    if shared:
-        one_shape = (shape((64, 864), BF16),) * 2
-    else:
-        one_shape = (shape((128, 864), F32),)
-    *ones, parts = call(
+        scratch=[pltpu.VMEM((9 * 128, 384), BF16)],
+    )
+    ones = call(
         functools.partial(kernel_back, pieces, rows_per),
-        one_shape + (shape((2, 256, CELLS), BF16),),
+        (shape((64, 864), BF16),) * 2 if shared else (shape((128, 864), F32),),
         place,
-        slab,
-        halo,
-        conv_one,
+        slot,
+        slope_t,
+        p1,
         conv_two,
         cot,
-        spaces={0: pltpu.SMEM, 1: pltpu.HBM, 3: pltpu.HBM, 4: pltpu.HBM},
-        scratch=forward
-        + [
-            pltpu.VMEM(conv_two.shape, BF16),
-            pltpu.VMEM((2, 4, CELLS, 128), BF16),
-            pltpu.VMEM((2, 4, 128, CELLS), F32),
-            pltpu.VMEM((384, 4 * CELLS), BF16),
-            pltpu.SemaphoreType.DMA((3,)),
-        ],
-        flops=FLOPS_BACK,
-    )
+        spaces={0: pltpu.SMEM, 1: pltpu.SMEM},
+        scratch=[pltpu.VMEM((384, 4 * CELLS), BF16)],
+    )
+
+    def latent_of(pack):
+        return call(kernel_latent, shape((slabs, 2 * group, CELLS), BF16), pack, conv_two)
+
+    def joined(parts):
+        got = lax.all_to_all(parts, "space", split_axis=0, concat_axis=0, tiled=True)
+        return call(kernel_join, shape((group, slabs, CELLS), BF16), got)[None]
 
     if not shared:
-        spread = parts.reshape(2, slabs, group, CELLS).transpose(1, 0, 2, 3)
-        spread = lax.all_to_all(spread, "space", split_axis=0, concat_axis=0, tiled=True)
-        next_ = jnp.pad(spread[:-1, 1].astype(F32), ((1, 0), (0, 0), (0, 0)))
-        latent = (spread[:, 0].astype(F32) + next_).astype(BF16)
         two = call(
-            functools.partial(kernel_two, 1, rows_per),
-            shape((256, 27 * 128), F32),
-            pack,
-            cot,
+            functools.partial(kernel_two, 1, rows_per), shape((256, 27 * 128), F32), pack, cot
         )
         one, two = lax.psum((ones[0], two), "dp")
         one = lax.psum_scatter(one, "space", scatter_dimension=0, tiled=True)
         two = lax.psum_scatter(two, "space", scatter_dimension=0, tiled=True)
-        return latent.transpose(1, 0, 2)[None], one, two
+        return joined(latent_of(pack)), one, two
 
     across = swap_ranks(pack, "dp", 2)
     beside = swap_ranks(pack, "dp", 1)
-    cots = []
-    for k in range(pieces):
-        piece = lax.dynamic_slice_in_dim(cot, (place[0] ^ k) * 2 * rows_per, 2 * rows_per, 1)
-        cots.append(swap_ranks(piece, "dp", k) if k else piece)
-    parcel = call(
+    own, *cots = call(
+        kernel_pieces,
+        (shape((slabs, 2 * rows_per, CELLS), BF16),) * pieces,
+        place,
+        slot,
+        cot,
+        spaces={0: pltpu.SMEM, 1: pltpu.SMEM},
+    )
+    cots = [own] + [swap_ranks(piece, "dp", k) for k, piece in enumerate(cots, 1)]
+    one_block = shape((rows_per, WIDTH), BF16)
+    kept, near_1, near_2, near_3, lent, own_far = call(
         functools.partial(kernel_two, samples, rows_per),
-        shape((slabs, rows_per, WIDTH), BF16),
+        (
+            shape((rows_per, WIDTH), F32),
+            one_block,
+            one_block,
+            one_block,
+            shape((2, rows_per, WIDTH), BF16),
+            shape((2, rows_per, WIDTH), F32),
+        ),
         pack,
         beside,
         across,
@@ -444,14 +436,16 @@
         *cots,
         ones[0],
         swap_ranks(ones[1], "dp", 1),
-        parts,
-    )
-    got = lax.all_to_all(parcel, "space", split_axis=0, concat_axis=0, tiled=True)
-    total, latent = call(
-        kernel_sum,
-        (shape((rows_per, LATENT_AT), BF16), shape((group, slabs, CELLS), BF16)),
-        got,
-    )
+    )
+    parts = latent_of(first_of(pack, lent))
+    lent = swap_ranks(lent, "space", 1)
+    far = call(kernel_far, (one_block, one_block), lent, own_far)
+    others = [
+        swap_ranks(block, "space", k)
+        for k, block in ((1, near_1), (2, near_2), (3, near_3), (4, far[0]), (6, far[1]))
+    ]
+    latent = joined(first_of(parts, *far))
+    total = call(kernel_sum, one_block, kept, *others)
     totals = [swap_ranks(total, "dp", k) if k else total for k in range(pieces)]
     one, two = call(
         functools.partial(kernel_final, pieces),
@@ -460,7 +454,7 @@
         *totals,
         spaces={0: pltpu.SMEM},
     )
-    return latent[None], one, two
+    return latent, one, two
 
 
 def solution(mesh):

time: 60.8 us -> 52.5 us (0.86)
  blocking collectives: 21.4 us -> 0 us
  starting transfers between devices: 15.6 us -> 26.2 us
  waiting for transfers between devices: 8.69 us -> 14.2 us
  local copies, waits for them, and re-layouts: 3.44 us -> 1.02 us
  Pallas kernels: 10.6 us -> 9.83 us
    all_to_all x1 -> x0, blocking collectives: 21.4 us -> none  [on_device(): lax.all_to_all(parcel, 'space', split_axis=0, concat_axis=0, tiled=True)]
    ppermute x10 -> x16, starting transfers between devices: 5.88 us -> 12.1 us  [swap_ranks(): lax.ppermute(block, axis, [(i, i ^ k) for i in range(lax.axis_size(axis))])]
    ppermute x10 -> x16, waiting for transfers between devices: 5.1 us -> 10 us  [swap_ranks(): lax.ppermute(block, axis, [(i, i ^ k) for i in range(lax.axis_size(axis))])]
    all_to_all x0 -> x1, starting transfers between devices: none -> 4.41 us  [joined(): lax.all_to_all(parts, 'space', split_axis=0, concat_axis=0, tiled=True)]
    unnamed x14 -> x10, local copies, waits for them, and re-layouts: 3.42 us -> 1.02 us
    pallas_call x6 -> x10, Pallas kernels: 10.6 us -> 9.83 us  [call(): pl.pallas_call(kernel, out_shape=out_shape, in_specs=[spec(n, spaces) for...]
  transfers between devices with their start and end apart: 12 -> 19, of which waited for: 4 -> 7; matrix products, arithmetic and copies ran while one was open for 0% -> 0% of each run, Pallas kernels for 11% -> 12%
where the time goes in v4:
time: 52.5 us; the launch traced here: 52.1 us
  starting transfers between devices  26.2 us (50%)
  waiting for transfers between devices  14.2 us (27%)
  Pallas kernels  9.83 us (19%)
  local copies, waits for them, and re-layouts  1.02 us (2%)
  between operations  0.82 us (2%)
    ppermute x16, starting transfers between devices, swap_ranks(): lax.ppermute(block, axis, [(i, i ^ k) for i in range(lax.axis_size(axis))])  12.1 us
    ppermute x16, waiting for transfers between devices, swap_ranks(): lax.ppermute(block, axis, [(i, i ^ k) for i in range(lax.axis_size(axis))])  10 us
    pallas_call x10, Pallas kernels, call(): pl.pallas_call(kernel, out_shape=out_shape, in_specs=[spec(n, spaces) for...  9.83 us
    all_to_all x1, starting transfers between devices, on_device(): lax.all_to_all(parcels, 'space', split_axis=0, concat_axis=0, tiled=True)  4.89 us
    ppermute x1, starting transfers between devices, from_below(): lax.ppermute(block, axis, [(i - 1, i) for i in range(1, lax.axis_size(axi...  4.85 us
    all_to_all x1, starting transfers between devices, joined(): lax.all_to_all(parts, 'space', split_axis=0, concat_axis=0, tiled=True)  4.41 us
    all_to_all x1, waiting for transfers between devices, on_device(): lax.all_to_all(parcels, 'space', split_axis=0, concat_axis=0, tiled=True)  3.56 us
  transfers between devices with their start and end apart: 19, of which 7 were waited for; matrix products, arithmetic and copies ran while one was open for 0% of the time, Pallas kernels for 12%

profile of v4, /device:TPU:0, one launch (start us, length us, event | category | flops | bytes accessed | tf_op | source)
XLA Modules:
  0.0 52.1 jit_solution(17562305954101052547)
XLA Ops:
  0.6 0.0 copy-start.1
  0.6 0.0 copy-start.2
  0.7 1.9 %shard_map.67 = (bf16[8,64,128]{2,1,0:T(8,128)(2,1)}, bf16[1,64,1024]{2,1,0:T(8,128)(2,1)}) custom-call(s32[1]{0:T(128)} %bitcast.1._.place, s32[1]{0:T(128)} %bitcast.2.__.slot, bf16[32,8,128]{2,1,0:T(8,128)(2,1)} %bitcast.7, bf16[4,64,1024]{2,1,0:T(8,128)(2,1)} %bitcast.5), custom_call_target="tpu_custom_call" | custom-call | flops 1000000000 | bytes 589832 | tf_op jit(solution)/shard_map/pallas_call | solution.py:318
  2.5 4.8 %collective-permute-start = (bf16[1,64,1024]{2,1,0:T(8,128)(2,1)}, bf16[1,64,1024]{2,1,0:T(8,128)(2,1)S(1)}, u32[]{:S(2)}, u32[]{:S(2)}) collective-permute-start(bf16[1,64,1024]{2,1,0:T(8,128)(2,1)} %get-tuple-element.27), channel_id=1, source_target_pairs={{0,1},{1,2},{2,3},{3,4},{4,5},{5,6},{6,7},{8,9},{9,10},{10,11},{11... | collective-permute-start | bytes 393224 | tf_op jit(solution)/shard_map/ppermute | solution.py:342
  7.4 4.9 %all-to-all-start = ((bf16[8,64,128]{2,1,0:T(8,128)(2,1)}), bf16[8,64,128]{2,1,0:T(8,128)(2,1)S(1)}, u32[]{:S(2)}, u32[]{:S(2)}) async-start(bf16[8,64,128]{2,1,0:T(8,128)(2,1)} %get-tuple-element.31), calls=%async_computation | async-start | bytes 262144 | tf_op jit(solution)/shard_map/all_to_all | solution.py:368
  12.3 0.0 collective-permute-done.halo
  12.3 0.0 copy-done.1
  12.3 0.0 copy-done.2
  12.3 1.2 %shard_map.68 = (bf16[16,64,128]{2,1,0:T(8,128)(2,1)S(1)}, f32[2,4,128,128]{3,2,1,0:T(8,128)S(1)}, bf16[2,256,1152]{2,1,0:T(8,128)(2,1)S(1)}) custom-call(bf16[4,64,1024]{2,1,0:T(8,128)(2,1)S(1)} %bitcast.6, bf16[1,64,1024]{2,1,0:T(8,128)(2,1)S(1)} %collective-permute-done.halo, bf16[864,128]{1,0:T(8,128)(2,1)S(1)} %copy-done.2), custom_call_target="tpu_custom_call" | custom-call | flops 1000000000 | bytes 876544 | tf_op jit(solution)/shard_map/pallas_call | solution.py:318
  13.5 0.0 copy-start.3
  13.5 1.0 %copy-done.3 = bf16[2,256,1152]{2,1,0:T(8,128)(2,1)} copy-done((bf16[2,256,1152]{2,1,0:T(8,128)(2,1)}, bf16[2,256,1152]{2,1,0:T(8,128)(2,1)S(1)}, u32[]{:S(2)}) %copy-start.3) | copy-done | bytes 1179672
  14.5 0.0 copy-start
  14.5 1.5 %collective-permute-start.2 = (bf16[16,64,128]{2,1,0:T(8,128)(2,1)S(1)}, bf16[16,64,128]{2,1,0:T(8,128)(2,1)S(1)}, u32[]{:S(2)}, u32[]{:S(2)}) collective-permute-start(bf16[16,64,128]{2,1,0:T(8,128)(2,1)S(1)} %get-tuple-element.40.refs_0_.pack), channel_id=1, source_target_pairs={{0,16},{8,24},{16,0},{24,8},{1,17},{9,25},{17,1},{25,9},{2,18},{10... | collective-permute-start | bytes 786440 | tf_op jit(solution)/shard_map/ppermute | solution.py:334
  16.0 0.0 collective-permute-start.1
  16.0 3.6 %all-to-all-done.cot = bf16[8,64,128]{2,1,0:T(8,128)(2,1)S(1)} async-done(((bf16[8,64,128]{2,1,0:T(8,128)(2,1)}), bf16[8,64,128]{2,1,0:T(8,128)(2,1)S(1)}, u32[]{:S(2)}, u32[]{:S(2)}) %all-to-all-start) | async-done | bytes 131104 | tf_op jit(solution)/shard_map/all_to_all | solution.py:368
  19.6 0.0 copy-start.4
  19.6 0.1 collective-permute-start.3
  19.7 1.6 %collective-permute-start.4 = (bf16[8,16,128]{2,1,0:T(8,128)(2,1)S(1)}, bf16[8,16,128]{2,1,0:T(8,128)(2,1)S(1)}, u32[]{:S(2)}, u32[]{:S(2)}) collective-permute-start(bf16[8,16,128]{2,1,0:T(8,128)(2,1)S(1)} %get-tuple-element.35), channel_id=1, source_target_pairs={{0,16},{8,24},{16,0},{24,8},{1,17},{9,25},{17,1},{25,9},{2,18},{10... | collective-permute-start | bytes 98312 | tf_op jit(solution)/shard_map/ppermute | solution.py:334
  21.3 0.3 collective-permute-start.5
  21.6 0.0 copy-done
  21.6 0.0 copy-done.4
  21.6 2.3 %shard_map.69 = (bf16[64,864]{1,0:T(8,128)(2,1)S(1)}, bf16[64,864]{1,0:T(8,128)(2,1)S(1)}) custom-call(s32[1]{0:T(128)} %bitcast.1._.place, s32[1]{0:T(128)} %bitcast.2.__.slot, f32[2,4,128,128]{3,2,1,0:T(8,128)S(1)} %get-tuple-element.29.slope_t, bf16[2,256,1152]{2,1,0:T(8,128)(2,1)S(1)} %copy-done.4, bf16[3456,256]{1,0:T(8,128)(2,1)S(1)} %copy-done, ...), custom_call_target="tpu_custom_call" | custom-call | flops 1000000000 | bytes 3604488 | tf_op jit(solution)/shard_map/pallas_call | solution.py:318
  23.9 0.0 collective-permute-done.3.refs_5_
  24.0 0.0 collective-permute-done.4.refs_6_
  24.0 0.7 %collective-permute-done.5.refs_7_ = bf16[8,16,128]{2,1,0:T(8,128)(2,1)S(1)} collective-permute-done((bf16[8,16,128]{2,1,0:T(8,128)(2,1)S(1)}, bf16[8,16,128]{2,1,0:T(8,128)(2,1)S(1)}, u32[]{:S(2)}, u32[]{:S(2)}) %collective-permute-start.5) | collective-permute-done | bytes 32800 | tf_op jit(solution)/shard_map/ppermute | solution.py:334
  24.7 0.0 collective-permute-done.2.refs_2_
  24.7 0.2 collective-permute-start.6
  24.8 0.3 collective-permute-start.7
  25.2 1.2 %collective-permute-done.7.refs_9_ = bf16[64,864]{1,0:T(8,128)(2,1)S(1)} collective-permute-done((bf16[64,864]{1,0:T(8,128)(2,1)S(1)}, bf16[64,864]{1,0:T(8,128)(2,1)S(1)}, u32[]{:S(2)}, u32[]{:S(2)}) %collective-permute-start.7) | collective-permute-done | bytes 110624 | tf_op jit(solution)/shard_map/ppermute | solution.py:334
  26.4 0.0 collective-permute-done.1.refs_1_
  26.4 0.0 collective-permute-done.6.refs_3_
  26.4 0.7 %shard_map.71 = (f32[8,4320]{1,0:T(8,128)S(1)}, bf16[8,4320]{1,0:T(8,128)(2,1)S(1)}, bf16[8,4320]{1,0:T(8,128)(2,1)S(1)}, bf16[8,4320]{1,0:T(8,128)(2,1)S(1)}, b...) custom-call(bf16[16,64,128]{2,1,0:T(8,128)(2,1)S(1)} %get-tuple-element.40.refs_0_.pack, ...), custom_call_target="tpu_custom_call" | custom-call | flops 1000000000 | bytes 1400832 | tf_op jit(solution)/shard_map/pallas_call | solution.py:318
  27.1 0.3 collective-permute-start.8
  27.4 1.5 %collective-permute-start.10 = (bf16[8,4320]{1,0:T(8,128)(2,1)S(1)}, bf16[8,4320]{1,0:T(8,128)(2,1)S(1)}, u32[]{:S(2)}, u32[]{:S(2)}) collective-permute-start(bf16[8,4320]{1,0:T(8,128)(2,1)S(1)} %get-tuple-element.47), channel_id=1, source_target_pairs={{0,2},{1,3},{2,0},{3,1},{4,6},{5,7},{6,4},{7,5},{8,10},{9,11},{10,... | collective-permute-start | bytes 207368 | tf_op jit(solution)/shard_map/ppermute | solution.py:334
  28.9 1.8 %collective-permute-start.11 = (bf16[8,4320]{1,0:T(8,128)(2,1)S(1)}, bf16[8,4320]{1,0:T(8,128)(2,1)S(1)}, u32[]{:S(2)}, u32[]{:S(2)}) collective-permute-start(bf16[8,4320]{1,0:T(8,128)(2,1)S(1)} %get-tuple-element.48), channel_id=1, source_target_pairs={{0,3},{1,2},{2,1},{3,0},{4,7},{5,6},{6,5},{7,4},{8,11},{9,10},{10,... | collective-permute-start | bytes 207368 | tf_op jit(solution)/shard_map/ppermute | solution.py:334
  30.6 0.2 collective-permute-start.9
  30.9 4.2 %collective-permute-done.8.lent = bf16[2,8,4320]{2,1,0:T(8,128)(2,1)S(1)} collective-permute-done((bf16[2,8,4320]{2,1,0:T(8,128)(2,1)S(1)}, bf16[2,8,4320]{2,1,0:T(8,128)(2,1)S(1)}, u32[]{:S(2)}, u32[]{:S(2)}) %collective-permute-start.8) | collective-permute-done | bytes 138272 | tf_op jit(solution)/shard_map/ppermute | solution.py:334
  35.1 0.1 collective-permute-start.12
  35.2 2.3 %collective-permute-start.13 = (bf16[8,4320]{1,0:T(8,128)(2,1)S(1)}, bf16[8,4320]{1,0:T(8,128)(2,1)S(1)}, u32[]{:S(2)}, u32[]{:S(2)}) collective-permute-start(bf16[8,4320]{1,0:T(8,128)(2,1)S(1)} %get-tuple-element.43), channel_id=1, source_target_pairs={{0,6},{1,7},{2,4},{3,5},{4,2},{5,3},{6,0},{7,1},{8,14},{9,15},{10,... | collective-permute-start | bytes 207368 | tf_op jit(solution)/shard_map/ppermute | solution.py:334
  37.5 2.0 %shard_map.72 = bf16[8,64,128]{2,1,0:T(8,128)(2,1)} custom-call(bf16[16,64,128]{2,1,0:T(8,128)(2,1)S(1)} %get-tuple-element.40.refs_0_.pack, bf16[3456,256]{1,0:T(8,128)(2,1)S(1)} %copy-done), custom_call_target="tpu_custom_call" | custom-call | flops 1000000000 | bytes 2031616 | tf_op jit(solution)/shard_map/pallas_call | solution.py:318
  39.5 4.4 %all-to-all-start.1 = ((bf16[8,64,128]{2,1,0:T(8,128)(2,1)}), bf16[8,64,128]{2,1,0:T(8,128)(2,1)S(1)}, u32[]{:S(2)}, u32[]{:S(2)}) async-start(bf16[8,64,128]{2,1,0:T(8,128)(2,1)} %shard_map.72), calls=%async_computation.1 | async-start | bytes 262144 | tf_op jit(solution)/shard_map/all_to_all | solution.py:398
  43.9 0.0 collective-permute-done.10.refs_1_
  43.9 0.0 collective-permute-done.11.refs_2_
  43.9 0.0 collective-permute-done.9.refs_0_
  43.9 0.0 collective-permute-done.12.refs_3_
  43.9 0.0 collective-permute-done.13.refs_4_
  44.0 0.1 shard_map.75.refs_0_
  44.0 0.1 collective-permute-start.14
  44.1 1.6 %collective-permute-start.15 = (bf16[8,4320]{1,0:T(8,128)(2,1)S(1)}, bf16[8,4320]{1,0:T(8,128)(2,1)S(1)}, u32[]{:S(2)}, u32[]{:S(2)}) collective-permute-start(bf16[8,4320]{1,0:T(8,128)(2,1)S(1)} %shard_map.75.refs_0_), channel_id=1, source_target_pairs={{0,16},{8,24},{16,0},{24,8},{1,17},{9,25},{17,1},{25,9},{2,18},{10... | collective-permute-start | bytes 207368 | tf_op jit(solution)/shard_map/ppermute | solution.py:334
  45.7 0.3 collective-permute-start.16
  46.0 0.0 collective-permute-done.14.refs_1_
  46.0 2.8 %collective-permute-done.15.refs_2_ = bf16[8,4320]{1,0:T(8,128)(2,1)S(1)} collective-permute-done((bf16[8,4320]{1,0:T(8,128)(2,1)S(1)}, bf16[8,4320]{1,0:T(8,128)(2,1)S(1)}, u32[]{:S(2)}, u32[]{:S(2)}) %collective-permute-start.15) | collective-permute-done | bytes 69152 | tf_op jit(solution)/shard_map/ppermute | solution.py:334
  48.7 1.1 %collective-permute-done.16.refs_3_ = bf16[8,4320]{1,0:T(8,128)(2,1)S(1)} collective-permute-done((bf16[8,4320]{1,0:T(8,128)(2,1)S(1)}, bf16[8,4320]{1,0:T(8,128)(2,1)S(1)}, u32[]{:S(2)}, u32[]{:S(2)}) %collective-permute-start.16) | collective-permute-done | bytes 69152 | tf_op jit(solution)/shard_map/ppermute | solution.py:334
  49.9 0.8 %shard_map.76 = (f32[16,864]{1,0:T(8,128)}, f32[32,3456]{1,0:T(8,128)}) custom-call(s32[1]{0:T(128)} %bitcast.1._.place, bf16[8,4320]{1,0:T(8,128)(2,1)S(1)} %shard_map.75.refs_0_, bf16[8,4320]{1,0:T(8,128)(2,1)S(1)} %collective-permute-done.14.refs_1_, bf16[8,4320]{1,0:T(8,128)(2,1)S(1)} %collective-permute-done.15.refs_2_, ...), custom_call_target="tpu_custom_call" | custom-call | flops 1000000000 | bytes 276484 | tf_op jit(solution)/shard_map/pallas_call | solution.py:318
  50.7 0.6 %all-to-all-done.1.got = bf16[8,64,128]{2,1,0:T(8,128)(2,1)S(1)} async-done(((bf16[8,64,128]{2,1,0:T(8,128)(2,1)}), bf16[8,64,128]{2,1,0:T(8,128)(2,1)S(1)}, u32[]{:S(2)}, u32[]{:S(2)}) %all-to-all-start.1) | async-done | bytes 131104 | tf_op jit(solution)/shard_map/all_to_all | solution.py:398
  51.2 0.8 %shard_map.74 = bf16[32,8,128]{2,1,0:T(8,128)(2,1)} custom-call(bf16[8,64,128]{2,1,0:T(8,128)(2,1)S(1)} %all-to-all-done.1.got), custom_call_target="tpu_custom_call" | custom-call | flops 1000000000 | bytes 131072 | tf_op jit(solution)/shard_map/pallas_call | solution.py:318
  (2 shorter events, 0.1 us)
Async XLA Ops:
  0.6 11.6 %copy-start.1 = (bf16[1,4,64,1024]{3,2,1,0:T(8,128)(2,1)S(1)}, bf16[1,4,64,1024]{3,2,1,0:T(8,128)(2,1)}, u32[]{:S(2)}) copy-start(bf16[1,4,64,1024]{3,2,1,0:T(8,128)(2,1)} %param.4) | copy-start | bytes 1572868
  0.6 11.6 %copy-start.2 = (bf16[864,128]{1,0:T(8,128)(2,1)S(1)}, bf16[864,128]{1,0:T(8,128)(2,1)}, u32[]{:S(2)}) copy-start(bf16[864,128]{1,0:T(8,128)(2,1)} %w1.1) | copy-start | bytes 663556
  2.5 9.8 %collective-permute-start = (bf16[1,64,1024]{2,1,0:T(8,128)(2,1)}, bf16[1,64,1024]{2,1,0:T(8,128)(2,1)S(1)}, u32[]{:S(2)}, u32[]{:S(2)}) collective-permute-start(bf16[1,64,1024]{2,1,0:T(8,128)(2,1)} %get-tuple-element.27), channel_id=1, source_target_pairs={{0,1},{1,2},{2,3},{3,4},{4,5},{5,6},{6,7},{8,9},{9,10},{10,11},{11... | collective-permute-start | bytes 393224 | tf_op jit(solution)/shard_map/ppermute | solution.py:342
  7.4 12.2 %all-to-all-start = ((bf16[8,64,128]{2,1,0:T(8,128)(2,1)}), bf16[8,64,128]{2,1,0:T(8,128)(2,1)S(1)}, u32[]{:S(2)}, u32[]{:S(2)}) async-start(bf16[8,64,128]{2,1,0:T(8,128)(2,1)} %get-tuple-element.31), calls=%async_computation | async-start | bytes 262144 | tf_op jit(solution)/shard_map/all_to_all | solution.py:368
  13.5 1.0 %copy-start.3 = (bf16[2,256,1152]{2,1,0:T(8,128)(2,1)}, bf16[2,256,1152]{2,1,0:T(8,128)(2,1)S(1)}, u32[]{:S(2)}) copy-start(bf16[2,256,1152]{2,1,0:T(8,128)(2,1)S(1)} %get-tuple-element.30.p1) | copy-start | bytes 3538948
  14.5 7.1 %copy-start = (bf16[3456,256]{1,0:T(8,128)(2,1)S(1)}, bf16[3456,256]{1,0:T(8,128)(2,1)}, u32[]{:S(2)}) copy-start(bf16[3456,256]{1,0:T(8,128)(2,1)} %w2.3) | copy-start | bytes 5308420
  14.5 10.1 %collective-permute-start.2 = (bf16[16,64,128]{2,1,0:T(8,128)(2,1)S(1)}, bf16[16,64,128]{2,1,0:T(8,128)(2,1)S(1)}, u32[]{:S(2)}, u32[]{:S(2)}) collective-permute-start(bf16[16,64,128]{2,1,0:T(8,128)(2,1)S(1)} %get-tuple-element.40.refs_0_.pack), channel_id=1, source_target_pairs={{0,16},{8,24},{16,0},{24,8},{1,17},{9,25},{17,1},{25,9},{2,18},{10... | collective-permute-start | bytes 786440 | tf_op jit(solution)/shard_map/ppermute | solution.py:334
  16.0 10.3 %collective-permute-start.1 = (bf16[16,64,128]{2,1,0:T(8,128)(2,1)S(1)}, bf16[16,64,128]{2,1,0:T(8,128)(2,1)S(1)}, u32[]{:S(2)}, u32[]{:S(2)}) collective-permute-start(bf16[16,64,128]{2,1,0:T(8,128)(2,1)S(1)} %get-tuple-element.40.refs_0_.pack), channel_id=1, source_target_pairs={{0,8},{8,0},{16,24},{24,16},{1,9},{9,1},{17,25},{25,17},{2,10},{10... | collective-permute-start | bytes 786440 | tf_op jit(solution)/shard_map/ppermute | solution.py:334
  19.6 2.0 %copy-start.4 = (bf16[2,256,1152]{2,1,0:T(8,128)(2,1)S(1)}, bf16[2,256,1152]{2,1,0:T(8,128)(2,1)}, u32[]{:S(2)}) copy-start(bf16[2,256,1152]{2,1,0:T(8,128)(2,1)} %copy-done.3) | copy-start | bytes 3538948
  19.6 4.3 %collective-permute-start.3 = (bf16[8,16,128]{2,1,0:T(8,128)(2,1)S(1)}, bf16[8,16,128]{2,1,0:T(8,128)(2,1)S(1)}, u32[]{:S(2)}, u32[]{:S(2)}) collective-permute-start(bf16[8,16,128]{2,1,0:T(8,128)(2,1)S(1)} %get-tuple-element.34), channel_id=1, source_target_pairs={{0,8},{8,0},{16,24},{24,16},{1,9},{9,1},{17,25},{25,17},{2,10},{10... | collective-permute-start | bytes 98312 | tf_op jit(solution)/shard_map/ppermute | solution.py:334
  19.7 4.2 %collective-permute-start.4 = (bf16[8,16,128]{2,1,0:T(8,128)(2,1)S(1)}, bf16[8,16,128]{2,1,0:T(8,128)(2,1)S(1)}, u32[]{:S(2)}, u32[]{:S(2)}) collective-permute-start(bf16[8,16,128]{2,1,0:T(8,128)(2,1)S(1)} %get-tuple-element.35), channel_id=1, source_target_pairs={{0,16},{8,24},{16,0},{24,8},{1,17},{9,25},{17,1},{25,9},{2,18},{10... | collective-permute-start | bytes 98312 | tf_op jit(solution)/shard_map/ppermute | solution.py:334
  21.3 3.3 %collective-permute-start.5 = (bf16[8,16,128]{2,1,0:T(8,128)(2,1)S(1)}, bf16[8,16,128]{2,1,0:T(8,128)(2,1)S(1)}, u32[]{:S(2)}, u32[]{:S(2)}) collective-permute-start(bf16[8,16,128]{2,1,0:T(8,128)(2,1)S(1)} %get-tuple-element.36), channel_id=1, source_target_pairs={{0,24},{8,16},{16,8},{24,0},{1,25},{9,17},{17,9},{25,1},{2,26},{10... | collective-permute-start | bytes 98312 | tf_op jit(solution)/shard_map/ppermute | solution.py:334
  24.7 1.7 %collective-permute-start.6 = (bf16[16,64,128]{2,1,0:T(8,128)(2,1)S(1)}, bf16[16,64,128]{2,1,0:T(8,128)(2,1)S(1)}, u32[]{:S(2)}, u32[]{:S(2)}) collective-permute-start(bf16[16,64,128]{2,1,0:T(8,128)(2,1)S(1)} %collective-permute-done.2.refs_2_), channel_id=1, source_target_pairs={{0,8},{8,0},{16,24},{24,16},{1,9},{9,1},{17,25},{25,17},{2,10},{10... | collective-permute-start | bytes 786440 | tf_op jit(solution)/shard_map/ppermute | solution.py:334
  24.8 1.5 %collective-permute-start.7 = (bf16[64,864]{1,0:T(8,128)(2,1)S(1)}, bf16[64,864]{1,0:T(8,128)(2,1)S(1)}, u32[]{:S(2)}, u32[]{:S(2)}) collective-permute-start(bf16[64,864]{1,0:T(8,128)(2,1)S(1)} %get-tuple-element.33), channel_id=1, source_target_pairs={{0,8},{8,0},{16,24},{24,16},{1,9},{9,1},{17,25},{25,17},{2,10},{10... | collective-permute-start | bytes 331784 | tf_op jit(solution)/shard_map/ppermute | solution.py:334
  27.1 8.0 %collective-permute-start.8 = (bf16[2,8,4320]{2,1,0:T(8,128)(2,1)S(1)}, bf16[2,8,4320]{2,1,0:T(8,128)(2,1)S(1)}, u32[]{:S(2)}, u32[]{:S(2)}) collective-permute-start(bf16[2,8,4320]{2,1,0:T(8,128)(2,1)S(1)} %get-tuple-element.39), channel_id=1, source_target_pairs={{0,1},{1,0},{2,3},{3,2},{4,5},{5,4},{6,7},{7,6},{8,9},{9,8},{10,11... | collective-permute-start | bytes 414728 | tf_op jit(solution)/shard_map/ppermute | solution.py:334
  27.4 16.5 %collective-permute-start.10 = (bf16[8,4320]{1,0:T(8,128)(2,1)S(1)}, bf16[8,4320]{1,0:T(8,128)(2,1)S(1)}, u32[]{:S(2)}, u32[]{:S(2)}) collective-permute-start(bf16[8,4320]{1,0:T(8,128)(2,1)S(1)} %get-tuple-element.47), channel_id=1, source_target_pairs={{0,2},{1,3},{2,0},{3,1},{4,6},{5,7},{6,4},{7,5},{8,10},{9,11},{10,... | collective-permute-start | bytes 207368 | tf_op jit(solution)/shard_map/ppermute | solution.py:334
  28.9 15.1 %collective-permute-start.11 = (bf16[8,4320]{1,0:T(8,128)(2,1)S(1)}, bf16[8,4320]{1,0:T(8,128)(2,1)S(1)}, u32[]{:S(2)}, u32[]{:S(2)}) collective-permute-start(bf16[8,4320]{1,0:T(8,128)(2,1)S(1)} %get-tuple-element.48), channel_id=1, source_target_pairs={{0,3},{1,2},{2,1},{3,0},{4,7},{5,6},{6,5},{7,4},{8,11},{9,10},{10,... | collective-permute-start | bytes 207368 | tf_op jit(solution)/shard_map/ppermute | solution.py:334
  30.6 13.3 %collective-permute-start.9 = (bf16[8,4320]{1,0:T(8,128)(2,1)S(1)}, bf16[8,4320]{1,0:T(8,128)(2,1)S(1)}, u32[]{:S(2)}, u32[]{:S(2)}) collective-permute-start(bf16[8,4320]{1,0:T(8,128)(2,1)S(1)} %get-tuple-element.46), channel_id=1, source_target_pairs={{0,1},{1,0},{2,3},{3,2},{4,5},{5,4},{6,7},{7,6},{8,9},{9,8},{10,11... | collective-permute-start | bytes 207368 | tf_op jit(solution)/shard_map/ppermute | solution.py:334
  35.1 8.8 %collective-permute-start.12 = (bf16[8,4320]{1,0:T(8,128)(2,1)S(1)}, bf16[8,4320]{1,0:T(8,128)(2,1)S(1)}, u32[]{:S(2)}, u32[]{:S(2)}) collective-permute-start(bf16[8,4320]{1,0:T(8,128)(2,1)S(1)} %get-tuple-element.42), channel_id=1, source_target_pairs={{0,4},{1,5},{2,6},{3,7},{4,0},{5,1},{6,2},{7,3},{8,12},{9,13},{10,... | collective-permute-start | bytes 207368 | tf_op jit(solution)/shard_map/ppermute | solution.py:334
  35.2 8.7 %collective-permute-start.13 = (bf16[8,4320]{1,0:T(8,128)(2,1)S(1)}, bf16[8,4320]{1,0:T(8,128)(2,1)S(1)}, u32[]{:S(2)}, u32[]{:S(2)}) collective-permute-start(bf16[8,4320]{1,0:T(8,128)(2,1)S(1)} %get-tuple-element.43), channel_id=1, source_target_pairs={{0,6},{1,7},{2,4},{3,5},{4,2},{5,3},{6,0},{7,1},{8,14},{9,15},{10,... | collective-permute-start | bytes 207368 | tf_op jit(solution)/shard_map/ppermute | solution.py:334
  39.5 11.8 %all-to-all-start.1 = ((bf16[8,64,128]{2,1,0:T(8,128)(2,1)}), bf16[8,64,128]{2,1,0:T(8,128)(2,1)S(1)}, u32[]{:S(2)}, u32[]{:S(2)}) async-start(bf16[8,64,128]{2,1,0:T(8,128)(2,1)} %shard_map.72), calls=%async_computation.1 | async-start | bytes 262144 | tf_op jit(solution)/shard_map/all_to_all | solution.py:398
  44.0 1.9 %collective-permute-start.14 = (bf16[8,4320]{1,0:T(8,128)(2,1)S(1)}, bf16[8,4320]{1,0:T(8,128)(2,1)S(1)}, u32[]{:S(2)}, u32[]{:S(2)}) collective-permute-start(bf16[8,4320]{1,0:T(8,128)(2,1)S(1)} %shard_map.75.refs_0_), channel_id=1, source_target_pairs={{0,8},{8,0},{16,24},{24,16},{1,9},{9,1},{17,25},{25,17},{2,10},{10... | collective-permute-start | bytes 207368 | tf_op jit(solution)/shard_map/ppermute | solution.py:334
  44.1 4.6 %collective-permute-start.15 = (bf16[8,4320]{1,0:T(8,128)(2,1)S(1)}, bf16[8,4320]{1,0:T(8,128)(2,1)S(1)}, u32[]{:S(2)}, u32[]{:S(2)}) collective-permute-start(bf16[8,4320]{1,0:T(8,128)(2,1)S(1)} %shard_map.75.refs_0_), channel_id=1, source_target_pairs={{0,16},{8,24},{16,0},{24,8},{1,17},{9,25},{17,1},{25,9},{2,18},{10... | collective-permute-start | bytes 207368 | tf_op jit(solution)/shard_map/ppermute | solution.py:334
  45.7 4.2 %collective-permute-start.16 = (bf16[8,4320]{1,0:T(8,128)(2,1)S(1)}, bf16[8,4320]{1,0:T(8,128)(2,1)S(1)}, u32[]{:S(2)}, u32[]{:S(2)}) collective-permute-start(bf16[8,4320]{1,0:T(8,128)(2,1)S(1)} %shard_map.75.refs_0_), channel_id=1, source_target_pairs={{0,24},{8,16},{16,8},{24,0},{1,25},{9,17},{17,9},{25,1},{2,26},{10... | collective-permute-start | bytes 207368 | tf_op jit(solution)/shard_map/ppermute | solution.py:334

commit v5 on v4

--- a/solution.py
+++ b/solution.py
@@ -37,19 +37,16 @@
     return one_hot((to_k < NK) & (row == to_j * NK + to_k))
 
 
-def fill_patches(planes, p1):
+def fill_picked(planes, picked):
     row, col = iota((80, 64), 0), iota((80, 64), 1)
     pick = one_hot(col == 4 * (row % NJ) + row // NJ - 1)
-    for a, rows in enumerate(planes):
-        picked = dot(pick, rows).astype(BF16)
-        for p in range(2):
-            for b in range(3):
-                rho = 2 * p + b
-                for k in range(NK):
-                    at = p * CELLS + k * NJ
-                    p1[at : at + NJ, (3 * a + b) * 128 : (3 * a + b + 1) * 128] = picked[
-                        rho * NJ : (rho + 1) * NJ, k * 128 : (k + 1) * 128
-                    ]
+    for x, rows in enumerate(planes):
+        value = dot(pick, rows).astype(BF16)
+        for rho in range(5):
+            for k in range(NK):
+                picked[x, rho, k * NJ : (k + 1) * NJ] = value[
+                    rho * NJ : (rho + 1) * NJ, k * 128 : (k + 1) * 128
+                ]
 
 
 def widen(w1, w_ext):
@@ -64,9 +61,10 @@
         w_ext[base + 96 : base + 128, 256:384] = w1[src : src + 32, :]
 
 
-def fill_hidden(p1, w_ext, hidden, slope_t):
+def fill_hidden(picked, i, w_ext, hidden, slope_t):
     for p in range(2):
-        full = dot(p1[p * CELLS : (p + 1) * CELLS, :], w_ext[...])
+        patches = [picked[2 * i + a, 2 * p + b] for a in range(3) for b in range(3)]
+        full = dot(jnp.concatenate(patches, axis=1), w_ext[...])
         before = jnp.concatenate(
             [jnp.zeros((NJ, 128), F32), full[: CELLS - NJ, 256:384]], axis=0
         )
@@ -107,11 +105,11 @@
         return self.pack[at : at + 2].reshape(CELLS, 128)
 
 
-def kernel_pack(snap, halo, w1, pack, slope_t, p1, w_ext):
+def kernel_pack(snap, halo, w1, pack, slope_t, picked, w_ext):
     widen(w1, w_ext)
-    for i, planes in enumerate(([halo[0], snap[0], snap[1]], [snap[1], snap[2], snap[3]])):
-        fill_patches(planes, p1.at[i])
-        fill_hidden(p1.at[i], w_ext, Phases(pack, i), slope_t.at[i])
+    fill_picked([halo[0], snap[0], snap[1], snap[2], snap[3]], picked)
+    for i in range(2):
+        fill_hidden(picked, i, w_ext, Phases(pack, i), slope_t.at[i])
 
 
 def kernel_pieces(place, slot, cot, *outs):
@@ -122,12 +120,12 @@
             out[n] = cot[slot[0] ^ n, pl.ds(at, height), :]
 
 
-def kernel_back(pieces, rows_per, place, slot, slope_t, p1, w2, cot, *rest):
+def kernel_back(pieces, rows_per, place, slot, slope_t, picked, w2, cot, *rest):
     *outs, grad_t = rest
-    grad_one_share(pieces, rows_per, place, slot, w2, cot, outs, p1, slope_t, grad_t)
-
-
-def grad_one_share(pieces, rows_per, place, slot, w2, cot, outs, p1, slope_t, grad_t):
+    grad_one_share(pieces, rows_per, place, slot, w2, cot, outs, picked, slope_t, grad_t)
+
+
+def grad_one_share(pieces, rows_per, place, slot, w2, cot, outs, picked, slope_t, grad_t):
     sources = cot.shape[0]
     moved = dot(cot[...].reshape(-1, CELLS), cell_order(True))
     moved = moved.reshape(sources * pieces, 2, rows_per, 4 * CELLS)
@@ -157,9 +155,8 @@
     lane = iota((128, 128), 1)
     frames = []
     for t in range(9):
-        cols = slice(t * 128, (t + 1) * 128)
-        full = dot(grad_t[:, : 2 * CELLS], p1[0, :, cols])
-        full = full + dot(grad_t[:, 2 * CELLS :], p1[1, :, cols])
+        blocks = [picked[2 * i + t // 3, 2 * p + t % 3] for i in range(2) for p in range(2)]
+        full = dot(grad_t[...], jnp.concatenate(blocks, axis=0))
         side = jnp.where(lane < 64, full[0:128], full[256:384])
         side = jnp.where((lane < 64) | (lane >= 96), side, 0.0)
         own = jnp.where(lane < 32, 0.0, full[128:256])
@@ -366,12 +363,12 @@
     )
     halo = from_below(last, "space")
     cot = lax.all_to_all(parcels, "space", split_axis=0, concat_axis=0, tiled=True)
-    pack, slope_t, p1 = call(
+    pack, slope_t, picked = call(
         kernel_pack,
         (
             shape((PACK, 64, CELLS), BF16),
             shape((2, 4, 128, CELLS), F32),
-            shape((2, 2 * CELLS, 9 * 128), BF16),
+            shape((5, 5, CELLS, 128), BF16),
         ),
         slab,
         halo,
@@ -384,7 +381,7 @@
         place,
         slot,
         slope_t,
-        p1,
+        picked,
         conv_two,
         cot,
         spaces={0: pltpu.SMEM, 1: pltpu.SMEM},
@@ -418,6 +415,7 @@
         spaces={0: pltpu.SMEM, 1: pltpu.SMEM},
     )
     cots = [own] + [swap_ranks(piece, "dp", k) for k, piece in enumerate(cots, 1)]
+    parts = latent_of(pack)
     one_block = shape((rows_per, WIDTH), BF16)
     kept, near_1, near_2, near_3, lent, own_far = call(
         functools.partial(kernel_two, samples, rows_per),
@@ -432,12 +430,11 @@
         pack,
         beside,
         across,
-        swap_ranks(first_of(across, *ones, *cots[1:]), "dp", 1),
+        swap_ranks(first_of(across, *ones, *cots[1:], parts), "dp", 1),
         *cots,
         ones[0],
         swap_ranks(ones[1], "dp", 1),
     )
-    parts = latent_of(first_of(pack, lent))
     lent = swap_ranks(lent, "space", 1)
     far = call(kernel_far, (one_block, one_block), lent, own_far)
     others = [

time: 52.5 us -> 50.7 us (0.966)
  waiting for transfers between devices: 14.2 us -> 10.2 us
  starting transfers between devices: 26.2 us -> 27.8 us
  local copies, waits for them, and re-layouts: 1.02 us -> 1.73 us
    all_to_all x1, waiting for transfers between devices: 3.56 us -> 0.91 us  [on_device(): lax.all_to_all(parcels, 'space', split_axis=0, concat_axis=0, tiled=True)]
    ppermute x16, starting transfers between devices: 12.1 us -> 13.7 us  [swap_ranks(): lax.ppermute(block, axis, [(i, i ^ k) for i in range(lax.axis_size(axis))])]
    ppermute x16, waiting for transfers between devices: 10 us -> 8.96 us  [swap_ranks(): lax.ppermute(block, axis, [(i, i ^ k) for i in range(lax.axis_size(axis))])]
    unnamed x10 -> x14, local copies, waits for them, and re-layouts: 1.02 us -> 1.73 us
  transfers between devices with their start and end apart: 19 -> 19, of which waited for: 7 -> 7; matrix products, arithmetic and copies ran while one was open for 0% -> 0% of each run, Pallas kernels for 12% -> 13%
where the time goes in v5:
time: 50.7 us; the launch traced here: 50.3 us
  starting transfers between devices  27.8 us (55%)
  waiting for transfers between devices  10.2 us (20%)
  Pallas kernels  9.68 us (19%)
  local copies, waits for them, and re-layouts  1.73 us (3%)
  between operations  0.82 us (2%)
    ppermute x16, starting transfers between devices, swap_ranks(): lax.ppermute(block, axis, [(i, i ^ k) for i in range(lax.axis_size(axis))])  13.7 us
    pallas_call x10, Pallas kernels, call(): pl.pallas_call(kernel, out_shape=out_shape, in_specs=[spec(n, spaces) for...  9.68 us
    ppermute x16, waiting for transfers between devices, swap_ranks(): lax.ppermute(block, axis, [(i, i ^ k) for i in range(lax.axis_size(axis))])  8.96 us
    all_to_all x1, starting transfers between devices, on_device(): lax.all_to_all(parcels, 'space', split_axis=0, concat_axis=0, tiled=True)  4.89 us
    ppermute x1, starting transfers between devices, from_below(): lax.ppermute(block, axis, [(i - 1, i) for i in range(1, lax.axis_size(axi...  4.85 us
    all_to_all x1, starting transfers between devices, joined(): lax.all_to_all(parts, 'space', split_axis=0, concat_axis=0, tiled=True)  4.39 us
    unnamed x14, local copies, waits for them, and re-layouts  1.73 us
  transfers between devices with their start and end apart: 19, of which 7 were waited for; matrix products, arithmetic and copies ran while one was open for 0% of the time, Pallas kernels for 13%

profile of v5, /device:TPU:0, one launch (start us, length us, event | category | flops | bytes accessed | tf_op | source)
XLA Modules:
  0.0 50.3 jit_solution(8949665311314553567)
XLA Ops:
  0.6 0.0 copy-start.1
  0.6 0.0 copy-start.2
  0.7 1.8 %shard_map.67 = (bf16[8,64,128]{2,1,0:T(8,128)(2,1)}, bf16[1,64,1024]{2,1,0:T(8,128)(2,1)}) custom-call(s32[1]{0:T(128)} %bitcast.1._.place, s32[1]{0:T(128)} %bitcast.2.__.slot, bf16[32,8,128]{2,1,0:T(8,128)(2,1)} %bitcast.7, bf16[4,64,1024]{2,1,0:T(8,128)(2,1)} %bitcast.5), custom_call_target="tpu_custom_call" | custom-call | flops 1000000000 | bytes 589832 | tf_op jit(solution)/shard_map/pallas_call | solution.py:315
  2.5 4.8 %collective-permute-start = (bf16[1,64,1024]{2,1,0:T(8,128)(2,1)}, bf16[1,64,1024]{2,1,0:T(8,128)(2,1)S(1)}, u32[]{:S(2)}, u32[]{:S(2)}) collective-permute-start(bf16[1,64,1024]{2,1,0:T(8,128)(2,1)} %get-tuple-element.26), channel_id=1, source_target_pairs={{0,1},{1,2},{2,3},{3,4},{4,5},{5,6},{6,7},{8,9},{9,10},{10,11},{11... | collective-permute-start | bytes 393224 | tf_op jit(solution)/shard_map/ppermute | solution.py:339
  7.4 4.9 %all-to-all-start = ((bf16[8,64,128]{2,1,0:T(8,128)(2,1)}), bf16[8,64,128]{2,1,0:T(8,128)(2,1)S(1)}, u32[]{:S(2)}, u32[]{:S(2)}) async-start(bf16[8,64,128]{2,1,0:T(8,128)(2,1)} %get-tuple-element.30), calls=%async_computation | async-start | bytes 262144 | tf_op jit(solution)/shard_map/all_to_all | solution.py:365
  12.3 0.0 copy-start
  12.3 0.0 collective-permute-done.halo
  12.3 0.0 copy-done.1
  12.3 0.0 copy-done.2
  12.3 1.2 %shard_map.68 = (bf16[16,64,128]{2,1,0:T(8,128)(2,1)S(1)}, f32[2,4,128,128]{3,2,1,0:T(8,128)S(1)}, bf16[5,5,128,128]{3,2,1,0:T(8,128)(2,1)S(1)}) custom-call(bf16[4,64,1024]{2,1,0:T(8,128)(2,1)S(1)} %bitcast.6, bf16[1,64,1024]{2,1,0:T(8,128)(2,1)S(1)} %collective-permute-done.halo, bf16[864,128]{1,0:T(8,128)(2,1)S(1)} %copy-done.2), custom_call_target="tpu_custom_call" | custom-call | flops 1000000000 | bytes 876544 | tf_op jit(solution)/shard_map/pallas_call | solution.py:315
  13.5 0.0 copy-start.3
  13.5 0.9 %copy-done.3 = bf16[5,5,128,128]{3,2,1,0:T(8,128)(2,1)} copy-done((bf16[5,5,128,128]{3,2,1,0:T(8,128)(2,1)}, bf16[5,5,128,128]{3,2,1,0:T(8,128)(2,1)S(1)}, u32[]{:S(2)}) %copy-start.3) | copy-done | bytes 819224
  14.4 0.0 copy-start.5
  14.4 0.8 %copy-done.5 = f32[2,4,128,128]{3,2,1,0:T(8,128)} copy-done((f32[2,4,128,128]{3,2,1,0:T(8,128)}, f32[2,4,128,128]{3,2,1,0:T(8,128)S(1)}, u32[]{:S(2)}) %copy-start.5) | copy-done | bytes 524312
  15.2 1.5 %collective-permute-start.2 = (bf16[16,64,128]{2,1,0:T(8,128)(2,1)S(1)}, bf16[16,64,128]{2,1,0:T(8,128)(2,1)S(1)}, u32[]{:S(2)}, u32[]{:S(2)}) collective-permute-start(bf16[16,64,128]{2,1,0:T(8,128)(2,1)S(1)} %get-tuple-element.27.pack.refs_0_), channel_id=1, source_target_pairs={{0,16},{8,24},{16,0},{24,8},{1,17},{9,25},{17,1},{25,9},{2,18},{10... | collective-permute-start | bytes 786440 | tf_op jit(solution)/shard_map/ppermute | solution.py:331
  16.7 0.0 collective-permute-start.1
  16.7 0.0 copy-done
  16.7 2.0 %shard_map.69 = bf16[8,64,128]{2,1,0:T(8,128)(2,1)} custom-call(bf16[16,64,128]{2,1,0:T(8,128)(2,1)S(1)} %get-tuple-element.27.pack.refs_0_, bf16[3456,256]{1,0:T(8,128)(2,1)S(1)} %copy-done), custom_call_target="tpu_custom_call" | custom-call | flops 1000000000 | bytes 2031616 | tf_op jit(solution)/shard_map/pallas_call | solution.py:315
  18.7 0.0 copy-start.4
  18.7 0.9 %all-to-all-done.cot = bf16[8,64,128]{2,1,0:T(8,128)(2,1)S(1)} async-done(((bf16[8,64,128]{2,1,0:T(8,128)(2,1)}), bf16[8,64,128]{2,1,0:T(8,128)(2,1)S(1)}, u32[]{:S(2)}, u32[]{:S(2)}) %all-to-all-start) | async-done | bytes 131104 | tf_op jit(solution)/shard_map/all_to_all | solution.py:365
  19.6 0.0 copy-start.6
  19.6 0.1 collective-permute-start.3
  19.7 1.6 %collective-permute-start.4 = (bf16[8,16,128]{2,1,0:T(8,128)(2,1)S(1)}, bf16[8,16,128]{2,1,0:T(8,128)(2,1)S(1)}, u32[]{:S(2)}, u32[]{:S(2)}) collective-permute-start(bf16[8,16,128]{2,1,0:T(8,128)(2,1)S(1)} %get-tuple-element.34), channel_id=1, source_target_pairs={{0,16},{8,24},{16,0},{24,8},{1,17},{9,25},{17,1},{25,9},{2,18},{10... | collective-permute-start | bytes 98312 | tf_op jit(solution)/shard_map/ppermute | solution.py:331
  21.3 0.3 collective-permute-start.5
  21.6 0.0 copy-done.4
  21.6 0.0 copy-done.6
  21.6 2.2 %shard_map.70 = (bf16[64,864]{1,0:T(8,128)(2,1)S(1)}, bf16[64,864]{1,0:T(8,128)(2,1)S(1)}) custom-call(s32[1]{0:T(128)} %bitcast.1._.place, s32[1]{0:T(128)} %bitcast.2.__.slot, f32[2,4,128,128]{3,2,1,0:T(8,128)S(1)} %copy-done.6, bf16[5,5,128,128]{3,2,1,0:T(8,128)(2,1)S(1)} %copy-done.4, bf16[3456,256]{1,0:T(8,128)(2,1)S(1)} %copy-done, ...), custom_call_target="tpu_custom_call" | custom-call | flops 1000000000 | bytes 3244040 | tf_op jit(solution)/shard_map/pallas_call | solution.py:315
  23.8 0.0 collective-permute-done.3.refs_5_
  23.8 0.0 collective-permute-done.4.refs_6_
  23.8 0.8 %collective-permute-done.5.refs_7_ = bf16[8,16,128]{2,1,0:T(8,128)(2,1)S(1)} collective-permute-done((bf16[8,16,128]{2,1,0:T(8,128)(2,1)S(1)}, bf16[8,16,128]{2,1,0:T(8,128)(2,1)S(1)}, u32[]{:S(2)}, u32[]{:S(2)}) %collective-permute-start.5) | collective-permute-done | bytes 32800 | tf_op jit(solution)/shard_map/ppermute | solution.py:331
  24.6 0.0 collective-permute-done.2.refs_2_
  24.7 0.2 collective-permute-start.6
  24.8 0.3 collective-permute-start.7
  25.2 1.2 %collective-permute-done.7.refs_9_ = bf16[64,864]{1,0:T(8,128)(2,1)S(1)} collective-permute-done((bf16[64,864]{1,0:T(8,128)(2,1)S(1)}, bf16[64,864]{1,0:T(8,128)(2,1)S(1)}, u32[]{:S(2)}, u32[]{:S(2)}) %collective-permute-start.7) | collective-permute-done | bytes 110624 | tf_op jit(solution)/shard_map/ppermute | solution.py:331
  26.4 0.0 collective-permute-done.1.refs_1_
  26.4 0.0 collective-permute-done.6.refs_3_
  26.4 0.7 %shard_map.72 = (f32[8,4320]{1,0:T(8,128)S(1)}, bf16[8,4320]{1,0:T(8,128)(2,1)S(1)}, bf16[8,4320]{1,0:T(8,128)(2,1)S(1)}, bf16[8,4320]{1,0:T(8,128)(2,1)S(1)}, b...) custom-call(bf16[16,64,128]{2,1,0:T(8,128)(2,1)S(1)} %get-tuple-element.27.pack.refs_0_, ...), custom_call_target="tpu_custom_call" | custom-call | flops 1000000000 | bytes 1400832 | tf_op jit(solution)/shard_map/pallas_call | solution.py:315
  27.1 0.9 %collective-permute-start.8 = (bf16[2,8,4320]{2,1,0:T(8,128)(2,1)S(1)}, bf16[2,8,4320]{2,1,0:T(8,128)(2,1)S(1)}, u32[]{:S(2)}, u32[]{:S(2)}) collective-permute-start(bf16[2,8,4320]{2,1,0:T(8,128)(2,1)S(1)} %get-tuple-element.38), channel_id=1, source_target_pairs={{0,1},{1,0},{2,3},{3,2},{4,5},{5,4},{6,7},{7,6},{8,9},{9,8},{10,11... | collective-permute-start | bytes 414728 | tf_op jit(solution)/shard_map/ppermute | solution.py:331
  28.0 1.2 %collective-permute-start.9 = (bf16[8,4320]{1,0:T(8,128)(2,1)S(1)}, bf16[8,4320]{1,0:T(8,128)(2,1)S(1)}, u32[]{:S(2)}, u32[]{:S(2)}) collective-permute-start(bf16[8,4320]{1,0:T(8,128)(2,1)S(1)} %get-tuple-element.44), channel_id=1, source_target_pairs={{0,1},{1,0},{2,3},{3,2},{4,5},{5,4},{6,7},{7,6},{8,9},{9,8},{10,11... | collective-permute-start | bytes 207368 | tf_op jit(solution)/shard_map/ppermute | solution.py:331
  29.2 0.9 %collective-permute-start.10 = (bf16[8,4320]{1,0:T(8,128)(2,1)S(1)}, bf16[8,4320]{1,0:T(8,128)(2,1)S(1)}, u32[]{:S(2)}, u32[]{:S(2)}) collective-permute-start(bf16[8,4320]{1,0:T(8,128)(2,1)S(1)} %get-tuple-element.45), channel_id=1, source_target_pairs={{0,2},{1,3},{2,0},{3,1},{4,6},{5,7},{6,4},{7,5},{8,10},{9,11},{10,... | collective-permute-start | bytes 207368 | tf_op jit(solution)/shard_map/ppermute | solution.py:331
  30.0 1.5 %collective-permute-start.11 = (bf16[8,4320]{1,0:T(8,128)(2,1)S(1)}, bf16[8,4320]{1,0:T(8,128)(2,1)S(1)}, u32[]{:S(2)}, u32[]{:S(2)}) collective-permute-start(bf16[8,4320]{1,0:T(8,128)(2,1)S(1)} %get-tuple-element.46), channel_id=1, source_target_pairs={{0,3},{1,2},{2,1},{3,0},{4,7},{5,6},{6,5},{7,4},{8,11},{9,10},{10,... | collective-permute-start | bytes 207368 | tf_op jit(solution)/shard_map/ppermute | solution.py:331
  31.5 2.8 %collective-permute-done.8.lent = bf16[2,8,4320]{2,1,0:T(8,128)(2,1)S(1)} collective-permute-done((bf16[2,8,4320]{2,1,0:T(8,128)(2,1)S(1)}, bf16[2,8,4320]{2,1,0:T(8,128)(2,1)S(1)}, u32[]{:S(2)}, u32[]{:S(2)}) %collective-permute-start.8) | collective-permute-done | bytes 138272 | tf_op jit(solution)/shard_map/ppermute | solution.py:331
  34.4 1.2 %collective-permute-start.12 = (bf16[8,4320]{1,0:T(8,128)(2,1)S(1)}, bf16[8,4320]{1,0:T(8,128)(2,1)S(1)}, u32[]{:S(2)}, u32[]{:S(2)}) collective-permute-start(bf16[8,4320]{1,0:T(8,128)(2,1)S(1)} %get-tuple-element.40), channel_id=1, source_target_pairs={{0,4},{1,5},{2,6},{3,7},{4,0},{5,1},{6,2},{7,3},{8,12},{9,13},{10,... | collective-permute-start | bytes 207368 | tf_op jit(solution)/shard_map/ppermute | solution.py:331
  35.5 2.2 %collective-permute-start.13 = (bf16[8,4320]{1,0:T(8,128)(2,1)S(1)}, bf16[8,4320]{1,0:T(8,128)(2,1)S(1)}, u32[]{:S(2)}, u32[]{:S(2)}) collective-permute-start(bf16[8,4320]{1,0:T(8,128)(2,1)S(1)} %get-tuple-element.41), channel_id=1, source_target_pairs={{0,6},{1,7},{2,4},{3,5},{4,2},{5,3},{6,0},{7,1},{8,14},{9,15},{10,... | collective-permute-start | bytes 207368 | tf_op jit(solution)/shard_map/ppermute | solution.py:331
  37.7 4.4 %all-to-all-start.1 = ((bf16[8,64,128]{2,1,0:T(8,128)(2,1)}), bf16[8,64,128]{2,1,0:T(8,128)(2,1)S(1)}, u32[]{:S(2)}, u32[]{:S(2)}) async-start(bf16[8,64,128]{2,1,0:T(8,128)(2,1)} %shard_map.69), calls=%async_computation.1 | async-start | bytes 262144 | tf_op jit(solution)/shard_map/all_to_all | solution.py:395
  42.1 0.0 collective-permute-done.9.refs_0_
  42.1 0.0 collective-permute-done.10.refs_1_
  42.1 0.0 collective-permute-done.11.refs_2_
  42.1 0.0 collective-permute-done.12.refs_3_
  42.1 0.0 collective-permute-done.13.refs_4_
  42.2 0.1 shard_map.75.refs_0_
  42.2 0.1 collective-permute-start.16
  42.3 1.8 %collective-permute-start.15 = (bf16[8,4320]{1,0:T(8,128)(2,1)S(1)}, bf16[8,4320]{1,0:T(8,128)(2,1)S(1)}, u32[]{:S(2)}, u32[]{:S(2)}) collective-permute-start(bf16[8,4320]{1,0:T(8,128)(2,1)S(1)} %shard_map.75.refs_0_), channel_id=1, source_target_pairs={{0,16},{8,24},{16,0},{24,8},{1,17},{9,25},{17,1},{25,9},{2,18},{10... | collective-permute-start | bytes 207368 | tf_op jit(solution)/shard_map/ppermute | solution.py:331
  44.1 0.1 collective-permute-start.14
  44.1 2.4 %collective-permute-done.16.refs_3_ = bf16[8,4320]{1,0:T(8,128)(2,1)S(1)} collective-permute-done((bf16[8,4320]{1,0:T(8,128)(2,1)S(1)}, bf16[8,4320]{1,0:T(8,128)(2,1)S(1)}, u32[]{:S(2)}, u32[]{:S(2)}) %collective-permute-start.16) | collective-permute-done | bytes 69152 | tf_op jit(solution)/shard_map/ppermute | solution.py:331
  46.5 1.7 %collective-permute-done.15.refs_2_ = bf16[8,4320]{1,0:T(8,128)(2,1)S(1)} collective-permute-done((bf16[8,4320]{1,0:T(8,128)(2,1)S(1)}, bf16[8,4320]{1,0:T(8,128)(2,1)S(1)}, u32[]{:S(2)}, u32[]{:S(2)}) %collective-permute-start.15) | collective-permute-done | bytes 69152 | tf_op jit(solution)/shard_map/ppermute | solution.py:331
  48.3 0.0 collective-permute-done.14.refs_1_
  48.3 0.8 %shard_map.76 = (f32[16,864]{1,0:T(8,128)}, f32[32,3456]{1,0:T(8,128)}) custom-call(s32[1]{0:T(128)} %bitcast.1._.place, bf16[8,4320]{1,0:T(8,128)(2,1)S(1)} %shard_map.75.refs_0_, bf16[8,4320]{1,0:T(8,128)(2,1)S(1)} %collective-permute-done.14.refs_1_, bf16[8,4320]{1,0:T(8,128)(2,1)S(1)} %collective-permute-done.15.refs_2_, ...), custom_call_target="tpu_custom_call" | custom-call | flops 1000000000 | bytes 276484 | tf_op jit(solution)/shard_map/pallas_call | solution.py:315
  49.1 0.4 all-to-all-done.1.got
  49.5 0.8 %shard_map.74 = bf16[32,8,128]{2,1,0:T(8,128)(2,1)} custom-call(bf16[8,64,128]{2,1,0:T(8,128)(2,1)S(1)} %all-to-all-done.1.got), custom_call_target="tpu_custom_call" | custom-call | flops 1000000000 | bytes 131072 | tf_op jit(solution)/shard_map/pallas_call | solution.py:315
  (2 shorter events, 0.1 us)
Async XLA Ops:
  0.6 11.6 %copy-start.1 = (bf16[1,4,64,1024]{3,2,1,0:T(8,128)(2,1)S(1)}, bf16[1,4,64,1024]{3,2,1,0:T(8,128)(2,1)}, u32[]{:S(2)}) copy-start(bf16[1,4,64,1024]{3,2,1,0:T(8,128)(2,1)} %param.4) | copy-start | bytes 1572868
  0.6 11.6 %copy-start.2 = (bf16[864,128]{1,0:T(8,128)(2,1)S(1)}, bf16[864,128]{1,0:T(8,128)(2,1)}, u32[]{:S(2)}) copy-start(bf16[864,128]{1,0:T(8,128)(2,1)} %w1.1) | copy-start | bytes 663556
  2.5 9.8 %collective-permute-start = (bf16[1,64,1024]{2,1,0:T(8,128)(2,1)}, bf16[1,64,1024]{2,1,0:T(8,128)(2,1)S(1)}, u32[]{:S(2)}, u32[]{:S(2)}) collective-permute-start(bf16[1,64,1024]{2,1,0:T(8,128)(2,1)} %get-tuple-element.26), channel_id=1, source_target_pairs={{0,1},{1,2},{2,3},{3,4},{4,5},{5,6},{6,7},{8,9},{9,10},{10,11},{11... | collective-permute-start | bytes 393224 | tf_op jit(solution)/shard_map/ppermute | solution.py:339
  7.4 12.2 %all-to-all-start = ((bf16[8,64,128]{2,1,0:T(8,128)(2,1)}), bf16[8,64,128]{2,1,0:T(8,128)(2,1)S(1)}, u32[]{:S(2)}, u32[]{:S(2)}) async-start(bf16[8,64,128]{2,1,0:T(8,128)(2,1)} %get-tuple-element.30), calls=%async_computation | async-start | bytes 262144 | tf_op jit(solution)/shard_map/all_to_all | solution.py:365
  12.3 4.4 %copy-start = (bf16[3456,256]{1,0:T(8,128)(2,1)S(1)}, bf16[3456,256]{1,0:T(8,128)(2,1)}, u32[]{:S(2)}) copy-start(bf16[3456,256]{1,0:T(8,128)(2,1)} %w2.3) | copy-start | bytes 5308420
  13.5 0.9 %copy-start.3 = (bf16[5,5,128,128]{3,2,1,0:T(8,128)(2,1)}, bf16[5,5,128,128]{3,2,1,0:T(8,128)(2,1)S(1)}, u32[]{:S(2)}) copy-start(bf16[5,5,128,128]{3,2,1,0:T(8,128)(2,1)S(1)} %get-tuple-element.29.picked) | copy-start | bytes 2457604
  14.4 0.8 %copy-start.5 = (f32[2,4,128,128]{3,2,1,0:T(8,128)}, f32[2,4,128,128]{3,2,1,0:T(8,128)S(1)}, u32[]{:S(2)}) copy-start(f32[2,4,128,128]{3,2,1,0:T(8,128)S(1)} %get-tuple-element.28.slope_t) | copy-start | bytes 1572868
  15.2 9.5 %collective-permute-start.2 = (bf16[16,64,128]{2,1,0:T(8,128)(2,1)S(1)}, bf16[16,64,128]{2,1,0:T(8,128)(2,1)S(1)}, u32[]{:S(2)}, u32[]{:S(2)}) collective-permute-start(bf16[16,64,128]{2,1,0:T(8,128)(2,1)S(1)} %get-tuple-element.27.pack.refs_0_), channel_id=1, source_target_pairs={{0,16},{8,24},{16,0},{24,8},{1,17},{9,25},{17,1},{25,9},{2,18},{10... | collective-permute-start | bytes 786440 | tf_op jit(solution)/shard_map/ppermute | solution.py:331
  16.7 9.7 %collective-permute-start.1 = (bf16[16,64,128]{2,1,0:T(8,128)(2,1)S(1)}, bf16[16,64,128]{2,1,0:T(8,128)(2,1)S(1)}, u32[]{:S(2)}, u32[]{:S(2)}) collective-permute-start(bf16[16,64,128]{2,1,0:T(8,128)(2,1)S(1)} %get-tuple-element.27.pack.refs_0_), channel_id=1, source_target_pairs={{0,8},{8,0},{16,24},{24,16},{1,9},{9,1},{17,25},{25,17},{2,10},{10... | collective-permute-start | bytes 786440 | tf_op jit(solution)/shard_map/ppermute | solution.py:331
  18.7 2.9 %copy-start.4 = (bf16[5,5,128,128]{3,2,1,0:T(8,128)(2,1)S(1)}, bf16[5,5,128,128]{3,2,1,0:T(8,128)(2,1)}, u32[]{:S(2)}) copy-start(bf16[5,5,128,128]{3,2,1,0:T(8,128)(2,1)} %copy-done.3) | copy-start | bytes 2457604
  19.6 2.0 %copy-start.6 = (f32[2,4,128,128]{3,2,1,0:T(8,128)S(1)}, f32[2,4,128,128]{3,2,1,0:T(8,128)}, u32[]{:S(2)}) copy-start(f32[2,4,128,128]{3,2,1,0:T(8,128)} %copy-done.5) | copy-start | bytes 1572868
  19.6 4.2 %collective-permute-start.3 = (bf16[8,16,128]{2,1,0:T(8,128)(2,1)S(1)}, bf16[8,16,128]{2,1,0:T(8,128)(2,1)S(1)}, u32[]{:S(2)}, u32[]{:S(2)}) collective-permute-start(bf16[8,16,128]{2,1,0:T(8,128)(2,1)S(1)} %get-tuple-element.33), channel_id=1, source_target_pairs={{0,8},{8,0},{16,24},{24,16},{1,9},{9,1},{17,25},{25,17},{2,10},{10... | collective-permute-start | bytes 98312 | tf_op jit(solution)/shard_map/ppermute | solution.py:331
  19.7 4.1 %collective-permute-start.4 = (bf16[8,16,128]{2,1,0:T(8,128)(2,1)S(1)}, bf16[8,16,128]{2,1,0:T(8,128)(2,1)S(1)}, u32[]{:S(2)}, u32[]{:S(2)}) collective-permute-start(bf16[8,16,128]{2,1,0:T(8,128)(2,1)S(1)} %get-tuple-element.34), channel_id=1, source_target_pairs={{0,16},{8,24},{16,0},{24,8},{1,17},{9,25},{17,1},{25,9},{2,18},{10... | collective-permute-start | bytes 98312 | tf_op jit(solution)/shard_map/ppermute | solution.py:331
  21.3 3.3 %collective-permute-start.5 = (bf16[8,16,128]{2,1,0:T(8,128)(2,1)S(1)}, bf16[8,16,128]{2,1,0:T(8,128)(2,1)S(1)}, u32[]{:S(2)}, u32[]{:S(2)}) collective-permute-start(bf16[8,16,128]{2,1,0:T(8,128)(2,1)S(1)} %get-tuple-element.35), channel_id=1, source_target_pairs={{0,24},{8,16},{16,8},{24,0},{1,25},{9,17},{17,9},{25,1},{2,26},{10... | collective-permute-start | bytes 98312 | tf_op jit(solution)/shard_map/ppermute | solution.py:331
  24.7 1.7 %collective-permute-start.6 = (bf16[16,64,128]{2,1,0:T(8,128)(2,1)S(1)}, bf16[16,64,128]{2,1,0:T(8,128)(2,1)S(1)}, u32[]{:S(2)}, u32[]{:S(2)}) collective-permute-start(bf16[16,64,128]{2,1,0:T(8,128)(2,1)S(1)} %collective-permute-done.2.refs_2_), channel_id=1, source_target_pairs={{0,8},{8,0},{16,24},{24,16},{1,9},{9,1},{17,25},{25,17},{2,10},{10... | collective-permute-start | bytes 786440 | tf_op jit(solution)/shard_map/ppermute | solution.py:331
  24.8 1.5 %collective-permute-start.7 = (bf16[64,864]{1,0:T(8,128)(2,1)S(1)}, bf16[64,864]{1,0:T(8,128)(2,1)S(1)}, u32[]{:S(2)}, u32[]{:S(2)}) collective-permute-start(bf16[64,864]{1,0:T(8,128)(2,1)S(1)} %get-tuple-element.32), channel_id=1, source_target_pairs={{0,8},{8,0},{16,24},{24,16},{1,9},{9,1},{17,25},{25,17},{2,10},{10... | collective-permute-start | bytes 331784 | tf_op jit(solution)/shard_map/ppermute | solution.py:331
  27.1 7.3 %collective-permute-start.8 = (bf16[2,8,4320]{2,1,0:T(8,128)(2,1)S(1)}, bf16[2,8,4320]{2,1,0:T(8,128)(2,1)S(1)}, u32[]{:S(2)}, u32[]{:S(2)}) collective-permute-start(bf16[2,8,4320]{2,1,0:T(8,128)(2,1)S(1)} %get-tuple-element.38), channel_id=1, source_target_pairs={{0,1},{1,0},{2,3},{3,2},{4,5},{5,4},{6,7},{7,6},{8,9},{9,8},{10,11... | collective-permute-start | bytes 414728 | tf_op jit(solution)/shard_map/ppermute | solution.py:331
  28.0 14.1 %collective-permute-start.9 = (bf16[8,4320]{1,0:T(8,128)(2,1)S(1)}, bf16[8,4320]{1,0:T(8,128)(2,1)S(1)}, u32[]{:S(2)}, u32[]{:S(2)}) collective-permute-start(bf16[8,4320]{1,0:T(8,128)(2,1)S(1)} %get-tuple-element.44), channel_id=1, source_target_pairs={{0,1},{1,0},{2,3},{3,2},{4,5},{5,4},{6,7},{7,6},{8,9},{9,8},{10,11... | collective-permute-start | bytes 207368 | tf_op jit(solution)/shard_map/ppermute | solution.py:331
  29.2 13.0 %collective-permute-start.10 = (bf16[8,4320]{1,0:T(8,128)(2,1)S(1)}, bf16[8,4320]{1,0:T(8,128)(2,1)S(1)}, u32[]{:S(2)}, u32[]{:S(2)}) collective-permute-start(bf16[8,4320]{1,0:T(8,128)(2,1)S(1)} %get-tuple-element.45), channel_id=1, source_target_pairs={{0,2},{1,3},{2,0},{3,1},{4,6},{5,7},{6,4},{7,5},{8,10},{9,11},{10,... | collective-permute-start | bytes 207368 | tf_op jit(solution)/shard_map/ppermute | solution.py:331
  30.0 12.1 %collective-permute-start.11 = (bf16[8,4320]{1,0:T(8,128)(2,1)S(1)}, bf16[8,4320]{1,0:T(8,128)(2,1)S(1)}, u32[]{:S(2)}, u32[]{:S(2)}) collective-permute-start(bf16[8,4320]{1,0:T(8,128)(2,1)S(1)} %get-tuple-element.46), channel_id=1, source_target_pairs={{0,3},{1,2},{2,1},{3,0},{4,7},{5,6},{6,5},{7,4},{8,11},{9,10},{10,... | collective-permute-start | bytes 207368 | tf_op jit(solution)/shard_map/ppermute | solution.py:331
  34.4 7.8 %collective-permute-start.12 = (bf16[8,4320]{1,0:T(8,128)(2,1)S(1)}, bf16[8,4320]{1,0:T(8,128)(2,1)S(1)}, u32[]{:S(2)}, u32[]{:S(2)}) collective-permute-start(bf16[8,4320]{1,0:T(8,128)(2,1)S(1)} %get-tuple-element.40), channel_id=1, source_target_pairs={{0,4},{1,5},{2,6},{3,7},{4,0},{5,1},{6,2},{7,3},{8,12},{9,13},{10,... | collective-permute-start | bytes 207368 | tf_op jit(solution)/shard_map/ppermute | solution.py:331
  35.5 6.6 %collective-permute-start.13 = (bf16[8,4320]{1,0:T(8,128)(2,1)S(1)}, bf16[8,4320]{1,0:T(8,128)(2,1)S(1)}, u32[]{:S(2)}, u32[]{:S(2)}) collective-permute-start(bf16[8,4320]{1,0:T(8,128)(2,1)S(1)} %get-tuple-element.41), channel_id=1, source_target_pairs={{0,6},{1,7},{2,4},{3,5},{4,2},{5,3},{6,0},{7,1},{8,14},{9,15},{10,... | collective-permute-start | bytes 207368 | tf_op jit(solution)/shard_map/ppermute | solution.py:331
  37.7 11.7 %all-to-all-start.1 = ((bf16[8,64,128]{2,1,0:T(8,128)(2,1)}), bf16[8,64,128]{2,1,0:T(8,128)(2,1)S(1)}, u32[]{:S(2)}, u32[]{:S(2)}) async-start(bf16[8,64,128]{2,1,0:T(8,128)(2,1)} %shard_map.69), calls=%async_computation.1 | async-start | bytes 262144 | tf_op jit(solution)/shard_map/all_to_all | solution.py:395
  42.2 4.3 %collective-permute-start.16 = (bf16[8,4320]{1,0:T(8,128)(2,1)S(1)}, bf16[8,4320]{1,0:T(8,128)(2,1)S(1)}, u32[]{:S(2)}, u32[]{:S(2)}) collective-permute-start(bf16[8,4320]{1,0:T(8,128)(2,1)S(1)} %shard_map.75.refs_0_), channel_id=1, source_target_pairs={{0,24},{8,16},{16,8},{24,0},{1,25},{9,17},{17,9},{25,1},{2,26},{10... | collective-permute-start | bytes 207368 | tf_op jit(solution)/shard_map/ppermute | solution.py:331
  42.3 6.0 %collective-permute-start.15 = (bf16[8,4320]{1,0:T(8,128)(2,1)S(1)}, bf16[8,4320]{1,0:T(8,128)(2,1)S(1)}, u32[]{:S(2)}, u32[]{:S(2)}) collective-permute-start(bf16[8,4320]{1,0:T(8,128)(2,1)S(1)} %shard_map.75.refs_0_), channel_id=1, source_target_pairs={{0,16},{8,24},{16,0},{24,8},{1,17},{9,25},{17,1},{25,9},{2,18},{10... | collective-permute-start | bytes 207368 | tf_op jit(solution)/shard_map/ppermute | solution.py:331
  44.1 4.2 %collective-permute-start.14 = (bf16[8,4320]{1,0:T(8,128)(2,1)S(1)}, bf16[8,4320]{1,0:T(8,128)(2,1)S(1)}, u32[]{:S(2)}, u32[]{:S(2)}) collective-permute-start(bf16[8,4320]{1,0:T(8,128)(2,1)S(1)} %shard_map.75.refs_0_), channel_id=1, source_target_pairs={{0,8},{8,0},{16,24},{24,16},{1,9},{9,1},{17,25},{25,17},{2,10},{10... | collective-permute-start | bytes 207368 | tf_op jit(solution)/shard_map/ppermute | solution.py:331

commit v6 on v5

--- a/solution.py
+++ b/solution.py
@@ -70,9 +70,11 @@
         )
         for q, pre in enumerate((full[:, 0:128] + before, full[:, 128:256])):
             logistic = 1.0 / (1.0 + jnp.exp(-pre))
-            hidden[2 * p + q] = (pre * logistic).astype(BF16)
-            slope = logistic * (1.0 + pre * (1.0 - logistic))
-            slope_t[2 * p + q] = slope.T
+            if hidden is not None:
+                hidden[2 * p + q] = (pre * logistic).astype(BF16)
+            if slope_t is not None:
+                slope = logistic * (1.0 + pre * (1.0 - logistic))
+                slope_t[2 * p + q] = slope.T
 
 
 def kernel_parcels(pieces, _, __, cot_hbm, snap, parcels, halo, cot, sems):
@@ -105,11 +107,11 @@
         return self.pack[at : at + 2].reshape(CELLS, 128)
 
 
-def kernel_pack(snap, halo, w1, pack, slope_t, picked, w_ext):
+def kernel_pack(snap, halo, w1, pack, picked, w_ext):
     widen(w1, w_ext)
     fill_picked([halo[0], snap[0], snap[1], snap[2], snap[3]], picked)
     for i in range(2):
-        fill_hidden(picked, i, w_ext, Phases(pack, i), slope_t.at[i])
+        fill_hidden(picked, i, w_ext, Phases(pack, i), None)
 
 
 def kernel_pieces(place, slot, cot, *outs):
@@ -120,8 +122,12 @@
             out[n] = cot[slot[0] ^ n, pl.ds(at, height), :]
 
 
-def kernel_back(pieces, rows_per, place, slot, slope_t, picked, w2, cot, *rest):
-    *outs, grad_t = rest
+def kernel_back(pieces, rows_per, place, slot, snap, halo, w1, w2, cot, *rest):
+    *outs, slope_t, picked, w_ext, grad_t = rest
+    widen(w1, w_ext)
+    fill_picked([halo[0], snap[0], snap[1], snap[2], snap[3]], picked)
+    for i in range(2):
+        fill_hidden(picked, i, w_ext, None, slope_t.at[i])
     grad_one_share(pieces, rows_per, place, slot, w2, cot, outs, picked, slope_t, grad_t)
 
 
@@ -183,7 +189,7 @@
     row, col = iota((CELLS, CELLS), 0), iota((CELLS, CELLS), 1)
     back = one_hot((row // NJ == col % NK) & (row % NJ == col // NK))
     for part, taps_x in enumerate(((1, 2), (0,))):
-        totals = {}
+        joined = {}
         for b in range(3):
             p, sj = TAP_PHASE[b]
             for c in range(3):
@@ -191,9 +197,15 @@
                 for a in taps_x:
                     tap = 9 * a + 3 * b + c
                     hidden = Phases(pack, 0 if a == 1 else 1)[2 * p + q]
-                    term = dot(hidden, w2[tap * 128 : (tap + 1) * 128, :])
-                    v = 2 * sj + sk
-                    totals[v] = totals[v] + term if v in totals else term
+                    weights = w2[tap * 128 : (tap + 1) * 128, :]
+                    joined.setdefault(2 * sj + sk, []).append((hidden, weights))
+        totals = {
+            v: dot(
+                jnp.concatenate([hidden for hidden, _ in pairs], axis=1),
+                jnp.concatenate([weights for _, weights in pairs], axis=0),
+            )
+            for v, pairs in joined.items()
+        }
         zero = jnp.zeros((NJ, totals[0].shape[1]), F32)
 
         def later(value):
@@ -220,13 +232,19 @@
     ]
 
 
+def kernel_left(rows_per, *refs):
+    *cots, out = refs
+    for s, values in enumerate(moved_rows(cots, rows_per, cell_order(True))):
+        for v, value in enumerate(values):
+            out[s, v] = value
+
+
 def kernel_two(samples, rows_per, *refs):
-    packs, cots, refs = refs[:samples], refs[samples : 2 * samples], refs[2 * samples :]
+    packs, left, refs = refs[:samples], refs[samples], refs[samples + 1 :]
     packed = samples > 1
     if packed:
         ones, outs = refs[:2], refs[2:]
-    left = moved_rows(cots, rows_per, cell_order(True))
-    height = left[0][0].shape[0]
+    height = left.shape[2]
     for p in range(2):
         for q in range(2):
             right_0, right_1 = [
@@ -241,8 +259,8 @@
                 if TAP_PHASE[b][0] == p and TAP_PHASE[c][0] == q
             ]
             shifts = [2 * TAP_PHASE[b][1] + TAP_PHASE[c][1] for b, c in taps]
-            same = dot(jnp.concatenate([left[0][v] for v in shifts], axis=0), both)
-            above = dot(jnp.concatenate([left[1][v] for v in shifts], axis=0), right_1)
+            same = dot(jnp.concatenate([left[0, v] for v in shifts], axis=0), both)
+            above = dot(jnp.concatenate([left[1, v] for v in shifts], axis=0), right_1)
             for n, (b, c) in enumerate(taps):
                 rows = slice(n * height, (n + 1) * height)
                 parts = (above[rows], same[rows, 0:128], same[rows, 128:256])
@@ -281,7 +299,7 @@
     total_out[...] = total.astype(BF16)
 
 
-def kernel_join(got, latent):
+def join(got, latent):
     slabs, group = got.shape[0], got.shape[1] // 2
     next_ = got[:, group:].astype(F32)
     next_ = jnp.concatenate([jnp.zeros_like(next_[:1]), next_[:-1]], axis=0)
@@ -293,7 +311,8 @@
 
 
 def kernel_final(pieces, place, *refs):
-    parts, (one, two) = refs[:pieces], refs[pieces:]
+    parts, (got, one, two, latent) = refs[:pieces], refs[pieces:]
+    join(got, latent)
     rows_per = parts[0].shape[0]
     for k in range(pieces):
         at = pl.multiple_of((place[0] ^ k) * rows_per, rows_per)
@@ -363,46 +382,48 @@
     )
     halo = from_below(last, "space")
     cot = lax.all_to_all(parcels, "space", split_axis=0, concat_axis=0, tiled=True)
-    pack, slope_t, picked = call(
-        kernel_pack,
-        (
-            shape((PACK, 64, CELLS), BF16),
-            shape((2, 4, 128, CELLS), F32),
-            shape((5, 5, CELLS, 128), BF16),
-        ),
-        slab,
-        halo,
-        conv_one,
-        scratch=[pltpu.VMEM((9 * 128, 384), BF16)],
+    forward = [pltpu.VMEM((5, 5, CELLS, 128), BF16), pltpu.VMEM((9 * 128, 384), BF16)]
+    pack = call(
+        kernel_pack, shape((PACK, 64, CELLS), BF16), slab, halo, conv_one, scratch=forward
     )
     ones = call(
         functools.partial(kernel_back, pieces, rows_per),
         (shape((64, 864), BF16),) * 2 if shared else (shape((128, 864), F32),),
         place,
         slot,
-        slope_t,
-        picked,
+        slab,
+        halo,
+        conv_one,
         conv_two,
         cot,
         spaces={0: pltpu.SMEM, 1: pltpu.SMEM},
-        scratch=[pltpu.VMEM((384, 4 * CELLS), BF16)],
-    )
+        scratch=[pltpu.VMEM((2, 4, 128, CELLS), F32), *forward]
+        + [pltpu.VMEM((384, 4 * CELLS), BF16)],
+    )
+
+    def left_of(height, *cots):
+        moved = shape((2, 4, height, len(cots) * CELLS), BF16)
+        return call(functools.partial(kernel_left, rows_per), moved, *cots)
 
     def latent_of(pack):
         return call(kernel_latent, shape((slabs, 2 * group, CELLS), BF16), pack, conv_two)
 
-    def joined(parts):
-        got = lax.all_to_all(parts, "space", split_axis=0, concat_axis=0, tiled=True)
-        return call(kernel_join, shape((group, slabs, CELLS), BF16), got)[None]
+    def exchanged(parts):
+        return lax.all_to_all(parts, "space", split_axis=0, concat_axis=0, tiled=True)
+
+    latent_shape = shape((group, slabs, CELLS), BF16)
 
     if not shared:
         two = call(
-            functools.partial(kernel_two, 1, rows_per), shape((256, 27 * 128), F32), pack, cot
+            functools.partial(kernel_two, 1, rows_per),
+            shape((256, 27 * 128), F32),
+            pack,
+            left_of(256, cot),
         )
         one, two = lax.psum((ones[0], two), "dp")
         one = lax.psum_scatter(one, "space", scatter_dimension=0, tiled=True)
         two = lax.psum_scatter(two, "space", scatter_dimension=0, tiled=True)
-        return joined(latent_of(pack)), one, two
+        return call(join, latent_shape, exchanged(latent_of(pack)))[None], one, two
 
     across = swap_ranks(pack, "dp", 2)
     beside = swap_ranks(pack, "dp", 1)
@@ -431,7 +452,7 @@
         beside,
         across,
         swap_ranks(first_of(across, *ones, *cots[1:], parts), "dp", 1),
-        *cots,
+        left_of(slabs * rows_per, *cots),
         ones[0],
         swap_ranks(ones[1], "dp", 1),
     )
@@ -441,17 +462,18 @@
         swap_ranks(block, "space", k)
         for k, block in ((1, near_1), (2, near_2), (3, near_3), (4, far[0]), (6, far[1]))
     ]
-    latent = joined(first_of(parts, *far))
+    got = exchanged(first_of(parts, *far))
     total = call(kernel_sum, one_block, kept, *others)
     totals = [swap_ranks(total, "dp", k) if k else total for k in range(pieces)]
-    one, two = call(
+    one, two, latent = call(
         functools.partial(kernel_final, pieces),
-        (shape((16, 864), F32), shape((32, 27 * 128), F32)),
+        (shape((16, 864), F32), shape((32, 27 * 128), F32), latent_shape),
         place,
         *totals,
+        got,
         spaces={0: pltpu.SMEM},
     )
-    return latent, one, two
+    return latent[None], one, two
 
 
 def solution(mesh):

time: 50.7 us -> 49.8 us (0.982)
  waiting for transfers between devices: 10.2 us -> 12.9 us
  starting transfers between devices: 27.8 us -> 25.5 us
  local copies, waits for them, and re-layouts: 1.73 us -> 0.66 us
    ppermute x16, starting transfers between devices: 13.7 us -> 10.9 us  [swap_ranks(): lax.ppermute(block, axis, [(i, i ^ k) for i in range(lax.axis_size(axis))])]
    all_to_all x1, waiting for transfers between devices: 0.91 us -> 2.44 us  [on_device(): lax.all_to_all(parcels, 'space', split_axis=0, concat_axis=0, tiled=True)]
    unnamed x14 -> x10, local copies, waits for them, and re-layouts: 1.73 us -> 0.66 us
    ppermute x16, waiting for transfers between devices: 8.96 us -> 9.54 us  [swap_ranks(): lax.ppermute(block, axis, [(i, i ^ k) for i in range(lax.axis_size(axis))])]
    all_to_all x1, waiting for transfers between devices: 0.38 us -> 0.95 us  [exchanged(): lax.all_to_all(parts, 'space', split_axis=0, concat_axis=0, tiled=True)]
where the time goes in v6:
time: 49.8 us; the launch traced here: 49.4 us
  starting transfers between devices  25.5 us (51%)
  waiting for transfers between devices  12.9 us (26%)
  Pallas kernels  9.47 us (19%)
  between operations  0.84 us (2%)
  local copies, waits for them, and re-layouts  0.66 us (1%)
    ppermute x16, starting transfers between devices, swap_ranks(): lax.ppermute(block, axis, [(i, i ^ k) for i in range(lax.axis_size(axis))])  10.9 us
    ppermute x16, waiting for transfers between devices, swap_ranks(): lax.ppermute(block, axis, [(i, i ^ k) for i in range(lax.axis_size(axis))])  9.54 us
    pallas_call x10, Pallas kernels, call(): pl.pallas_call(kernel, out_shape=out_shape, in_specs=[spec(n, spaces) for...  9.47 us
    all_to_all x1, starting transfers between devices, on_device(): lax.all_to_all(parcels, 'space', split_axis=0, concat_axis=0, tiled=True)  4.89 us
    all_to_all x1, starting transfers between devices, exchanged(): lax.all_to_all(parts, 'space', split_axis=0, concat_axis=0, tiled=True)  4.88 us
    ppermute x1, starting transfers between devices, from_below(): lax.ppermute(block, axis, [(i - 1, i) for i in range(1, lax.axis_size(axi...  4.85 us
    all_to_all x1, waiting for transfers between devices, on_device(): lax.all_to_all(parcels, 'space', split_axis=0, concat_axis=0, tiled=True)  2.44 us
  transfers between devices with their start and end apart: 19, of which 7 were waited for; matrix products, arithmetic and copies ran while one was open for 0% of the time, Pallas kernels for 13%

profile of v6, /device:TPU:0, one launch (start us, length us, event | category | flops | bytes accessed | tf_op | source)
XLA Modules:
  0.0 49.4 jit_solution(777195560851396900)
XLA Ops:
  0.6 0.0 copy-start.1
  0.6 0.0 copy-start.2
  0.7 1.9 %shard_map.67 = (bf16[8,64,128]{2,1,0:T(8,128)(2,1)}, bf16[1,64,1024]{2,1,0:T(8,128)(2,1)}) custom-call(s32[1]{0:T(128)} %bitcast._.place, s32[1]{0:T(128)} %bitcast.2.__.slot, bf16[32,8,128]{2,1,0:T(8,128)(2,1)} %bitcast.8, bf16[4,64,1024]{2,1,0:T(8,128)(2,1)} %bitcast.5), custom_call_target="tpu_custom_call" | custom-call | flops 1000000000 | bytes 589832 | tf_op jit(solution)/shard_map/pallas_call | solution.py:334
  2.5 4.8 %collective-permute-start = (bf16[1,64,1024]{2,1,0:T(8,128)(2,1)}, bf16[1,64,1024]{2,1,0:T(8,128)(2,1)S(1)}, u32[]{:S(2)}, u32[]{:S(2)}) collective-permute-start(bf16[1,64,1024]{2,1,0:T(8,128)(2,1)} %get-tuple-element.24), channel_id=1, source_target_pairs={{0,1},{1,2},{2,3},{3,4},{4,5},{5,6},{6,7},{8,9},{9,10},{10,11},{11... | collective-permute-start | bytes 393224 | tf_op jit(solution)/shard_map/ppermute | solution.py:358
  7.4 4.9 %all-to-all-start = ((bf16[8,64,128]{2,1,0:T(8,128)(2,1)}), bf16[8,64,128]{2,1,0:T(8,128)(2,1)S(1)}, u32[]{:S(2)}, u32[]{:S(2)}) async-start(bf16[8,64,128]{2,1,0:T(8,128)(2,1)} %get-tuple-element.25), calls=%async_computation | async-start | bytes 262144 | tf_op jit(solution)/shard_map/all_to_all | solution.py:384
  12.3 0.0 copy-start
  12.3 0.0 collective-permute-done.halo
  12.3 0.0 copy-done.1
  12.3 0.0 copy-done.2
  12.3 1.1 %shard_map.68.pack.refs_0_ = bf16[16,64,128]{2,1,0:T(8,128)(2,1)S(1)} custom-call(bf16[4,64,1024]{2,1,0:T(8,128)(2,1)S(1)} %bitcast.6, bf16[1,64,1024]{2,1,0:T(8,128)(2,1)S(1)} %collective-permute-done.halo, bf16[864,128]{1,0:T(8,128)(2,1)S(1)} %copy-done.2), custom_call_target="tpu_custom_call" | custom-call | flops 1000000000 | bytes 876544 | tf_op jit(solution)/shard_map/pallas_call | solution.py:334
  13.4 0.0 copy-start.3
  13.4 0.6 %copy-done.3 = bf16[1,64,1024]{2,1,0:T(8,128)(2,1)} copy-done((bf16[1,64,1024]{2,1,0:T(8,128)(2,1)}, bf16[1,64,1024]{2,1,0:T(8,128)(2,1)S(1)}, u32[]{:S(2)}) %copy-start.3) | copy-done | bytes 131096
  14.0 1.5 %collective-permute-start.2 = (bf16[16,64,128]{2,1,0:T(8,128)(2,1)S(1)}, bf16[16,64,128]{2,1,0:T(8,128)(2,1)S(1)}, u32[]{:S(2)}, u32[]{:S(2)}) collective-permute-start(bf16[16,64,128]{2,1,0:T(8,128)(2,1)S(1)} %shard_map.68.pack.refs_0_), channel_id=1, source_target_pairs={{0,16},{8,24},{16,0},{24,8},{1,17},{9,25},{17,1},{25,9},{2,18},{10... | collective-permute-start | bytes 786440 | tf_op jit(solution)/shard_map/ppermute | solution.py:350
  15.5 0.0 collective-permute-start.1
  15.5 0.0 copy-done
  15.6 1.6 %shard_map.71 = bf16[8,64,128]{2,1,0:T(8,128)(2,1)} custom-call(bf16[16,64,128]{2,1,0:T(8,128)(2,1)S(1)} %shard_map.68.pack.refs_0_, bf16[3456,256]{1,0:T(8,128)(2,1)S(1)} %copy-done), custom_call_target="tpu_custom_call" | custom-call | flops 1000000000 | bytes 2031616 | tf_op jit(solution)/shard_map/pallas_call | solution.py:334
  17.2 2.4 %all-to-all-done.cot = bf16[8,64,128]{2,1,0:T(8,128)(2,1)S(1)} async-done(((bf16[8,64,128]{2,1,0:T(8,128)(2,1)}), bf16[8,64,128]{2,1,0:T(8,128)(2,1)S(1)}, u32[]{:S(2)}, u32[]{:S(2)}) %all-to-all-start) | async-done | bytes 131104 | tf_op jit(solution)/shard_map/all_to_all | solution.py:384
  19.6 0.0 copy-start.4
  19.6 0.1 collective-permute-start.3
  19.7 1.6 %collective-permute-start.4 = (bf16[8,16,128]{2,1,0:T(8,128)(2,1)S(1)}, bf16[8,16,128]{2,1,0:T(8,128)(2,1)S(1)}, u32[]{:S(2)}, u32[]{:S(2)}) collective-permute-start(bf16[8,16,128]{2,1,0:T(8,128)(2,1)S(1)} %get-tuple-element.29), channel_id=1, source_target_pairs={{0,16},{8,24},{16,0},{24,8},{1,17},{9,25},{17,1},{25,9},{2,18},{10... | collective-permute-start | bytes 98312 | tf_op jit(solution)/shard_map/ppermute | solution.py:350
  21.3 0.3 collective-permute-start.5
  21.6 0.0 copy-done.4
  21.6 3.1 %shard_map.69 = (bf16[64,864]{1,0:T(8,128)(2,1)S(1)}, bf16[64,864]{1,0:T(8,128)(2,1)S(1)}) custom-call(s32[1]{0:T(128)} %bitcast._.place, s32[1]{0:T(128)} %bitcast.2.__.slot, bf16[4,64,1024]{2,1,0:T(8,128)(2,1)S(1)} %bitcast.7, bf16[1,64,1024]{2,1,0:T(8,128)(2,1)S(1)} %copy-done.4, bf16[864,128]{1,0:T(8,128)(2,1)S(1)} %copy-done.2, ...), custom_call_target="tpu_custom_call" | custom-call | flops 1000000000 | bytes 2777096 | tf_op jit(solution)/shard_map/pallas_call | solution.py:334
  24.7 0.0 collective-permute-done.3.refs_1_
  24.7 0.0 collective-permute-done.4.refs_2_
  24.7 0.0 collective-permute-done.5.refs_3_
  24.8 0.0 collective-permute-done.2.refs_2_
  24.8 0.4 collective-permute-start.6
  25.2 0.2 collective-permute-start.7
  25.3 0.3 shard_map.72.refs_4_
  25.7 0.9 %collective-permute-done.7.refs_6_ = bf16[64,864]{1,0:T(8,128)(2,1)S(1)} collective-permute-done((bf16[64,864]{1,0:T(8,128)(2,1)S(1)}, bf16[64,864]{1,0:T(8,128)(2,1)S(1)}, u32[]{:S(2)}, u32[]{:S(2)}) %collective-permute-start.7) | collective-permute-done | bytes 110624 | tf_op jit(solution)/shard_map/ppermute | solution.py:350
  26.5 0.0 collective-permute-done.1.refs_1_
  26.5 0.0 collective-permute-done.6.refs_3_
  26.5 0.5 shard_map.73
  27.0 0.3 collective-permute-start.11
  27.3 1.8 %collective-permute-start.8 = (bf16[8,4320]{1,0:T(8,128)(2,1)S(1)}, bf16[8,4320]{1,0:T(8,128)(2,1)S(1)}, u32[]{:S(2)}, u32[]{:S(2)}) collective-permute-start(bf16[8,4320]{1,0:T(8,128)(2,1)S(1)} %get-tuple-element.34), channel_id=1, source_target_pairs={{0,1},{1,0},{2,3},{3,2},{4,5},{5,4},{6,7},{7,6},{8,9},{9,8},{10,11... | collective-permute-start | bytes 207368 | tf_op jit(solution)/shard_map/ppermute | solution.py:350
  29.1 0.0 collective-permute-start.9
  29.1 1.7 %collective-permute-start.10 = (bf16[8,4320]{1,0:T(8,128)(2,1)S(1)}, bf16[8,4320]{1,0:T(8,128)(2,1)S(1)}, u32[]{:S(2)}, u32[]{:S(2)}) collective-permute-start(bf16[8,4320]{1,0:T(8,128)(2,1)S(1)} %get-tuple-element.36), channel_id=1, source_target_pairs={{0,3},{1,2},{2,1},{3,0},{4,7},{5,6},{6,5},{7,4},{8,11},{9,10},{10,... | collective-permute-start | bytes 207368 | tf_op jit(solution)/shard_map/ppermute | solution.py:350
  30.8 4.3 %collective-permute-done.11.lent = bf16[2,8,4320]{2,1,0:T(8,128)(2,1)S(1)} collective-permute-done((bf16[2,8,4320]{2,1,0:T(8,128)(2,1)S(1)}, bf16[2,8,4320]{2,1,0:T(8,128)(2,1)S(1)}, u32[]{:S(2)}, u32[]{:S(2)}) %collective-permute-start.11) | collective-permute-done | bytes 138272 | tf_op jit(solution)/shard_map/ppermute | solution.py:350
  35.1 0.1 collective-permute-start.12
  35.2 1.1 %collective-permute-start.13 = (bf16[8,4320]{1,0:T(8,128)(2,1)S(1)}, bf16[8,4320]{1,0:T(8,128)(2,1)S(1)}, u32[]{:S(2)}, u32[]{:S(2)}) collective-permute-start(bf16[8,4320]{1,0:T(8,128)(2,1)S(1)} %get-tuple-element.40), channel_id=1, source_target_pairs={{0,6},{1,7},{2,4},{3,5},{4,2},{5,3},{6,0},{7,1},{8,14},{9,15},{10,... | collective-permute-start | bytes 207368 | tf_op jit(solution)/shard_map/ppermute | solution.py:350
  36.3 4.9 %all-to-all-start.1 = ((bf16[8,64,128]{2,1,0:T(8,128)(2,1)}), bf16[8,64,128]{2,1,0:T(8,128)(2,1)S(1)}, u32[]{:S(2)}, u32[]{:S(2)}) async-start(bf16[8,64,128]{2,1,0:T(8,128)(2,1)} %shard_map.71), calls=%async_computation.1 | async-start | bytes 262144 | tf_op jit(solution)/shard_map/all_to_all | solution.py:412
  41.2 0.0 collective-permute-done.8.refs_0_
  41.2 0.0 collective-permute-done.9.refs_1_
  41.2 0.0 collective-permute-done.10.refs_2_
  41.2 0.0 collective-permute-done.12.refs_3_
  41.2 0.3 collective-permute-done.13.refs_4_
  41.5 0.1 shard_map.75.refs_0_
  41.5 0.1 collective-permute-start.16
  41.6 1.7 %collective-permute-start.15 = (bf16[8,4320]{1,0:T(8,128)(2,1)S(1)}, bf16[8,4320]{1,0:T(8,128)(2,1)S(1)}, u32[]{:S(2)}, u32[]{:S(2)}) collective-permute-start(bf16[8,4320]{1,0:T(8,128)(2,1)S(1)} %shard_map.75.refs_0_), channel_id=1, source_target_pairs={{0,16},{8,24},{16,0},{24,8},{1,17},{9,25},{17,1},{25,9},{2,18},{10... | collective-permute-start | bytes 207368 | tf_op jit(solution)/shard_map/ppermute | solution.py:350
  43.3 0.2 collective-permute-start.14
  43.5 2.4 %collective-permute-done.16.refs_3_ = bf16[8,4320]{1,0:T(8,128)(2,1)S(1)} collective-permute-done((bf16[8,4320]{1,0:T(8,128)(2,1)S(1)}, bf16[8,4320]{1,0:T(8,128)(2,1)S(1)}, u32[]{:S(2)}, u32[]{:S(2)}) %collective-permute-start.16) | collective-permute-done | bytes 69152 | tf_op jit(solution)/shard_map/ppermute | solution.py:350
  45.9 1.7 %collective-permute-done.15.refs_2_ = bf16[8,4320]{1,0:T(8,128)(2,1)S(1)} collective-permute-done((bf16[8,4320]{1,0:T(8,128)(2,1)S(1)}, bf16[8,4320]{1,0:T(8,128)(2,1)S(1)}, u32[]{:S(2)}, u32[]{:S(2)}) %collective-permute-start.15) | collective-permute-done | bytes 69152 | tf_op jit(solution)/shard_map/ppermute | solution.py:350
  47.6 0.0 collective-permute-done.14.refs_1_
  47.6 0.9 %all-to-all-done.1.refs_4_ = bf16[8,64,128]{2,1,0:T(8,128)(2,1)S(1)} async-done(((bf16[8,64,128]{2,1,0:T(8,128)(2,1)}), bf16[8,64,128]{2,1,0:T(8,128)(2,1)S(1)}, u32[]{:S(2)}, u32[]{:S(2)}) %all-to-all-start.1) | async-done | bytes 131104 | tf_op jit(solution)/shard_map/all_to_all | solution.py:412
  48.5 0.9 %shard_map.76 = (f32[16,864]{1,0:T(8,128)}, f32[32,3456]{1,0:T(8,128)}, bf16[32,8,128]{2,1,0:T(8,128)(2,1)}) custom-call(s32[1]{0:T(128)} %bitcast._.place, bf16[8,4320]{1,0:T(8,128)(2,1)S(1)} %shard_map.75.refs_0_, bf16[8,4320]{1,0:T(8,128)(2,1)S(1)} %collective-permute-done.14.refs_1_, bf16[8,4320]{1,0:T(8,128)(2,1)S(1)} %collective-permute-done.15.refs_2_, ...), custom_call_target="tpu_custom_call" | custom-call | flops 1000000000 | bytes 407556 | tf_op jit(solution)/shard_map/pallas_call | solution.py:334
  (2 shorter events, 0.1 us)
Async XLA Ops:
  0.6 11.6 %copy-start.1 = (bf16[1,4,64,1024]{3,2,1,0:T(8,128)(2,1)S(1)}, bf16[1,4,64,1024]{3,2,1,0:T(8,128)(2,1)}, u32[]{:S(2)}) copy-start(bf16[1,4,64,1024]{3,2,1,0:T(8,128)(2,1)} %param.4) | copy-start | bytes 1572868
  0.6 11.6 %copy-start.2 = (bf16[864,128]{1,0:T(8,128)(2,1)S(1)}, bf16[864,128]{1,0:T(8,128)(2,1)}, u32[]{:S(2)}) copy-start(bf16[864,128]{1,0:T(8,128)(2,1)} %w1.3) | copy-start | bytes 663556
  2.5 9.8 %collective-permute-start = (bf16[1,64,1024]{2,1,0:T(8,128)(2,1)}, bf16[1,64,1024]{2,1,0:T(8,128)(2,1)S(1)}, u32[]{:S(2)}, u32[]{:S(2)}) collective-permute-start(bf16[1,64,1024]{2,1,0:T(8,128)(2,1)} %get-tuple-element.24), channel_id=1, source_target_pairs={{0,1},{1,2},{2,3},{3,4},{4,5},{5,6},{6,7},{8,9},{9,10},{10,11},{11... | collective-permute-start | bytes 393224 | tf_op jit(solution)/shard_map/ppermute | solution.py:358
  7.4 12.2 %all-to-all-start = ((bf16[8,64,128]{2,1,0:T(8,128)(2,1)}), bf16[8,64,128]{2,1,0:T(8,128)(2,1)S(1)}, u32[]{:S(2)}, u32[]{:S(2)}) async-start(bf16[8,64,128]{2,1,0:T(8,128)(2,1)} %get-tuple-element.25), calls=%async_computation | async-start | bytes 262144 | tf_op jit(solution)/shard_map/all_to_all | solution.py:384
  12.3 3.3 %copy-start = (bf16[3456,256]{1,0:T(8,128)(2,1)S(1)}, bf16[3456,256]{1,0:T(8,128)(2,1)}, u32[]{:S(2)}) copy-start(bf16[3456,256]{1,0:T(8,128)(2,1)} %w2.3) | copy-start | bytes 5308420
  13.4 0.7 %copy-start.3 = (bf16[1,64,1024]{2,1,0:T(8,128)(2,1)}, bf16[1,64,1024]{2,1,0:T(8,128)(2,1)S(1)}, u32[]{:S(2)}) copy-start(bf16[1,64,1024]{2,1,0:T(8,128)(2,1)S(1)} %collective-permute-done.halo) | copy-start | bytes 393220
  14.0 10.7 %collective-permute-start.2 = (bf16[16,64,128]{2,1,0:T(8,128)(2,1)S(1)}, bf16[16,64,128]{2,1,0:T(8,128)(2,1)S(1)}, u32[]{:S(2)}, u32[]{:S(2)}) collective-permute-start(bf16[16,64,128]{2,1,0:T(8,128)(2,1)S(1)} %shard_map.68.pack.refs_0_), channel_id=1, source_target_pairs={{0,16},{8,24},{16,0},{24,8},{1,17},{9,25},{17,1},{25,9},{2,18},{10... | collective-permute-start | bytes 786440 | tf_op jit(solution)/shard_map/ppermute | solution.py:350
  15.5 11.0 %collective-permute-start.1 = (bf16[16,64,128]{2,1,0:T(8,128)(2,1)S(1)}, bf16[16,64,128]{2,1,0:T(8,128)(2,1)S(1)}, u32[]{:S(2)}, u32[]{:S(2)}) collective-permute-start(bf16[16,64,128]{2,1,0:T(8,128)(2,1)S(1)} %shard_map.68.pack.refs_0_), channel_id=1, source_target_pairs={{0,8},{8,0},{16,24},{24,16},{1,9},{9,1},{17,25},{25,17},{2,10},{10... | collective-permute-start | bytes 786440 | tf_op jit(solution)/shard_map/ppermute | solution.py:350
  19.6 2.0 %copy-start.4 = (bf16[1,64,1024]{2,1,0:T(8,128)(2,1)S(1)}, bf16[1,64,1024]{2,1,0:T(8,128)(2,1)}, u32[]{:S(2)}) copy-start(bf16[1,64,1024]{2,1,0:T(8,128)(2,1)} %copy-done.3) | copy-start | bytes 393220
  19.6 5.1 %collective-permute-start.3 = (bf16[8,16,128]{2,1,0:T(8,128)(2,1)S(1)}, bf16[8,16,128]{2,1,0:T(8,128)(2,1)S(1)}, u32[]{:S(2)}, u32[]{:S(2)}) collective-permute-start(bf16[8,16,128]{2,1,0:T(8,128)(2,1)S(1)} %get-tuple-element.28), channel_id=1, source_target_pairs={{0,8},{8,0},{16,24},{24,16},{1,9},{9,1},{17,25},{25,17},{2,10},{10... | collective-permute-start | bytes 98312 | tf_op jit(solution)/shard_map/ppermute | solution.py:350
  19.7 5.0 %collective-permute-start.4 = (bf16[8,16,128]{2,1,0:T(8,128)(2,1)S(1)}, bf16[8,16,128]{2,1,0:T(8,128)(2,1)S(1)}, u32[]{:S(2)}, u32[]{:S(2)}) collective-permute-start(bf16[8,16,128]{2,1,0:T(8,128)(2,1)S(1)} %get-tuple-element.29), channel_id=1, source_target_pairs={{0,16},{8,24},{16,0},{24,8},{1,17},{9,25},{17,1},{25,9},{2,18},{10... | collective-permute-start | bytes 98312 | tf_op jit(solution)/shard_map/ppermute | solution.py:350
  21.3 3.4 %collective-permute-start.5 = (bf16[8,16,128]{2,1,0:T(8,128)(2,1)S(1)}, bf16[8,16,128]{2,1,0:T(8,128)(2,1)S(1)}, u32[]{:S(2)}, u32[]{:S(2)}) collective-permute-start(bf16[8,16,128]{2,1,0:T(8,128)(2,1)S(1)} %get-tuple-element.30), channel_id=1, source_target_pairs={{0,24},{8,16},{16,8},{24,0},{1,25},{9,17},{17,9},{25,1},{2,26},{10... | collective-permute-start | bytes 98312 | tf_op jit(solution)/shard_map/ppermute | solution.py:350
  24.8 1.8 %collective-permute-start.6 = (bf16[16,64,128]{2,1,0:T(8,128)(2,1)S(1)}, bf16[16,64,128]{2,1,0:T(8,128)(2,1)S(1)}, u32[]{:S(2)}, u32[]{:S(2)}) collective-permute-start(bf16[16,64,128]{2,1,0:T(8,128)(2,1)S(1)} %collective-permute-done.2.refs_2_), channel_id=1, source_target_pairs={{0,8},{8,0},{16,24},{24,16},{1,9},{9,1},{17,25},{25,17},{2,10},{10... | collective-permute-start | bytes 786440 | tf_op jit(solution)/shard_map/ppermute | solution.py:350
  25.2 1.4 %collective-permute-start.7 = (bf16[64,864]{1,0:T(8,128)(2,1)S(1)}, bf16[64,864]{1,0:T(8,128)(2,1)S(1)}, u32[]{:S(2)}, u32[]{:S(2)}) collective-permute-start(bf16[64,864]{1,0:T(8,128)(2,1)S(1)} %get-tuple-element.27), channel_id=1, source_target_pairs={{0,8},{8,0},{16,24},{24,16},{1,9},{9,1},{17,25},{25,17},{2,10},{10... | collective-permute-start | bytes 331784 | tf_op jit(solution)/shard_map/ppermute | solution.py:350
  27.0 8.0 %collective-permute-start.11 = (bf16[2,8,4320]{2,1,0:T(8,128)(2,1)S(1)}, bf16[2,8,4320]{2,1,0:T(8,128)(2,1)S(1)}, u32[]{:S(2)}, u32[]{:S(2)}) collective-permute-start(bf16[2,8,4320]{2,1,0:T(8,128)(2,1)S(1)} %get-tuple-element.37), channel_id=1, source_target_pairs={{0,1},{1,0},{2,3},{3,2},{4,5},{5,4},{6,7},{7,6},{8,9},{9,8},{10,11... | collective-permute-start | bytes 414728 | tf_op jit(solution)/shard_map/ppermute | solution.py:350
  27.3 13.9 %collective-permute-start.8 = (bf16[8,4320]{1,0:T(8,128)(2,1)S(1)}, bf16[8,4320]{1,0:T(8,128)(2,1)S(1)}, u32[]{:S(2)}, u32[]{:S(2)}) collective-permute-start(bf16[8,4320]{1,0:T(8,128)(2,1)S(1)} %get-tuple-element.34), channel_id=1, source_target_pairs={{0,1},{1,0},{2,3},{3,2},{4,5},{5,4},{6,7},{7,6},{8,9},{9,8},{10,11... | collective-permute-start | bytes 207368 | tf_op jit(solution)/shard_map/ppermute | solution.py:350
  29.1 12.1 %collective-permute-start.9 = (bf16[8,4320]{1,0:T(8,128)(2,1)S(1)}, bf16[8,4320]{1,0:T(8,128)(2,1)S(1)}, u32[]{:S(2)}, u32[]{:S(2)}) collective-permute-start(bf16[8,4320]{1,0:T(8,128)(2,1)S(1)} %get-tuple-element.35), channel_id=1, source_target_pairs={{0,2},{1,3},{2,0},{3,1},{4,6},{5,7},{6,4},{7,5},{8,10},{9,11},{10,... | collective-permute-start | bytes 207368 | tf_op jit(solution)/shard_map/ppermute | solution.py:350
  29.1 12.1 %collective-permute-start.10 = (bf16[8,4320]{1,0:T(8,128)(2,1)S(1)}, bf16[8,4320]{1,0:T(8,128)(2,1)S(1)}, u32[]{:S(2)}, u32[]{:S(2)}) collective-permute-start(bf16[8,4320]{1,0:T(8,128)(2,1)S(1)} %get-tuple-element.36), channel_id=1, source_target_pairs={{0,3},{1,2},{2,1},{3,0},{4,7},{5,6},{6,5},{7,4},{8,11},{9,10},{10,... | collective-permute-start | bytes 207368 | tf_op jit(solution)/shard_map/ppermute | solution.py:350
  35.1 6.1 %collective-permute-start.12 = (bf16[8,4320]{1,0:T(8,128)(2,1)S(1)}, bf16[8,4320]{1,0:T(8,128)(2,1)S(1)}, u32[]{:S(2)}, u32[]{:S(2)}) collective-permute-start(bf16[8,4320]{1,0:T(8,128)(2,1)S(1)} %get-tuple-element.39), channel_id=1, source_target_pairs={{0,4},{1,5},{2,6},{3,7},{4,0},{5,1},{6,2},{7,3},{8,12},{9,13},{10,... | collective-permute-start | bytes 207368 | tf_op jit(solution)/shard_map/ppermute | solution.py:350
  35.2 6.3 %collective-permute-start.13 = (bf16[8,4320]{1,0:T(8,128)(2,1)S(1)}, bf16[8,4320]{1,0:T(8,128)(2,1)S(1)}, u32[]{:S(2)}, u32[]{:S(2)}) collective-permute-start(bf16[8,4320]{1,0:T(8,128)(2,1)S(1)} %get-tuple-element.40), channel_id=1, source_target_pairs={{0,6},{1,7},{2,4},{3,5},{4,2},{5,3},{6,0},{7,1},{8,14},{9,15},{10,... | collective-permute-start | bytes 207368 | tf_op jit(solution)/shard_map/ppermute | solution.py:350
  36.3 12.2 %all-to-all-start.1 = ((bf16[8,64,128]{2,1,0:T(8,128)(2,1)}), bf16[8,64,128]{2,1,0:T(8,128)(2,1)S(1)}, u32[]{:S(2)}, u32[]{:S(2)}) async-start(bf16[8,64,128]{2,1,0:T(8,128)(2,1)} %shard_map.71), calls=%async_computation.1 | async-start | bytes 262144 | tf_op jit(solution)/shard_map/all_to_all | solution.py:412
  41.5 4.4 %collective-permute-start.16 = (bf16[8,4320]{1,0:T(8,128)(2,1)S(1)}, bf16[8,4320]{1,0:T(8,128)(2,1)S(1)}, u32[]{:S(2)}, u32[]{:S(2)}) collective-permute-start(bf16[8,4320]{1,0:T(8,128)(2,1)S(1)} %shard_map.75.refs_0_), channel_id=1, source_target_pairs={{0,24},{8,16},{16,8},{24,0},{1,25},{9,17},{17,9},{25,1},{2,26},{10... | collective-permute-start | bytes 207368 | tf_op jit(solution)/shard_map/ppermute | solution.py:350
  41.6 6.0 %collective-permute-start.15 = (bf16[8,4320]{1,0:T(8,128)(2,1)S(1)}, bf16[8,4320]{1,0:T(8,128)(2,1)S(1)}, u32[]{:S(2)}, u32[]{:S(2)}) collective-permute-start(bf16[8,4320]{1,0:T(8,128)(2,1)S(1)} %shard_map.75.refs_0_), channel_id=1, source_target_pairs={{0,16},{8,24},{16,0},{24,8},{1,17},{9,25},{17,1},{25,9},{2,18},{10... | collective-permute-start | bytes 207368 | tf_op jit(solution)/shard_map/ppermute | solution.py:350
  43.3 4.3 %collective-permute-start.14 = (bf16[8,4320]{1,0:T(8,128)(2,1)S(1)}, bf16[8,4320]{1,0:T(8,128)(2,1)S(1)}, u32[]{:S(2)}, u32[]{:S(2)}) collective-permute-start(bf16[8,4320]{1,0:T(8,128)(2,1)S(1)} %shard_map.75.refs_0_), channel_id=1, source_target_pairs={{0,8},{8,0},{16,24},{24,16},{1,9},{9,1},{17,25},{25,17},{2,10},{10... | collective-permute-start | bytes 207368 | tf_op jit(solution)/shard_map/ppermute | solution.py:350

commit v7 on v6

--- a/solution.py
+++ b/solution.py
@@ -426,7 +426,7 @@
         return call(join, latent_shape, exchanged(latent_of(pack)))[None], one, two
 
     across = swap_ranks(pack, "dp", 2)
-    beside = swap_ranks(pack, "dp", 1)
+    beside = swap_ranks(first_of(pack, cot), "dp", 1)
     own, *cots = call(
         kernel_pieces,
         (shape((slabs, 2 * rows_per, CELLS), BF16),) * pieces,

time: 49.8 us -> 49.4 us (level)
  local copies, waits for them, and re-layouts: 0.66 us -> 0.01 us
  waiting for transfers between devices: 12.9 us -> 13.5 us
    ppermute x16, waiting for transfers between devices: 9.54 us -> 10.4 us  [swap_ranks(): lax.ppermute(block, axis, [(i, i ^ k) for i in range(lax.axis_size(axis))])]
    all_to_all x1, waiting for transfers between devices: 0.95 us -> 0.11 us  [exchanged(): lax.all_to_all(parts, 'space', split_axis=0, concat_axis=0, tiled=True)]
    unnamed x10 -> x6, local copies, waits for them, and re-layouts: 0.66 us -> 0.01 us
    all_to_all x1, waiting for transfers between devices: 2.44 us -> 3 us  [on_device(): lax.all_to_all(parcels, 'space', split_axis=0, concat_axis=0, tiled=True)]
where the time goes in v7:
time: 49.4 us; the launch traced here: 49 us
  starting transfers between devices  25.1 us (51%)
  waiting for transfers between devices  13.5 us (27%)
  Pallas kernels  9.57 us (19%)
  between operations  0.82 us (2%)
    ppermute x16, starting transfers between devices, swap_ranks(): lax.ppermute(block, axis, [(i, i ^ k) for i in range(lax.axis_size(axis))])  11 us
    ppermute x16, waiting for transfers between devices, swap_ranks(): lax.ppermute(block, axis, [(i, i ^ k) for i in range(lax.axis_size(axis))])  10.4 us
    pallas_call x10, Pallas kernels, call(): pl.pallas_call(kernel, out_shape=out_shape, in_specs=[spec(n, spaces) for...  9.57 us
    all_to_all x1, starting transfers between devices, on_device(): lax.all_to_all(parcels, 'space', split_axis=0, concat_axis=0, tiled=True)  4.89 us
    ppermute x1, starting transfers between devices, from_below(): lax.ppermute(block, axis, [(i - 1, i) for i in range(1, lax.axis_size(axi...  4.85 us
    all_to_all x1, starting transfers between devices, exchanged(): lax.all_to_all(parts, 'space', split_axis=0, concat_axis=0, tiled=True)  4.39 us
    all_to_all x1, waiting for transfers between devices, on_device(): lax.all_to_all(parcels, 'space', split_axis=0, concat_axis=0, tiled=True)  3 us
  transfers between devices with their start and end apart: 19, of which 7 were waited for; matrix products, arithmetic and copies ran while one was open for 0% of the time, Pallas kernels for 13%

profile of v7, /device:TPU:0, one launch (start us, length us, event | category | flops | bytes accessed | tf_op | source)
XLA Modules:
  0.0 49.0 jit_solution(3978594228836998330)
XLA Ops:
  0.6 0.0 copy-start.1
  0.6 0.0 copy-start.2
  0.7 1.9 %shard_map.67 = (bf16[8,64,128]{2,1,0:T(8,128)(2,1)}, bf16[1,64,1024]{2,1,0:T(8,128)(2,1)}) custom-call(s32[1]{0:T(128)} %bitcast._.place, s32[1]{0:T(128)} %bitcast.2.__.slot, bf16[32,8,128]{2,1,0:T(8,128)(2,1)} %bitcast.8, bf16[4,64,1024]{2,1,0:T(8,128)(2,1)} %bitcast.5), custom_call_target="tpu_custom_call" | custom-call | flops 1000000000 | bytes 589832 | tf_op jit(solution)/shard_map/pallas_call | solution.py:334
  2.5 4.8 %collective-permute-start = (bf16[1,64,1024]{2,1,0:T(8,128)(2,1)}, bf16[1,64,1024]{2,1,0:T(8,128)(2,1)S(1)}, u32[]{:S(2)}, u32[]{:S(2)}) collective-permute-start(bf16[1,64,1024]{2,1,0:T(8,128)(2,1)} %get-tuple-element.25), channel_id=1, source_target_pairs={{0,1},{1,2},{2,3},{3,4},{4,5},{5,6},{6,7},{8,9},{9,10},{10,11},{11... | collective-permute-start | bytes 393224 | tf_op jit(solution)/shard_map/ppermute | solution.py:358
  7.4 4.9 %all-to-all-start = ((bf16[8,64,128]{2,1,0:T(8,128)(2,1)}), bf16[8,64,128]{2,1,0:T(8,128)(2,1)S(1)}, u32[]{:S(2)}, u32[]{:S(2)}) async-start(bf16[8,64,128]{2,1,0:T(8,128)(2,1)} %get-tuple-element.26), calls=%async_computation | async-start | bytes 262144 | tf_op jit(solution)/shard_map/all_to_all | solution.py:384
  12.3 0.0 copy-start
  12.3 0.0 collective-permute-done.halo
  12.3 0.0 copy-done.1
  12.3 0.0 copy-done.2
  12.3 1.1 %shard_map.68.pack.refs_0_ = bf16[16,64,128]{2,1,0:T(8,128)(2,1)S(1)} custom-call(bf16[4,64,1024]{2,1,0:T(8,128)(2,1)S(1)} %bitcast.6, bf16[1,64,1024]{2,1,0:T(8,128)(2,1)S(1)} %collective-permute-done.halo, bf16[864,128]{1,0:T(8,128)(2,1)S(1)} %copy-done.2), custom_call_target="tpu_custom_call" | custom-call | flops 1000000000 | bytes 876544 | tf_op jit(solution)/shard_map/pallas_call | solution.py:334
  13.4 1.6 %collective-permute-start.2 = (bf16[16,64,128]{2,1,0:T(8,128)(2,1)S(1)}, bf16[16,64,128]{2,1,0:T(8,128)(2,1)S(1)}, u32[]{:S(2)}, u32[]{:S(2)}) collective-permute-start(bf16[16,64,128]{2,1,0:T(8,128)(2,1)S(1)} %shard_map.68.pack.refs_0_), channel_id=1, source_target_pairs={{0,16},{8,24},{16,0},{24,8},{1,17},{9,25},{17,1},{25,9},{2,18},{10... | collective-permute-start | bytes 786440 | tf_op jit(solution)/shard_map/ppermute | solution.py:350
  15.0 0.0 copy-done
  15.0 1.7 %shard_map.71 = bf16[8,64,128]{2,1,0:T(8,128)(2,1)} custom-call(bf16[16,64,128]{2,1,0:T(8,128)(2,1)S(1)} %shard_map.68.pack.refs_0_, bf16[3456,256]{1,0:T(8,128)(2,1)S(1)} %copy-done), custom_call_target="tpu_custom_call" | custom-call | flops 1000000000 | bytes 2031616 | tf_op jit(solution)/shard_map/pallas_call | solution.py:334
  16.6 3.0 %all-to-all-done.cot = bf16[8,64,128]{2,1,0:T(8,128)(2,1)S(1)} async-done(((bf16[8,64,128]{2,1,0:T(8,128)(2,1)}), bf16[8,64,128]{2,1,0:T(8,128)(2,1)S(1)}, u32[]{:S(2)}, u32[]{:S(2)}) %all-to-all-start) | async-done | bytes 131104 | tf_op jit(solution)/shard_map/all_to_all | solution.py:384
  19.6 0.1 collective-permute-start.3
  19.7 1.6 %collective-permute-start.4 = (bf16[8,16,128]{2,1,0:T(8,128)(2,1)S(1)}, bf16[8,16,128]{2,1,0:T(8,128)(2,1)S(1)}, u32[]{:S(2)}, u32[]{:S(2)}) collective-permute-start(bf16[8,16,128]{2,1,0:T(8,128)(2,1)S(1)} %get-tuple-element.31), channel_id=1, source_target_pairs={{0,16},{8,24},{16,0},{24,8},{1,17},{9,25},{17,1},{25,9},{2,18},{10... | collective-permute-start | bytes 98312 | tf_op jit(solution)/shard_map/ppermute | solution.py:350
  21.3 0.3 collective-permute-start.5
  21.6 0.3 collective-permute-start.1
  21.9 3.2 %shard_map.69 = (bf16[64,864]{1,0:T(8,128)(2,1)S(1)}, bf16[64,864]{1,0:T(8,128)(2,1)S(1)}) custom-call(s32[1]{0:T(128)} %bitcast._.place, s32[1]{0:T(128)} %bitcast.2.__.slot, bf16[4,64,1024]{2,1,0:T(8,128)(2,1)S(1)} %bitcast.7, bf16[1,64,1024]{2,1,0:T(8,128)(2,1)S(1)} %collective-permute-done.halo, bf16[864,128]{1,0:T(8,128)(2,1)S(1)} %copy-done.2, ...), custom_call_target="tpu_custom_call" | custom-call | flops 1000000000 | bytes 2777096 | tf_op jit(solution)/shard_map/pallas_call | solution.py:334
  25.1 0.0 collective-permute-done.3.refs_1_
  25.1 0.0 collective-permute-done.4.refs_2_
  25.1 0.0 collective-permute-done.5.refs_3_
  25.1 0.0 collective-permute-done.2.refs_2_
  25.1 0.2 collective-permute-start.6
  25.4 0.3 collective-permute-start.7
  25.7 0.3 shard_map.72.refs_4_
  26.0 0.9 %collective-permute-done.7.refs_6_ = bf16[64,864]{1,0:T(8,128)(2,1)S(1)} collective-permute-done((bf16[64,864]{1,0:T(8,128)(2,1)S(1)}, bf16[64,864]{1,0:T(8,128)(2,1)S(1)}, u32[]{:S(2)}, u32[]{:S(2)}) %collective-permute-start.7) | collective-permute-done | bytes 110624 | tf_op jit(solution)/shard_map/ppermute | solution.py:350
  26.9 0.0 collective-permute-done.1.refs_1_
  26.9 0.0 collective-permute-done.6.refs_3_
  26.9 0.5 %shard_map.73 = (f32[8,4320]{1,0:T(8,128)S(1)}, bf16[8,4320]{1,0:T(8,128)(2,1)S(1)}, bf16[8,4320]{1,0:T(8,128)(2,1)S(1)}, bf16[8,4320]{1,0:T(8,128)(2,1)S(1)}, b...) custom-call(bf16[16,64,128]{2,1,0:T(8,128)(2,1)S(1)} %shard_map.68.pack.refs_0_, ...), custom_call_target="tpu_custom_call" | custom-call | flops 1000000000 | bytes 1794048 | tf_op jit(solution)/shard_map/pallas_call | solution.py:334
  27.4 0.3 collective-permute-start.11
  27.7 1.8 %collective-permute-start.8 = (bf16[8,4320]{1,0:T(8,128)(2,1)S(1)}, bf16[8,4320]{1,0:T(8,128)(2,1)S(1)}, u32[]{:S(2)}, u32[]{:S(2)}) collective-permute-start(bf16[8,4320]{1,0:T(8,128)(2,1)S(1)} %get-tuple-element.36), channel_id=1, source_target_pairs={{0,1},{1,0},{2,3},{3,2},{4,5},{5,4},{6,7},{7,6},{8,9},{9,8},{10,11... | collective-permute-start | bytes 207368 | tf_op jit(solution)/shard_map/ppermute | solution.py:350
  29.5 0.0 collective-permute-start.9
  29.5 1.7 %collective-permute-start.10 = (bf16[8,4320]{1,0:T(8,128)(2,1)S(1)}, bf16[8,4320]{1,0:T(8,128)(2,1)S(1)}, u32[]{:S(2)}, u32[]{:S(2)}) collective-permute-start(bf16[8,4320]{1,0:T(8,128)(2,1)S(1)} %get-tuple-element.38), channel_id=1, source_target_pairs={{0,3},{1,2},{2,1},{3,0},{4,7},{5,6},{6,5},{7,4},{8,11},{9,10},{10,... | collective-permute-start | bytes 207368 | tf_op jit(solution)/shard_map/ppermute | solution.py:350
  31.2 4.3 %collective-permute-done.11.lent = bf16[2,8,4320]{2,1,0:T(8,128)(2,1)S(1)} collective-permute-done((bf16[2,8,4320]{2,1,0:T(8,128)(2,1)S(1)}, bf16[2,8,4320]{2,1,0:T(8,128)(2,1)S(1)}, u32[]{:S(2)}, u32[]{:S(2)}) %collective-permute-start.11) | collective-permute-done | bytes 138272 | tf_op jit(solution)/shard_map/ppermute | solution.py:350
  35.5 0.1 collective-permute-start.12
  35.6 0.8 %collective-permute-start.13 = (bf16[8,4320]{1,0:T(8,128)(2,1)S(1)}, bf16[8,4320]{1,0:T(8,128)(2,1)S(1)}, u32[]{:S(2)}, u32[]{:S(2)}) collective-permute-start(bf16[8,4320]{1,0:T(8,128)(2,1)S(1)} %get-tuple-element.42), channel_id=1, source_target_pairs={{0,6},{1,7},{2,4},{3,5},{4,2},{5,3},{6,0},{7,1},{8,14},{9,15},{10,... | collective-permute-start | bytes 207368 | tf_op jit(solution)/shard_map/ppermute | solution.py:350
  36.4 4.4 %all-to-all-start.1 = ((bf16[8,64,128]{2,1,0:T(8,128)(2,1)}), bf16[8,64,128]{2,1,0:T(8,128)(2,1)S(1)}, u32[]{:S(2)}, u32[]{:S(2)}) async-start(bf16[8,64,128]{2,1,0:T(8,128)(2,1)} %shard_map.71), calls=%async_computation.1 | async-start | bytes 262144 | tf_op jit(solution)/shard_map/all_to_all | solution.py:412
  40.8 0.0 collective-permute-done.8.refs_0_
  40.8 0.0 collective-permute-done.9.refs_1_
  40.8 0.0 collective-permute-done.10.refs_2_
  40.8 0.0 collective-permute-done.12.refs_3_
  40.8 1.1 %collective-permute-done.13.refs_4_ = bf16[8,4320]{1,0:T(8,128)(2,1)S(1)} collective-permute-done((bf16[8,4320]{1,0:T(8,128)(2,1)S(1)}, bf16[8,4320]{1,0:T(8,128)(2,1)S(1)}, u32[]{:S(2)}, u32[]{:S(2)}) %collective-permute-start.13) | collective-permute-done | bytes 69152 | tf_op jit(solution)/shard_map/ppermute | solution.py:350
  41.9 0.1 shard_map.75.refs_0_
  42.0 0.1 collective-permute-start.16
  42.0 1.6 %collective-permute-start.15 = (bf16[8,4320]{1,0:T(8,128)(2,1)S(1)}, bf16[8,4320]{1,0:T(8,128)(2,1)S(1)}, u32[]{:S(2)}, u32[]{:S(2)}) collective-permute-start(bf16[8,4320]{1,0:T(8,128)(2,1)S(1)} %shard_map.75.refs_0_), channel_id=1, source_target_pairs={{0,16},{8,24},{16,0},{24,8},{1,17},{9,25},{17,1},{25,9},{2,18},{10... | collective-permute-start | bytes 207368 | tf_op jit(solution)/shard_map/ppermute | solution.py:350
  43.6 0.3 collective-permute-start.14
  43.9 2.5 %collective-permute-done.16.refs_3_ = bf16[8,4320]{1,0:T(8,128)(2,1)S(1)} collective-permute-done((bf16[8,4320]{1,0:T(8,128)(2,1)S(1)}, bf16[8,4320]{1,0:T(8,128)(2,1)S(1)}, u32[]{:S(2)}, u32[]{:S(2)}) %collective-permute-start.16) | collective-permute-done | bytes 69152 | tf_op jit(solution)/shard_map/ppermute | solution.py:350
  46.4 1.6 %collective-permute-done.15.refs_2_ = bf16[8,4320]{1,0:T(8,128)(2,1)S(1)} collective-permute-done((bf16[8,4320]{1,0:T(8,128)(2,1)S(1)}, bf16[8,4320]{1,0:T(8,128)(2,1)S(1)}, u32[]{:S(2)}, u32[]{:S(2)}) %collective-permute-start.15) | collective-permute-done | bytes 69152 | tf_op jit(solution)/shard_map/ppermute | solution.py:350
  48.0 0.0 collective-permute-done.14.refs_1_
  48.0 0.1 all-to-all-done.1.refs_4_
  48.1 0.9 %shard_map.76 = (f32[16,864]{1,0:T(8,128)}, f32[32,3456]{1,0:T(8,128)}, bf16[32,8,128]{2,1,0:T(8,128)(2,1)}) custom-call(s32[1]{0:T(128)} %bitcast._.place, bf16[8,4320]{1,0:T(8,128)(2,1)S(1)} %shard_map.75.refs_0_, bf16[8,4320]{1,0:T(8,128)(2,1)S(1)} %collective-permute-done.14.refs_1_, bf16[8,4320]{1,0:T(8,128)(2,1)S(1)} %collective-permute-done.15.refs_2_, ...), custom_call_target="tpu_custom_call" | custom-call | flops 1000000000 | bytes 407556 | tf_op jit(solution)/shard_map/pallas_call | solution.py:334
  (2 shorter events, 0.1 us)
Async XLA Ops:
  0.6 11.6 %copy-start.1 = (bf16[1,4,64,1024]{3,2,1,0:T(8,128)(2,1)S(1)}, bf16[1,4,64,1024]{3,2,1,0:T(8,128)(2,1)}, u32[]{:S(2)}) copy-start(bf16[1,4,64,1024]{3,2,1,0:T(8,128)(2,1)} %param.4) | copy-start | bytes 1572868
  0.6 11.6 %copy-start.2 = (bf16[864,128]{1,0:T(8,128)(2,1)S(1)}, bf16[864,128]{1,0:T(8,128)(2,1)}, u32[]{:S(2)}) copy-start(bf16[864,128]{1,0:T(8,128)(2,1)} %w1.3) | copy-start | bytes 663556
  2.5 9.8 %collective-permute-start = (bf16[1,64,1024]{2,1,0:T(8,128)(2,1)}, bf16[1,64,1024]{2,1,0:T(8,128)(2,1)S(1)}, u32[]{:S(2)}, u32[]{:S(2)}) collective-permute-start(bf16[1,64,1024]{2,1,0:T(8,128)(2,1)} %get-tuple-element.25), channel_id=1, source_target_pairs={{0,1},{1,2},{2,3},{3,4},{4,5},{5,6},{6,7},{8,9},{9,10},{10,11},{11... | collective-permute-start | bytes 393224 | tf_op jit(solution)/shard_map/ppermute | solution.py:358
  7.4 12.2 %all-to-all-start = ((bf16[8,64,128]{2,1,0:T(8,128)(2,1)}), bf16[8,64,128]{2,1,0:T(8,128)(2,1)S(1)}, u32[]{:S(2)}, u32[]{:S(2)}) async-start(bf16[8,64,128]{2,1,0:T(8,128)(2,1)} %get-tuple-element.26), calls=%async_computation | async-start | bytes 262144 | tf_op jit(solution)/shard_map/all_to_all | solution.py:384
  12.3 2.7 %copy-start = (bf16[3456,256]{1,0:T(8,128)(2,1)S(1)}, bf16[3456,256]{1,0:T(8,128)(2,1)}, u32[]{:S(2)}) copy-start(bf16[3456,256]{1,0:T(8,128)(2,1)} %w2.3) | copy-start | bytes 5308420
  13.4 11.8 %collective-permute-start.2 = (bf16[16,64,128]{2,1,0:T(8,128)(2,1)S(1)}, bf16[16,64,128]{2,1,0:T(8,128)(2,1)S(1)}, u32[]{:S(2)}, u32[]{:S(2)}) collective-permute-start(bf16[16,64,128]{2,1,0:T(8,128)(2,1)S(1)} %shard_map.68.pack.refs_0_), channel_id=1, source_target_pairs={{0,16},{8,24},{16,0},{24,8},{1,17},{9,25},{17,1},{25,9},{2,18},{10... | collective-permute-start | bytes 786440 | tf_op jit(solution)/shard_map/ppermute | solution.py:350
  19.6 5.5 %collective-permute-start.3 = (bf16[8,16,128]{2,1,0:T(8,128)(2,1)S(1)}, bf16[8,16,128]{2,1,0:T(8,128)(2,1)S(1)}, u32[]{:S(2)}, u32[]{:S(2)}) collective-permute-start(bf16[8,16,128]{2,1,0:T(8,128)(2,1)S(1)} %get-tuple-element.30), channel_id=1, source_target_pairs={{0,8},{8,0},{16,24},{24,16},{1,9},{9,1},{17,25},{25,17},{2,10},{10... | collective-permute-start | bytes 98312 | tf_op jit(solution)/shard_map/ppermute | solution.py:350
  19.7 5.4 %collective-permute-start.4 = (bf16[8,16,128]{2,1,0:T(8,128)(2,1)S(1)}, bf16[8,16,128]{2,1,0:T(8,128)(2,1)S(1)}, u32[]{:S(2)}, u32[]{:S(2)}) collective-permute-start(bf16[8,16,128]{2,1,0:T(8,128)(2,1)S(1)} %get-tuple-element.31), channel_id=1, source_target_pairs={{0,16},{8,24},{16,0},{24,8},{1,17},{9,25},{17,1},{25,9},{2,18},{10... | collective-permute-start | bytes 98312 | tf_op jit(solution)/shard_map/ppermute | solution.py:350
  21.3 3.8 %collective-permute-start.5 = (bf16[8,16,128]{2,1,0:T(8,128)(2,1)S(1)}, bf16[8,16,128]{2,1,0:T(8,128)(2,1)S(1)}, u32[]{:S(2)}, u32[]{:S(2)}) collective-permute-start(bf16[8,16,128]{2,1,0:T(8,128)(2,1)S(1)} %get-tuple-element.32), channel_id=1, source_target_pairs={{0,24},{8,16},{16,8},{24,0},{1,25},{9,17},{17,9},{25,1},{2,26},{10... | collective-permute-start | bytes 98312 | tf_op jit(solution)/shard_map/ppermute | solution.py:350
  21.6 5.3 %collective-permute-start.1 = (bf16[16,64,128]{2,1,0:T(8,128)(2,1)S(1)}, bf16[16,64,128]{2,1,0:T(8,128)(2,1)S(1)}, u32[]{:S(2)}, u32[]{:S(2)}) collective-permute-start(bf16[16,64,128]{2,1,0:T(8,128)(2,1)S(1)} %shard_map.68.pack.refs_0_), channel_id=1, source_target_pairs={{0,8},{8,0},{16,24},{24,16},{1,9},{9,1},{17,25},{25,17},{2,10},{10... | collective-permute-start | bytes 786440 | tf_op jit(solution)/shard_map/ppermute | solution.py:350
  25.1 1.8 %collective-permute-start.6 = (bf16[16,64,128]{2,1,0:T(8,128)(2,1)S(1)}, bf16[16,64,128]{2,1,0:T(8,128)(2,1)S(1)}, u32[]{:S(2)}, u32[]{:S(2)}) collective-permute-start(bf16[16,64,128]{2,1,0:T(8,128)(2,1)S(1)} %collective-permute-done.2.refs_2_), channel_id=1, source_target_pairs={{0,8},{8,0},{16,24},{24,16},{1,9},{9,1},{17,25},{25,17},{2,10},{10... | collective-permute-start | bytes 786440 | tf_op jit(solution)/shard_map/ppermute | solution.py:350
  25.4 1.5 %collective-permute-start.7 = (bf16[64,864]{1,0:T(8,128)(2,1)S(1)}, bf16[64,864]{1,0:T(8,128)(2,1)S(1)}, u32[]{:S(2)}, u32[]{:S(2)}) collective-permute-start(bf16[64,864]{1,0:T(8,128)(2,1)S(1)} %get-tuple-element.29), channel_id=1, source_target_pairs={{0,8},{8,0},{16,24},{24,16},{1,9},{9,1},{17,25},{25,17},{2,10},{10... | collective-permute-start | bytes 331784 | tf_op jit(solution)/shard_map/ppermute | solution.py:350
  27.4 8.0 %collective-permute-start.11 = (bf16[2,8,4320]{2,1,0:T(8,128)(2,1)S(1)}, bf16[2,8,4320]{2,1,0:T(8,128)(2,1)S(1)}, u32[]{:S(2)}, u32[]{:S(2)}) collective-permute-start(bf16[2,8,4320]{2,1,0:T(8,128)(2,1)S(1)} %get-tuple-element.39), channel_id=1, source_target_pairs={{0,1},{1,0},{2,3},{3,2},{4,5},{5,4},{6,7},{7,6},{8,9},{9,8},{10,11... | collective-permute-start | bytes 414728 | tf_op jit(solution)/shard_map/ppermute | solution.py:350
  27.7 13.1 %collective-permute-start.8 = (bf16[8,4320]{1,0:T(8,128)(2,1)S(1)}, bf16[8,4320]{1,0:T(8,128)(2,1)S(1)}, u32[]{:S(2)}, u32[]{:S(2)}) collective-permute-start(bf16[8,4320]{1,0:T(8,128)(2,1)S(1)} %get-tuple-element.36), channel_id=1, source_target_pairs={{0,1},{1,0},{2,3},{3,2},{4,5},{5,4},{6,7},{7,6},{8,9},{9,8},{10,11... | collective-permute-start | bytes 207368 | tf_op jit(solution)/shard_map/ppermute | solution.py:350
  29.5 11.2 %collective-permute-start.9 = (bf16[8,4320]{1,0:T(8,128)(2,1)S(1)}, bf16[8,4320]{1,0:T(8,128)(2,1)S(1)}, u32[]{:S(2)}, u32[]{:S(2)}) collective-permute-start(bf16[8,4320]{1,0:T(8,128)(2,1)S(1)} %get-tuple-element.37), channel_id=1, source_target_pairs={{0,2},{1,3},{2,0},{3,1},{4,6},{5,7},{6,4},{7,5},{8,10},{9,11},{10,... | collective-permute-start | bytes 207368 | tf_op jit(solution)/shard_map/ppermute | solution.py:350
  29.5 11.3 %collective-permute-start.10 = (bf16[8,4320]{1,0:T(8,128)(2,1)S(1)}, bf16[8,4320]{1,0:T(8,128)(2,1)S(1)}, u32[]{:S(2)}, u32[]{:S(2)}) collective-permute-start(bf16[8,4320]{1,0:T(8,128)(2,1)S(1)} %get-tuple-element.38), channel_id=1, source_target_pairs={{0,3},{1,2},{2,1},{3,0},{4,7},{5,6},{6,5},{7,4},{8,11},{9,10},{10,... | collective-permute-start | bytes 207368 | tf_op jit(solution)/shard_map/ppermute | solution.py:350
  35.5 5.3 %collective-permute-start.12 = (bf16[8,4320]{1,0:T(8,128)(2,1)S(1)}, bf16[8,4320]{1,0:T(8,128)(2,1)S(1)}, u32[]{:S(2)}, u32[]{:S(2)}) collective-permute-start(bf16[8,4320]{1,0:T(8,128)(2,1)S(1)} %get-tuple-element.41), channel_id=1, source_target_pairs={{0,4},{1,5},{2,6},{3,7},{4,0},{5,1},{6,2},{7,3},{8,12},{9,13},{10,... | collective-permute-start | bytes 207368 | tf_op jit(solution)/shard_map/ppermute | solution.py:350
  35.6 6.3 %collective-permute-start.13 = (bf16[8,4320]{1,0:T(8,128)(2,1)S(1)}, bf16[8,4320]{1,0:T(8,128)(2,1)S(1)}, u32[]{:S(2)}, u32[]{:S(2)}) collective-permute-start(bf16[8,4320]{1,0:T(8,128)(2,1)S(1)} %get-tuple-element.42), channel_id=1, source_target_pairs={{0,6},{1,7},{2,4},{3,5},{4,2},{5,3},{6,0},{7,1},{8,14},{9,15},{10,... | collective-permute-start | bytes 207368 | tf_op jit(solution)/shard_map/ppermute | solution.py:350
  36.4 11.7 %all-to-all-start.1 = ((bf16[8,64,128]{2,1,0:T(8,128)(2,1)}), bf16[8,64,128]{2,1,0:T(8,128)(2,1)S(1)}, u32[]{:S(2)}, u32[]{:S(2)}) async-start(bf16[8,64,128]{2,1,0:T(8,128)(2,1)} %shard_map.71), calls=%async_computation.1 | async-start | bytes 262144 | tf_op jit(solution)/shard_map/all_to_all | solution.py:412
  42.0 4.5 %collective-permute-start.16 = (bf16[8,4320]{1,0:T(8,128)(2,1)S(1)}, bf16[8,4320]{1,0:T(8,128)(2,1)S(1)}, u32[]{:S(2)}, u32[]{:S(2)}) collective-permute-start(bf16[8,4320]{1,0:T(8,128)(2,1)S(1)} %shard_map.75.refs_0_), channel_id=1, source_target_pairs={{0,24},{8,16},{16,8},{24,0},{1,25},{9,17},{17,9},{25,1},{2,26},{10... | collective-permute-start | bytes 207368 | tf_op jit(solution)/shard_map/ppermute | solution.py:350
  42.0 6.0 %collective-permute-start.15 = (bf16[8,4320]{1,0:T(8,128)(2,1)S(1)}, bf16[8,4320]{1,0:T(8,128)(2,1)S(1)}, u32[]{:S(2)}, u32[]{:S(2)}) collective-permute-start(bf16[8,4320]{1,0:T(8,128)(2,1)S(1)} %shard_map.75.refs_0_), channel_id=1, source_target_pairs={{0,16},{8,24},{16,0},{24,8},{1,17},{9,25},{17,1},{25,9},{2,18},{10... | collective-permute-start | bytes 207368 | tf_op jit(solution)/shard_map/ppermute | solution.py:350
  43.6 4.4 %collective-permute-start.14 = (bf16[8,4320]{1,0:T(8,128)(2,1)S(1)}, bf16[8,4320]{1,0:T(8,128)(2,1)S(1)}, u32[]{:S(2)}, u32[]{:S(2)}) collective-permute-start(bf16[8,4320]{1,0:T(8,128)(2,1)S(1)} %shard_map.75.refs_0_), channel_id=1, source_target_pairs={{0,8},{8,0},{16,24},{24,16},{1,9},{9,1},{17,25},{25,17},{2,10},{10... | collective-permute-start | bytes 207368 | tf_op jit(solution)/shard_map/ppermute | solution.py:350

commit v8 on v7

--- a/solution.py
+++ b/solution.py
@@ -160,9 +160,15 @@
                     grad_t[256:384, at : at + CELLS] = ahead.astype(BF16)
     lane = iota((128, 128), 1)
     frames = []
-    for t in range(9):
-        blocks = [picked[2 * i + t // 3, 2 * p + t % 3] for i in range(2) for p in range(2)]
-        full = dot(grad_t[...], jnp.concatenate(blocks, axis=0))
+    products = []
+    for first in range(0, 9, 2):
+        columns = []
+        for t in range(first, min(first + 2, 9)):
+            blocks = [picked[2 * i + t // 3, 2 * p + t % 3] for i in range(2) for p in range(2)]
+            columns.append(jnp.concatenate(blocks, axis=0))
+        both = dot(grad_t[...], jnp.concatenate(columns, axis=1))
+        products += [both[:, n * 128 : (n + 1) * 128] for n in range(len(columns))]
+    for full in products:
         side = jnp.where(lane < 64, full[0:128], full[256:384])
         side = jnp.where((lane < 64) | (lane >= 96), side, 0.0)
         own = jnp.where(lane < 32, 0.0, full[128:256])
@@ -175,12 +181,20 @@
     share = owned // 2
     row, col = iota((128 // 2, 128), 0), iota((128 // 2, 128), 1)
     frames = [frame.astype(BF16) for frame in frames]
+    halves = []
     for k in range(2):
         half = (place[0] ^ k) & 1
-        chosen = one_hot(col == (row // share ^ slot[0]) * owned + half * share + row % share)
-        for t in range(9):
-            value = dot(chosen, frames[t])
-            outs[k][:, t * 96 : (t + 1) * 96] = value[:, 32:].astype(BF16)
+        halves.append(
+            one_hot(col == (row // share ^ slot[0]) * owned + half * share + row % share)
+        )
+    chosen = jnp.concatenate(halves, axis=0)
+    for first in range(0, 9, 2):
+        value = dot(chosen, jnp.concatenate(frames[first : first + 2], axis=1))
+        for t in range(first, min(first + 2, 9)):
+            at = (t - first) * 128 + 32
+            for k in range(2):
+                part = value[k * 64 : (k + 1) * 64, at : at + 96]
+                outs[k][:, t * 96 : (t + 1) * 96] = part.astype(BF16)
 
 
 def kernel_latent(pack, w2, parts):

time: 49.4 us -> 49 us (level)
  transfers between devices with their start and end apart: 19 -> 19, of which waited for: 7 -> 7; matrix products, arithmetic and copies ran while one was open for 0% -> 0% of each run, Pallas kernels for 13% -> 12%
where the time goes in v8:
time: 49 us; the launch traced here: 48.5 us
  starting transfers between devices  25.1 us (51%)
  waiting for transfers between devices  13.5 us (28%)
  Pallas kernels  9.12 us (19%)
  between operations  0.82 us (2%)
    ppermute x16, starting transfers between devices, swap_ranks(): lax.ppermute(block, axis, [(i, i ^ k) for i in range(lax.axis_size(axis))])  11 us
    ppermute x16, waiting for transfers between devices, swap_ranks(): lax.ppermute(block, axis, [(i, i ^ k) for i in range(lax.axis_size(axis))])  10.4 us
    pallas_call x10, Pallas kernels, call(): pl.pallas_call(kernel, out_shape=out_shape, in_specs=[spec(n, spaces) for...  9.12 us
    all_to_all x1, starting transfers between devices, on_device(): lax.all_to_all(parcels, 'space', split_axis=0, concat_axis=0, tiled=True)  4.89 us
    ppermute x1, starting transfers between devices, from_below(): lax.ppermute(block, axis, [(i - 1, i) for i in range(1, lax.axis_size(axi...  4.85 us
    all_to_all x1, starting transfers between devices, exchanged(): lax.all_to_all(parts, 'space', split_axis=0, concat_axis=0, tiled=True)  4.4 us
    all_to_all x1, waiting for transfers between devices, on_device(): lax.all_to_all(parcels, 'space', split_axis=0, concat_axis=0, tiled=True)  3 us
  transfers between devices with their start and end apart: 19, of which 7 were waited for; matrix products, arithmetic and copies ran while one was open for 0% of the time, Pallas kernels for 12%

profile of v8, /device:TPU:0, one launch (start us, length us, event | category | flops | bytes accessed | tf_op | source)
XLA Modules:
  0.0 48.5 jit_solution(13210377438127876979)
XLA Ops:
  0.6 0.0 copy-start.1
  0.6 0.0 copy-start.2
  0.7 1.9 %shard_map.67 = (bf16[8,64,128]{2,1,0:T(8,128)(2,1)}, bf16[1,64,1024]{2,1,0:T(8,128)(2,1)}) custom-call(s32[1]{0:T(128)} %bitcast._.place, s32[1]{0:T(128)} %bitcast.2.__.slot, bf16[32,8,128]{2,1,0:T(8,128)(2,1)} %bitcast.8, bf16[4,64,1024]{2,1,0:T(8,128)(2,1)} %bitcast.5), custom_call_target="tpu_custom_call" | custom-call | flops 1000000000 | bytes 589832 | tf_op jit(solution)/shard_map/pallas_call | solution.py:348
  2.5 4.8 %collective-permute-start = (bf16[1,64,1024]{2,1,0:T(8,128)(2,1)}, bf16[1,64,1024]{2,1,0:T(8,128)(2,1)S(1)}, u32[]{:S(2)}, u32[]{:S(2)}) collective-permute-start(bf16[1,64,1024]{2,1,0:T(8,128)(2,1)} %get-tuple-element.25), channel_id=1, source_target_pairs={{0,1},{1,2},{2,3},{3,4},{4,5},{5,6},{6,7},{8,9},{9,10},{10,11},{11... | collective-permute-start | bytes 393224 | tf_op jit(solution)/shard_map/ppermute | solution.py:372
  7.4 4.9 %all-to-all-start = ((bf16[8,64,128]{2,1,0:T(8,128)(2,1)}), bf16[8,64,128]{2,1,0:T(8,128)(2,1)S(1)}, u32[]{:S(2)}, u32[]{:S(2)}) async-start(bf16[8,64,128]{2,1,0:T(8,128)(2,1)} %get-tuple-element.26), calls=%async_computation | async-start | bytes 262144 | tf_op jit(solution)/shard_map/all_to_all | solution.py:398
  12.3 0.0 copy-start
  12.3 0.0 collective-permute-done.halo
  12.3 0.0 copy-done.1
  12.3 0.0 copy-done.2
  12.3 1.1 %shard_map.68.pack.refs_0_ = bf16[16,64,128]{2,1,0:T(8,128)(2,1)S(1)} custom-call(bf16[4,64,1024]{2,1,0:T(8,128)(2,1)S(1)} %bitcast.6, bf16[1,64,1024]{2,1,0:T(8,128)(2,1)S(1)} %collective-permute-done.halo, bf16[864,128]{1,0:T(8,128)(2,1)S(1)} %copy-done.2), custom_call_target="tpu_custom_call" | custom-call | flops 1000000000 | bytes 876544 | tf_op jit(solution)/shard_map/pallas_call | solution.py:348
  13.4 1.6 %collective-permute-start.2 = (bf16[16,64,128]{2,1,0:T(8,128)(2,1)S(1)}, bf16[16,64,128]{2,1,0:T(8,128)(2,1)S(1)}, u32[]{:S(2)}, u32[]{:S(2)}) collective-permute-start(bf16[16,64,128]{2,1,0:T(8,128)(2,1)S(1)} %shard_map.68.pack.refs_0_), channel_id=1, source_target_pairs={{0,16},{8,24},{16,0},{24,8},{1,17},{9,25},{17,1},{25,9},{2,18},{10... | collective-permute-start | bytes 786440 | tf_op jit(solution)/shard_map/ppermute | solution.py:364
  15.0 0.0 copy-done
  15.0 1.7 %shard_map.71 = bf16[8,64,128]{2,1,0:T(8,128)(2,1)} custom-call(bf16[16,64,128]{2,1,0:T(8,128)(2,1)S(1)} %shard_map.68.pack.refs_0_, bf16[3456,256]{1,0:T(8,128)(2,1)S(1)} %copy-done), custom_call_target="tpu_custom_call" | custom-call | flops 1000000000 | bytes 2031616 | tf_op jit(solution)/shard_map/pallas_call | solution.py:348
  16.6 3.0 %all-to-all-done.cot = bf16[8,64,128]{2,1,0:T(8,128)(2,1)S(1)} async-done(((bf16[8,64,128]{2,1,0:T(8,128)(2,1)}), bf16[8,64,128]{2,1,0:T(8,128)(2,1)S(1)}, u32[]{:S(2)}, u32[]{:S(2)}) %all-to-all-start) | async-done | bytes 131104 | tf_op jit(solution)/shard_map/all_to_all | solution.py:398
  19.6 0.1 collective-permute-start.3
  19.7 1.6 %collective-permute-start.4 = (bf16[8,16,128]{2,1,0:T(8,128)(2,1)S(1)}, bf16[8,16,128]{2,1,0:T(8,128)(2,1)S(1)}, u32[]{:S(2)}, u32[]{:S(2)}) collective-permute-start(bf16[8,16,128]{2,1,0:T(8,128)(2,1)S(1)} %get-tuple-element.31), channel_id=1, source_target_pairs={{0,16},{8,24},{16,0},{24,8},{1,17},{9,25},{17,1},{25,9},{2,18},{10... | collective-permute-start | bytes 98312 | tf_op jit(solution)/shard_map/ppermute | solution.py:364
  21.3 0.3 collective-permute-start.5
  21.6 0.3 collective-permute-start.1
  21.9 2.7 %shard_map.69 = (bf16[64,864]{1,0:T(8,128)(2,1)S(1)}, bf16[64,864]{1,0:T(8,128)(2,1)S(1)}) custom-call(s32[1]{0:T(128)} %bitcast._.place, s32[1]{0:T(128)} %bitcast.2.__.slot, bf16[4,64,1024]{2,1,0:T(8,128)(2,1)S(1)} %bitcast.7, bf16[1,64,1024]{2,1,0:T(8,128)(2,1)S(1)} %collective-permute-done.halo, bf16[864,128]{1,0:T(8,128)(2,1)S(1)} %copy-done.2, ...), custom_call_target="tpu_custom_call" | custom-call | flops 1000000000 | bytes 2777096 | tf_op jit(solution)/shard_map/pallas_call | solution.py:348
  24.6 0.0 collective-permute-done.3.refs_1_
  24.7 0.0 collective-permute-done.4.refs_2_
  24.7 0.0 collective-permute-done.5.refs_3_
  24.7 0.0 collective-permute-done.2.refs_2_
  24.7 0.2 collective-permute-start.6
  24.9 0.3 collective-permute-start.7
  25.3 0.3 shard_map.72.refs_4_
  25.6 0.9 %collective-permute-done.7.refs_6_ = bf16[64,864]{1,0:T(8,128)(2,1)S(1)} collective-permute-done((bf16[64,864]{1,0:T(8,128)(2,1)S(1)}, bf16[64,864]{1,0:T(8,128)(2,1)S(1)}, u32[]{:S(2)}, u32[]{:S(2)}) %collective-permute-start.7) | collective-permute-done | bytes 110624 | tf_op jit(solution)/shard_map/ppermute | solution.py:364
  26.5 0.0 collective-permute-done.1.refs_1_
  26.5 0.0 collective-permute-done.6.refs_3_
  26.5 0.5 %shard_map.73 = (f32[8,4320]{1,0:T(8,128)S(1)}, bf16[8,4320]{1,0:T(8,128)(2,1)S(1)}, bf16[8,4320]{1,0:T(8,128)(2,1)S(1)}, bf16[8,4320]{1,0:T(8,128)(2,1)S(1)}, b...) custom-call(bf16[16,64,128]{2,1,0:T(8,128)(2,1)S(1)} %shard_map.68.pack.refs_0_, ...), custom_call_target="tpu_custom_call" | custom-call | flops 1000000000 | bytes 1794048 | tf_op jit(solution)/shard_map/pallas_call | solution.py:348
  27.0 0.3 collective-permute-start.11
  27.2 1.8 %collective-permute-start.8 = (bf16[8,4320]{1,0:T(8,128)(2,1)S(1)}, bf16[8,4320]{1,0:T(8,128)(2,1)S(1)}, u32[]{:S(2)}, u32[]{:S(2)}) collective-permute-start(bf16[8,4320]{1,0:T(8,128)(2,1)S(1)} %get-tuple-element.36), channel_id=1, source_target_pairs={{0,1},{1,0},{2,3},{3,2},{4,5},{5,4},{6,7},{7,6},{8,9},{9,8},{10,11... | collective-permute-start | bytes 207368 | tf_op jit(solution)/shard_map/ppermute | solution.py:364
  29.1 0.0 collective-permute-start.9
  29.1 1.7 %collective-permute-start.10 = (bf16[8,4320]{1,0:T(8,128)(2,1)S(1)}, bf16[8,4320]{1,0:T(8,128)(2,1)S(1)}, u32[]{:S(2)}, u32[]{:S(2)}) collective-permute-start(bf16[8,4320]{1,0:T(8,128)(2,1)S(1)} %get-tuple-element.38), channel_id=1, source_target_pairs={{0,3},{1,2},{2,1},{3,0},{4,7},{5,6},{6,5},{7,4},{8,11},{9,10},{10,... | collective-permute-start | bytes 207368 | tf_op jit(solution)/shard_map/ppermute | solution.py:364
  30.7 4.3 %collective-permute-done.11.lent = bf16[2,8,4320]{2,1,0:T(8,128)(2,1)S(1)} collective-permute-done((bf16[2,8,4320]{2,1,0:T(8,128)(2,1)S(1)}, bf16[2,8,4320]{2,1,0:T(8,128)(2,1)S(1)}, u32[]{:S(2)}, u32[]{:S(2)}) %collective-permute-start.11) | collective-permute-done | bytes 138272 | tf_op jit(solution)/shard_map/ppermute | solution.py:364
  35.1 0.1 collective-permute-start.12
  35.1 0.8 %collective-permute-start.13 = (bf16[8,4320]{1,0:T(8,128)(2,1)S(1)}, bf16[8,4320]{1,0:T(8,128)(2,1)S(1)}, u32[]{:S(2)}, u32[]{:S(2)}) collective-permute-start(bf16[8,4320]{1,0:T(8,128)(2,1)S(1)} %get-tuple-element.42), channel_id=1, source_target_pairs={{0,6},{1,7},{2,4},{3,5},{4,2},{5,3},{6,0},{7,1},{8,14},{9,15},{10,... | collective-permute-start | bytes 207368 | tf_op jit(solution)/shard_map/ppermute | solution.py:364
  35.9 4.4 %all-to-all-start.1 = ((bf16[8,64,128]{2,1,0:T(8,128)(2,1)}), bf16[8,64,128]{2,1,0:T(8,128)(2,1)S(1)}, u32[]{:S(2)}, u32[]{:S(2)}) async-start(bf16[8,64,128]{2,1,0:T(8,128)(2,1)} %shard_map.71), calls=%async_computation.1 | async-start | bytes 262144 | tf_op jit(solution)/shard_map/all_to_all | solution.py:426
  40.3 0.0 collective-permute-done.8.refs_0_
  40.3 0.0 collective-permute-done.9.refs_1_
  40.3 0.0 collective-permute-done.10.refs_2_
  40.3 0.0 collective-permute-done.12.refs_3_
  40.3 1.1 %collective-permute-done.13.refs_4_ = bf16[8,4320]{1,0:T(8,128)(2,1)S(1)} collective-permute-done((bf16[8,4320]{1,0:T(8,128)(2,1)S(1)}, bf16[8,4320]{1,0:T(8,128)(2,1)S(1)}, u32[]{:S(2)}, u32[]{:S(2)}) %collective-permute-start.13) | collective-permute-done | bytes 69152 | tf_op jit(solution)/shard_map/ppermute | solution.py:364
  41.4 0.1 shard_map.75.refs_0_
  41.5 0.1 collective-permute-start.16
  41.6 1.6 %collective-permute-start.15 = (bf16[8,4320]{1,0:T(8,128)(2,1)S(1)}, bf16[8,4320]{1,0:T(8,128)(2,1)S(1)}, u32[]{:S(2)}, u32[]{:S(2)}) collective-permute-start(bf16[8,4320]{1,0:T(8,128)(2,1)S(1)} %shard_map.75.refs_0_), channel_id=1, source_target_pairs={{0,16},{8,24},{16,0},{24,8},{1,17},{9,25},{17,1},{25,9},{2,18},{10... | collective-permute-start | bytes 207368 | tf_op jit(solution)/shard_map/ppermute | solution.py:364
  43.2 0.3 collective-permute-start.14
  43.4 2.5 %collective-permute-done.16.refs_3_ = bf16[8,4320]{1,0:T(8,128)(2,1)S(1)} collective-permute-done((bf16[8,4320]{1,0:T(8,128)(2,1)S(1)}, bf16[8,4320]{1,0:T(8,128)(2,1)S(1)}, u32[]{:S(2)}, u32[]{:S(2)}) %collective-permute-start.16) | collective-permute-done | bytes 69152 | tf_op jit(solution)/shard_map/ppermute | solution.py:364
  46.0 1.6 %collective-permute-done.15.refs_2_ = bf16[8,4320]{1,0:T(8,128)(2,1)S(1)} collective-permute-done((bf16[8,4320]{1,0:T(8,128)(2,1)S(1)}, bf16[8,4320]{1,0:T(8,128)(2,1)S(1)}, u32[]{:S(2)}, u32[]{:S(2)}) %collective-permute-start.15) | collective-permute-done | bytes 69152 | tf_op jit(solution)/shard_map/ppermute | solution.py:364
  47.5 0.0 collective-permute-done.14.refs_1_
  47.5 0.1 all-to-all-done.1.refs_4_
  47.6 0.9 %shard_map.76 = (f32[16,864]{1,0:T(8,128)}, f32[32,3456]{1,0:T(8,128)}, bf16[32,8,128]{2,1,0:T(8,128)(2,1)}) custom-call(s32[1]{0:T(128)} %bitcast._.place, bf16[8,4320]{1,0:T(8,128)(2,1)S(1)} %shard_map.75.refs_0_, bf16[8,4320]{1,0:T(8,128)(2,1)S(1)} %collective-permute-done.14.refs_1_, bf16[8,4320]{1,0:T(8,128)(2,1)S(1)} %collective-permute-done.15.refs_2_, ...), custom_call_target="tpu_custom_call" | custom-call | flops 1000000000 | bytes 407556 | tf_op jit(solution)/shard_map/pallas_call | solution.py:348
  (2 shorter events, 0.1 us)
Async XLA Ops:
  0.6 11.6 %copy-start.1 = (bf16[1,4,64,1024]{3,2,1,0:T(8,128)(2,1)S(1)}, bf16[1,4,64,1024]{3,2,1,0:T(8,128)(2,1)}, u32[]{:S(2)}) copy-start(bf16[1,4,64,1024]{3,2,1,0:T(8,128)(2,1)} %param.4) | copy-start | bytes 1572868
  0.6 11.6 %copy-start.2 = (bf16[864,128]{1,0:T(8,128)(2,1)S(1)}, bf16[864,128]{1,0:T(8,128)(2,1)}, u32[]{:S(2)}) copy-start(bf16[864,128]{1,0:T(8,128)(2,1)} %w1.3) | copy-start | bytes 663556
  2.5 9.8 %collective-permute-start = (bf16[1,64,1024]{2,1,0:T(8,128)(2,1)}, bf16[1,64,1024]{2,1,0:T(8,128)(2,1)S(1)}, u32[]{:S(2)}, u32[]{:S(2)}) collective-permute-start(bf16[1,64,1024]{2,1,0:T(8,128)(2,1)} %get-tuple-element.25), channel_id=1, source_target_pairs={{0,1},{1,2},{2,3},{3,4},{4,5},{5,6},{6,7},{8,9},{9,10},{10,11},{11... | collective-permute-start | bytes 393224 | tf_op jit(solution)/shard_map/ppermute | solution.py:372
  7.4 12.2 %all-to-all-start = ((bf16[8,64,128]{2,1,0:T(8,128)(2,1)}), bf16[8,64,128]{2,1,0:T(8,128)(2,1)S(1)}, u32[]{:S(2)}, u32[]{:S(2)}) async-start(bf16[8,64,128]{2,1,0:T(8,128)(2,1)} %get-tuple-element.26), calls=%async_computation | async-start | bytes 262144 | tf_op jit(solution)/shard_map/all_to_all | solution.py:398
  12.3 2.7 %copy-start = (bf16[3456,256]{1,0:T(8,128)(2,1)S(1)}, bf16[3456,256]{1,0:T(8,128)(2,1)}, u32[]{:S(2)}) copy-start(bf16[3456,256]{1,0:T(8,128)(2,1)} %w2.3) | copy-start | bytes 5308420
  13.4 11.3 %collective-permute-start.2 = (bf16[16,64,128]{2,1,0:T(8,128)(2,1)S(1)}, bf16[16,64,128]{2,1,0:T(8,128)(2,1)S(1)}, u32[]{:S(2)}, u32[]{:S(2)}) collective-permute-start(bf16[16,64,128]{2,1,0:T(8,128)(2,1)S(1)} %shard_map.68.pack.refs_0_), channel_id=1, source_target_pairs={{0,16},{8,24},{16,0},{24,8},{1,17},{9,25},{17,1},{25,9},{2,18},{10... | collective-permute-start | bytes 786440 | tf_op jit(solution)/shard_map/ppermute | solution.py:364
  19.6 5.0 %collective-permute-start.3 = (bf16[8,16,128]{2,1,0:T(8,128)(2,1)S(1)}, bf16[8,16,128]{2,1,0:T(8,128)(2,1)S(1)}, u32[]{:S(2)}, u32[]{:S(2)}) collective-permute-start(bf16[8,16,128]{2,1,0:T(8,128)(2,1)S(1)} %get-tuple-element.30), channel_id=1, source_target_pairs={{0,8},{8,0},{16,24},{24,16},{1,9},{9,1},{17,25},{25,17},{2,10},{10... | collective-permute-start | bytes 98312 | tf_op jit(solution)/shard_map/ppermute | solution.py:364
  19.7 4.9 %collective-permute-start.4 = (bf16[8,16,128]{2,1,0:T(8,128)(2,1)S(1)}, bf16[8,16,128]{2,1,0:T(8,128)(2,1)S(1)}, u32[]{:S(2)}, u32[]{:S(2)}) collective-permute-start(bf16[8,16,128]{2,1,0:T(8,128)(2,1)S(1)} %get-tuple-element.31), channel_id=1, source_target_pairs={{0,16},{8,24},{16,0},{24,8},{1,17},{9,25},{17,1},{25,9},{2,18},{10... | collective-permute-start | bytes 98312 | tf_op jit(solution)/shard_map/ppermute | solution.py:364
  21.3 3.4 %collective-permute-start.5 = (bf16[8,16,128]{2,1,0:T(8,128)(2,1)S(1)}, bf16[8,16,128]{2,1,0:T(8,128)(2,1)S(1)}, u32[]{:S(2)}, u32[]{:S(2)}) collective-permute-start(bf16[8,16,128]{2,1,0:T(8,128)(2,1)S(1)} %get-tuple-element.32), channel_id=1, source_target_pairs={{0,24},{8,16},{16,8},{24,0},{1,25},{9,17},{17,9},{25,1},{2,26},{10... | collective-permute-start | bytes 98312 | tf_op jit(solution)/shard_map/ppermute | solution.py:364
  21.6 4.9 %collective-permute-start.1 = (bf16[16,64,128]{2,1,0:T(8,128)(2,1)S(1)}, bf16[16,64,128]{2,1,0:T(8,128)(2,1)S(1)}, u32[]{:S(2)}, u32[]{:S(2)}) collective-permute-start(bf16[16,64,128]{2,1,0:T(8,128)(2,1)S(1)} %shard_map.68.pack.refs_0_), channel_id=1, source_target_pairs={{0,8},{8,0},{16,24},{24,16},{1,9},{9,1},{17,25},{25,17},{2,10},{10... | collective-permute-start | bytes 786440 | tf_op jit(solution)/shard_map/ppermute | solution.py:364
  24.7 1.8 %collective-permute-start.6 = (bf16[16,64,128]{2,1,0:T(8,128)(2,1)S(1)}, bf16[16,64,128]{2,1,0:T(8,128)(2,1)S(1)}, u32[]{:S(2)}, u32[]{:S(2)}) collective-permute-start(bf16[16,64,128]{2,1,0:T(8,128)(2,1)S(1)} %collective-permute-done.2.refs_2_), channel_id=1, source_target_pairs={{0,8},{8,0},{16,24},{24,16},{1,9},{9,1},{17,25},{25,17},{2,10},{10... | collective-permute-start | bytes 786440 | tf_op jit(solution)/shard_map/ppermute | solution.py:364
  24.9 1.5 %collective-permute-start.7 = (bf16[64,864]{1,0:T(8,128)(2,1)S(1)}, bf16[64,864]{1,0:T(8,128)(2,1)S(1)}, u32[]{:S(2)}, u32[]{:S(2)}) collective-permute-start(bf16[64,864]{1,0:T(8,128)(2,1)S(1)} %get-tuple-element.29), channel_id=1, source_target_pairs={{0,8},{8,0},{16,24},{24,16},{1,9},{9,1},{17,25},{25,17},{2,10},{10... | collective-permute-start | bytes 331784 | tf_op jit(solution)/shard_map/ppermute | solution.py:364
  27.0 8.0 %collective-permute-start.11 = (bf16[2,8,4320]{2,1,0:T(8,128)(2,1)S(1)}, bf16[2,8,4320]{2,1,0:T(8,128)(2,1)S(1)}, u32[]{:S(2)}, u32[]{:S(2)}) collective-permute-start(bf16[2,8,4320]{2,1,0:T(8,128)(2,1)S(1)} %get-tuple-element.39), channel_id=1, source_target_pairs={{0,1},{1,0},{2,3},{3,2},{4,5},{5,4},{6,7},{7,6},{8,9},{9,8},{10,11... | collective-permute-start | bytes 414728 | tf_op jit(solution)/shard_map/ppermute | solution.py:364
  27.2 13.1 %collective-permute-start.8 = (bf16[8,4320]{1,0:T(8,128)(2,1)S(1)}, bf16[8,4320]{1,0:T(8,128)(2,1)S(1)}, u32[]{:S(2)}, u32[]{:S(2)}) collective-permute-start(bf16[8,4320]{1,0:T(8,128)(2,1)S(1)} %get-tuple-element.36), channel_id=1, source_target_pairs={{0,1},{1,0},{2,3},{3,2},{4,5},{5,4},{6,7},{7,6},{8,9},{9,8},{10,11... | collective-permute-start | bytes 207368 | tf_op jit(solution)/shard_map/ppermute | solution.py:364
  29.1 11.2 %collective-permute-start.9 = (bf16[8,4320]{1,0:T(8,128)(2,1)S(1)}, bf16[8,4320]{1,0:T(8,128)(2,1)S(1)}, u32[]{:S(2)}, u32[]{:S(2)}) collective-permute-start(bf16[8,4320]{1,0:T(8,128)(2,1)S(1)} %get-tuple-element.37), channel_id=1, source_target_pairs={{0,2},{1,3},{2,0},{3,1},{4,6},{5,7},{6,4},{7,5},{8,10},{9,11},{10,... | collective-permute-start | bytes 207368 | tf_op jit(solution)/shard_map/ppermute | solution.py:364
  29.1 11.3 %collective-permute-start.10 = (bf16[8,4320]{1,0:T(8,128)(2,1)S(1)}, bf16[8,4320]{1,0:T(8,128)(2,1)S(1)}, u32[]{:S(2)}, u32[]{:S(2)}) collective-permute-start(bf16[8,4320]{1,0:T(8,128)(2,1)S(1)} %get-tuple-element.38), channel_id=1, source_target_pairs={{0,3},{1,2},{2,1},{3,0},{4,7},{5,6},{6,5},{7,4},{8,11},{9,10},{10,... | collective-permute-start | bytes 207368 | tf_op jit(solution)/shard_map/ppermute | solution.py:364
  35.1 5.3 %collective-permute-start.12 = (bf16[8,4320]{1,0:T(8,128)(2,1)S(1)}, bf16[8,4320]{1,0:T(8,128)(2,1)S(1)}, u32[]{:S(2)}, u32[]{:S(2)}) collective-permute-start(bf16[8,4320]{1,0:T(8,128)(2,1)S(1)} %get-tuple-element.41), channel_id=1, source_target_pairs={{0,4},{1,5},{2,6},{3,7},{4,0},{5,1},{6,2},{7,3},{8,12},{9,13},{10,... | collective-permute-start | bytes 207368 | tf_op jit(solution)/shard_map/ppermute | solution.py:364
  35.1 6.3 %collective-permute-start.13 = (bf16[8,4320]{1,0:T(8,128)(2,1)S(1)}, bf16[8,4320]{1,0:T(8,128)(2,1)S(1)}, u32[]{:S(2)}, u32[]{:S(2)}) collective-permute-start(bf16[8,4320]{1,0:T(8,128)(2,1)S(1)} %get-tuple-element.42), channel_id=1, source_target_pairs={{0,6},{1,7},{2,4},{3,5},{4,2},{5,3},{6,0},{7,1},{8,14},{9,15},{10,... | collective-permute-start | bytes 207368 | tf_op jit(solution)/shard_map/ppermute | solution.py:364
  35.9 11.7 %all-to-all-start.1 = ((bf16[8,64,128]{2,1,0:T(8,128)(2,1)}), bf16[8,64,128]{2,1,0:T(8,128)(2,1)S(1)}, u32[]{:S(2)}, u32[]{:S(2)}) async-start(bf16[8,64,128]{2,1,0:T(8,128)(2,1)} %shard_map.71), calls=%async_computation.1 | async-start | bytes 262144 | tf_op jit(solution)/shard_map/all_to_all | solution.py:426
  41.5 4.5 %collective-permute-start.16 = (bf16[8,4320]{1,0:T(8,128)(2,1)S(1)}, bf16[8,4320]{1,0:T(8,128)(2,1)S(1)}, u32[]{:S(2)}, u32[]{:S(2)}) collective-permute-start(bf16[8,4320]{1,0:T(8,128)(2,1)S(1)} %shard_map.75.refs_0_), channel_id=1, source_target_pairs={{0,24},{8,16},{16,8},{24,0},{1,25},{9,17},{17,9},{25,1},{2,26},{10... | collective-permute-start | bytes 207368 | tf_op jit(solution)/shard_map/ppermute | solution.py:364
  41.6 6.0 %collective-permute-start.15 = (bf16[8,4320]{1,0:T(8,128)(2,1)S(1)}, bf16[8,4320]{1,0:T(8,128)(2,1)S(1)}, u32[]{:S(2)}, u32[]{:S(2)}) collective-permute-start(bf16[8,4320]{1,0:T(8,128)(2,1)S(1)} %shard_map.75.refs_0_), channel_id=1, source_target_pairs={{0,16},{8,24},{16,0},{24,8},{1,17},{9,25},{17,1},{25,9},{2,18},{10... | collective-permute-start | bytes 207368 | tf_op jit(solution)/shard_map/ppermute | solution.py:364
  43.2 4.4 %collective-permute-start.14 = (bf16[8,4320]{1,0:T(8,128)(2,1)S(1)}, bf16[8,4320]{1,0:T(8,128)(2,1)S(1)}, u32[]{:S(2)}, u32[]{:S(2)}) collective-permute-start(bf16[8,4320]{1,0:T(8,128)(2,1)S(1)} %shard_map.75.refs_0_), channel_id=1, source_target_pairs={{0,8},{8,0},{16,24},{24,16},{1,9},{9,1},{17,25},{25,17},{2,10},{10... | collective-permute-start | bytes 207368 | tf_op jit(solution)/shard_map/ppermute | solution.py:364

commit v9 on v8

--- a/solution.py
+++ b/solution.py
@@ -84,13 +84,14 @@
     last.start()
     group, slabs = cot.shape[:2]
     rows_per = group // pieces
-    row, col = iota((2 * group * slabs, group * slabs), 0), iota((2 * group * slabs, group * slabs), 1)
-    slab = row // (2 * group) + row // rows_per % 2
-    channel = row % (2 * group) // (2 * rows_per) * rows_per + row % rows_per
-    chosen = one_hot((slab < slabs) & (col == channel * slabs + slab))
+    row, col = iota((group * slabs, group * slabs), 0), iota((group * slabs, group * slabs), 1)
+    chosen = one_hot(col == row % group * slabs + row // group)
     whole.wait()
     flat = cot[...].astype(F32).reshape(-1, CELLS).astype(BF16)
-    parcels[...] = dot(chosen, flat).astype(BF16).reshape(slabs, 2 * group, CELLS)
+    here = dot(chosen, flat).reshape(slabs, pieces, 1, rows_per, CELLS)
+    next_ = jnp.concatenate([here[1:], jnp.zeros_like(here[:1])], axis=0)
+    pair = jnp.concatenate([here, next_], axis=2)
+    parcels[...] = pair.reshape(slabs, 2 * group, CELLS).astype(BF16)
     last.wait()
 
 
@@ -392,7 +393,7 @@
         slab,
         spaces={0: pltpu.SMEM, 1: pltpu.SMEM, 2: pltpu.HBM, 3: pltpu.HBM},
         scratch=[pltpu.VMEM((group, slabs, CELLS), BF16), pltpu.SemaphoreType.DMA((2,))],
-        vmem=60 * 1024 * 1024,
+        vmem=62 * 1024 * 1024,
     )
     halo = from_below(last, "space")
     cot = lax.all_to_all(parcels, "space", split_axis=0, concat_axis=0, tiled=True)

time: 49 us -> 48.8 us (level)
  no operation moved by 1% of the time
where the time goes in v9:
time: 48.8 us; the launch traced here: 48.4 us
  starting transfers between devices  25.1 us (51%)
  waiting for transfers between devices  13.5 us (28%)
  Pallas kernels  8.99 us (18%)
  between operations  0.81 us (2%)
    ppermute x16, starting transfers between devices, swap_ranks(): lax.ppermute(block, axis, [(i, i ^ k) for i in range(lax.axis_size(axis))])  11 us
    ppermute x16, waiting for transfers between devices, swap_ranks(): lax.ppermute(block, axis, [(i, i ^ k) for i in range(lax.axis_size(axis))])  10.4 us
    pallas_call x10, Pallas kernels, call(): pl.pallas_call(kernel, out_shape=out_shape, in_specs=[spec(n, spaces) for...  8.99 us
    all_to_all x1, starting transfers between devices, on_device(): lax.all_to_all(parcels, 'space', split_axis=0, concat_axis=0, tiled=True)  4.88 us
    ppermute x1, starting transfers between devices, from_below(): lax.ppermute(block, axis, [(i - 1, i) for i in range(1, lax.axis_size(axi...  4.85 us
    all_to_all x1, starting transfers between devices, exchanged(): lax.all_to_all(parts, 'space', split_axis=0, concat_axis=0, tiled=True)  4.39 us
    all_to_all x1, waiting for transfers between devices, on_device(): lax.all_to_all(parcels, 'space', split_axis=0, concat_axis=0, tiled=True)  3.02 us
  transfers between devices with their start and end apart: 19, of which 7 were waited for; matrix products, arithmetic and copies ran while one was open for 0% of the time, Pallas kernels for 12%

profile of v9, /device:TPU:0, one launch (start us, length us, event | category | flops | bytes accessed | tf_op | source)
XLA Modules:
  0.0 48.4 jit_solution(4529953154138781777)
XLA Ops:
  0.6 0.0 copy-start.1
  0.6 0.0 copy-start.2
  0.7 1.8 %shard_map.67 = (bf16[8,64,128]{2,1,0:T(8,128)(2,1)}, bf16[1,64,1024]{2,1,0:T(8,128)(2,1)}) custom-call(s32[1]{0:T(128)} %bitcast._.place, s32[1]{0:T(128)} %bitcast.2.__.slot, bf16[32,8,128]{2,1,0:T(8,128)(2,1)} %bitcast.8, bf16[4,64,1024]{2,1,0:T(8,128)(2,1)} %bitcast.5), custom_call_target="tpu_custom_call" | custom-call | flops 1000000000 | bytes 589832 | tf_op jit(solution)/shard_map/pallas_call | solution.py:349
  2.5 4.8 %collective-permute-start = (bf16[1,64,1024]{2,1,0:T(8,128)(2,1)}, bf16[1,64,1024]{2,1,0:T(8,128)(2,1)S(1)}, u32[]{:S(2)}, u32[]{:S(2)}) collective-permute-start(bf16[1,64,1024]{2,1,0:T(8,128)(2,1)} %get-tuple-element.25), channel_id=1, source_target_pairs={{0,1},{1,2},{2,3},{3,4},{4,5},{5,6},{6,7},{8,9},{9,10},{10,11},{11... | collective-permute-start | bytes 393224 | tf_op jit(solution)/shard_map/ppermute | solution.py:373
  7.3 4.9 %all-to-all-start = ((bf16[8,64,128]{2,1,0:T(8,128)(2,1)}), bf16[8,64,128]{2,1,0:T(8,128)(2,1)S(1)}, u32[]{:S(2)}, u32[]{:S(2)}) async-start(bf16[8,64,128]{2,1,0:T(8,128)(2,1)} %get-tuple-element.26), calls=%async_computation | async-start | bytes 262144 | tf_op jit(solution)/shard_map/all_to_all | solution.py:399
  12.2 0.0 copy-start
  12.2 0.0 collective-permute-done.halo
  12.2 0.0 copy-done.1
  12.2 0.0 copy-done.2
  12.2 1.1 %shard_map.68.pack.refs_0_ = bf16[16,64,128]{2,1,0:T(8,128)(2,1)S(1)} custom-call(bf16[4,64,1024]{2,1,0:T(8,128)(2,1)S(1)} %bitcast.6, bf16[1,64,1024]{2,1,0:T(8,128)(2,1)S(1)} %collective-permute-done.halo, bf16[864,128]{1,0:T(8,128)(2,1)S(1)} %copy-done.2), custom_call_target="tpu_custom_call" | custom-call | flops 1000000000 | bytes 876544 | tf_op jit(solution)/shard_map/pallas_call | solution.py:349
  13.3 1.6 %collective-permute-start.2 = (bf16[16,64,128]{2,1,0:T(8,128)(2,1)S(1)}, bf16[16,64,128]{2,1,0:T(8,128)(2,1)S(1)}, u32[]{:S(2)}, u32[]{:S(2)}) collective-permute-start(bf16[16,64,128]{2,1,0:T(8,128)(2,1)S(1)} %shard_map.68.pack.refs_0_), channel_id=1, source_target_pairs={{0,16},{8,24},{16,0},{24,8},{1,17},{9,25},{17,1},{25,9},{2,18},{10... | collective-permute-start | bytes 786440 | tf_op jit(solution)/shard_map/ppermute | solution.py:365
  14.9 0.0 copy-done
  14.9 1.6 %shard_map.71 = bf16[8,64,128]{2,1,0:T(8,128)(2,1)} custom-call(bf16[16,64,128]{2,1,0:T(8,128)(2,1)S(1)} %shard_map.68.pack.refs_0_, bf16[3456,256]{1,0:T(8,128)(2,1)S(1)} %copy-done), custom_call_target="tpu_custom_call" | custom-call | flops 1000000000 | bytes 2031616 | tf_op jit(solution)/shard_map/pallas_call | solution.py:349
  16.5 3.0 %all-to-all-done.cot = bf16[8,64,128]{2,1,0:T(8,128)(2,1)S(1)} async-done(((bf16[8,64,128]{2,1,0:T(8,128)(2,1)}), bf16[8,64,128]{2,1,0:T(8,128)(2,1)S(1)}, u32[]{:S(2)}, u32[]{:S(2)}) %all-to-all-start) | async-done | bytes 131104 | tf_op jit(solution)/shard_map/all_to_all | solution.py:399
  19.6 0.1 collective-permute-start.3
  19.7 1.6 %collective-permute-start.4 = (bf16[8,16,128]{2,1,0:T(8,128)(2,1)S(1)}, bf16[8,16,128]{2,1,0:T(8,128)(2,1)S(1)}, u32[]{:S(2)}, u32[]{:S(2)}) collective-permute-start(bf16[8,16,128]{2,1,0:T(8,128)(2,1)S(1)} %get-tuple-element.31), channel_id=1, source_target_pairs={{0,16},{8,24},{16,0},{24,8},{1,17},{9,25},{17,1},{25,9},{2,18},{10... | collective-permute-start | bytes 98312 | tf_op jit(solution)/shard_map/ppermute | solution.py:365
  21.2 0.3 collective-permute-start.5
  21.5 0.3 collective-permute-start.1
  21.9 2.7 %shard_map.69 = (bf16[64,864]{1,0:T(8,128)(2,1)S(1)}, bf16[64,864]{1,0:T(8,128)(2,1)S(1)}) custom-call(s32[1]{0:T(128)} %bitcast._.place, s32[1]{0:T(128)} %bitcast.2.__.slot, bf16[4,64,1024]{2,1,0:T(8,128)(2,1)S(1)} %bitcast.7, bf16[1,64,1024]{2,1,0:T(8,128)(2,1)S(1)} %collective-permute-done.halo, bf16[864,128]{1,0:T(8,128)(2,1)S(1)} %copy-done.2, ...), custom_call_target="tpu_custom_call" | custom-call | flops 1000000000 | bytes 2777096 | tf_op jit(solution)/shard_map/pallas_call | solution.py:349
  24.5 0.0 collective-permute-done.3.refs_1_
  24.6 0.0 collective-permute-done.4.refs_2_
  24.6 0.0 collective-permute-done.5.refs_3_
  24.6 0.0 collective-permute-done.2.refs_2_
  24.6 0.2 collective-permute-start.6
  24.8 0.3 collective-permute-start.7
  25.2 0.3 shard_map.72.refs_4_
  25.5 0.9 %collective-permute-done.7.refs_6_ = bf16[64,864]{1,0:T(8,128)(2,1)S(1)} collective-permute-done((bf16[64,864]{1,0:T(8,128)(2,1)S(1)}, bf16[64,864]{1,0:T(8,128)(2,1)S(1)}, u32[]{:S(2)}, u32[]{:S(2)}) %collective-permute-start.7) | collective-permute-done | bytes 110624 | tf_op jit(solution)/shard_map/ppermute | solution.py:365
  26.3 0.0 collective-permute-done.1.refs_1_
  26.4 0.0 collective-permute-done.6.refs_3_
  26.4 0.5 %shard_map.73 = (f32[8,4320]{1,0:T(8,128)S(1)}, bf16[8,4320]{1,0:T(8,128)(2,1)S(1)}, bf16[8,4320]{1,0:T(8,128)(2,1)S(1)}, bf16[8,4320]{1,0:T(8,128)(2,1)S(1)}, b...) custom-call(bf16[16,64,128]{2,1,0:T(8,128)(2,1)S(1)} %shard_map.68.pack.refs_0_, ...), custom_call_target="tpu_custom_call" | custom-call | flops 1000000000 | bytes 1794048 | tf_op jit(solution)/shard_map/pallas_call | solution.py:349
  26.8 0.3 collective-permute-start.11
  27.1 1.8 %collective-permute-start.8 = (bf16[8,4320]{1,0:T(8,128)(2,1)S(1)}, bf16[8,4320]{1,0:T(8,128)(2,1)S(1)}, u32[]{:S(2)}, u32[]{:S(2)}) collective-permute-start(bf16[8,4320]{1,0:T(8,128)(2,1)S(1)} %get-tuple-element.36), channel_id=1, source_target_pairs={{0,1},{1,0},{2,3},{3,2},{4,5},{5,4},{6,7},{7,6},{8,9},{9,8},{10,11... | collective-permute-start | bytes 207368 | tf_op jit(solution)/shard_map/ppermute | solution.py:365
  28.9 0.0 collective-permute-start.9
  28.9 1.7 %collective-permute-start.10 = (bf16[8,4320]{1,0:T(8,128)(2,1)S(1)}, bf16[8,4320]{1,0:T(8,128)(2,1)S(1)}, u32[]{:S(2)}, u32[]{:S(2)}) collective-permute-start(bf16[8,4320]{1,0:T(8,128)(2,1)S(1)} %get-tuple-element.38), channel_id=1, source_target_pairs={{0,3},{1,2},{2,1},{3,0},{4,7},{5,6},{6,5},{7,4},{8,11},{9,10},{10,... | collective-permute-start | bytes 207368 | tf_op jit(solution)/shard_map/ppermute | solution.py:365
  30.6 4.3 %collective-permute-done.11.lent = bf16[2,8,4320]{2,1,0:T(8,128)(2,1)S(1)} collective-permute-done((bf16[2,8,4320]{2,1,0:T(8,128)(2,1)S(1)}, bf16[2,8,4320]{2,1,0:T(8,128)(2,1)S(1)}, u32[]{:S(2)}, u32[]{:S(2)}) %collective-permute-start.11) | collective-permute-done | bytes 138272 | tf_op jit(solution)/shard_map/ppermute | solution.py:365
  34.9 0.1 collective-permute-start.12
  35.0 0.8 %collective-permute-start.13 = (bf16[8,4320]{1,0:T(8,128)(2,1)S(1)}, bf16[8,4320]{1,0:T(8,128)(2,1)S(1)}, u32[]{:S(2)}, u32[]{:S(2)}) collective-permute-start(bf16[8,4320]{1,0:T(8,128)(2,1)S(1)} %get-tuple-element.42), channel_id=1, source_target_pairs={{0,6},{1,7},{2,4},{3,5},{4,2},{5,3},{6,0},{7,1},{8,14},{9,15},{10,... | collective-permute-start | bytes 207368 | tf_op jit(solution)/shard_map/ppermute | solution.py:365
  35.8 4.4 %all-to-all-start.1 = ((bf16[8,64,128]{2,1,0:T(8,128)(2,1)}), bf16[8,64,128]{2,1,0:T(8,128)(2,1)S(1)}, u32[]{:S(2)}, u32[]{:S(2)}) async-start(bf16[8,64,128]{2,1,0:T(8,128)(2,1)} %shard_map.71), calls=%async_computation.1 | async-start | bytes 262144 | tf_op jit(solution)/shard_map/all_to_all | solution.py:427
  40.2 0.0 collective-permute-done.8.refs_0_
  40.2 0.0 collective-permute-done.9.refs_1_
  40.2 0.0 collective-permute-done.10.refs_2_
  40.2 0.0 collective-permute-done.12.refs_3_
  40.2 1.1 %collective-permute-done.13.refs_4_ = bf16[8,4320]{1,0:T(8,128)(2,1)S(1)} collective-permute-done((bf16[8,4320]{1,0:T(8,128)(2,1)S(1)}, bf16[8,4320]{1,0:T(8,128)(2,1)S(1)}, u32[]{:S(2)}, u32[]{:S(2)}) %collective-permute-start.13) | collective-permute-done | bytes 69152 | tf_op jit(solution)/shard_map/ppermute | solution.py:365
  41.3 0.1 shard_map.75.refs_0_
  41.4 0.1 collective-permute-start.16
  41.4 1.6 %collective-permute-start.15 = (bf16[8,4320]{1,0:T(8,128)(2,1)S(1)}, bf16[8,4320]{1,0:T(8,128)(2,1)S(1)}, u32[]{:S(2)}, u32[]{:S(2)}) collective-permute-start(bf16[8,4320]{1,0:T(8,128)(2,1)S(1)} %shard_map.75.refs_0_), channel_id=1, source_target_pairs={{0,16},{8,24},{16,0},{24,8},{1,17},{9,25},{17,1},{25,9},{2,18},{10... | collective-permute-start | bytes 207368 | tf_op jit(solution)/shard_map/ppermute | solution.py:365
  43.0 0.3 collective-permute-start.14
  43.3 2.5 %collective-permute-done.16.refs_3_ = bf16[8,4320]{1,0:T(8,128)(2,1)S(1)} collective-permute-done((bf16[8,4320]{1,0:T(8,128)(2,1)S(1)}, bf16[8,4320]{1,0:T(8,128)(2,1)S(1)}, u32[]{:S(2)}, u32[]{:S(2)}) %collective-permute-start.16) | collective-permute-done | bytes 69152 | tf_op jit(solution)/shard_map/ppermute | solution.py:365
  45.8 1.6 %collective-permute-done.15.refs_2_ = bf16[8,4320]{1,0:T(8,128)(2,1)S(1)} collective-permute-done((bf16[8,4320]{1,0:T(8,128)(2,1)S(1)}, bf16[8,4320]{1,0:T(8,128)(2,1)S(1)}, u32[]{:S(2)}, u32[]{:S(2)}) %collective-permute-start.15) | collective-permute-done | bytes 69152 | tf_op jit(solution)/shard_map/ppermute | solution.py:365
  47.4 0.0 collective-permute-done.14.refs_1_
  47.4 0.1 all-to-all-done.1.refs_4_
  47.5 0.9 %shard_map.76 = (f32[16,864]{1,0:T(8,128)}, f32[32,3456]{1,0:T(8,128)}, bf16[32,8,128]{2,1,0:T(8,128)(2,1)}) custom-call(s32[1]{0:T(128)} %bitcast._.place, bf16[8,4320]{1,0:T(8,128)(2,1)S(1)} %shard_map.75.refs_0_, bf16[8,4320]{1,0:T(8,128)(2,1)S(1)} %collective-permute-done.14.refs_1_, bf16[8,4320]{1,0:T(8,128)(2,1)S(1)} %collective-permute-done.15.refs_2_, ...), custom_call_target="tpu_custom_call" | custom-call | flops 1000000000 | bytes 407556 | tf_op jit(solution)/shard_map/pallas_call | solution.py:349
  (2 shorter events, 0.1 us)
Async XLA Ops:
  0.6 11.6 %copy-start.1 = (bf16[1,4,64,1024]{3,2,1,0:T(8,128)(2,1)S(1)}, bf16[1,4,64,1024]{3,2,1,0:T(8,128)(2,1)}, u32[]{:S(2)}) copy-start(bf16[1,4,64,1024]{3,2,1,0:T(8,128)(2,1)} %param.4) | copy-start | bytes 1572868
  0.6 11.6 %copy-start.2 = (bf16[864,128]{1,0:T(8,128)(2,1)S(1)}, bf16[864,128]{1,0:T(8,128)(2,1)}, u32[]{:S(2)}) copy-start(bf16[864,128]{1,0:T(8,128)(2,1)} %w1.3) | copy-start | bytes 663556
  2.5 9.8 %collective-permute-start = (bf16[1,64,1024]{2,1,0:T(8,128)(2,1)}, bf16[1,64,1024]{2,1,0:T(8,128)(2,1)S(1)}, u32[]{:S(2)}, u32[]{:S(2)}) collective-permute-start(bf16[1,64,1024]{2,1,0:T(8,128)(2,1)} %get-tuple-element.25), channel_id=1, source_target_pairs={{0,1},{1,2},{2,3},{3,4},{4,5},{5,6},{6,7},{8,9},{9,10},{10,11},{11... | collective-permute-start | bytes 393224 | tf_op jit(solution)/shard_map/ppermute | solution.py:373
  7.3 12.2 %all-to-all-start = ((bf16[8,64,128]{2,1,0:T(8,128)(2,1)}), bf16[8,64,128]{2,1,0:T(8,128)(2,1)S(1)}, u32[]{:S(2)}, u32[]{:S(2)}) async-start(bf16[8,64,128]{2,1,0:T(8,128)(2,1)} %get-tuple-element.26), calls=%async_computation | async-start | bytes 262144 | tf_op jit(solution)/shard_map/all_to_all | solution.py:399
  12.2 2.7 %copy-start = (bf16[3456,256]{1,0:T(8,128)(2,1)S(1)}, bf16[3456,256]{1,0:T(8,128)(2,1)}, u32[]{:S(2)}) copy-start(bf16[3456,256]{1,0:T(8,128)(2,1)} %w2.3) | copy-start | bytes 5308420
  13.3 11.3 %collective-permute-start.2 = (bf16[16,64,128]{2,1,0:T(8,128)(2,1)S(1)}, bf16[16,64,128]{2,1,0:T(8,128)(2,1)S(1)}, u32[]{:S(2)}, u32[]{:S(2)}) collective-permute-start(bf16[16,64,128]{2,1,0:T(8,128)(2,1)S(1)} %shard_map.68.pack.refs_0_), channel_id=1, source_target_pairs={{0,16},{8,24},{16,0},{24,8},{1,17},{9,25},{17,1},{25,9},{2,18},{10... | collective-permute-start | bytes 786440 | tf_op jit(solution)/shard_map/ppermute | solution.py:365
  19.6 5.0 %collective-permute-start.3 = (bf16[8,16,128]{2,1,0:T(8,128)(2,1)S(1)}, bf16[8,16,128]{2,1,0:T(8,128)(2,1)S(1)}, u32[]{:S(2)}, u32[]{:S(2)}) collective-permute-start(bf16[8,16,128]{2,1,0:T(8,128)(2,1)S(1)} %get-tuple-element.30), channel_id=1, source_target_pairs={{0,8},{8,0},{16,24},{24,16},{1,9},{9,1},{17,25},{25,17},{2,10},{10... | collective-permute-start | bytes 98312 | tf_op jit(solution)/shard_map/ppermute | solution.py:365
  19.7 4.9 %collective-permute-start.4 = (bf16[8,16,128]{2,1,0:T(8,128)(2,1)S(1)}, bf16[8,16,128]{2,1,0:T(8,128)(2,1)S(1)}, u32[]{:S(2)}, u32[]{:S(2)}) collective-permute-start(bf16[8,16,128]{2,1,0:T(8,128)(2,1)S(1)} %get-tuple-element.31), channel_id=1, source_target_pairs={{0,16},{8,24},{16,0},{24,8},{1,17},{9,25},{17,1},{25,9},{2,18},{10... | collective-permute-start | bytes 98312 | tf_op jit(solution)/shard_map/ppermute | solution.py:365
  21.2 3.3 %collective-permute-start.5 = (bf16[8,16,128]{2,1,0:T(8,128)(2,1)S(1)}, bf16[8,16,128]{2,1,0:T(8,128)(2,1)S(1)}, u32[]{:S(2)}, u32[]{:S(2)}) collective-permute-start(bf16[8,16,128]{2,1,0:T(8,128)(2,1)S(1)} %get-tuple-element.32), channel_id=1, source_target_pairs={{0,24},{8,16},{16,8},{24,0},{1,25},{9,17},{17,9},{25,1},{2,26},{10... | collective-permute-start | bytes 98312 | tf_op jit(solution)/shard_map/ppermute | solution.py:365
  21.5 4.8 %collective-permute-start.1 = (bf16[16,64,128]{2,1,0:T(8,128)(2,1)S(1)}, bf16[16,64,128]{2,1,0:T(8,128)(2,1)S(1)}, u32[]{:S(2)}, u32[]{:S(2)}) collective-permute-start(bf16[16,64,128]{2,1,0:T(8,128)(2,1)S(1)} %shard_map.68.pack.refs_0_), channel_id=1, source_target_pairs={{0,8},{8,0},{16,24},{24,16},{1,9},{9,1},{17,25},{25,17},{2,10},{10... | collective-permute-start | bytes 786440 | tf_op jit(solution)/shard_map/ppermute | solution.py:365
  24.6 1.8 %collective-permute-start.6 = (bf16[16,64,128]{2,1,0:T(8,128)(2,1)S(1)}, bf16[16,64,128]{2,1,0:T(8,128)(2,1)S(1)}, u32[]{:S(2)}, u32[]{:S(2)}) collective-permute-start(bf16[16,64,128]{2,1,0:T(8,128)(2,1)S(1)} %collective-permute-done.2.refs_2_), channel_id=1, source_target_pairs={{0,8},{8,0},{16,24},{24,16},{1,9},{9,1},{17,25},{25,17},{2,10},{10... | collective-permute-start | bytes 786440 | tf_op jit(solution)/shard_map/ppermute | solution.py:365
  24.8 1.5 %collective-permute-start.7 = (bf16[64,864]{1,0:T(8,128)(2,1)S(1)}, bf16[64,864]{1,0:T(8,128)(2,1)S(1)}, u32[]{:S(2)}, u32[]{:S(2)}) collective-permute-start(bf16[64,864]{1,0:T(8,128)(2,1)S(1)} %get-tuple-element.29), channel_id=1, source_target_pairs={{0,8},{8,0},{16,24},{24,16},{1,9},{9,1},{17,25},{25,17},{2,10},{10... | collective-permute-start | bytes 331784 | tf_op jit(solution)/shard_map/ppermute | solution.py:365
  26.8 8.0 %collective-permute-start.11 = (bf16[2,8,4320]{2,1,0:T(8,128)(2,1)S(1)}, bf16[2,8,4320]{2,1,0:T(8,128)(2,1)S(1)}, u32[]{:S(2)}, u32[]{:S(2)}) collective-permute-start(bf16[2,8,4320]{2,1,0:T(8,128)(2,1)S(1)} %get-tuple-element.39), channel_id=1, source_target_pairs={{0,1},{1,0},{2,3},{3,2},{4,5},{5,4},{6,7},{7,6},{8,9},{9,8},{10,11... | collective-permute-start | bytes 414728 | tf_op jit(solution)/shard_map/ppermute | solution.py:365
  27.1 13.1 %collective-permute-start.8 = (bf16[8,4320]{1,0:T(8,128)(2,1)S(1)}, bf16[8,4320]{1,0:T(8,128)(2,1)S(1)}, u32[]{:S(2)}, u32[]{:S(2)}) collective-permute-start(bf16[8,4320]{1,0:T(8,128)(2,1)S(1)} %get-tuple-element.36), channel_id=1, source_target_pairs={{0,1},{1,0},{2,3},{3,2},{4,5},{5,4},{6,7},{7,6},{8,9},{9,8},{10,11... | collective-permute-start | bytes 207368 | tf_op jit(solution)/shard_map/ppermute | solution.py:365
  28.9 11.2 %collective-permute-start.9 = (bf16[8,4320]{1,0:T(8,128)(2,1)S(1)}, bf16[8,4320]{1,0:T(8,128)(2,1)S(1)}, u32[]{:S(2)}, u32[]{:S(2)}) collective-permute-start(bf16[8,4320]{1,0:T(8,128)(2,1)S(1)} %get-tuple-element.37), channel_id=1, source_target_pairs={{0,2},{1,3},{2,0},{3,1},{4,6},{5,7},{6,4},{7,5},{8,10},{9,11},{10,... | collective-permute-start | bytes 207368 | tf_op jit(solution)/shard_map/ppermute | solution.py:365
  28.9 11.3 %collective-permute-start.10 = (bf16[8,4320]{1,0:T(8,128)(2,1)S(1)}, bf16[8,4320]{1,0:T(8,128)(2,1)S(1)}, u32[]{:S(2)}, u32[]{:S(2)}) collective-permute-start(bf16[8,4320]{1,0:T(8,128)(2,1)S(1)} %get-tuple-element.38), channel_id=1, source_target_pairs={{0,3},{1,2},{2,1},{3,0},{4,7},{5,6},{6,5},{7,4},{8,11},{9,10},{10,... | collective-permute-start | bytes 207368 | tf_op jit(solution)/shard_map/ppermute | solution.py:365
  34.9 5.3 %collective-permute-start.12 = (bf16[8,4320]{1,0:T(8,128)(2,1)S(1)}, bf16[8,4320]{1,0:T(8,128)(2,1)S(1)}, u32[]{:S(2)}, u32[]{:S(2)}) collective-permute-start(bf16[8,4320]{1,0:T(8,128)(2,1)S(1)} %get-tuple-element.41), channel_id=1, source_target_pairs={{0,4},{1,5},{2,6},{3,7},{4,0},{5,1},{6,2},{7,3},{8,12},{9,13},{10,... | collective-permute-start | bytes 207368 | tf_op jit(solution)/shard_map/ppermute | solution.py:365
  35.0 6.3 %collective-permute-start.13 = (bf16[8,4320]{1,0:T(8,128)(2,1)S(1)}, bf16[8,4320]{1,0:T(8,128)(2,1)S(1)}, u32[]{:S(2)}, u32[]{:S(2)}) collective-permute-start(bf16[8,4320]{1,0:T(8,128)(2,1)S(1)} %get-tuple-element.42), channel_id=1, source_target_pairs={{0,6},{1,7},{2,4},{3,5},{4,2},{5,3},{6,0},{7,1},{8,14},{9,15},{10,... | collective-permute-start | bytes 207368 | tf_op jit(solution)/shard_map/ppermute | solution.py:365
  35.8 11.7 %all-to-all-start.1 = ((bf16[8,64,128]{2,1,0:T(8,128)(2,1)}), bf16[8,64,128]{2,1,0:T(8,128)(2,1)S(1)}, u32[]{:S(2)}, u32[]{:S(2)}) async-start(bf16[8,64,128]{2,1,0:T(8,128)(2,1)} %shard_map.71), calls=%async_computation.1 | async-start | bytes 262144 | tf_op jit(solution)/shard_map/all_to_all | solution.py:427
  41.4 4.5 %collective-permute-start.16 = (bf16[8,4320]{1,0:T(8,128)(2,1)S(1)}, bf16[8,4320]{1,0:T(8,128)(2,1)S(1)}, u32[]{:S(2)}, u32[]{:S(2)}) collective-permute-start(bf16[8,4320]{1,0:T(8,128)(2,1)S(1)} %shard_map.75.refs_0_), channel_id=1, source_target_pairs={{0,24},{8,16},{16,8},{24,0},{1,25},{9,17},{17,9},{25,1},{2,26},{10... | collective-permute-start | bytes 207368 | tf_op jit(solution)/shard_map/ppermute | solution.py:365
  41.4 6.0 %collective-permute-start.15 = (bf16[8,4320]{1,0:T(8,128)(2,1)S(1)}, bf16[8,4320]{1,0:T(8,128)(2,1)S(1)}, u32[]{:S(2)}, u32[]{:S(2)}) collective-permute-start(bf16[8,4320]{1,0:T(8,128)(2,1)S(1)} %shard_map.75.refs_0_), channel_id=1, source_target_pairs={{0,16},{8,24},{16,0},{24,8},{1,17},{9,25},{17,1},{25,9},{2,18},{10... | collective-permute-start | bytes 207368 | tf_op jit(solution)/shard_map/ppermute | solution.py:365
  43.0 4.4 %collective-permute-start.14 = (bf16[8,4320]{1,0:T(8,128)(2,1)S(1)}, bf16[8,4320]{1,0:T(8,128)(2,1)S(1)}, u32[]{:S(2)}, u32[]{:S(2)}) collective-permute-start(bf16[8,4320]{1,0:T(8,128)(2,1)S(1)} %shard_map.75.refs_0_), channel_id=1, source_target_pairs={{0,8},{8,0},{16,24},{24,16},{1,9},{9,1},{17,25},{25,17},{2,10},{10... | collective-permute-start | bytes 207368 | tf_op jit(solution)/shard_map/ppermute | solution.py:365

commit v10 on v8

--- a/solution.py
+++ b/solution.py
@@ -62,9 +62,13 @@
 
 
 def fill_hidden(picked, i, w_ext, hidden, slope_t):
+    rows = []
     for p in range(2):
         patches = [picked[2 * i + a, 2 * p + b] for a in range(3) for b in range(3)]
-        full = dot(jnp.concatenate(patches, axis=1), w_ext[...])
+        rows.append(jnp.concatenate(patches, axis=1))
+    product = dot(jnp.concatenate(rows, axis=0), w_ext[...])
+    for p in range(2):
+        full = product[p * CELLS : (p + 1) * CELLS]
         before = jnp.concatenate(
             [jnp.zeros((NJ, 128), F32), full[: CELLS - NJ, 256:384]], axis=0
         )
@@ -170,9 +174,7 @@
         products += [both[:, n * 128 : (n + 1) * 128] for n in range(len(columns))]
     for full in products:
         side = jnp.where(lane < 64, full[0:128], full[256:384])
-        side = jnp.where((lane < 64) | (lane >= 96), side, 0.0)
-        own = jnp.where(lane < 32, 0.0, full[128:256])
-        frames.append(own + pltpu.roll(side, 64, axis=1))
+        frames.append(full[128:256] + pltpu.roll(side, 64, axis=1))
     if pieces == 1:
         for t in range(9):
             outs[0][:, t * 96 : (t + 1) * 96] = frames[t][:, 32:]

time: 49 us -> 48.9 us (level)
  no operation moved by 1% of the time
where the time goes in v10:
time: 48.9 us; the launch traced here: 48.5 us
  starting transfers between devices  25.1 us (51%)
  waiting for transfers between devices  13.5 us (28%)
  Pallas kernels  9.06 us (19%)
  between operations  0.81 us (2%)
    ppermute x16, starting transfers between devices, swap_ranks(): lax.ppermute(block, axis, [(i, i ^ k) for i in range(lax.axis_size(axis))])  11 us
    ppermute x16, waiting for transfers between devices, swap_ranks(): lax.ppermute(block, axis, [(i, i ^ k) for i in range(lax.axis_size(axis))])  10.4 us
    pallas_call x10, Pallas kernels, call(): pl.pallas_call(kernel, out_shape=out_shape, in_specs=[spec(n, spaces) for...  9.06 us
    all_to_all x1, starting transfers between devices, on_device(): lax.all_to_all(parcels, 'space', split_axis=0, concat_axis=0, tiled=True)  4.89 us
    ppermute x1, starting transfers between devices, from_below(): lax.ppermute(block, axis, [(i - 1, i) for i in range(1, lax.axis_size(axi...  4.85 us
    all_to_all x1, starting transfers between devices, exchanged(): lax.all_to_all(parts, 'space', split_axis=0, concat_axis=0, tiled=True)  4.4 us
    all_to_all x1, waiting for transfers between devices, on_device(): lax.all_to_all(parcels, 'space', split_axis=0, concat_axis=0, tiled=True)  3.02 us
  transfers between devices with their start and end apart: 19, of which 7 were waited for; matrix products, arithmetic and copies ran while one was open for 0% of the time, Pallas kernels for 12%

profile of v10, /device:TPU:0, one launch (start us, length us, event | category | flops | bytes accessed | tf_op | source)
XLA Modules:
  0.0 48.5 jit_solution(8947940567523639830)
XLA Ops:
  0.6 0.0 copy-start.1
  0.6 0.0 copy-start.2
  0.7 1.9 %shard_map.67 = (bf16[8,64,128]{2,1,0:T(8,128)(2,1)}, bf16[1,64,1024]{2,1,0:T(8,128)(2,1)}) custom-call(s32[1]{0:T(128)} %bitcast._.place, s32[1]{0:T(128)} %bitcast.2.__.slot, bf16[32,8,128]{2,1,0:T(8,128)(2,1)} %bitcast.8, bf16[4,64,1024]{2,1,0:T(8,128)(2,1)} %bitcast.5), custom_call_target="tpu_custom_call" | custom-call | flops 1000000000 | bytes 589832 | tf_op jit(solution)/shard_map/pallas_call | solution.py:350
  2.5 4.8 %collective-permute-start = (bf16[1,64,1024]{2,1,0:T(8,128)(2,1)}, bf16[1,64,1024]{2,1,0:T(8,128)(2,1)S(1)}, u32[]{:S(2)}, u32[]{:S(2)}) collective-permute-start(bf16[1,64,1024]{2,1,0:T(8,128)(2,1)} %get-tuple-element.25), channel_id=1, source_target_pairs={{0,1},{1,2},{2,3},{3,4},{4,5},{5,6},{6,7},{8,9},{9,10},{10,11},{11... | collective-permute-start | bytes 393224 | tf_op jit(solution)/shard_map/ppermute | solution.py:374
  7.4 4.9 %all-to-all-start = ((bf16[8,64,128]{2,1,0:T(8,128)(2,1)}), bf16[8,64,128]{2,1,0:T(8,128)(2,1)S(1)}, u32[]{:S(2)}, u32[]{:S(2)}) async-start(bf16[8,64,128]{2,1,0:T(8,128)(2,1)} %get-tuple-element.26), calls=%async_computation | async-start | bytes 262144 | tf_op jit(solution)/shard_map/all_to_all | solution.py:400
  12.3 0.0 copy-start
  12.3 0.0 collective-permute-done.halo
  12.3 0.0 copy-done.1
  12.3 0.0 copy-done.2
  12.3 1.0 %shard_map.68.pack.refs_0_ = bf16[16,64,128]{2,1,0:T(8,128)(2,1)S(1)} custom-call(bf16[4,64,1024]{2,1,0:T(8,128)(2,1)S(1)} %bitcast.6, bf16[1,64,1024]{2,1,0:T(8,128)(2,1)S(1)} %collective-permute-done.halo, bf16[864,128]{1,0:T(8,128)(2,1)S(1)} %copy-done.2), custom_call_target="tpu_custom_call" | custom-call | flops 1000000000 | bytes 876544 | tf_op jit(solution)/shard_map/pallas_call | solution.py:350
  13.3 1.6 %collective-permute-start.2 = (bf16[16,64,128]{2,1,0:T(8,128)(2,1)S(1)}, bf16[16,64,128]{2,1,0:T(8,128)(2,1)S(1)}, u32[]{:S(2)}, u32[]{:S(2)}) collective-permute-start(bf16[16,64,128]{2,1,0:T(8,128)(2,1)S(1)} %shard_map.68.pack.refs_0_), channel_id=1, source_target_pairs={{0,16},{8,24},{16,0},{24,8},{1,17},{9,25},{17,1},{25,9},{2,18},{10... | collective-permute-start | bytes 786440 | tf_op jit(solution)/shard_map/ppermute | solution.py:366
  14.9 0.0 copy-done
  14.9 1.7 %shard_map.71 = bf16[8,64,128]{2,1,0:T(8,128)(2,1)} custom-call(bf16[16,64,128]{2,1,0:T(8,128)(2,1)S(1)} %shard_map.68.pack.refs_0_, bf16[3456,256]{1,0:T(8,128)(2,1)S(1)} %copy-done), custom_call_target="tpu_custom_call" | custom-call | flops 1000000000 | bytes 2031616 | tf_op jit(solution)/shard_map/pallas_call | solution.py:350
  16.6 3.0 %all-to-all-done.cot = bf16[8,64,128]{2,1,0:T(8,128)(2,1)S(1)} async-done(((bf16[8,64,128]{2,1,0:T(8,128)(2,1)}), bf16[8,64,128]{2,1,0:T(8,128)(2,1)S(1)}, u32[]{:S(2)}, u32[]{:S(2)}) %all-to-all-start) | async-done | bytes 131104 | tf_op jit(solution)/shard_map/all_to_all | solution.py:400
  19.6 0.1 collective-permute-start.3
  19.7 1.6 %collective-permute-start.4 = (bf16[8,16,128]{2,1,0:T(8,128)(2,1)S(1)}, bf16[8,16,128]{2,1,0:T(8,128)(2,1)S(1)}, u32[]{:S(2)}, u32[]{:S(2)}) collective-permute-start(bf16[8,16,128]{2,1,0:T(8,128)(2,1)S(1)} %get-tuple-element.31), channel_id=1, source_target_pairs={{0,16},{8,24},{16,0},{24,8},{1,17},{9,25},{17,1},{25,9},{2,18},{10... | collective-permute-start | bytes 98312 | tf_op jit(solution)/shard_map/ppermute | solution.py:366
  21.3 0.3 collective-permute-start.5
  21.6 0.3 collective-permute-start.1
  21.9 2.7 %shard_map.69 = (bf16[64,864]{1,0:T(8,128)(2,1)S(1)}, bf16[64,864]{1,0:T(8,128)(2,1)S(1)}) custom-call(s32[1]{0:T(128)} %bitcast._.place, s32[1]{0:T(128)} %bitcast.2.__.slot, bf16[4,64,1024]{2,1,0:T(8,128)(2,1)S(1)} %bitcast.7, bf16[1,64,1024]{2,1,0:T(8,128)(2,1)S(1)} %collective-permute-done.halo, bf16[864,128]{1,0:T(8,128)(2,1)S(1)} %copy-done.2, ...), custom_call_target="tpu_custom_call" | custom-call | flops 1000000000 | bytes 2777096 | tf_op jit(solution)/shard_map/pallas_call | solution.py:350
  24.6 0.0 collective-permute-done.3.refs_1_
  24.6 0.0 collective-permute-done.4.refs_2_
  24.6 0.0 collective-permute-done.5.refs_3_
  24.6 0.0 collective-permute-done.2.refs_2_
  24.7 0.2 collective-permute-start.6
  24.9 0.3 collective-permute-start.7
  25.2 0.3 shard_map.72.refs_4_
  25.6 0.9 %collective-permute-done.7.refs_6_ = bf16[64,864]{1,0:T(8,128)(2,1)S(1)} collective-permute-done((bf16[64,864]{1,0:T(8,128)(2,1)S(1)}, bf16[64,864]{1,0:T(8,128)(2,1)S(1)}, u32[]{:S(2)}, u32[]{:S(2)}) %collective-permute-start.7) | collective-permute-done | bytes 110624 | tf_op jit(solution)/shard_map/ppermute | solution.py:366
  26.4 0.0 collective-permute-done.1.refs_1_
  26.4 0.0 collective-permute-done.6.refs_3_
  26.4 0.5 %shard_map.73 = (f32[8,4320]{1,0:T(8,128)S(1)}, bf16[8,4320]{1,0:T(8,128)(2,1)S(1)}, bf16[8,4320]{1,0:T(8,128)(2,1)S(1)}, bf16[8,4320]{1,0:T(8,128)(2,1)S(1)}, b...) custom-call(bf16[16,64,128]{2,1,0:T(8,128)(2,1)S(1)} %shard_map.68.pack.refs_0_, ...), custom_call_target="tpu_custom_call" | custom-call | flops 1000000000 | bytes 1794048 | tf_op jit(solution)/shard_map/pallas_call | solution.py:350
  26.9 0.3 collective-permute-start.11
  27.2 1.8 %collective-permute-start.8 = (bf16[8,4320]{1,0:T(8,128)(2,1)S(1)}, bf16[8,4320]{1,0:T(8,128)(2,1)S(1)}, u32[]{:S(2)}, u32[]{:S(2)}) collective-permute-start(bf16[8,4320]{1,0:T(8,128)(2,1)S(1)} %get-tuple-element.36), channel_id=1, source_target_pairs={{0,1},{1,0},{2,3},{3,2},{4,5},{5,4},{6,7},{7,6},{8,9},{9,8},{10,11... | collective-permute-start | bytes 207368 | tf_op jit(solution)/shard_map/ppermute | solution.py:366
  29.0 0.0 collective-permute-start.9
  29.0 1.7 %collective-permute-start.10 = (bf16[8,4320]{1,0:T(8,128)(2,1)S(1)}, bf16[8,4320]{1,0:T(8,128)(2,1)S(1)}, u32[]{:S(2)}, u32[]{:S(2)}) collective-permute-start(bf16[8,4320]{1,0:T(8,128)(2,1)S(1)} %get-tuple-element.38), channel_id=1, source_target_pairs={{0,3},{1,2},{2,1},{3,0},{4,7},{5,6},{6,5},{7,4},{8,11},{9,10},{10,... | collective-permute-start | bytes 207368 | tf_op jit(solution)/shard_map/ppermute | solution.py:366
  30.7 4.3 %collective-permute-done.11.lent = bf16[2,8,4320]{2,1,0:T(8,128)(2,1)S(1)} collective-permute-done((bf16[2,8,4320]{2,1,0:T(8,128)(2,1)S(1)}, bf16[2,8,4320]{2,1,0:T(8,128)(2,1)S(1)}, u32[]{:S(2)}, u32[]{:S(2)}) %collective-permute-start.11) | collective-permute-done | bytes 138272 | tf_op jit(solution)/shard_map/ppermute | solution.py:366
  35.0 0.1 collective-permute-start.12
  35.1 0.8 %collective-permute-start.13 = (bf16[8,4320]{1,0:T(8,128)(2,1)S(1)}, bf16[8,4320]{1,0:T(8,128)(2,1)S(1)}, u32[]{:S(2)}, u32[]{:S(2)}) collective-permute-start(bf16[8,4320]{1,0:T(8,128)(2,1)S(1)} %get-tuple-element.42), channel_id=1, source_target_pairs={{0,6},{1,7},{2,4},{3,5},{4,2},{5,3},{6,0},{7,1},{8,14},{9,15},{10,... | collective-permute-start | bytes 207368 | tf_op jit(solution)/shard_map/ppermute | solution.py:366
  35.9 4.4 %all-to-all-start.1 = ((bf16[8,64,128]{2,1,0:T(8,128)(2,1)}), bf16[8,64,128]{2,1,0:T(8,128)(2,1)S(1)}, u32[]{:S(2)}, u32[]{:S(2)}) async-start(bf16[8,64,128]{2,1,0:T(8,128)(2,1)} %shard_map.71), calls=%async_computation.1 | async-start | bytes 262144 | tf_op jit(solution)/shard_map/all_to_all | solution.py:428
  40.3 0.0 collective-permute-done.8.refs_0_
  40.3 0.0 collective-permute-done.9.refs_1_
  40.3 0.0 collective-permute-done.10.refs_2_
  40.3 0.0 collective-permute-done.12.refs_3_
  40.3 1.1 %collective-permute-done.13.refs_4_ = bf16[8,4320]{1,0:T(8,128)(2,1)S(1)} collective-permute-done((bf16[8,4320]{1,0:T(8,128)(2,1)S(1)}, bf16[8,4320]{1,0:T(8,128)(2,1)S(1)}, u32[]{:S(2)}, u32[]{:S(2)}) %collective-permute-start.13) | collective-permute-done | bytes 69152 | tf_op jit(solution)/shard_map/ppermute | solution.py:366
  41.4 0.1 shard_map.75.refs_0_
  41.5 0.1 collective-permute-start.16
  41.5 1.6 %collective-permute-start.15 = (bf16[8,4320]{1,0:T(8,128)(2,1)S(1)}, bf16[8,4320]{1,0:T(8,128)(2,1)S(1)}, u32[]{:S(2)}, u32[]{:S(2)}) collective-permute-start(bf16[8,4320]{1,0:T(8,128)(2,1)S(1)} %shard_map.75.refs_0_), channel_id=1, source_target_pairs={{0,16},{8,24},{16,0},{24,8},{1,17},{9,25},{17,1},{25,9},{2,18},{10... | collective-permute-start | bytes 207368 | tf_op jit(solution)/shard_map/ppermute | solution.py:366
  43.1 0.3 collective-permute-start.14
  43.4 2.5 %collective-permute-done.16.refs_3_ = bf16[8,4320]{1,0:T(8,128)(2,1)S(1)} collective-permute-done((bf16[8,4320]{1,0:T(8,128)(2,1)S(1)}, bf16[8,4320]{1,0:T(8,128)(2,1)S(1)}, u32[]{:S(2)}, u32[]{:S(2)}) %collective-permute-start.16) | collective-permute-done | bytes 69152 | tf_op jit(solution)/shard_map/ppermute | solution.py:366
  45.9 1.6 %collective-permute-done.15.refs_2_ = bf16[8,4320]{1,0:T(8,128)(2,1)S(1)} collective-permute-done((bf16[8,4320]{1,0:T(8,128)(2,1)S(1)}, bf16[8,4320]{1,0:T(8,128)(2,1)S(1)}, u32[]{:S(2)}, u32[]{:S(2)}) %collective-permute-start.15) | collective-permute-done | bytes 69152 | tf_op jit(solution)/shard_map/ppermute | solution.py:366
  47.5 0.0 collective-permute-done.14.refs_1_
  47.5 0.1 all-to-all-done.1.refs_4_
  47.6 0.9 %shard_map.76 = (f32[16,864]{1,0:T(8,128)}, f32[32,3456]{1,0:T(8,128)}, bf16[32,8,128]{2,1,0:T(8,128)(2,1)}) custom-call(s32[1]{0:T(128)} %bitcast._.place, bf16[8,4320]{1,0:T(8,128)(2,1)S(1)} %shard_map.75.refs_0_, bf16[8,4320]{1,0:T(8,128)(2,1)S(1)} %collective-permute-done.14.refs_1_, bf16[8,4320]{1,0:T(8,128)(2,1)S(1)} %collective-permute-done.15.refs_2_, ...), custom_call_target="tpu_custom_call" | custom-call | flops 1000000000 | bytes 407556 | tf_op jit(solution)/shard_map/pallas_call | solution.py:350
  (2 shorter events, 0.1 us)
Async XLA Ops:
  0.6 11.6 %copy-start.1 = (bf16[1,4,64,1024]{3,2,1,0:T(8,128)(2,1)S(1)}, bf16[1,4,64,1024]{3,2,1,0:T(8,128)(2,1)}, u32[]{:S(2)}) copy-start(bf16[1,4,64,1024]{3,2,1,0:T(8,128)(2,1)} %param.4) | copy-start | bytes 1572868
  0.6 11.6 %copy-start.2 = (bf16[864,128]{1,0:T(8,128)(2,1)S(1)}, bf16[864,128]{1,0:T(8,128)(2,1)}, u32[]{:S(2)}) copy-start(bf16[864,128]{1,0:T(8,128)(2,1)} %w1.3) | copy-start | bytes 663556
  2.5 9.8 %collective-permute-start = (bf16[1,64,1024]{2,1,0:T(8,128)(2,1)}, bf16[1,64,1024]{2,1,0:T(8,128)(2,1)S(1)}, u32[]{:S(2)}, u32[]{:S(2)}) collective-permute-start(bf16[1,64,1024]{2,1,0:T(8,128)(2,1)} %get-tuple-element.25), channel_id=1, source_target_pairs={{0,1},{1,2},{2,3},{3,4},{4,5},{5,6},{6,7},{8,9},{9,10},{10,11},{11... | collective-permute-start | bytes 393224 | tf_op jit(solution)/shard_map/ppermute | solution.py:374
  7.4 12.2 %all-to-all-start = ((bf16[8,64,128]{2,1,0:T(8,128)(2,1)}), bf16[8,64,128]{2,1,0:T(8,128)(2,1)S(1)}, u32[]{:S(2)}, u32[]{:S(2)}) async-start(bf16[8,64,128]{2,1,0:T(8,128)(2,1)} %get-tuple-element.26), calls=%async_computation | async-start | bytes 262144 | tf_op jit(solution)/shard_map/all_to_all | solution.py:400
  12.3 2.7 %copy-start = (bf16[3456,256]{1,0:T(8,128)(2,1)S(1)}, bf16[3456,256]{1,0:T(8,128)(2,1)}, u32[]{:S(2)}) copy-start(bf16[3456,256]{1,0:T(8,128)(2,1)} %w2.3) | copy-start | bytes 5308420
  13.3 11.3 %collective-permute-start.2 = (bf16[16,64,128]{2,1,0:T(8,128)(2,1)S(1)}, bf16[16,64,128]{2,1,0:T(8,128)(2,1)S(1)}, u32[]{:S(2)}, u32[]{:S(2)}) collective-permute-start(bf16[16,64,128]{2,1,0:T(8,128)(2,1)S(1)} %shard_map.68.pack.refs_0_), channel_id=1, source_target_pairs={{0,16},{8,24},{16,0},{24,8},{1,17},{9,25},{17,1},{25,9},{2,18},{10... | collective-permute-start | bytes 786440 | tf_op jit(solution)/shard_map/ppermute | solution.py:366
  19.6 5.0 %collective-permute-start.3 = (bf16[8,16,128]{2,1,0:T(8,128)(2,1)S(1)}, bf16[8,16,128]{2,1,0:T(8,128)(2,1)S(1)}, u32[]{:S(2)}, u32[]{:S(2)}) collective-permute-start(bf16[8,16,128]{2,1,0:T(8,128)(2,1)S(1)} %get-tuple-element.30), channel_id=1, source_target_pairs={{0,8},{8,0},{16,24},{24,16},{1,9},{9,1},{17,25},{25,17},{2,10},{10... | collective-permute-start | bytes 98312 | tf_op jit(solution)/shard_map/ppermute | solution.py:366
  19.7 4.9 %collective-permute-start.4 = (bf16[8,16,128]{2,1,0:T(8,128)(2,1)S(1)}, bf16[8,16,128]{2,1,0:T(8,128)(2,1)S(1)}, u32[]{:S(2)}, u32[]{:S(2)}) collective-permute-start(bf16[8,16,128]{2,1,0:T(8,128)(2,1)S(1)} %get-tuple-element.31), channel_id=1, source_target_pairs={{0,16},{8,24},{16,0},{24,8},{1,17},{9,25},{17,1},{25,9},{2,18},{10... | collective-permute-start | bytes 98312 | tf_op jit(solution)/shard_map/ppermute | solution.py:366
  21.3 3.3 %collective-permute-start.5 = (bf16[8,16,128]{2,1,0:T(8,128)(2,1)S(1)}, bf16[8,16,128]{2,1,0:T(8,128)(2,1)S(1)}, u32[]{:S(2)}, u32[]{:S(2)}) collective-permute-start(bf16[8,16,128]{2,1,0:T(8,128)(2,1)S(1)} %get-tuple-element.32), channel_id=1, source_target_pairs={{0,24},{8,16},{16,8},{24,0},{1,25},{9,17},{17,9},{25,1},{2,26},{10... | collective-permute-start | bytes 98312 | tf_op jit(solution)/shard_map/ppermute | solution.py:366
  21.6 4.8 %collective-permute-start.1 = (bf16[16,64,128]{2,1,0:T(8,128)(2,1)S(1)}, bf16[16,64,128]{2,1,0:T(8,128)(2,1)S(1)}, u32[]{:S(2)}, u32[]{:S(2)}) collective-permute-start(bf16[16,64,128]{2,1,0:T(8,128)(2,1)S(1)} %shard_map.68.pack.refs_0_), channel_id=1, source_target_pairs={{0,8},{8,0},{16,24},{24,16},{1,9},{9,1},{17,25},{25,17},{2,10},{10... | collective-permute-start | bytes 786440 | tf_op jit(solution)/shard_map/ppermute | solution.py:366
  24.7 1.8 %collective-permute-start.6 = (bf16[16,64,128]{2,1,0:T(8,128)(2,1)S(1)}, bf16[16,64,128]{2,1,0:T(8,128)(2,1)S(1)}, u32[]{:S(2)}, u32[]{:S(2)}) collective-permute-start(bf16[16,64,128]{2,1,0:T(8,128)(2,1)S(1)} %collective-permute-done.2.refs_2_), channel_id=1, source_target_pairs={{0,8},{8,0},{16,24},{24,16},{1,9},{9,1},{17,25},{25,17},{2,10},{10... | collective-permute-start | bytes 786440 | tf_op jit(solution)/shard_map/ppermute | solution.py:366
  24.9 1.5 %collective-permute-start.7 = (bf16[64,864]{1,0:T(8,128)(2,1)S(1)}, bf16[64,864]{1,0:T(8,128)(2,1)S(1)}, u32[]{:S(2)}, u32[]{:S(2)}) collective-permute-start(bf16[64,864]{1,0:T(8,128)(2,1)S(1)} %get-tuple-element.29), channel_id=1, source_target_pairs={{0,8},{8,0},{16,24},{24,16},{1,9},{9,1},{17,25},{25,17},{2,10},{10... | collective-permute-start | bytes 331784 | tf_op jit(solution)/shard_map/ppermute | solution.py:366
  26.9 8.0 %collective-permute-start.11 = (bf16[2,8,4320]{2,1,0:T(8,128)(2,1)S(1)}, bf16[2,8,4320]{2,1,0:T(8,128)(2,1)S(1)}, u32[]{:S(2)}, u32[]{:S(2)}) collective-permute-start(bf16[2,8,4320]{2,1,0:T(8,128)(2,1)S(1)} %get-tuple-element.39), channel_id=1, source_target_pairs={{0,1},{1,0},{2,3},{3,2},{4,5},{5,4},{6,7},{7,6},{8,9},{9,8},{10,11... | collective-permute-start | bytes 414728 | tf_op jit(solution)/shard_map/ppermute | solution.py:366
  27.2 13.1 %collective-permute-start.8 = (bf16[8,4320]{1,0:T(8,128)(2,1)S(1)}, bf16[8,4320]{1,0:T(8,128)(2,1)S(1)}, u32[]{:S(2)}, u32[]{:S(2)}) collective-permute-start(bf16[8,4320]{1,0:T(8,128)(2,1)S(1)} %get-tuple-element.36), channel_id=1, source_target_pairs={{0,1},{1,0},{2,3},{3,2},{4,5},{5,4},{6,7},{7,6},{8,9},{9,8},{10,11... | collective-permute-start | bytes 207368 | tf_op jit(solution)/shard_map/ppermute | solution.py:366
  29.0 11.2 %collective-permute-start.9 = (bf16[8,4320]{1,0:T(8,128)(2,1)S(1)}, bf16[8,4320]{1,0:T(8,128)(2,1)S(1)}, u32[]{:S(2)}, u32[]{:S(2)}) collective-permute-start(bf16[8,4320]{1,0:T(8,128)(2,1)S(1)} %get-tuple-element.37), channel_id=1, source_target_pairs={{0,2},{1,3},{2,0},{3,1},{4,6},{5,7},{6,4},{7,5},{8,10},{9,11},{10,... | collective-permute-start | bytes 207368 | tf_op jit(solution)/shard_map/ppermute | solution.py:366
  29.0 11.3 %collective-permute-start.10 = (bf16[8,4320]{1,0:T(8,128)(2,1)S(1)}, bf16[8,4320]{1,0:T(8,128)(2,1)S(1)}, u32[]{:S(2)}, u32[]{:S(2)}) collective-permute-start(bf16[8,4320]{1,0:T(8,128)(2,1)S(1)} %get-tuple-element.38), channel_id=1, source_target_pairs={{0,3},{1,2},{2,1},{3,0},{4,7},{5,6},{6,5},{7,4},{8,11},{9,10},{10,... | collective-permute-start | bytes 207368 | tf_op jit(solution)/shard_map/ppermute | solution.py:366
  35.0 5.3 %collective-permute-start.12 = (bf16[8,4320]{1,0:T(8,128)(2,1)S(1)}, bf16[8,4320]{1,0:T(8,128)(2,1)S(1)}, u32[]{:S(2)}, u32[]{:S(2)}) collective-permute-start(bf16[8,4320]{1,0:T(8,128)(2,1)S(1)} %get-tuple-element.41), channel_id=1, source_target_pairs={{0,4},{1,5},{2,6},{3,7},{4,0},{5,1},{6,2},{7,3},{8,12},{9,13},{10,... | collective-permute-start | bytes 207368 | tf_op jit(solution)/shard_map/ppermute | solution.py:366
  35.1 6.3 %collective-permute-start.13 = (bf16[8,4320]{1,0:T(8,128)(2,1)S(1)}, bf16[8,4320]{1,0:T(8,128)(2,1)S(1)}, u32[]{:S(2)}, u32[]{:S(2)}) collective-permute-start(bf16[8,4320]{1,0:T(8,128)(2,1)S(1)} %get-tuple-element.42), channel_id=1, source_target_pairs={{0,6},{1,7},{2,4},{3,5},{4,2},{5,3},{6,0},{7,1},{8,14},{9,15},{10,... | collective-permute-start | bytes 207368 | tf_op jit(solution)/shard_map/ppermute | solution.py:366
  35.9 11.7 %all-to-all-start.1 = ((bf16[8,64,128]{2,1,0:T(8,128)(2,1)}), bf16[8,64,128]{2,1,0:T(8,128)(2,1)S(1)}, u32[]{:S(2)}, u32[]{:S(2)}) async-start(bf16[8,64,128]{2,1,0:T(8,128)(2,1)} %shard_map.71), calls=%async_computation.1 | async-start | bytes 262144 | tf_op jit(solution)/shard_map/all_to_all | solution.py:428
  41.5 4.5 %collective-permute-start.16 = (bf16[8,4320]{1,0:T(8,128)(2,1)S(1)}, bf16[8,4320]{1,0:T(8,128)(2,1)S(1)}, u32[]{:S(2)}, u32[]{:S(2)}) collective-permute-start(bf16[8,4320]{1,0:T(8,128)(2,1)S(1)} %shard_map.75.refs_0_), channel_id=1, source_target_pairs={{0,24},{8,16},{16,8},{24,0},{1,25},{9,17},{17,9},{25,1},{2,26},{10... | collective-permute-start | bytes 207368 | tf_op jit(solution)/shard_map/ppermute | solution.py:366
  41.5 6.0 %collective-permute-start.15 = (bf16[8,4320]{1,0:T(8,128)(2,1)S(1)}, bf16[8,4320]{1,0:T(8,128)(2,1)S(1)}, u32[]{:S(2)}, u32[]{:S(2)}) collective-permute-start(bf16[8,4320]{1,0:T(8,128)(2,1)S(1)} %shard_map.75.refs_0_), channel_id=1, source_target_pairs={{0,16},{8,24},{16,0},{24,8},{1,17},{9,25},{17,1},{25,9},{2,18},{10... | collective-permute-start | bytes 207368 | tf_op jit(solution)/shard_map/ppermute | solution.py:366
  43.1 4.4 %collective-permute-start.14 = (bf16[8,4320]{1,0:T(8,128)(2,1)S(1)}, bf16[8,4320]{1,0:T(8,128)(2,1)S(1)}, u32[]{:S(2)}, u32[]{:S(2)}) collective-permute-start(bf16[8,4320]{1,0:T(8,128)(2,1)S(1)} %shard_map.75.refs_0_), channel_id=1, source_target_pairs={{0,8},{8,0},{16,24},{24,16},{1,9},{9,1},{17,25},{25,17},{2,10},{10... | collective-permute-start | bytes 207368 | tf_op jit(solution)/shard_map/ppermute | solution.py:366

commit v11 on v10

--- a/solution.py
+++ b/solution.py
@@ -88,13 +88,14 @@
     last.start()
     group, slabs = cot.shape[:2]
     rows_per = group // pieces
-    row, col = iota((2 * group * slabs, group * slabs), 0), iota((2 * group * slabs, group * slabs), 1)
-    slab = row // (2 * group) + row // rows_per % 2
-    channel = row % (2 * group) // (2 * rows_per) * rows_per + row % rows_per
-    chosen = one_hot((slab < slabs) & (col == channel * slabs + slab))
+    row, col = iota((group * slabs, group * slabs), 0), iota((group * slabs, group * slabs), 1)
+    chosen = one_hot(col == row % group * slabs + row // group)
     whole.wait()
     flat = cot[...].astype(F32).reshape(-1, CELLS).astype(BF16)
-    parcels[...] = dot(chosen, flat).astype(BF16).reshape(slabs, 2 * group, CELLS)
+    here = dot(chosen, flat).reshape(slabs, pieces, 1, rows_per, CELLS)
+    next_ = jnp.concatenate([here[1:], jnp.zeros_like(here[:1])], axis=0)
+    pair = jnp.concatenate([here, next_], axis=2)
+    parcels[...] = pair.reshape(slabs, 2 * group, CELLS).astype(BF16)
     last.wait()
 
 

time: 48.9 us -> 48.9 us (level)
  no operation moved by 1% of the time
where the time goes in v11:
time: 48.9 us; the launch traced here: 48.4 us
  starting transfers between devices  25.1 us (51%)
  waiting for transfers between devices  13.5 us (28%)
  Pallas kernels  9 us (18%)
  between operations  0.81 us (2%)
    ppermute x16, starting transfers between devices, swap_ranks(): lax.ppermute(block, axis, [(i, i ^ k) for i in range(lax.axis_size(axis))])  11 us
    ppermute x16, waiting for transfers between devices, swap_ranks(): lax.ppermute(block, axis, [(i, i ^ k) for i in range(lax.axis_size(axis))])  10.4 us
    pallas_call x10, Pallas kernels, call(): pl.pallas_call(kernel, out_shape=out_shape, in_specs=[spec(n, spaces) for...  9 us
    all_to_all x1, starting transfers between devices, on_device(): lax.all_to_all(parcels, 'space', split_axis=0, concat_axis=0, tiled=True)  4.88 us
    ppermute x1, starting transfers between devices, from_below(): lax.ppermute(block, axis, [(i - 1, i) for i in range(1, lax.axis_size(axi...  4.85 us
    all_to_all x1, starting transfers between devices, exchanged(): lax.all_to_all(parts, 'space', split_axis=0, concat_axis=0, tiled=True)  4.38 us
    all_to_all x1, waiting for transfers between devices, on_device(): lax.all_to_all(parcels, 'space', split_axis=0, concat_axis=0, tiled=True)  3.02 us
  transfers between devices with their start and end apart: 19, of which 7 were waited for; matrix products, arithmetic and copies ran while one was open for 0% of the time, Pallas kernels for 12%

profile of v11, /device:TPU:0, one launch (start us, length us, event | category | flops | bytes accessed | tf_op | source)
XLA Modules:
  0.0 48.4 jit_solution(10644050981627752984)
XLA Ops:
  0.6 0.0 copy-start.1
  0.6 0.0 copy-start.2
  0.7 1.8 %shard_map.67 = (bf16[8,64,128]{2,1,0:T(8,128)(2,1)}, bf16[1,64,1024]{2,1,0:T(8,128)(2,1)}) custom-call(s32[1]{0:T(128)} %bitcast._.place, s32[1]{0:T(128)} %bitcast.2.__.slot, bf16[32,8,128]{2,1,0:T(8,128)(2,1)} %bitcast.8, bf16[4,64,1024]{2,1,0:T(8,128)(2,1)} %bitcast.5), custom_call_target="tpu_custom_call" | custom-call | flops 1000000000 | bytes 589832 | tf_op jit(solution)/shard_map/pallas_call | solution.py:351
  2.5 4.8 %collective-permute-start = (bf16[1,64,1024]{2,1,0:T(8,128)(2,1)}, bf16[1,64,1024]{2,1,0:T(8,128)(2,1)S(1)}, u32[]{:S(2)}, u32[]{:S(2)}) collective-permute-start(bf16[1,64,1024]{2,1,0:T(8,128)(2,1)} %get-tuple-element.25), channel_id=1, source_target_pairs={{0,1},{1,2},{2,3},{3,4},{4,5},{5,6},{6,7},{8,9},{9,10},{10,11},{11... | collective-permute-start | bytes 393224 | tf_op jit(solution)/shard_map/ppermute | solution.py:375
  7.3 4.9 %all-to-all-start = ((bf16[8,64,128]{2,1,0:T(8,128)(2,1)}), bf16[8,64,128]{2,1,0:T(8,128)(2,1)S(1)}, u32[]{:S(2)}, u32[]{:S(2)}) async-start(bf16[8,64,128]{2,1,0:T(8,128)(2,1)} %get-tuple-element.26), calls=%async_computation | async-start | bytes 262144 | tf_op jit(solution)/shard_map/all_to_all | solution.py:401
  12.2 0.0 copy-start
  12.2 0.0 collective-permute-done.halo
  12.2 0.0 copy-done.1
  12.2 0.0 copy-done.2
  12.2 1.0 %shard_map.68.pack.refs_0_ = bf16[16,64,128]{2,1,0:T(8,128)(2,1)S(1)} custom-call(bf16[4,64,1024]{2,1,0:T(8,128)(2,1)S(1)} %bitcast.6, bf16[1,64,1024]{2,1,0:T(8,128)(2,1)S(1)} %collective-permute-done.halo, bf16[864,128]{1,0:T(8,128)(2,1)S(1)} %copy-done.2), custom_call_target="tpu_custom_call" | custom-call | flops 1000000000 | bytes 876544 | tf_op jit(solution)/shard_map/pallas_call | solution.py:351
  13.3 1.6 %collective-permute-start.2 = (bf16[16,64,128]{2,1,0:T(8,128)(2,1)S(1)}, bf16[16,64,128]{2,1,0:T(8,128)(2,1)S(1)}, u32[]{:S(2)}, u32[]{:S(2)}) collective-permute-start(bf16[16,64,128]{2,1,0:T(8,128)(2,1)S(1)} %shard_map.68.pack.refs_0_), channel_id=1, source_target_pairs={{0,16},{8,24},{16,0},{24,8},{1,17},{9,25},{17,1},{25,9},{2,18},{10... | collective-permute-start | bytes 786440 | tf_op jit(solution)/shard_map/ppermute | solution.py:367
  14.9 0.0 copy-done
  14.9 1.7 %shard_map.71 = bf16[8,64,128]{2,1,0:T(8,128)(2,1)} custom-call(bf16[16,64,128]{2,1,0:T(8,128)(2,1)S(1)} %shard_map.68.pack.refs_0_, bf16[3456,256]{1,0:T(8,128)(2,1)S(1)} %copy-done), custom_call_target="tpu_custom_call" | custom-call | flops 1000000000 | bytes 2031616 | tf_op jit(solution)/shard_map/pallas_call | solution.py:351
  16.5 3.0 %all-to-all-done.cot = bf16[8,64,128]{2,1,0:T(8,128)(2,1)S(1)} async-done(((bf16[8,64,128]{2,1,0:T(8,128)(2,1)}), bf16[8,64,128]{2,1,0:T(8,128)(2,1)S(1)}, u32[]{:S(2)}, u32[]{:S(2)}) %all-to-all-start) | async-done | bytes 131104 | tf_op jit(solution)/shard_map/all_to_all | solution.py:401
  19.6 0.1 collective-permute-start.3
  19.7 1.6 %collective-permute-start.4 = (bf16[8,16,128]{2,1,0:T(8,128)(2,1)S(1)}, bf16[8,16,128]{2,1,0:T(8,128)(2,1)S(1)}, u32[]{:S(2)}, u32[]{:S(2)}) collective-permute-start(bf16[8,16,128]{2,1,0:T(8,128)(2,1)S(1)} %get-tuple-element.31), channel_id=1, source_target_pairs={{0,16},{8,24},{16,0},{24,8},{1,17},{9,25},{17,1},{25,9},{2,18},{10... | collective-permute-start | bytes 98312 | tf_op jit(solution)/shard_map/ppermute | solution.py:367
  21.2 0.3 collective-permute-start.5
  21.5 0.3 collective-permute-start.1
  21.9 2.7 %shard_map.69 = (bf16[64,864]{1,0:T(8,128)(2,1)S(1)}, bf16[64,864]{1,0:T(8,128)(2,1)S(1)}) custom-call(s32[1]{0:T(128)} %bitcast._.place, s32[1]{0:T(128)} %bitcast.2.__.slot, bf16[4,64,1024]{2,1,0:T(8,128)(2,1)S(1)} %bitcast.7, bf16[1,64,1024]{2,1,0:T(8,128)(2,1)S(1)} %collective-permute-done.halo, bf16[864,128]{1,0:T(8,128)(2,1)S(1)} %copy-done.2, ...), custom_call_target="tpu_custom_call" | custom-call | flops 1000000000 | bytes 2777096 | tf_op jit(solution)/shard_map/pallas_call | solution.py:351
  24.6 0.0 collective-permute-done.3.refs_1_
  24.6 0.0 collective-permute-done.4.refs_2_
  24.6 0.0 collective-permute-done.5.refs_3_
  24.6 0.0 collective-permute-done.2.refs_2_
  24.6 0.2 collective-permute-start.6
  24.8 0.3 collective-permute-start.7
  25.2 0.3 shard_map.72.refs_4_
  25.5 0.9 %collective-permute-done.7.refs_6_ = bf16[64,864]{1,0:T(8,128)(2,1)S(1)} collective-permute-done((bf16[64,864]{1,0:T(8,128)(2,1)S(1)}, bf16[64,864]{1,0:T(8,128)(2,1)S(1)}, u32[]{:S(2)}, u32[]{:S(2)}) %collective-permute-start.7) | collective-permute-done | bytes 110624 | tf_op jit(solution)/shard_map/ppermute | solution.py:367
  26.4 0.0 collective-permute-done.1.refs_1_
  26.4 0.0 collective-permute-done.6.refs_3_
  26.4 0.5 %shard_map.73 = (f32[8,4320]{1,0:T(8,128)S(1)}, bf16[8,4320]{1,0:T(8,128)(2,1)S(1)}, bf16[8,4320]{1,0:T(8,128)(2,1)S(1)}, bf16[8,4320]{1,0:T(8,128)(2,1)S(1)}, b...) custom-call(bf16[16,64,128]{2,1,0:T(8,128)(2,1)S(1)} %shard_map.68.pack.refs_0_, ...), custom_call_target="tpu_custom_call" | custom-call | flops 1000000000 | bytes 1794048 | tf_op jit(solution)/shard_map/pallas_call | solution.py:351
  26.9 0.3 collective-permute-start.11
  27.2 1.8 %collective-permute-start.8 = (bf16[8,4320]{1,0:T(8,128)(2,1)S(1)}, bf16[8,4320]{1,0:T(8,128)(2,1)S(1)}, u32[]{:S(2)}, u32[]{:S(2)}) collective-permute-start(bf16[8,4320]{1,0:T(8,128)(2,1)S(1)} %get-tuple-element.36), channel_id=1, source_target_pairs={{0,1},{1,0},{2,3},{3,2},{4,5},{5,4},{6,7},{7,6},{8,9},{9,8},{10,11... | collective-permute-start | bytes 207368 | tf_op jit(solution)/shard_map/ppermute | solution.py:367
  29.0 0.0 collective-permute-start.9
  29.0 1.7 %collective-permute-start.10 = (bf16[8,4320]{1,0:T(8,128)(2,1)S(1)}, bf16[8,4320]{1,0:T(8,128)(2,1)S(1)}, u32[]{:S(2)}, u32[]{:S(2)}) collective-permute-start(bf16[8,4320]{1,0:T(8,128)(2,1)S(1)} %get-tuple-element.38), channel_id=1, source_target_pairs={{0,3},{1,2},{2,1},{3,0},{4,7},{5,6},{6,5},{7,4},{8,11},{9,10},{10,... | collective-permute-start | bytes 207368 | tf_op jit(solution)/shard_map/ppermute | solution.py:367
  30.6 4.3 %collective-permute-done.11.lent = bf16[2,8,4320]{2,1,0:T(8,128)(2,1)S(1)} collective-permute-done((bf16[2,8,4320]{2,1,0:T(8,128)(2,1)S(1)}, bf16[2,8,4320]{2,1,0:T(8,128)(2,1)S(1)}, u32[]{:S(2)}, u32[]{:S(2)}) %collective-permute-start.11) | collective-permute-done | bytes 138272 | tf_op jit(solution)/shard_map/ppermute | solution.py:367
  35.0 0.1 collective-permute-start.12
  35.0 0.8 %collective-permute-start.13 = (bf16[8,4320]{1,0:T(8,128)(2,1)S(1)}, bf16[8,4320]{1,0:T(8,128)(2,1)S(1)}, u32[]{:S(2)}, u32[]{:S(2)}) collective-permute-start(bf16[8,4320]{1,0:T(8,128)(2,1)S(1)} %get-tuple-element.42), channel_id=1, source_target_pairs={{0,6},{1,7},{2,4},{3,5},{4,2},{5,3},{6,0},{7,1},{8,14},{9,15},{10,... | collective-permute-start | bytes 207368 | tf_op jit(solution)/shard_map/ppermute | solution.py:367
  35.8 4.4 %all-to-all-start.1 = ((bf16[8,64,128]{2,1,0:T(8,128)(2,1)}), bf16[8,64,128]{2,1,0:T(8,128)(2,1)S(1)}, u32[]{:S(2)}, u32[]{:S(2)}) async-start(bf16[8,64,128]{2,1,0:T(8,128)(2,1)} %shard_map.71), calls=%async_computation.1 | async-start | bytes 262144 | tf_op jit(solution)/shard_map/all_to_all | solution.py:429
  40.2 0.0 collective-permute-done.8.refs_0_
  40.2 0.0 collective-permute-done.9.refs_1_
  40.2 0.0 collective-permute-done.10.refs_2_
  40.2 0.0 collective-permute-done.12.refs_3_
  40.3 1.1 %collective-permute-done.13.refs_4_ = bf16[8,4320]{1,0:T(8,128)(2,1)S(1)} collective-permute-done((bf16[8,4320]{1,0:T(8,128)(2,1)S(1)}, bf16[8,4320]{1,0:T(8,128)(2,1)S(1)}, u32[]{:S(2)}, u32[]{:S(2)}) %collective-permute-start.13) | collective-permute-done | bytes 69152 | tf_op jit(solution)/shard_map/ppermute | solution.py:367
  41.3 0.1 shard_map.75.refs_0_
  41.4 0.1 collective-permute-start.16
  41.5 1.6 %collective-permute-start.15 = (bf16[8,4320]{1,0:T(8,128)(2,1)S(1)}, bf16[8,4320]{1,0:T(8,128)(2,1)S(1)}, u32[]{:S(2)}, u32[]{:S(2)}) collective-permute-start(bf16[8,4320]{1,0:T(8,128)(2,1)S(1)} %shard_map.75.refs_0_), channel_id=1, source_target_pairs={{0,16},{8,24},{16,0},{24,8},{1,17},{9,25},{17,1},{25,9},{2,18},{10... | collective-permute-start | bytes 207368 | tf_op jit(solution)/shard_map/ppermute | solution.py:367
  43.1 0.3 collective-permute-start.14
  43.3 2.5 %collective-permute-done.16.refs_3_ = bf16[8,4320]{1,0:T(8,128)(2,1)S(1)} collective-permute-done((bf16[8,4320]{1,0:T(8,128)(2,1)S(1)}, bf16[8,4320]{1,0:T(8,128)(2,1)S(1)}, u32[]{:S(2)}, u32[]{:S(2)}) %collective-permute-start.16) | collective-permute-done | bytes 69152 | tf_op jit(solution)/shard_map/ppermute | solution.py:367
  45.9 1.6 %collective-permute-done.15.refs_2_ = bf16[8,4320]{1,0:T(8,128)(2,1)S(1)} collective-permute-done((bf16[8,4320]{1,0:T(8,128)(2,1)S(1)}, bf16[8,4320]{1,0:T(8,128)(2,1)S(1)}, u32[]{:S(2)}, u32[]{:S(2)}) %collective-permute-start.15) | collective-permute-done | bytes 69152 | tf_op jit(solution)/shard_map/ppermute | solution.py:367
  47.4 0.0 collective-permute-done.14.refs_1_
  47.4 0.1 all-to-all-done.1.refs_4_
  47.5 0.9 %shard_map.76 = (f32[16,864]{1,0:T(8,128)}, f32[32,3456]{1,0:T(8,128)}, bf16[32,8,128]{2,1,0:T(8,128)(2,1)}) custom-call(s32[1]{0:T(128)} %bitcast._.place, bf16[8,4320]{1,0:T(8,128)(2,1)S(1)} %shard_map.75.refs_0_, bf16[8,4320]{1,0:T(8,128)(2,1)S(1)} %collective-permute-done.14.refs_1_, bf16[8,4320]{1,0:T(8,128)(2,1)S(1)} %collective-permute-done.15.refs_2_, ...), custom_call_target="tpu_custom_call" | custom-call | flops 1000000000 | bytes 407556 | tf_op jit(solution)/shard_map/pallas_call | solution.py:351
  (2 shorter events, 0.1 us)
Async XLA Ops:
  0.6 11.6 %copy-start.1 = (bf16[1,4,64,1024]{3,2,1,0:T(8,128)(2,1)S(1)}, bf16[1,4,64,1024]{3,2,1,0:T(8,128)(2,1)}, u32[]{:S(2)}) copy-start(bf16[1,4,64,1024]{3,2,1,0:T(8,128)(2,1)} %param.4) | copy-start | bytes 1572868
  0.6 11.6 %copy-start.2 = (bf16[864,128]{1,0:T(8,128)(2,1)S(1)}, bf16[864,128]{1,0:T(8,128)(2,1)}, u32[]{:S(2)}) copy-start(bf16[864,128]{1,0:T(8,128)(2,1)} %w1.3) | copy-start | bytes 663556
  2.5 9.8 %collective-permute-start = (bf16[1,64,1024]{2,1,0:T(8,128)(2,1)}, bf16[1,64,1024]{2,1,0:T(8,128)(2,1)S(1)}, u32[]{:S(2)}, u32[]{:S(2)}) collective-permute-start(bf16[1,64,1024]{2,1,0:T(8,128)(2,1)} %get-tuple-element.25), channel_id=1, source_target_pairs={{0,1},{1,2},{2,3},{3,4},{4,5},{5,6},{6,7},{8,9},{9,10},{10,11},{11... | collective-permute-start | bytes 393224 | tf_op jit(solution)/shard_map/ppermute | solution.py:375
  7.3 12.2 %all-to-all-start = ((bf16[8,64,128]{2,1,0:T(8,128)(2,1)}), bf16[8,64,128]{2,1,0:T(8,128)(2,1)S(1)}, u32[]{:S(2)}, u32[]{:S(2)}) async-start(bf16[8,64,128]{2,1,0:T(8,128)(2,1)} %get-tuple-element.26), calls=%async_computation | async-start | bytes 262144 | tf_op jit(solution)/shard_map/all_to_all | solution.py:401
  12.2 2.7 %copy-start = (bf16[3456,256]{1,0:T(8,128)(2,1)S(1)}, bf16[3456,256]{1,0:T(8,128)(2,1)}, u32[]{:S(2)}) copy-start(bf16[3456,256]{1,0:T(8,128)(2,1)} %w2.3) | copy-start | bytes 5308420
  13.3 11.3 %collective-permute-start.2 = (bf16[16,64,128]{2,1,0:T(8,128)(2,1)S(1)}, bf16[16,64,128]{2,1,0:T(8,128)(2,1)S(1)}, u32[]{:S(2)}, u32[]{:S(2)}) collective-permute-start(bf16[16,64,128]{2,1,0:T(8,128)(2,1)S(1)} %shard_map.68.pack.refs_0_), channel_id=1, source_target_pairs={{0,16},{8,24},{16,0},{24,8},{1,17},{9,25},{17,1},{25,9},{2,18},{10... | collective-permute-start | bytes 786440 | tf_op jit(solution)/shard_map/ppermute | solution.py:367
  19.6 5.0 %collective-permute-start.3 = (bf16[8,16,128]{2,1,0:T(8,128)(2,1)S(1)}, bf16[8,16,128]{2,1,0:T(8,128)(2,1)S(1)}, u32[]{:S(2)}, u32[]{:S(2)}) collective-permute-start(bf16[8,16,128]{2,1,0:T(8,128)(2,1)S(1)} %get-tuple-element.30), channel_id=1, source_target_pairs={{0,8},{8,0},{16,24},{24,16},{1,9},{9,1},{17,25},{25,17},{2,10},{10... | collective-permute-start | bytes 98312 | tf_op jit(solution)/shard_map/ppermute | solution.py:367
  19.7 4.9 %collective-permute-start.4 = (bf16[8,16,128]{2,1,0:T(8,128)(2,1)S(1)}, bf16[8,16,128]{2,1,0:T(8,128)(2,1)S(1)}, u32[]{:S(2)}, u32[]{:S(2)}) collective-permute-start(bf16[8,16,128]{2,1,0:T(8,128)(2,1)S(1)} %get-tuple-element.31), channel_id=1, source_target_pairs={{0,16},{8,24},{16,0},{24,8},{1,17},{9,25},{17,1},{25,9},{2,18},{10... | collective-permute-start | bytes 98312 | tf_op jit(solution)/shard_map/ppermute | solution.py:367
  21.2 3.3 %collective-permute-start.5 = (bf16[8,16,128]{2,1,0:T(8,128)(2,1)S(1)}, bf16[8,16,128]{2,1,0:T(8,128)(2,1)S(1)}, u32[]{:S(2)}, u32[]{:S(2)}) collective-permute-start(bf16[8,16,128]{2,1,0:T(8,128)(2,1)S(1)} %get-tuple-element.32), channel_id=1, source_target_pairs={{0,24},{8,16},{16,8},{24,0},{1,25},{9,17},{17,9},{25,1},{2,26},{10... | collective-permute-start | bytes 98312 | tf_op jit(solution)/shard_map/ppermute | solution.py:367
  21.5 4.8 %collective-permute-start.1 = (bf16[16,64,128]{2,1,0:T(8,128)(2,1)S(1)}, bf16[16,64,128]{2,1,0:T(8,128)(2,1)S(1)}, u32[]{:S(2)}, u32[]{:S(2)}) collective-permute-start(bf16[16,64,128]{2,1,0:T(8,128)(2,1)S(1)} %shard_map.68.pack.refs_0_), channel_id=1, source_target_pairs={{0,8},{8,0},{16,24},{24,16},{1,9},{9,1},{17,25},{25,17},{2,10},{10... | collective-permute-start | bytes 786440 | tf_op jit(solution)/shard_map/ppermute | solution.py:367
  24.6 1.8 %collective-permute-start.6 = (bf16[16,64,128]{2,1,0:T(8,128)(2,1)S(1)}, bf16[16,64,128]{2,1,0:T(8,128)(2,1)S(1)}, u32[]{:S(2)}, u32[]{:S(2)}) collective-permute-start(bf16[16,64,128]{2,1,0:T(8,128)(2,1)S(1)} %collective-permute-done.2.refs_2_), channel_id=1, source_target_pairs={{0,8},{8,0},{16,24},{24,16},{1,9},{9,1},{17,25},{25,17},{2,10},{10... | collective-permute-start | bytes 786440 | tf_op jit(solution)/shard_map/ppermute | solution.py:367
  24.8 1.5 %collective-permute-start.7 = (bf16[64,864]{1,0:T(8,128)(2,1)S(1)}, bf16[64,864]{1,0:T(8,128)(2,1)S(1)}, u32[]{:S(2)}, u32[]{:S(2)}) collective-permute-start(bf16[64,864]{1,0:T(8,128)(2,1)S(1)} %get-tuple-element.29), channel_id=1, source_target_pairs={{0,8},{8,0},{16,24},{24,16},{1,9},{9,1},{17,25},{25,17},{2,10},{10... | collective-permute-start | bytes 331784 | tf_op jit(solution)/shard_map/ppermute | solution.py:367
  26.9 8.0 %collective-permute-start.11 = (bf16[2,8,4320]{2,1,0:T(8,128)(2,1)S(1)}, bf16[2,8,4320]{2,1,0:T(8,128)(2,1)S(1)}, u32[]{:S(2)}, u32[]{:S(2)}) collective-permute-start(bf16[2,8,4320]{2,1,0:T(8,128)(2,1)S(1)} %get-tuple-element.39), channel_id=1, source_target_pairs={{0,1},{1,0},{2,3},{3,2},{4,5},{5,4},{6,7},{7,6},{8,9},{9,8},{10,11... | collective-permute-start | bytes 414728 | tf_op jit(solution)/shard_map/ppermute | solution.py:367
  27.2 13.1 %collective-permute-start.8 = (bf16[8,4320]{1,0:T(8,128)(2,1)S(1)}, bf16[8,4320]{1,0:T(8,128)(2,1)S(1)}, u32[]{:S(2)}, u32[]{:S(2)}) collective-permute-start(bf16[8,4320]{1,0:T(8,128)(2,1)S(1)} %get-tuple-element.36), channel_id=1, source_target_pairs={{0,1},{1,0},{2,3},{3,2},{4,5},{5,4},{6,7},{7,6},{8,9},{9,8},{10,11... | collective-permute-start | bytes 207368 | tf_op jit(solution)/shard_map/ppermute | solution.py:367
  29.0 11.2 %collective-permute-start.9 = (bf16[8,4320]{1,0:T(8,128)(2,1)S(1)}, bf16[8,4320]{1,0:T(8,128)(2,1)S(1)}, u32[]{:S(2)}, u32[]{:S(2)}) collective-permute-start(bf16[8,4320]{1,0:T(8,128)(2,1)S(1)} %get-tuple-element.37), channel_id=1, source_target_pairs={{0,2},{1,3},{2,0},{3,1},{4,6},{5,7},{6,4},{7,5},{8,10},{9,11},{10,... | collective-permute-start | bytes 207368 | tf_op jit(solution)/shard_map/ppermute | solution.py:367
  29.0 11.3 %collective-permute-start.10 = (bf16[8,4320]{1,0:T(8,128)(2,1)S(1)}, bf16[8,4320]{1,0:T(8,128)(2,1)S(1)}, u32[]{:S(2)}, u32[]{:S(2)}) collective-permute-start(bf16[8,4320]{1,0:T(8,128)(2,1)S(1)} %get-tuple-element.38), channel_id=1, source_target_pairs={{0,3},{1,2},{2,1},{3,0},{4,7},{5,6},{6,5},{7,4},{8,11},{9,10},{10,... | collective-permute-start | bytes 207368 | tf_op jit(solution)/shard_map/ppermute | solution.py:367
  35.0 5.3 %collective-permute-start.12 = (bf16[8,4320]{1,0:T(8,128)(2,1)S(1)}, bf16[8,4320]{1,0:T(8,128)(2,1)S(1)}, u32[]{:S(2)}, u32[]{:S(2)}) collective-permute-start(bf16[8,4320]{1,0:T(8,128)(2,1)S(1)} %get-tuple-element.41), channel_id=1, source_target_pairs={{0,4},{1,5},{2,6},{3,7},{4,0},{5,1},{6,2},{7,3},{8,12},{9,13},{10,... | collective-permute-start | bytes 207368 | tf_op jit(solution)/shard_map/ppermute | solution.py:367
  35.0 6.3 %collective-permute-start.13 = (bf16[8,4320]{1,0:T(8,128)(2,1)S(1)}, bf16[8,4320]{1,0:T(8,128)(2,1)S(1)}, u32[]{:S(2)}, u32[]{:S(2)}) collective-permute-start(bf16[8,4320]{1,0:T(8,128)(2,1)S(1)} %get-tuple-element.42), channel_id=1, source_target_pairs={{0,6},{1,7},{2,4},{3,5},{4,2},{5,3},{6,0},{7,1},{8,14},{9,15},{10,... | collective-permute-start | bytes 207368 | tf_op jit(solution)/shard_map/ppermute | solution.py:367
  35.8 11.7 %all-to-all-start.1 = ((bf16[8,64,128]{2,1,0:T(8,128)(2,1)}), bf16[8,64,128]{2,1,0:T(8,128)(2,1)S(1)}, u32[]{:S(2)}, u32[]{:S(2)}) async-start(bf16[8,64,128]{2,1,0:T(8,128)(2,1)} %shard_map.71), calls=%async_computation.1 | async-start | bytes 262144 | tf_op jit(solution)/shard_map/all_to_all | solution.py:429
  41.4 4.5 %collective-permute-start.16 = (bf16[8,4320]{1,0:T(8,128)(2,1)S(1)}, bf16[8,4320]{1,0:T(8,128)(2,1)S(1)}, u32[]{:S(2)}, u32[]{:S(2)}) collective-permute-start(bf16[8,4320]{1,0:T(8,128)(2,1)S(1)} %shard_map.75.refs_0_), channel_id=1, source_target_pairs={{0,24},{8,16},{16,8},{24,0},{1,25},{9,17},{17,9},{25,1},{2,26},{10... | collective-permute-start | bytes 207368 | tf_op jit(solution)/shard_map/ppermute | solution.py:367
  41.5 6.0 %collective-permute-start.15 = (bf16[8,4320]{1,0:T(8,128)(2,1)S(1)}, bf16[8,4320]{1,0:T(8,128)(2,1)S(1)}, u32[]{:S(2)}, u32[]{:S(2)}) collective-permute-start(bf16[8,4320]{1,0:T(8,128)(2,1)S(1)} %shard_map.75.refs_0_), channel_id=1, source_target_pairs={{0,16},{8,24},{16,0},{24,8},{1,17},{9,25},{17,1},{25,9},{2,18},{10... | collective-permute-start | bytes 207368 | tf_op jit(solution)/shard_map/ppermute | solution.py:367
  43.1 4.4 %collective-permute-start.14 = (bf16[8,4320]{1,0:T(8,128)(2,1)S(1)}, bf16[8,4320]{1,0:T(8,128)(2,1)S(1)}, u32[]{:S(2)}, u32[]{:S(2)}) collective-permute-start(bf16[8,4320]{1,0:T(8,128)(2,1)S(1)} %shard_map.75.refs_0_), channel_id=1, source_target_pairs={{0,8},{8,0},{16,24},{24,16},{1,9},{9,1},{17,25},{25,17},{2,10},{10... | collective-permute-start | bytes 207368 | tf_op jit(solution)/shard_map/ppermute | solution.py:367
